TPU v7x, 32 devices: a whole 2x2x4 slice. The times are simulated.
32 devices in a mesh: dom: 16 (over z, x, core), sub: 2 (over y).
Axes of the slice: x: 2, y: 2, z: 4, core: 2. Of those that a mesh axis runs over, the one named last changes fastest.
Arguments:
- rhs_local: float32 [128, 64, 128], P('dom', 'sub'), may hold values from -8 to 8
- coefficient: float32 [128, 64, 128], P('dom', 'sub'), may hold values from 0.3 to 3
Outputs:
- preconditioned: float32 [128, 64, 128], P('dom', 'sub')
- coarse_solution: float32 [32, 16, 32], P('dom', 'sub')
All inputs are finite; a program needn't handle non-finite values.
Results may differ from a plain program's by a relative error of at most 0.0003.
Values sent between devices are 32-bit elements; how exact they have to be, the bound alone decides.
No kernel may reach another device: no remote copies, remote signals or barrier semaphores. Data moves between devices by JAX's collectives and lax.ppermute only.
A program may use at most 64 MiB of HBM per device.

v0:
```python
import jax
import jax.numpy as jnp
import numpy as np
from jax import lax
from jax.sharding import PartitionSpec as P

EZ = 16


def extended(block, sides, width):
    for axis, dim in sides:
        count = lax.axis_size(axis)
        forward = [(i, i + 1) for i in range(count - 1)]
        backward = [(target, source) for source, target in forward]
        low = lax.ppermute(
            lax.slice_in_dim(block, block.shape[dim] - width, None, axis=dim), axis, forward
        )
        high = lax.ppermute(lax.slice_in_dim(block, 0, width, axis=dim), axis, backward)
        block = jnp.concatenate([low, block, high], axis=dim)
    return block


def legendre_value(points, degree):
    previous = np.ones(points.shape)
    current = points.copy()
    for level in range(1, degree):
        following = ((2 * level + 1) * points * current - level * previous) / (level + 1)
        previous = current
        current = following
    return current


def tables():
    degree = 7
    points = np.array(
        [
            -1.0,
            -0.8717401485096066,
            -0.5917001814331423,
            -0.2092992179024789,
            0.2092992179024789,
            0.5917001814331423,
            0.8717401485096066,
            1.0,
        ]
    )
    values = legendre_value(points, degree)
    weights = 2.0 / (degree * (degree + 1) * values**2)
    derivative = np.zeros((8, 8))
    for row_at in range(8):
        for col_at in range(8):
            if row_at != col_at:
                derivative[row_at, col_at] = values[row_at] / (
                    values[col_at] * (points[row_at] - points[col_at])
                )
    derivative[0, 0] = -degree * (degree + 1) / 4.0
    derivative[7, 7] = degree * (degree + 1) / 4.0
    interp = np.stack([(1.0 - points) / 2.0, (1.0 + points) / 2.0], axis=1)
    slopes = np.array([-0.5, 0.5])
    return (derivative, weights, interp, slopes)


def fold_local(field, axis_at, per_elem):
    dims_of = field.shape
    elements = dims_of[axis_at] // per_elem
    split = field.reshape(dims_of[:axis_at] + (elements, per_elem) + dims_of[axis_at + 1 :])
    first_face = lax.index_in_dim(split, 0, axis_at + 1, keepdims=False)
    last_face = lax.index_in_dim(split, per_elem - 1, axis_at + 1, keepdims=False)
    empty_face = jnp.zeros_like(lax.slice_in_dim(first_face, 0, 1, axis=axis_at))
    from_left = jnp.concatenate(
        [empty_face, lax.slice_in_dim(last_face, 0, elements - 1, axis=axis_at)], axis_at
    )
    from_right = jnp.concatenate(
        [lax.slice_in_dim(first_face, 1, elements, axis=axis_at), empty_face], axis_at
    )
    middle = lax.slice_in_dim(split, 1, per_elem - 1, axis=axis_at + 1)
    joined = jnp.concatenate(
        [
            jnp.expand_dims(first_face + from_left, axis_at + 1),
            middle,
            jnp.expand_dims(last_face + from_right, axis_at + 1),
        ],
        axis_at + 1,
    )
    return joined.reshape(dims_of)


def fold_rim(padded, axis_at):
    length = padded.shape[axis_at] - 2
    inside = lax.slice_in_dim(padded, 1, length + 1, axis=axis_at)
    low_side = lax.slice_in_dim(inside, 0, 1, axis=axis_at) + lax.slice_in_dim(
        padded, 0, 1, axis=axis_at
    )
    high_side = lax.slice_in_dim(inside, length - 1, length, axis=axis_at) + lax.slice_in_dim(
        padded, length + 1, length + 2, axis=axis_at
    )
    return jnp.concatenate(
        [low_side, lax.slice_in_dim(inside, 1, length - 1, axis=axis_at), high_side], axis_at
    )


def assemble(stacked):
    local = fold_local(fold_local(fold_local(stacked, 1, 8), 2, 8), 3, 8)
    padded = extended(local, (("dom", 1),), 1)
    partial_value = fold_rim(padded, 1)
    padded_y = extended(partial_value, (("sub", 2),), 1)
    result = fold_rim(padded_y, 2)
    return result


def coarse_assemble(stacked):
    local = fold_local(fold_local(fold_local(stacked, 1, 2), 2, 2), 3, 2)
    padded = extended(local, (("dom", 1), ("sub", 2)), 1)
    result = fold_rim(fold_rim(padded, 1), 2)
    return result


def edge_mask(length, start, total):
    spots = jnp.arange(length) + start
    return ((spots > 0) & (spots < total - 1)).astype(jnp.float32)


def weight_field(size_x, size_y, size_z, weights):
    wvec = jnp.asarray(weights, jnp.float32)
    along_x = jnp.tile(wvec, size_x // 8)
    along_y = jnp.tile(wvec, size_y // 8)
    along_z = jnp.tile(wvec, size_z // 8)
    return along_x[:, None, None] * along_y[None, :, None] * along_z[None, None, :]


def local_operator(field, weighted, derivative, z_matrix):
    size_x, size_y, size_z = field.shape
    precise = lax.Precision.HIGHEST
    z_block = z_matrix.shape[0]
    grad_x = jnp.einsum(
        "ab,ebyz->eayz",
        derivative,
        field.reshape(size_x // 8, 8, size_y, size_z),
        precision=precise,
    ).reshape(field.shape)
    grad_y = jnp.einsum(
        "ab,xebz->xeaz",
        derivative,
        field.reshape(size_x, size_y // 8, 8, size_z),
        precision=precise,
    ).reshape(field.shape)
    grad_z = jnp.dot(
        field.reshape(-1, z_block),
        z_matrix.T,
        precision=precise,
        preferred_element_type=jnp.float32,
    ).reshape(field.shape)
    flux_x = (weighted * grad_x).reshape(size_x // 8, 8, size_y, size_z)
    flux_y = (weighted * grad_y).reshape(size_x, size_y // 8, 8, size_z)
    flux_z = (weighted * grad_z).reshape(-1, z_block)
    back_x = jnp.einsum("ab,eayz->ebyz", derivative, flux_x, precision=precise).reshape(field.shape)
    back_y = jnp.einsum("ab,xeaz->xebz", derivative, flux_y, precision=precise).reshape(field.shape)
    back_z = jnp.dot(
        flux_z, z_matrix, precision=precise, preferred_element_type=jnp.float32
    ).reshape(field.shape)
    return back_x + back_y + back_z


def diagonal_local(weighted, derivative, z_matrix):
    size_x, size_y, size_z = weighted.shape
    precise = lax.Precision.HIGHEST
    squared = derivative * derivative
    z_block = z_matrix.shape[0]
    part_x = jnp.einsum(
        "ka,ekyz->eayz",
        squared,
        weighted.reshape(size_x // 8, 8, size_y, size_z),
        precision=precise,
    ).reshape(weighted.shape)
    part_y = jnp.einsum(
        "ka,xekz->xeaz",
        squared,
        weighted.reshape(size_x, size_y // 8, 8, size_z),
        precision=precise,
    ).reshape(weighted.shape)
    part_z = jnp.dot(
        weighted.reshape(-1, z_block),
        z_matrix * z_matrix,
        precision=precise,
        preferred_element_type=jnp.float32,
    ).reshape(weighted.shape)
    return part_x + part_y + part_z


def restrict(field, interp):
    size_x, size_y, size_z = field.shape
    precise = lax.Precision.HIGHEST
    section_x = jnp.einsum(
        "ai,eayz->eiyz", interp, field.reshape(size_x // 8, 8, size_y, size_z), precision=precise
    ).reshape(size_x // 4, size_y, size_z)
    section_y = jnp.einsum(
        "ai,xeaz->xeiz",
        interp,
        section_x.reshape(size_x // 4, size_y // 8, 8, size_z),
        precision=precise,
    ).reshape(size_x // 4, size_y // 4, size_z)
    section_z = jnp.einsum(
        "ai,xyea->xyei",
        interp,
        section_y.reshape(size_x // 4, size_y // 4, size_z // 8, 8),
        precision=precise,
    )
    return section_z.reshape(size_x // 4, size_y // 4, size_z // 4)


def prolong(coarse, interp):
    size_x, size_y, size_z = coarse.shape
    precise = lax.Precision.HIGHEST
    section_z = jnp.einsum(
        "ai,xyei->xyea", interp, coarse.reshape(size_x, size_y, size_z // 2, 2), precision=precise
    ).reshape(size_x, size_y, size_z * 4)
    section_y = jnp.einsum(
        "ai,xeiz->xeaz",
        interp,
        section_z.reshape(size_x, size_y // 2, 2, size_z * 4),
        precision=precise,
    ).reshape(size_x, size_y * 4, size_z * 4)
    section_x = jnp.einsum(
        "ai,eiyz->eayz",
        interp,
        section_y.reshape(size_x // 2, 2, size_y * 4, size_z * 4),
        precision=precise,
    )
    return section_x.reshape(size_x * 4, size_y * 4, size_z * 4)


def coarse_matrices(weighted, interp, slopes):
    size_x, size_y, size_z = weighted.shape
    precise = lax.Precision.HIGHEST
    shaped = weighted.reshape(size_x // 8, 8, size_y // 8, 8, size_z // 8, 8)
    interp_t = interp.T
    mass_pair = jnp.asarray(interp_t[:, None, :] * interp_t[None, :, :], jnp.float32)
    grad_pair = jnp.asarray(
        slopes[:, None, None] * slopes[None, :, None] * np.ones((1, 1, 8)), jnp.float32
    )
    form = "xaybzc,ipa,jqb,krc->ijkpqrxyz"
    total = jnp.einsum(form, shaped, grad_pair, mass_pair, mass_pair, precision=precise)
    total = total + jnp.einsum(form, shaped, mass_pair, grad_pair, mass_pair, precision=precise)
    total = total + jnp.einsum(form, shaped, mass_pair, mass_pair, grad_pair, precision=precise)
    return total.reshape(8, 8, -1)


def coarse_diagonal(galerkin, ex_n, ey_n, ez_n):
    eye_table = jnp.eye(8, dtype=jnp.float32)
    flat = jnp.sum(galerkin * eye_table[:, :, None], axis=1)
    return (
        flat.reshape(2, 2, 2, ex_n, ey_n, ez_n)
        .transpose(3, 0, 4, 1, 5, 2)
        .reshape(2 * ex_n, 2 * ey_n, 2 * ez_n)
    )


def coarse_apply(galerkin, coarse):
    size_x, size_y, size_z = coarse.shape
    ex_n, ey_n, ez_n = (size_x // 2, size_y // 2, size_z // 2)
    flat = coarse.reshape(ex_n, 2, ey_n, 2, ez_n, 2).transpose(1, 3, 5, 0, 2, 4).reshape(8, -1)
    result = jnp.sum(galerkin * flat[None, :, :], axis=1)
    return (
        result.reshape(2, 2, 2, ex_n, ey_n, ez_n).transpose(3, 0, 4, 1, 5, 2).reshape(coarse.shape)
    )


def shards(rhs_local, coefficient):
    derivative_np, weights, interp_np, slopes = tables()
    derivative = jnp.asarray(derivative_np, jnp.float32)
    interp = jnp.asarray(interp_np, jnp.float32)
    z_block = min(EZ, 16)
    z_matrix = jnp.asarray(np.kron(np.eye(z_block), derivative_np), jnp.float32)
    size_x, size_y, size_z = rhs_local.shape
    dom_count = lax.axis_size("dom")
    sub_count = lax.axis_size("sub")
    dom_index = lax.axis_index("dom")
    sub_index = lax.axis_index("sub")
    weighted = coefficient * weight_field(size_x, size_y, size_z, weights)
    fmask = (
        edge_mask(size_x, dom_index * size_x, size_x * dom_count)[:, None, None]
        * edge_mask(size_y, sub_index * size_y, size_y * sub_count)[None, :, None]
        * edge_mask(size_z, 0, size_z)[None, None, :]
    )

    def operate(field):
        return fmask * assemble(local_operator(field, weighted, derivative, z_matrix)[None])[0]

    summed = assemble(jnp.stack([rhs_local, diagonal_local(weighted, derivative, z_matrix)]))
    residual = fmask * summed[0]
    inverse = fmask / summed[1]
    theta = 1.1
    delta = 0.9
    sigma_val = theta / delta
    rho_prev = 1.0 / sigma_val
    rho_next = 1.0 / (2.0 * sigma_val - rho_prev)
    step_one = inverse * residual / theta
    res_one = residual - operate(step_one)
    second = step_one + rho_next * rho_prev * step_one + 2.0 * rho_next / delta * inverse * res_one
    res_two = residual - operate(second)
    elem_x, elem_y, elem_z = (size_x // 8, size_y // 8, size_z // 8)
    galerkin = coarse_matrices(weighted, interp_np, slopes)
    coarse_stack = jnp.stack(
        [restrict(res_two, interp), coarse_diagonal(galerkin, elem_x, elem_y, elem_z)]
    )
    own_y = coarse_stack.shape[2]
    y_start = sub_index * own_y
    coarse_x, coarse_y, coarse_z = coarse_stack.shape[1:]
    cmask = (
        edge_mask(coarse_x, dom_index * coarse_x, coarse_x * dom_count)[:, None, None]
        * edge_mask(coarse_y, y_start, own_y * sub_count)[None, :, None]
        * edge_mask(coarse_z, 0, coarse_z)[None, None, :]
    )
    assembled = coarse_assemble(coarse_stack)
    coarse_rhs = cmask * assembled[0]
    coarse_diag = assembled[1]
    coarse_one = 2.0 / 3.0 * coarse_rhs / coarse_diag
    image_c = cmask * coarse_assemble(coarse_apply(galerkin, coarse_one)[None])[0]
    coarse_solution = coarse_one + 2.0 / 3.0 * (coarse_rhs - image_c) / coarse_diag
    preconditioned = second + fmask * prolong(coarse_solution, interp)
    return (preconditioned, coarse_solution)


def solution(mesh):
    return jax.shard_map(
        shards,
        mesh=mesh,
        in_specs=(P("dom", "sub", None), P("dom", "sub", None)),
        out_specs=(P("dom", "sub", None), P("dom", "sub", None)),
        check_vma=False,
    )
```

profile of v0, /device:TPU:19, one launch (start us, length us, event | category | flops | bytes accessed | tf_op | source)
XLA Modules:
  0.0 167.4 jit_solution(15602116947673312817)
XLA Ops:
  1.4 0.7 broadcast_multiply_fusion.1
  2.8 1.0 copy_multiply_fusion
  3.9 0.9 convolution_bitcast_fusion.13
  4.9 0.9 copy_dynamic-update-slice_fusion.1
  5.9 0.9 fusion.4
  6.8 1.1 convolution_add_fusion.2
  8.3 3.7 %reshape_reshape.36 = f32[2,8,32,16,8]{4,3,2,1,0:T(8,128)} reshape(f32[2,8,4,8,128]{4,3,2,1,0:T(8,128)S(1)} %pad_maximum_fusion) | data formatting | bytes 524288 | tf_op jit(solution)/shard_map/reshape;reshape | solution.py:66
  12.1 8.1 %fusion.146 = (f32[2,8,32,16,1]{4,3,2,1,0:T(8,128)}, f32[2,8,32,16,1]{4,3,2,1,0:T(8,128)}) fusion(f32[2,8,32,16,8]{4,3,2,1,0:T(8,128)} %reshape_reshape.36), kind=kLoop, calls=%fused_computation.285 | loop fusion | bytes 131072 | tf_op jit(solution)/shard_map/slice | solution.py:68
  20.2 3.2 %slice.428 = f32[2,8,32,16,6]{4,3,2,1,0:T(8,128)} slice(f32[2,8,32,16,8]{4,3,2,1,0:T(8,128)S(1)} %copy-done), slice={[0:2], [0:8], [0:32], [0:16], [1:7]} | slice | bytes 393216 | tf_op jit(solution)/shard_map/slice | solution.py:76
  23.4 3.3 %copy.530 = f32[2,8,32,16,1]{2,3,4,1,0:T(8,128)S(1)} copy(f32[2,8,32,16,1]{4,3,2,1,0:T(8,128)} %get-tuple-element.30) | data formatting | bytes 65536 | tf_op jit(solution)/shard_map/slice | solution.py:68
  26.7 3.3 %copy.529 = f32[2,8,32,16,1]{2,3,4,1,0:T(8,128)S(1)} copy(f32[2,8,32,16,1]{4,3,2,1,0:T(8,128)} %get-tuple-element.31) | data formatting | bytes 65536 | tf_op jit(solution)/shard_map/slice | solution.py:67
  30.0 3.4 %copy.532 = f32[2,8,32,16,6]{2,4,3,1,0:T(8,128)S(1)} copy(f32[2,8,32,16,6]{4,3,2,1,0:T(8,128)} %slice.428) | data formatting | bytes 393216 | tf_op jit(solution)/shard_map/slice | solution.py:76
  34.0 3.7 %collective-permute-start = (f32[2,1,32,128]{3,1,2,0:T(1,128)S(1)}, f32[2,1,32,128]{3,1,2,0:T(1,128)S(1)}, u32[]{:S(2)}, u32[]{:S(2)}) collective-permute-start(f32[2,1,32,128]{3,1,2,0:T(1,128)S(1)} %copy.668), channel_id=1, source_target_pairs={{0,2},{2,4},{4,6},{6,8},{8,10},{10,12},{12,14},{14,16},{16,18},{18... | collective-permute-start | bytes 98312 | tf_op jit(solution)/shard_map/ppermute | solution.py:15
  37.8 2.1 %collective-permute-start.1 = (f32[2,1,32,128]{3,1,2,0:T(1,128)S(1)}, f32[2,1,32,128]{3,1,2,0:T(1,128)}, u32[]{:S(2)}, u32[]{:S(2)}) collective-permute-start(f32[2,1,32,128]{3,1,2,0:T(1,128)S(1)} %copy.667), channel_id=1, source_target_pairs={{2,0},{4,2},{6,4},{8,6},{10,8},{12,10},{14,12},{16,14},{18,16},{20... | collective-permute-start | bytes 98312 | tf_op jit(solution)/shard_map/ppermute | solution.py:18
  40.0 1.1 reshape.541
  41.8 1.3 convolution_bitcast_fusion
  43.2 1.3 convolution_bitcast_fusion.1
  44.6 1.0 convolution_bitcast_fusion.3
  45.7 1.0 convolution_bitcast_fusion.4
  47.3 1.2 convolution_add_fusion.4
  49.0 0.8 add.292
  49.8 3.3 %collective-permute-start.2 = (f32[2,8,1,128]{3,1,2,0:T(8,128)S(1)}, f32[2,8,1,128]{3,1,2,0:T(8,128)S(1)}, u32[]{:S(2)}, u32[]{:S(2)}) collective-permute-start(f32[2,8,1,128]{3,1,2,0:T(8,128)S(1)} %pad_maximum_fusion.13), channel_id=1, source_target_pairs={{0,1},{2,3},{4,5},{6,7},{8,9},{10,11},{12,13},{14,15},{16,17},{18,... | collective-permute-start | bytes 24584 | tf_op jit(solution)/shard_map/ppermute | solution.py:15
  53.1 0.8 collective-permute-done.2
  53.9 1.5 collective-permute-start.3
  55.4 2.9 %collective-permute-done.3 = f32[2,8,1,128]{3,1,2,0:T(8,128)S(1)} collective-permute-done((f32[2,8,1,128]{3,1,2,0:T(8,128)S(1)}, f32[2,8,1,128]{3,1,2,0:T(8,128)S(1)}, u32[]{:S(2)}, u32[]{:S(2)}) %collective-permute-start.3) | collective-permute-done | bytes 8224 | tf_op jit(solution)/shard_map/ppermute | solution.py:18
  61.5 1.1 reshape_reshape.38
  62.6 2.7 %fusion.148 = (f32[1,8,32,16,1]{4,3,2,1,0:T(8,128)}, f32[1,8,32,16,1]{4,3,2,1,0:T(8,128)}) fusion(f32[1,8,32,16,8]{4,3,2,1,0:T(8,128)S(1)} %reshape_reshape.38), kind=kLoop, calls=%fused_computation.287 | loop fusion | bytes 65536 | tf_op jit(solution)/shard_map/slice | solution.py:68
  65.3 2.0 %slice.443 = f32[1,8,32,16,6]{4,3,2,1,0:T(8,128)} slice(f32[1,8,32,16,8]{4,3,2,1,0:T(8,128)S(1)} %reshape_reshape.38), slice={[0:1], [0:8], [0:32], [0:16], [1:7]} | slice | bytes 196608 | tf_op jit(solution)/shard_map/slice | solution.py:76
  67.3 2.6 %copy.551 = f32[1,8,32,16,1]{2,3,4,1,0:T(8,128)S(1)} copy(f32[1,8,32,16,1]{4,3,2,1,0:T(8,128)} %get-tuple-element.34) | data formatting | bytes 32768 | tf_op jit(solution)/shard_map/slice | solution.py:68
  69.8 2.4 %copy.550 = f32[1,8,32,16,1]{2,3,4,1,0:T(8,128)S(1)} copy(f32[1,8,32,16,1]{4,3,2,1,0:T(8,128)} %get-tuple-element.35) | data formatting | bytes 32768 | tf_op jit(solution)/shard_map/slice | solution.py:67
  72.4 1.7 %copy.553 = f32[1,8,32,16,6]{2,4,3,1,0:T(8,128)} copy(f32[1,8,32,16,6]{4,3,2,1,0:T(8,128)S(1)} %copy-done.1) | data formatting | bytes 196608 | tf_op jit(solution)/shard_map/slice | solution.py:76
  74.1 1.2 maximum_bitcast_fusion.1
  75.4 6.7 %collective-permute-start.4 = (f32[1,1,32,128]{3,1,2,0:T(1,128)S(1)}, f32[1,1,32,128]{3,1,2,0:T(1,128)S(1)}, u32[]{:S(2)}, u32[]{:S(2)}) collective-permute-start(f32[1,1,32,128]{3,1,2,0:T(1,128)S(1)} %copy.674), channel_id=1, source_target_pairs={{0,2},{2,4},{4,6},{6,8},{8,10},{10,12},{12,14},{14,16},{16,18},{18... | collective-permute-start | bytes 49160 | tf_op jit(solution)/shard_map/ppermute | solution.py:15
  82.2 1.9 %collective-permute-start.5 = (f32[1,1,32,128]{3,1,2,0:T(1,128)S(1)}, f32[1,1,32,128]{3,1,2,0:T(1,128)S(1)}, u32[]{:S(2)}, u32[]{:S(2)}) collective-permute-start(f32[1,1,32,128]{3,1,2,0:T(1,128)S(1)} %copy.673), channel_id=1, source_target_pairs={{2,0},{4,2},{6,4},{8,6},{10,8},{12,10},{14,12},{16,14},{18,16},{20... | collective-permute-start | bytes 49160 | tf_op jit(solution)/shard_map/ppermute | solution.py:18
  85.0 3.1 %collective-permute-done.5 = f32[1,1,32,128]{3,1,2,0:T(1,128)S(1)} collective-permute-done((f32[1,1,32,128]{3,1,2,0:T(1,128)S(1)}, f32[1,1,32,128]{3,1,2,0:T(1,128)S(1)}, u32[]{:S(2)}, u32[]{:S(2)}) %collective-permute-start.5) | collective-permute-done | bytes 16416 | tf_op jit(solution)/shard_map/ppermute | solution.py:18
  88.2 1.4 collective-permute-start.6
  90.3 1.5 collective-permute-start.7
  91.9 2.8 %collective-permute-done.7 = f32[1,8,1,128]{3,1,2,0:T(8,128)S(1)} collective-permute-done((f32[1,8,1,128]{3,1,2,0:T(8,128)S(1)}, f32[1,8,1,128]{3,1,2,0:T(8,128)S(1)}, u32[]{:S(2)}, u32[]{:S(2)}) %collective-permute-start.7) | collective-permute-done | bytes 4128 | tf_op jit(solution)/shard_map/ppermute | solution.py:18
  97.3 1.1 reshape_reshape.40
  98.4 2.7 %fusion.147 = (f32[1,8,32,16,1]{4,3,2,1,0:T(8,128)}, f32[1,8,32,16,1]{4,3,2,1,0:T(8,128)}) fusion(f32[1,8,32,16,8]{4,3,2,1,0:T(8,128)S(1)} %reshape_reshape.40), kind=kLoop, calls=%fused_computation.286 | loop fusion | bytes 65536 | tf_op jit(solution)/shard_map/slice | solution.py:68
  101.1 2.0 %slice.456 = f32[1,8,32,16,6]{4,3,2,1,0:T(8,128)} slice(f32[1,8,32,16,8]{4,3,2,1,0:T(8,128)S(1)} %reshape_reshape.40), slice={[0:1], [0:8], [0:32], [0:16], [1:7]} | slice | bytes 196608 | tf_op jit(solution)/shard_map/slice | solution.py:76
  103.1 2.6 %copy.571 = f32[1,8,32,16,1]{2,3,4,1,0:T(8,128)S(1)} copy(f32[1,8,32,16,1]{4,3,2,1,0:T(8,128)} %get-tuple-element.32) | data formatting | bytes 32768 | tf_op jit(solution)/shard_map/slice | solution.py:68
  105.6 2.4 %copy.570 = f32[1,8,32,16,1]{2,3,4,1,0:T(8,128)S(1)} copy(f32[1,8,32,16,1]{4,3,2,1,0:T(8,128)} %get-tuple-element.33) | data formatting | bytes 32768 | tf_op jit(solution)/shard_map/slice | solution.py:67
  108.2 1.7 %copy.573 = f32[1,8,32,16,6]{2,4,3,1,0:T(8,128)} copy(f32[1,8,32,16,6]{4,3,2,1,0:T(8,128)S(1)} %copy-done.2) | data formatting | bytes 196608 | tf_op jit(solution)/shard_map/slice | solution.py:76
  109.9 1.3 maximum_bitcast_fusion.2
  111.3 3.9 %collective-permute-start.8 = (f32[1,1,32,128]{3,1,2,0:T(1,128)S(1)}, f32[1,1,32,128]{3,1,2,0:T(1,128)S(1)}, u32[]{:S(2)}, u32[]{:S(2)}) collective-permute-start(f32[1,1,32,128]{3,1,2,0:T(1,128)S(1)} %copy.680), channel_id=1, source_target_pairs={{0,2},{2,4},{4,6},{6,8},{8,10},{10,12},{12,14},{14,16},{16,18},{18... | collective-permute-start | bytes 49160 | tf_op jit(solution)/shard_map/ppermute | solution.py:15
  115.3 1.9 %collective-permute-start.9 = (f32[1,1,32,128]{3,1,2,0:T(1,128)S(1)}, f32[1,1,32,128]{3,1,2,0:T(1,128)S(1)}, u32[]{:S(2)}, u32[]{:S(2)}) collective-permute-start(f32[1,1,32,128]{3,1,2,0:T(1,128)S(1)} %copy.679), channel_id=1, source_target_pairs={{2,0},{4,2},{6,4},{8,6},{10,8},{12,10},{14,12},{16,14},{18,16},{20... | collective-permute-start | bytes 49160 | tf_op jit(solution)/shard_map/ppermute | solution.py:18
  117.5 3.7 %collective-permute-done.9 = f32[1,1,32,128]{3,1,2,0:T(1,128)S(1)} collective-permute-done((f32[1,1,32,128]{3,1,2,0:T(1,128)S(1)}, f32[1,1,32,128]{3,1,2,0:T(1,128)S(1)}, u32[]{:S(2)}, u32[]{:S(2)}) %collective-permute-start.9) | collective-permute-done | bytes 16416 | tf_op jit(solution)/shard_map/ppermute | solution.py:18
  121.3 1.4 collective-permute-start.10
  122.6 1.0 convolution_bitcast_fusion.2
  123.7 1.3 collective-permute-start.11
  125.9 2.2 %collective-permute-done.11 = f32[1,8,1,128]{3,1,2,0:T(8,128)S(1)} collective-permute-done((f32[1,8,1,128]{3,1,2,0:T(8,128)S(1)}, f32[1,8,1,128]{3,1,2,0:T(8,128)S(1)}, u32[]{:S(2)}, u32[]{:S(2)}) %collective-permute-start.11) | collective-permute-done | bytes 4128 | tf_op jit(solution)/shard_map/ppermute | solution.py:18
  129.9 3.6 %collective-permute-start.12 = (f32[2,1,8,32]{2,3,1,0:T(8,128)S(1)}, f32[2,1,8,32]{2,3,1,0:T(8,128)S(1)}, u32[]{:S(2)}, u32[]{:S(2)}) collective-permute-start(f32[2,1,8,32]{2,3,1,0:T(8,128)S(1)} %get-tuple-element.60), channel_id=1, source_target_pairs={{0,2},{2,4},{4,6},{6,8},{8,10},{10,12},{12,14},{14,16},{16,18},{18... | collective-permute-start | bytes 6152 | tf_op jit(solution)/shard_map/ppermute | solution.py:15
  133.5 1.9 %collective-permute-start.13 = (f32[2,1,8,32]{2,3,1,0:T(8,128)S(1)}, f32[2,1,8,32]{2,3,1,0:T(8,128)S(1)}, u32[]{:S(2)}, u32[]{:S(2)}) collective-permute-start(f32[2,1,8,32]{2,3,1,0:T(8,128)S(1)} %get-tuple-element.61), channel_id=1, source_target_pairs={{2,0},{4,2},{6,4},{8,6},{10,8},{12,10},{14,12},{16,14},{18,16},{20... | collective-permute-start | bytes 6152 | tf_op jit(solution)/shard_map/ppermute | solution.py:18
  135.5 4.2 %collective-permute-done.13 = f32[2,1,8,32]{2,3,1,0:T(8,128)S(1)} collective-permute-done((f32[2,1,8,32]{2,3,1,0:T(8,128)S(1)}, f32[2,1,8,32]{2,3,1,0:T(8,128)S(1)}, u32[]{:S(2)}, u32[]{:S(2)}) %collective-permute-start.13) | collective-permute-done | bytes 2080 | tf_op jit(solution)/shard_map/ppermute | solution.py:18
  139.8 1.4 collective-permute-start.14
  141.2 1.3 collective-permute-start.15
  143.2 3.7 %collective-permute-done.15 = f32[2,4,1,32]{2,3,1,0:T(8,128)S(1)} collective-permute-done((f32[2,4,1,32]{2,3,1,0:T(8,128)S(1)}, f32[2,4,1,32]{2,3,1,0:T(8,128)S(1)}, u32[]{:S(2)}, u32[]{:S(2)}) %collective-permute-start.15) | collective-permute-done | bytes 1056 | tf_op jit(solution)/shard_map/ppermute | solution.py:18
  148.7 3.3 %collective-permute-start.16 = (f32[1,1,8,32]{2,3,1,0:T(8,128)S(1)}, f32[1,1,8,32]{2,3,1,0:T(8,128)S(1)}, u32[]{:S(2)}, u32[]{:S(2)}) collective-permute-start(f32[1,1,8,32]{2,3,1,0:T(8,128)S(1)} %get-tuple-element.64), channel_id=1, source_target_pairs={{0,2},{2,4},{4,6},{6,8},{8,10},{10,12},{12,14},{14,16},{16,18},{18... | collective-permute-start | bytes 3080 | tf_op jit(solution)/shard_map/ppermute | solution.py:15
  152.1 1.9 %collective-permute-start.17 = (f32[1,1,8,32]{2,3,1,0:T(8,128)S(1)}, f32[1,1,8,32]{2,3,1,0:T(8,128)S(1)}, u32[]{:S(2)}, u32[]{:S(2)}) collective-permute-start(f32[1,1,8,32]{2,3,1,0:T(8,128)S(1)} %get-tuple-element.65), channel_id=1, source_target_pairs={{2,0},{4,2},{6,4},{8,6},{10,8},{12,10},{14,12},{16,14},{18,16},{20... | collective-permute-start | bytes 3080 | tf_op jit(solution)/shard_map/ppermute | solution.py:18
  154.1 4.0 %collective-permute-done.17 = f32[1,1,8,32]{2,3,1,0:T(8,128)S(1)} collective-permute-done((f32[1,1,8,32]{2,3,1,0:T(8,128)S(1)}, f32[1,1,8,32]{2,3,1,0:T(8,128)S(1)}, u32[]{:S(2)}, u32[]{:S(2)}) %collective-permute-start.17) | collective-permute-done | bytes 1056 | tf_op jit(solution)/shard_map/ppermute | solution.py:18
  158.1 1.3 collective-permute-start.18
  159.4 1.3 collective-permute-start.19
  161.1 3.4 %collective-permute-done.19 = f32[1,4,1,32]{2,3,1,0:T(8,128)S(1)} collective-permute-done((f32[1,4,1,32]{2,3,1,0:T(8,128)S(1)}, f32[1,4,1,32]{2,3,1,0:T(8,128)S(1)}, u32[]{:S(2)}, u32[]{:S(2)}) %collective-permute-start.19) | collective-permute-done | bytes 544 | tf_op jit(solution)/shard_map/ppermute | solution.py:18
  (241 shorter events, 20.7 us)
Async XLA Ops:
  12.1 8.2 %copy-start = (f32[2,8,32,16,8]{4,3,2,1,0:T(8,128)S(1)}, f32[2,8,32,16,8]{4,3,2,1,0:T(8,128)}, u32[]{:S(2)}) copy-start(f32[2,8,32,16,8]{4,3,2,1,0:T(8,128)} %reshape_reshape.36) | copy-start | bytes 786436
  33.9 6.0 %copy-start.3 = (f32[2,8,32,128]{2,3,1,0:T(8,128)}, f32[2,8,32,128]{2,3,1,0:T(8,128)S(1)}, u32[]{:S(2)}) copy-start(f32[2,8,32,128]{2,3,1,0:T(8,128)S(1)} %maximum_bitcast_fusion) | copy-start | bytes 786436
  34.0 14.9 %collective-permute-start = (f32[2,1,32,128]{3,1,2,0:T(1,128)S(1)}, f32[2,1,32,128]{3,1,2,0:T(1,128)S(1)}, u32[]{:S(2)}, u32[]{:S(2)}) collective-permute-start(f32[2,1,32,128]{3,1,2,0:T(1,128)S(1)} %copy.668), channel_id=1, source_target_pairs={{0,2},{2,4},{4,6},{6,8},{8,10},{10,12},{12,14},{14,16},{16,18},{18... | collective-permute-start | bytes 98312 | tf_op jit(solution)/shard_map/ppermute | solution.py:15
  37.8 11.2 %collective-permute-start.1 = (f32[2,1,32,128]{3,1,2,0:T(1,128)S(1)}, f32[2,1,32,128]{3,1,2,0:T(1,128)}, u32[]{:S(2)}, u32[]{:S(2)}) collective-permute-start(f32[2,1,32,128]{3,1,2,0:T(1,128)S(1)} %copy.667), channel_id=1, source_target_pairs={{2,0},{4,2},{6,4},{8,6},{10,8},{12,10},{14,12},{16,14},{18,16},{20... | collective-permute-start | bytes 98312 | tf_op jit(solution)/shard_map/ppermute | solution.py:18
  41.1 0.7 copy-start.21
  41.1 2.0 %copy-start.20 = (f32[2,2,8,1,1,1]{2,1,5,4,3,0:T(2,128)S(1)}, f32[2,2,8,1,1,1]{2,1,5,4,3,0:T(2,128)}, u32[]{:S(2)}) copy-start(f32[2,2,8,1,1,1]{2,1,5,4,3,0:T(2,128)} %constant.128) | copy-start | bytes 388
  41.8 2.8 %copy-start.19 = (f32[2,2,8,1,1,1,1]{2,1,0,6,5,4,3:T(2,128)S(1)}, f32[2,2,8,1,1,1,1]{2,1,0,6,5,4,3:T(2,128)}, u32[]{:S(2)}) copy-start(f32[2,2,8,1,1,1,1]{2,1,0,6,5,4,3:T(2,128)} %constant.132) | copy-start | bytes 388
  41.8 3.8 %copy-start.17 = (f32[2,2,8,1,1,1,1]{2,1,0,6,5,4,3:T(2,128)S(1)}, f32[2,2,8,1,1,1,1]{2,1,0,6,5,4,3:T(2,128)}, u32[]{:S(2)}) copy-start(f32[2,2,8,1,1,1,1]{2,1,0,6,5,4,3:T(2,128)} %constant.129) | copy-start | bytes 388
  41.8 4.9 %copy-start.18 = (f32[2,2,8,1,1,1,1,1]{2,1,0,7,6,5,4,3:T(2,128)S(1)}, f32[2,2,8,1,1,1,1,1]{2,1,0,7,6,5,4,3:T(2,128)}, u32[]{:S(2)}) copy-start(f32[2,2,8,1,1,1,1,1]{2,1,0,7,6,5,4,3:T(2,128)} %constant.130) | copy-start | bytes 388
  44.5 4.0 %slice-start = ((f32[2,8,32,128]{2,3,1,0:T(8,128)}), f32[2,6,32,128]{2,3,1,0:T(8,128)S(1)}, s32[]{:S(2)}) async-start(f32[2,8,32,128]{2,3,1,0:T(8,128)} %copy-done.3), calls=%async_computation | async-start | bytes 1572864 | tf_op jit(solution)/shard_map/slice | solution.py:98
  44.6 13.8 %copy-start.14 = (f32[8,4,8]{2,1,0:T(4,128)}, f32[8,4,8]{2,1,0:T(4,128)S(1)}, u32[]{:S(2)}) copy-start(f32[8,4,8]{2,1,0:T(4,128)S(1)} %broadcast_multiply_fusion) | copy-start | bytes 3076
  48.5 10.5 %copy-start.12 = (f32[8,8,1,1]{1,0,3,2:T(8,128)S(1)}, f32[8,8,1,1]{1,0,3,2:T(8,128)}, u32[]{:S(2)}) copy-start(f32[8,8,1,1]{1,0,3,2:T(8,128)} %constant.124) | copy-start | bytes 772
  48.6 10.9 %copy-start.4 = (f32[8,32,128]{2,1,0:T(8,128)S(1)}, f32[8,32,128]{2,1,0:T(8,128)}, u32[]{:S(2)}) copy-start(f32[8,32,128]{2,1,0:T(8,128)} %param.9) | copy-start | bytes 393220
  48.9 11.1 %copy-start.11 = (f32[8,8,1]{1,0,2:T(8,128)S(1)}, f32[8,8,1]{1,0,2:T(8,128)}, u32[]{:S(2)}) copy-start(f32[8,8,1]{1,0,2:T(8,128)} %constant.123) | copy-start | bytes 772
  49.8 10.6 %copy-start.5 = (f32[128,128,1]{1,0,2:T(8,128)S(1)}, f32[128,128,1]{1,0,2:T(8,128)}, u32[]{:S(2)}) copy-start(f32[128,128,1]{1,0,2:T(8,128)} %constant.125) | copy-start | bytes 196612
  49.8 4.1 %collective-permute-start.2 = (f32[2,8,1,128]{3,1,2,0:T(8,128)S(1)}, f32[2,8,1,128]{3,1,2,0:T(8,128)S(1)}, u32[]{:S(2)}, u32[]{:S(2)}) collective-permute-start(f32[2,8,1,128]{3,1,2,0:T(8,128)S(1)} %pad_maximum_fusion.13), channel_id=1, source_target_pairs={{0,1},{2,3},{4,5},{6,7},{8,9},{10,11},{12,13},{14,15},{16,17},{18,... | collective-permute-start | bytes 24584 | tf_op jit(solution)/shard_map/ppermute | solution.py:15
  53.9 4.4 %collective-permute-start.3 = (f32[2,8,1,128]{3,1,2,0:T(8,128)S(1)}, f32[2,8,1,128]{3,1,2,0:T(8,128)S(1)}, u32[]{:S(2)}, u32[]{:S(2)}) collective-permute-start(f32[2,8,1,128]{3,1,2,0:T(8,128)S(1)} %get-tuple-element.29), channel_id=1, source_target_pairs={{1,0},{3,2},{5,4},{7,6},{9,8},{11,10},{13,12},{15,14},{17,16},{19,... | collective-permute-start | bytes 24584 | tf_op jit(solution)/shard_map/ppermute | solution.py:18
  58.4 0.7 copy-start.7
  58.4 1.2 copy-start.9
  67.3 5.1 %copy-start.1 = (f32[1,8,32,16,6]{4,3,2,1,0:T(8,128)S(1)}, f32[1,8,32,16,6]{4,3,2,1,0:T(8,128)}, u32[]{:S(2)}) copy-start(f32[1,8,32,16,6]{4,3,2,1,0:T(8,128)} %slice.443) | copy-start | bytes 294916
  75.3 19.8 %copy-start.8 = (f32[1,8,32,128]{3,1,2,0:T(8,128)S(1)}, f32[1,8,32,128]{3,1,2,0:T(8,128)}, u32[]{:S(2)}) copy-start(f32[1,8,32,128]{3,1,2,0:T(8,128)} %copy-done.7) | copy-start | bytes 393220
  75.3 19.8 %copy-start.10 = (f32[1,8,32,128]{3,1,2,0:T(8,128)S(1)}, f32[1,8,32,128]{3,1,2,0:T(8,128)}, u32[]{:S(2)}) copy-start(f32[1,8,32,128]{3,1,2,0:T(8,128)} %copy-done.9) | copy-start | bytes 393220
  75.4 19.8 %copy-start.15 = (f32[8,4,8]{2,1,0:T(4,128)S(1)}, f32[8,4,8]{2,1,0:T(4,128)}, u32[]{:S(2)}) copy-start(f32[8,4,8]{2,1,0:T(4,128)} %copy-done.14) | copy-start | bytes 3076
  75.4 9.6 %collective-permute-start.4 = (f32[1,1,32,128]{3,1,2,0:T(1,128)S(1)}, f32[1,1,32,128]{3,1,2,0:T(1,128)S(1)}, u32[]{:S(2)}, u32[]{:S(2)}) collective-permute-start(f32[1,1,32,128]{3,1,2,0:T(1,128)S(1)} %copy.674), channel_id=1, source_target_pairs={{0,2},{2,4},{4,6},{6,8},{8,10},{10,12},{12,14},{14,16},{16,18},{18... | collective-permute-start | bytes 49160 | tf_op jit(solution)/shard_map/ppermute | solution.py:15
  82.2 6.0 %collective-permute-start.5 = (f32[1,1,32,128]{3,1,2,0:T(1,128)S(1)}, f32[1,1,32,128]{3,1,2,0:T(1,128)S(1)}, u32[]{:S(2)}, u32[]{:S(2)}) collective-permute-start(f32[1,1,32,128]{3,1,2,0:T(1,128)S(1)} %copy.673), channel_id=1, source_target_pairs={{2,0},{4,2},{6,4},{8,6},{10,8},{12,10},{14,12},{16,14},{18,16},{20... | collective-permute-start | bytes 49160 | tf_op jit(solution)/shard_map/ppermute | solution.py:18
  88.2 2.1 %collective-permute-start.6 = (f32[1,8,1,128]{3,1,2,0:T(8,128)S(1)}, f32[1,8,1,128]{3,1,2,0:T(8,128)S(1)}, u32[]{:S(2)}, u32[]{:S(2)}) collective-permute-start(f32[1,8,1,128]{3,1,2,0:T(8,128)S(1)} %pad_maximum_fusion.18), channel_id=1, source_target_pairs={{0,1},{2,3},{4,5},{6,7},{8,9},{10,11},{12,13},{14,15},{16,17},{18,... | collective-permute-start | bytes 12296 | tf_op jit(solution)/shard_map/ppermute | solution.py:15
  90.3 4.3 %collective-permute-start.7 = (f32[1,8,1,128]{3,1,2,0:T(8,128)S(1)}, f32[1,8,1,128]{3,1,2,0:T(8,128)S(1)}, u32[]{:S(2)}, u32[]{:S(2)}) collective-permute-start(f32[1,8,1,128]{3,1,2,0:T(8,128)S(1)} %get-tuple-element.27), channel_id=1, source_target_pairs={{1,0},{3,2},{5,4},{7,6},{9,8},{11,10},{13,12},{15,14},{17,16},{19,... | collective-permute-start | bytes 12296 | tf_op jit(solution)/shard_map/ppermute | solution.py:18
  103.1 5.1 %copy-start.2 = (f32[1,8,32,16,6]{4,3,2,1,0:T(8,128)S(1)}, f32[1,8,32,16,6]{4,3,2,1,0:T(8,128)}, u32[]{:S(2)}) copy-start(f32[1,8,32,16,6]{4,3,2,1,0:T(8,128)} %slice.456) | copy-start | bytes 294916
  109.9 15.1 %copy-start.6 = (f32[2,2,4,16,2,2,2,2]{3,7,6,5,4,2,1,0:T(2,128)S(1)}, f32[2,2,4,16,2,2,2,2]{3,7,6,5,4,2,1,0:T(2,128)}, u32[]{:S(2)}) copy-start(f32[2,2,4,16,2,2,2,2]{3,7,6,5,4,2,1,0:T(2,128)} %convolution_add_fusion.4) | copy-start | bytes 49156
  109.9 15.1 %copy-start.13 = (f32[2,2,2,2,2,2]{5,2,4,1,3,0:T(2,128)S(1)}, f32[2,2,2,2,2,2]{5,2,4,1,3,0:T(2,128)}, u32[]{:S(2)}) copy-start(f32[2,2,2,2,2,2]{5,2,4,1,3,0:T(2,128)} %compare_convert_fusion) | copy-start | bytes 772
  109.9 15.2 %copy-start.23 = (f32[2,2,8,1,1,1,1,1]{2,1,0,7,6,5,4,3:T(2,128)S(1)}, f32[2,2,8,1,1,1,1,1]{2,1,0,7,6,5,4,3:T(2,128)}, u32[]{:S(2)}) copy-start(f32[2,2,8,1,1,1,1,1]{2,1,0,7,6,5,4,3:T(2,128)} %constant.133) | copy-start | bytes 388
  111.2 16.9 %copy-start.22 = (f32[8,2,1]{0,1,2:T(2,128)S(1)}, f32[8,2,1]{0,1,2:T(2,128)}, u32[]{:S(2)}) copy-start(f32[8,2,1]{0,1,2:T(2,128)} %constant.126) | copy-start | bytes 196
  111.3 6.2 %collective-permute-start.8 = (f32[1,1,32,128]{3,1,2,0:T(1,128)S(1)}, f32[1,1,32,128]{3,1,2,0:T(1,128)S(1)}, u32[]{:S(2)}, u32[]{:S(2)}) collective-permute-start(f32[1,1,32,128]{3,1,2,0:T(1,128)S(1)} %copy.680), channel_id=1, source_target_pairs={{0,2},{2,4},{4,6},{6,8},{8,10},{10,12},{12,14},{14,16},{16,18},{18... | collective-permute-start | bytes 49160 | tf_op jit(solution)/shard_map/ppermute | solution.py:15
  115.3 6.0 %collective-permute-start.9 = (f32[1,1,32,128]{3,1,2,0:T(1,128)S(1)}, f32[1,1,32,128]{3,1,2,0:T(1,128)S(1)}, u32[]{:S(2)}, u32[]{:S(2)}) collective-permute-start(f32[1,1,32,128]{3,1,2,0:T(1,128)S(1)} %copy.679), channel_id=1, source_target_pairs={{2,0},{4,2},{6,4},{8,6},{10,8},{12,10},{14,12},{16,14},{18,16},{20... | collective-permute-start | bytes 49160 | tf_op jit(solution)/shard_map/ppermute | solution.py:18
  117.3 11.1 %copy-start.16 = (f32[8,2,1,1]{0,1,3,2:T(2,128)S(1)}, f32[8,2,1,1]{0,1,3,2:T(2,128)}, u32[]{:S(2)}) copy-start(f32[8,2,1,1]{0,1,3,2:T(2,128)} %constant.127) | copy-start | bytes 196
  121.3 2.4 %collective-permute-start.10 = (f32[1,8,1,128]{3,1,2,0:T(8,128)S(1)}, f32[1,8,1,128]{3,1,2,0:T(8,128)S(1)}, u32[]{:S(2)}, u32[]{:S(2)}) collective-permute-start(f32[1,8,1,128]{3,1,2,0:T(8,128)S(1)} %pad_maximum_fusion.16), channel_id=1, source_target_pairs={{0,1},{2,3},{4,5},{6,7},{8,9},{10,11},{12,13},{14,15},{16,17},{18,... | collective-permute-start | bytes 12296 | tf_op jit(solution)/shard_map/ppermute | solution.py:15
  123.7 4.4 %collective-permute-start.11 = (f32[1,8,1,128]{3,1,2,0:T(8,128)S(1)}, f32[1,8,1,128]{3,1,2,0:T(8,128)S(1)}, u32[]{:S(2)}, u32[]{:S(2)}) collective-permute-start(f32[1,8,1,128]{3,1,2,0:T(8,128)S(1)} %get-tuple-element.23), channel_id=1, source_target_pairs={{1,0},{3,2},{5,4},{7,6},{9,8},{11,10},{13,12},{15,14},{17,16},{19,... | collective-permute-start | bytes 12296 | tf_op jit(solution)/shard_map/ppermute | solution.py:18
  129.9 5.6 %collective-permute-start.12 = (f32[2,1,8,32]{2,3,1,0:T(8,128)S(1)}, f32[2,1,8,32]{2,3,1,0:T(8,128)S(1)}, u32[]{:S(2)}, u32[]{:S(2)}) collective-permute-start(f32[2,1,8,32]{2,3,1,0:T(8,128)S(1)} %get-tuple-element.60), channel_id=1, source_target_pairs={{0,2},{2,4},{4,6},{6,8},{8,10},{10,12},{12,14},{14,16},{16,18},{18... | collective-permute-start | bytes 6152 | tf_op jit(solution)/shard_map/ppermute | solution.py:15
  133.5 6.1 %collective-permute-start.13 = (f32[2,1,8,32]{2,3,1,0:T(8,128)S(1)}, f32[2,1,8,32]{2,3,1,0:T(8,128)S(1)}, u32[]{:S(2)}, u32[]{:S(2)}) collective-permute-start(f32[2,1,8,32]{2,3,1,0:T(8,128)S(1)} %get-tuple-element.61), channel_id=1, source_target_pairs={{2,0},{4,2},{6,4},{8,6},{10,8},{12,10},{14,12},{16,14},{18,16},{20... | collective-permute-start | bytes 6152 | tf_op jit(solution)/shard_map/ppermute | solution.py:18
  139.8 3.3 %collective-permute-start.14 = (f32[2,4,1,32]{2,3,1,0:T(8,128)S(1)}, f32[2,4,1,32]{2,3,1,0:T(8,128)S(1)}, u32[]{:S(2)}, u32[]{:S(2)}) collective-permute-start(f32[2,4,1,32]{2,3,1,0:T(8,128)S(1)} %get-tuple-element.48), channel_id=1, source_target_pairs={{0,1},{2,3},{4,5},{6,7},{8,9},{10,11},{12,13},{14,15},{16,17},{18,... | collective-permute-start | bytes 3080 | tf_op jit(solution)/shard_map/ppermute | solution.py:15
  141.2 5.7 %collective-permute-start.15 = (f32[2,4,1,32]{2,3,1,0:T(8,128)S(1)}, f32[2,4,1,32]{2,3,1,0:T(8,128)S(1)}, u32[]{:S(2)}, u32[]{:S(2)}) collective-permute-start(f32[2,4,1,32]{2,3,1,0:T(8,128)S(1)} %get-tuple-element.49), channel_id=1, source_target_pairs={{1,0},{3,2},{5,4},{7,6},{9,8},{11,10},{13,12},{15,14},{17,16},{19,... | collective-permute-start | bytes 3080 | tf_op jit(solution)/shard_map/ppermute | solution.py:18
  148.7 5.4 %collective-permute-start.16 = (f32[1,1,8,32]{2,3,1,0:T(8,128)S(1)}, f32[1,1,8,32]{2,3,1,0:T(8,128)S(1)}, u32[]{:S(2)}, u32[]{:S(2)}) collective-permute-start(f32[1,1,8,32]{2,3,1,0:T(8,128)S(1)} %get-tuple-element.64), channel_id=1, source_target_pairs={{0,2},{2,4},{4,6},{6,8},{8,10},{10,12},{12,14},{14,16},{16,18},{18... | collective-permute-start | bytes 3080 | tf_op jit(solution)/shard_map/ppermute | solution.py:15
  152.1 6.0 %collective-permute-start.17 = (f32[1,1,8,32]{2,3,1,0:T(8,128)S(1)}, f32[1,1,8,32]{2,3,1,0:T(8,128)S(1)}, u32[]{:S(2)}, u32[]{:S(2)}) collective-permute-start(f32[1,1,8,32]{2,3,1,0:T(8,128)S(1)} %get-tuple-element.65), channel_id=1, source_target_pairs={{2,0},{4,2},{6,4},{8,6},{10,8},{12,10},{14,12},{16,14},{18,16},{20... | collective-permute-start | bytes 3080 | tf_op jit(solution)/shard_map/ppermute | solution.py:18
  158.1 2.9 %collective-permute-start.18 = (f32[1,4,1,32]{2,3,1,0:T(8,128)S(1)}, f32[1,4,1,32]{2,3,1,0:T(8,128)S(1)}, u32[]{:S(2)}, u32[]{:S(2)}) collective-permute-start(f32[1,4,1,32]{2,3,1,0:T(8,128)S(1)} %get-tuple-element.54), channel_id=1, source_target_pairs={{0,1},{2,3},{4,5},{6,7},{8,9},{10,11},{12,13},{14,15},{16,17},{18,... | collective-permute-start | bytes 1544 | tf_op jit(solution)/shard_map/ppermute | solution.py:15
  159.4 5.0 %collective-permute-start.19 = (f32[1,4,1,32]{2,3,1,0:T(8,128)S(1)}, f32[1,4,1,32]{2,3,1,0:T(8,128)S(1)}, u32[]{:S(2)}, u32[]{:S(2)}) collective-permute-start(f32[1,4,1,32]{2,3,1,0:T(8,128)S(1)} %get-tuple-element.55), channel_id=1, source_target_pairs={{1,0},{3,2},{5,4},{7,6},{9,8},{11,10},{13,12},{15,14},{17,16},{19,... | collective-permute-start | bytes 1544 | tf_op jit(solution)/shard_map/ppermute | solution.py:18
where the time goes:
time: 168 us; the launch traced here: 167 us
  local copies, waits for them, and re-layouts  61.1 us (36%)
  starting transfers between devices  46.7 us (28%)
  waiting for transfers between devices  31.8 us (19%)
  matrix products  16.6 us (10%)
  other arithmetic  8.99 us (5%)
  between operations  2.18 us (1%)
    ppermute x10, starting transfers between devices, extended(): lax.ppermute(lax.slice_in_dim(block, block.shape[dim] - width, None, axis...  30 us
    ppermute x10, waiting for transfers between devices, extended(): lax.ppermute(lax.slice_in_dim(block, 0, width, axis=dim), axis, backward)  29.8 us
    slice x9, local copies, waits for them, and re-layouts, fold_local(): lax.index_in_dim(split, per_elem - 1, axis_at + 1, keepdims=False)  22.2 us
    ppermute x10, starting transfers between devices, extended(): lax.ppermute(lax.slice_in_dim(block, 0, width, axis=dim), axis, backward)  16.7 us
    slice x10, local copies, waits for them, and re-layouts, fold_local(): middle = lax.slice_in_dim(split, 1, per_elem - 1, axis=axis_at + 1)  14.2 us
    slice x4, local copies, waits for them, and re-layouts, fold_local(): first_face = lax.index_in_dim(split, 0, axis_at + 1, keepdims=False)  8.43 us
    another operation x5, local copies, waits for them, and re-layouts, fold_local(): field.reshape(dims_of[:axis_at] + (elements, per_elem) + dims_of[axis_at...  6.26 us
    dot_general x3, matrix products, coarse_matrices(): jnp.einsum(form, shaped, mass_pair, grad_pair, mass_pair, precision=precise)  3.57 us
  transfers between devices with their start and end apart: 20, of which 12 were waited for; matrix products, arithmetic and copies ran while one was open for 8% of the time, Pallas kernels for 0%

commit v1 on v0

v1 whole, which is shorter than its diff:
```python
import functools

import jax
import jax.numpy as jnp
import numpy as np
from jax import lax
from jax.experimental import pallas as pl
from jax.experimental.pallas import tpu as pltpu
from jax.sharding import PartitionSpec as P

N = 8
THETA = 1.1
DELTA = 0.9
SIGMA = THETA / DELTA
RHO0 = 1.0 / SIGMA
RHO1 = 1.0 / (2.0 * SIGMA - RHO0)
F32 = jnp.float32
BF16 = jnp.bfloat16
VMEM_LIMIT = 48 * 1024 * 1024


def legendre_value(points, degree):
    previous = np.ones(points.shape)
    current = points.copy()
    for level in range(1, degree):
        following = ((2 * level + 1) * points * current - level * previous) / (level + 1)
        previous = current
        current = following
    return current


def tables():
    degree = 7
    points = np.array(
        [
            -1.0,
            -0.8717401485096066,
            -0.5917001814331423,
            -0.2092992179024789,
            0.2092992179024789,
            0.5917001814331423,
            0.8717401485096066,
            1.0,
        ]
    )
    values = legendre_value(points, degree)
    weights = 2.0 / (degree * (degree + 1) * values**2)
    derivative = np.zeros((8, 8))
    for row_at in range(8):
        for col_at in range(8):
            if row_at != col_at:
                derivative[row_at, col_at] = values[row_at] / (
                    values[col_at] * (points[row_at] - points[col_at])
                )
    derivative[0, 0] = -degree * (degree + 1) / 4.0
    derivative[7, 7] = degree * (degree + 1) / 4.0
    interp = np.stack([(1.0 - points) / 2.0, (1.0 + points) / 2.0], axis=1)
    return derivative, weights, interp


DM, WEIGHTS, INTERP = tables()
MULT = np.array([2.0] + [1.0] * 6 + [2.0])
RHO = MULT[:, None] * INTERP
DRHO = DM @ RHO


def blockdiag(block, count):
    return np.kron(np.eye(count), block)


def hi_lo(matrix):
    hi = matrix.astype(jnp.bfloat16)
    lo = (matrix - hi.astype(np.float64)).astype(jnp.bfloat16)
    return hi, lo


def right_table(matrix):
    hi, lo = hi_lo(matrix)
    return np.concatenate([hi, hi, lo], axis=0)


def left_table(matrix):
    hi, lo = hi_lo(matrix)
    return np.concatenate([hi, hi, lo], axis=1)


def vertex_table(per_node, elements, columns, wrap):
    out = np.zeros((8 * elements, columns))
    for e in range(elements):
        for i in range(2):
            v = e + i
            if v >= columns:
                if not wrap:
                    continue
                v -= columns
            out[8 * e : 8 * e + 8, v] += per_node[:, i]
    return out


def moment_table(per_node, elements, columns):
    out = np.zeros((8 * elements, columns))
    for e in range(elements):
        out[8 * e : 8 * e + 8, e] = per_node
    return out


PAIRS = [(0, 0), (0, 1), (1, 1)]
MASS = [INTERP[:, i] * INTERP[:, j] for i, j in PAIRS]


def round_up(value, to):
    return -(-value // to) * to


def make_tables(ny, nz, own_y, wrap):
    ey, ez = ny // N, nz // N
    cr = round_up(ey, 8)
    t = {}
    t["z_d"] = right_table(blockdiag(DM, ez).T)
    t["z_dt"] = right_table(blockdiag(DM, ez))
    t["z_sq"] = right_table(blockdiag(DM * DM, ez))
    t["y_d"] = left_table(blockdiag(DM, ey))
    t["y_dt"] = left_table(blockdiag(DM, ey).T)
    t["y_sq"] = left_table(blockdiag(DM * DM, ey).T)
    py = vertex_table(RHO, ey, cr, wrap)
    dpy = blockdiag(DM, ey) @ py
    pz = vertex_table(RHO, ez, nz, False)
    dpz = blockdiag(DM, ez) @ pz
    t["ry"] = np.concatenate([py, dpy], axis=0).T.astype(np.float32)
    t["rz"] = np.concatenate([pz, dpz], axis=0).astype(np.float32)
    t["my"] = np.concatenate([moment_table(m, ey, cr) for m in MASS], axis=1).T.astype(np.float32)
    t["mz"] = np.concatenate([moment_table(m, ez, nz) for m in MASS], axis=1).astype(np.float32)
    t["py"] = vertex_table(INTERP, ey, cr, wrap).astype(np.float32)
    t["pz"] = vertex_table(INTERP, ez, nz, False).T.astype(np.float32)
    sy = np.zeros((2 * ey, cr))
    for e in range(ey):
        for i in range(2):
            v = e + i
            if v >= cr:
                v = v - cr if wrap else 0
            sy[2 * e + i, v] = 1.0
    t["sy"] = sy.astype(np.float32)
    sz = np.zeros((nz, 2 * ez))
    for e in range(ez):
        for i in range(2):
            sz[e + i, 2 * e + i] = 1.0
    t["sz"] = sz.astype(np.float32)
    w3 = WEIGHTS[:, None, None] * WEIGHTS[None, :, None] * np.ones((1, 1, nz))
    t["w3"] = (w3 * np.tile(WEIGHTS, ez)[None, None, :]).astype(np.float32)
    return t


def even_odd(matrix, values, sign):
    even = [values[b] + values[7 - b] for b in range(4)]
    odd = [values[b] - values[7 - b] for b in range(4)]
    out = [None] * 8
    for a in range(4):
        pe = po = None
        for b in range(4):
            ce = float((matrix[a, b] + matrix[a, 7 - b]) / 2.0)
            co = float((matrix[a, b] - matrix[a, 7 - b]) / 2.0)
            te = ce * even[b]
            to = co * odd[b]
            pe = te if pe is None else pe + te
            po = to if po is None else po + to
        out[a] = pe + po
        out[7 - a] = pe - po if sign > 0 else po - pe
    return out


def split(x):
    hi = x.astype(BF16)
    lo = (x - hi.astype(F32)).astype(BF16)
    return hi, lo


def dot(a, b):
    return jnp.dot(a, b, preferred_element_type=F32)


def exact_dot(a, b):
    return jnp.dot(a, b, preferred_element_type=F32, precision=lax.Precision.HIGHEST)


def z_apply(hi, lo, table):
    return dot(jnp.concatenate([hi, lo, hi], axis=1), table)


def y_apply(hi, lo, table):
    return dot(table, jnp.concatenate([hi, lo, hi], axis=0))


def assemble_yz(v):
    ny, nz = v.shape
    row = lax.broadcasted_iota(jnp.int32, (N, nz), 0)
    lane = lax.broadcasted_iota(jnp.int32, (1, nz), 1)
    top = (row == N - 1).astype(F32)
    bottom = (row == 0).astype(F32)
    blocks = [v[N * e : N * e + N] for e in range(ny // N)]
    ups = [pltpu.roll(b, N - 1, 0) for b in blocks]
    downs = [pltpu.roll(b, 1, 0) for b in blocks]
    out = []
    for e, b in enumerate(blocks):
        if e + 1 < len(blocks):
            b = b + top * ups[e + 1]
        if e > 0:
            b = b + bottom * downs[e - 1]
        out.append(b)
    v = jnp.concatenate(out, axis=0)
    last = ((lane % N == N - 1) & (lane < nz - 1)).astype(F32)
    first = ((lane % N == 0) & (lane > 0)).astype(F32)
    return v + last * pltpu.roll(v, nz - 1, 1) + first * pltpu.roll(v, 1, 1)


def yz_mask(ny, nz, start, total):
    row = lax.broadcasted_iota(jnp.int32, (ny, nz), 0) + start
    lane = lax.broadcasted_iota(jnp.int32, (ny, nz), 1)
    return (row > 0) & (row < total - 1) & (lane > 0) & (lane < nz - 1)


class Layout:
    def __init__(self, own_y, nz, dom, sub):
        self.own_y, self.nz, self.dom, self.sub = own_y, nz, dom, sub
        self.blocks = min(sub, 3)
        self.ny = own_y * self.blocks
        self.total_y = own_y * sub
        self.wrap = sub <= 2
        self.ey, self.ez = self.ny // N, nz // N
        self.cr = round_up(self.ey, 8)

    def where(self):
        d = lax.axis_index("dom")
        h = lax.axis_index("sub")
        parity = lax.rem(d, 2)
        pair = lax.div(d, 2)
        if self.sub <= 2:
            start = 0
            offset = h * self.own_y
        else:
            start = (h - 1) * self.own_y
            offset = self.own_y
        low = (pair > 0).astype(F32)
        high = (pair < self.dom // 2 - 1).astype(F32)
        return parity, h, start, offset, low, high


def gather_window(lay, own, others, h, store):
    y = lay.own_y
    if lay.sub == 1:
        store(pl.ds(0, y), own)
    elif lay.sub == 2:
        store(pl.ds(pl.multiple_of(h * y, y), y), own)
        store(pl.ds(pl.multiple_of((1 - h) * y, y), y), others[0])
    else:
        store(pl.ds(0, y), others[0])
        store(pl.ds(y, y), own)
        store(pl.ds(2 * y, y), others[1])


def first_kernel(lay, n_other, *refs):
    own_r, own_c, mate = refs[:3]
    other = refs[3 : 3 + n_other]
    mate_other = refs[3 + n_other : 3 + 2 * n_other]
    refs = refs[3 + 2 * n_other :]
    z_sq, y_sq, w3 = refs[:3]
    msg, w_out, rhs_out, u_out, inv_out, res_out = refs[3:9]
    d_s = refs[9]
    ny, nz = lay.ny, lay.nz
    parity, h, start, offset, low, high = lay.where()
    for side, k_own, k_mate, target in (
        (0, own_r[...], mate[0], rhs_out),
        (1, own_c[...], mate[1], w_out),
    ):
        def store(base):
            def put(rows, value):
                target[pl.ds(base, N), rows, :] = value
            return put
        gather_window(lay, k_own, [o[side] for o in other], h, store(parity * N))
        gather_window(lay, k_mate, [o[side] for o in mate_other], h, store((1 - parity) * N))
    table3 = w3[...]
    for el in range(2):
        for e in range(lay.ey):
            rows = pl.ds(N * e, N)
            w = [w_out[N * el + a, rows, :] * table3[a] for a in range(N)]
            dx = even_odd((DM * DM).T, w, 1)
            for a in range(N):
                w_out[N * el + a, rows, :] = w[a]
                d_s[N * el + a, rows, :] = dx[a]
    hi, lo = split(w_out[...].reshape(2 * N * ny, nz))
    dz = z_apply(hi, lo, z_sq[...])
    mask = yz_mask(ny, nz, start, lay.total_y)
    inside = mask.astype(F32)
    own_plane = 15 * parity
    sx_own = d_s[own_plane]
    msg[2] = assemble_yz(sx_own)
    msg[3] = w_out[own_plane]
    for p in range(2 * N):
        cut = slice(p * ny, (p + 1) * ny)
        dy = y_apply(hi[cut], lo[cut], y_sq[...])
        d_s[p] = assemble_yz(d_s[p] + dz[cut] + dy)
        res_out[p] = assemble_yz(rhs_out[p])
    for s in (d_s, res_out):
        both = s[N - 1] + s[N]
        s[N - 1] = both
        s[N] = both
    msg[0] = res_out[own_plane]
    msg[1] = d_s[own_plane]
    for p in range(2 * N):
        if p in (0, 2 * N - 1):
            u_out[p] = jnp.zeros((ny, nz), F32)
            inv_out[p] = d_s[p]
        else:
            inv = inside / jnp.where(mask, d_s[p], 1.0)
            res = inside * res_out[p]
            inv_out[p] = inv
            res_out[p] = res
            u_out[p] = inv * res * (1.0 / THETA)
    base = parity * N
    acc = []
    col = [jnp.where(parity == 0, float(DM[a, 0]), float(DM[a, N - 1])) for a in range(N)]
    for e in range(lay.ey):
        rows = pl.ds(N * e, N)
        u = [u_out[base + a, rows, :] for a in range(N)]
        g = even_odd(DM, u, -1)
        total = None
        for a in range(N):
            term = (w_out[base + a, rows, :] * g[a]) * col[a]
            total = term if total is None else total + term
        acc.append(total)
    msg[4] = assemble_yz(jnp.concatenate(acc, axis=0))


def coarse_tables_kernel(lay, w_ref, rhs_ref, my, mz, ry, rz, g_out, r_out):
    ny, nz, cr = lay.ny, lay.nz, lay.cr
    lhs = []
    for el in range(2):
        for m in MASS:
            total = None
            for a in range(N):
                term = float(m[a]) * w_ref[N * el + a]
                total = term if total is None else total + term
            lhs.append(total)
    along_z = exact_dot(jnp.concatenate(lhs, axis=0), mz[...])
    for el in range(2):
        mom = {}
        for alpha in range(3):
            at = (3 * el + alpha) * ny
            block = exact_dot(my[...], along_z[at : at + ny])
            for beta in range(3):
                for gamma in range(3):
                    mom[alpha, beta, gamma] = block[
                        beta * cr : (beta + 1) * cr, gamma * nz : (gamma + 1) * nz
                    ]
        x_sum, y_sum, z_sum = {}, {}, {}
        for i in range(3):
            for j in range(3):
                x_sum[i, j] = mom[0, i, j] + 2.0 * mom[1, i, j] + mom[2, i, j]
                y_sum[i, j] = mom[i, 0, j] + 2.0 * mom[i, 1, j] + mom[i, 2, j]
                z_sum[i, j] = mom[i, j, 0] + 2.0 * mom[i, j, 1] + mom[i, j, 2]
        sign = (1.0, -1.0, 1.0)
        for alpha in range(3):
            for beta in range(3):
                for gamma in range(3):
                    g_out[el, 9 * alpha + 3 * beta + gamma] = 0.25 * (
                        sign[alpha] * x_sum[beta, gamma]
                        + sign[beta] * y_sum[alpha, gamma]
                        + sign[gamma] * z_sum[alpha, beta]
                    )
    for el in range(2):
        for i in range(2):
            total = None
            for a in range(N):
                term = float(RHO[a, i]) * rhs_ref[N * el + a]
                total = term if total is None else total + term
            part = exact_dot(ry[:, :ny], total)
            r_out[el, i] = exact_dot(part, rz[:nz])


def gradient_flux(lay, u_ref, w_ref, w_low, w_high, z_d, y_d, fx, fy, fz):
    ny, nz = lay.ny, lay.nz
    for el in range(2):
        for e in range(lay.ey):
            rows = pl.ds(N * e, N)
            u = [u_ref[N * el + a, rows, :] for a in range(N)]
            g = even_odd(DM, u, -1)
            for a in range(N):
                fx[N * el + a, rows, :] = w_ref[N * el + a, rows, :] * g[a]
    hi, lo = split(u_ref[...].reshape(2 * N * ny, nz))
    gz = z_apply(hi, lo, z_d[...])
    for p in range(2 * N):
        cut = slice(p * ny, (p + 1) * ny)
        gy = y_apply(hi[cut], lo[cut], y_d[...])
        w = w_ref[p]
        if p == 0 and w_low is not None:
            w = w + w_low
        if p == 2 * N - 1 and w_high is not None:
            w = w + w_high
        fy[p] = w * gy
        fz[p] = w * gz[cut]


def pair_index(i, j):
    return i + j


def shifted(c, q, r):
    if q:
        c = pltpu.roll(c, c.shape[0] - 1, 0)
    if r:
        c = pltpu.roll(c, c.shape[1] - 1, 1)
    return c


def scatter(parts):
    cr, nz = parts[0, 0].shape
    first = parts[0, 0] + pltpu.roll(parts[0, 1], 1, 1)
    second = parts[1, 0] + pltpu.roll(parts[1, 1], 1, 1)
    return first + pltpu.roll(second, 1, 0)


def gathered(c):
    return {(q, r): shifted(c, q, r) for q in range(2) for r in range(2)}


def face_apply(entry, c, out=None):
    out = {} if out is None else out
    for j in range(2):
        for k in range(2):
            for q in range(2):
                for r in range(2):
                    term = entry(pair_index(j, q), pair_index(k, r)) * c[q, r]
                    out[j, k] = term if (j, k) not in out else out[j, k] + term
    return out


def coarse_diag(entry):
    return scatter({(j, k): entry(2 * j, 2 * k) for j in range(2) for k in range(2)})


def coarse_mask(lay, start):
    row = lax.broadcasted_iota(jnp.int32, (lay.cr, lay.nz), 0) + lax.div(start, N)
    lane = lax.broadcasted_iota(jnp.int32, (lay.cr, lay.nz), 1)
    return (row > 0) & (row < lay.total_y // N) & (lane > 0) & (lane < lay.ez)


def second_kernel(lay, *refs):
    own_msg, mate_msg, w_ref, u_in, inv_in, res_in, g_ref, r_ref = refs[:8]
    z_d, z_dt, y_d, y_dt, ry, rz = refs[8:14]
    out, msg, state = refs[14:17]
    u, inv_s, res_s, sec, fx, fy, fz, back = refs[17:]
    ny, nz, cr = lay.ny, lay.nz, lay.cr
    parity, h, start, offset, low, high = lay.where()
    mask = yz_mask(ny, nz, start, lay.total_y)
    inside = mask.astype(F32)
    is_even = parity == 0
    lo_msg = [jnp.where(is_even, own_msg[k], mate_msg[k]) for k in range(5)]
    hi_msg = [jnp.where(is_even, mate_msg[k], own_msg[k]) for k in range(5)]
    u[...] = u_in[...]
    inv_s[...] = inv_in[...]
    res_s[...] = res_in[...]
    for p, m, flag in ((0, lo_msg, low), (2 * N - 1, hi_msg, high)):
        inv = inside * flag / jnp.where(mask, inv_in[p] + m[1], 1.0)
        res = inside * flag * (res_in[p] + m[0])
        inv_s[p] = inv
        res_s[p] = res
        u[p] = inv * res * (1.0 / THETA)
    gradient_flux(lay, u, w_ref, lo_msg[3], hi_msg[3], z_d, y_d, fx, fy, fz)
    for el in range(2):
        for e in range(lay.ey):
            rows = pl.ds(N * e, N)
            b = even_odd(DM.T, [fx[N * el + a, rows, :] for a in range(N)], -1)
            for a in range(N):
                back[N * el + a, rows, :] = b[a]
    hi, lo = split(fz[...].reshape(2 * N * ny, nz))
    bz = z_apply(hi, lo, z_dt[...])
    for p in range(2 * N):
        hi, lo = split(fy[p])
        by = y_apply(hi, lo, y_dt[...])
        back[p] = assemble_yz(back[p] + by + bz[p * ny : (p + 1) * ny])
    both = back[N - 1] + back[N]
    back[N - 1] = both
    back[N] = both
    back[0] = back[0] + lo_msg[4] + lo_msg[2] * u[0]
    back[2 * N - 1] = back[2 * N - 1] + hi_msg[4] + hi_msg[2] * u[2 * N - 1]
    for p in range(2 * N):
        res_one = res_s[p] - inside * back[p]
        sec[p] = (1.0 + RHO1 * RHO0) * u[p] + (2.0 * RHO1 / DELTA) * inv_s[p] * res_one
    out[...] = sec[pl.ds(parity * N, N), pl.ds(pl.multiple_of(offset, N), lay.own_y), :]
    gradient_flux(lay, sec, w_ref, None, None, z_d, y_d, fx, fy, fz)
    r = {}
    for el in range(2):
        for i in range(2):
            sums = []
            for f, weight in ((fx, DRHO), (fy, RHO), (fz, RHO)):
                total = None
                for a in range(N):
                    term = float(weight[a, i]) * f[N * el + a]
                    total = term if total is None else total + term
                sums.append(total)
            first = exact_dot(ry[...], jnp.concatenate(sums[:2], axis=0))
            second = exact_dot(ry[:, :ny], sums[2])
            both = exact_dot(jnp.concatenate([first, second], axis=1), rz[...])
            r[el, i] = r_ref[el, i] - both
    planes = [r[0, 0], r[0, 1] + r[1, 0], r[1, 1]]
    cmask = coarse_mask(lay, start)

    def entry(el, alpha):
        return lambda beta, gamma: g_ref[el, 9 * alpha + 3 * beta + gamma]

    d = [
        coarse_diag(entry(0, 0)),
        coarse_diag(entry(0, 2)) + coarse_diag(entry(1, 0)),
        coarse_diag(entry(1, 2)),
    ]
    cin = cmask.astype(F32)
    mid = (2.0 / 3.0) * cin * planes[1] / jnp.where(cmask, d[1], 1.0)
    c = gathered(mid)
    g_low = scatter(face_apply(entry(0, 1), c))
    g_high = scatter(face_apply(entry(1, 1), c))
    g_mid = scatter(face_apply(entry(1, 0), c, face_apply(entry(0, 2), c)))
    state[0] = planes[0]
    state[1] = planes[1]
    state[2] = planes[2]
    state[3] = d[0]
    state[4] = d[1]
    state[5] = d[2]
    state[6] = g_low
    state[7] = g_mid
    state[8] = g_high
    state[9] = mid
    msg[0] = jnp.where(is_even, planes[0], planes[2])
    msg[1] = jnp.where(is_even, d[0], d[2])
    msg[2] = jnp.where(is_even, g_low, g_high)
    for k in range(9):
        msg[3 + k] = jnp.where(is_even, g_ref[0, k], g_ref[1, 18 + k])


def third_kernel(lay, *refs):
    own_msg, mate_msg, sec, state, g_ref, py, pz, sy, sz, out, coarse = refs
    ny, nz, cr = lay.ny, lay.nz, lay.cr
    parity, h, start, offset, low, high = lay.where()
    is_even = parity == 0
    cmask = coarse_mask(lay, start)
    cin = cmask.astype(F32)
    lo_msg = [jnp.where(is_even, own_msg[k], mate_msg[k]) for k in range(12)]
    hi_msg = [jnp.where(is_even, mate_msg[k], own_msg[k]) for k in range(12)]

    def entry(el, alpha):
        return lambda beta, gamma: g_ref[el, 9 * alpha + 3 * beta + gamma]

    def outer(at, m, flag, el, alpha):
        rhs = cin * flag * (state[at] + m[0])
        d = jnp.where(cmask, state[3 + at] + m[1], 1.0)
        one = (2.0 / 3.0) * rhs / d
        c = gathered(one)
        here = lambda beta, gamma: g_ref[el, 9 * alpha + 3 * beta + gamma] + m[3 + 3 * beta + gamma]
        image = scatter(face_apply(here, c)) + state[6 + at] + m[2]
        cross = face_apply(entry(el, 1), c)
        solution = one + (2.0 / 3.0) * (rhs - cin * flag * image) / d
        return solution, cross

    c_low, cross_low = outer(0, lo_msg, low, 0, 0)
    c_high, cross_high = outer(2, hi_msg, high, 1, 2)
    cross = scatter({k: cross_low[k] + cross_high[k] for k in cross_low})
    rhs = cin * state[1]
    d = jnp.where(cmask, state[4], 1.0)
    c_mid = state[9] + (2.0 / 3.0) * (rhs - cin * (state[7] + cross)) / d
    left = jnp.where(is_even, c_low, c_mid)
    right = jnp.where(is_even, c_mid, c_high)
    both = jnp.concatenate([left, right], axis=1)
    rows = pl.ds(pl.multiple_of(offset, N), lay.own_y)
    along_y = exact_dot(py[rows, :], both)
    q_left = exact_dot(along_y[:, :nz], pz[...])
    q_right = exact_dot(along_y[:, nz:], pz[...])
    inside = yz_mask(lay.own_y, nz, start + offset, lay.total_y).astype(F32)
    q_left = inside * q_left
    q_right = inside * q_right
    first_flag = jnp.where(is_even, low, 1.0)
    last_flag = jnp.where(is_even, 1.0, high)
    for a in range(N):
        add = float(INTERP[a, 0]) * q_left + float(INTERP[a, 1]) * q_right
        if a == 0:
            add = first_flag * add
        if a == N - 1:
            add = last_flag * add
        out[a] = sec[a] + add
    crows = pl.ds(pl.multiple_of(lax.div(offset, 4), lay.own_y // 4), lay.own_y // 4)
    picked = exact_dot(sy[crows, :], both)
    coarse[0] = exact_dot(picked[:, :nz], sz[...])
    coarse[1] = exact_dot(picked[:, nz:], sz[...])


def run(kernel, args, outs, scratch=()):
    vm = pl.BlockSpec(memory_space=pltpu.VMEM)
    return pl.pallas_call(
        kernel,
        out_shape=[jax.ShapeDtypeStruct(o, F32) for o in outs],
        in_specs=[vm] * len(args),
        out_specs=[vm] * len(outs),
        scratch_shapes=[pltpu.VMEM(s, F32) for s in scratch],
        compiler_params=pltpu.CompilerParams(vmem_limit_bytes=VMEM_LIMIT),
    )(*args)


def swap_pairs(count, first):
    pairs = []
    for i in range(first, count - 1, 2):
        pairs += [(i, i + 1), (i + 1, i)]
    return pairs


def shards(dom, sub, rhs_local, coefficient):
    size_x, own_y, nz = rhs_local.shape
    lay = Layout(own_y, nz, dom, sub)
    ny, cr = lay.ny, lay.cr
    t = {k: jnp.asarray(v) for k, v in make_tables(ny, nz, own_y, lay.wrap).items()}
    even = lambda v: lax.ppermute(v, "dom", swap_pairs(dom, 0))
    odd = lambda v: lax.ppermute(v, "dom", swap_pairs(dom, 1))
    raw = jnp.stack([rhs_local, coefficient])
    if sub == 1:
        others = []
    elif sub == 2:
        others = [lax.ppermute(raw, "sub", [(0, 1), (1, 0)])]
    else:
        up = [(i, i + 1) for i in range(sub - 1)]
        others = [
            lax.ppermute(raw, "sub", up),
            lax.ppermute(raw, "sub", [(b, a) for a, b in up]),
        ]
    mate = even(raw)
    mate_others = [even(o) for o in others]
    pair = (2 * N, ny, nz)
    plane = (ny, nz)
    msg, w, rhs, u, inv, res = run(
        functools.partial(first_kernel, lay, len(others)),
        [rhs_local, coefficient, mate, *others, *mate_others, t["z_sq"], t["y_sq"], t["w3"]],
        [(5,) + plane] + [pair] * 5,
        [pair],
    )
    from_odd = odd(msg)
    g, r = run(
        functools.partial(coarse_tables_kernel, lay),
        [w, rhs, t["my"], t["mz"], t["ry"], t["rz"]],
        [(2, 27, cr, nz), (2, 2, cr, nz)],
    )
    from_mate = even(from_odd)
    sec, msg, state = run(
        functools.partial(second_kernel, lay),
        [from_odd, from_mate, w, u, inv, res, g, r]
        + [t[k] for k in ("z_d", "z_dt", "y_d", "y_dt", "ry", "rz")],
        [(N, own_y, nz), (12, cr, nz), (10, cr, nz)],
        [pair] * 8,
    )
    from_odd = odd(msg)
    from_mate = even(from_odd)
    return tuple(
        run(
            functools.partial(third_kernel, lay),
            [from_odd, from_mate, sec, state, g, t["py"], t["pz"], t["sy"], t["sz"]],
            [(N, own_y, nz), (size_x // 4, own_y // 4, nz // 4)],
        )
    )


def solution(mesh):
    dom, sub = mesh.shape["dom"], mesh.shape["sub"]
    return jax.shard_map(
        functools.partial(shards, dom, sub),
        mesh=mesh,
        in_specs=(P("dom", "sub", None), P("dom", "sub", None)),
        out_specs=(P("dom", "sub", None), P("dom", "sub", None)),
        check_vma=False,
    )
```

time: 168 us -> 35.7 us (0.21)
  local copies, waits for them, and re-layouts: 61.1 us -> 0.11 us
  starting transfers between devices: 46.7 us -> 11.6 us
  waiting for transfers between devices: 31.8 us -> 14.7 us
  matrix products: 16.6 us -> 0 us
  other arithmetic: 8.99 us -> 1.07 us
  Pallas kernels: 0 us -> 7.3 us
    slice x49 -> x0, local copies, waits for them, and re-layouts: 45.6 us -> none  [the longest x9 22.2 us: fold_local(): lax.index_in_dim(split, per_elem - 1, axis_at + 1, keepdims=False)]
    ppermute x20 -> x7, starting transfers between devices: 46.7 us -> 11.6 us  [the longest x2 6.63 us: shards(): odd = lambda v: lax.ppermute(v, 'dom', swap_pairs(dom, 1))]
    ppermute x20 -> x7, waiting for transfers between devices: 31.8 us -> 14.7 us  [the longest x2 7.3 us: shards(): odd = lambda v: lax.ppermute(v, 'dom', swap_pairs(dom, 1))]
    dot_general x29 -> x0, matrix products: 16.6 us -> none  [the longest x3 3.57 us: coarse_matrices(): jnp.einsum(form, shaped, mass_pair, grad_pair, mass_pair, precision=precise)]
    another operation x14 -> x0, local copies, waits for them, and re-layouts: 9.87 us -> none  [the longest x5 6.26 us: fold_local(): field.reshape(dims_of[:axis_at] + (elements, per_elem) + dims_of[axis_at...]
    pallas_call x0 -> x4, Pallas kernels: none -> 7.3 us  [run(): pl.pallas_call(kernel, out_shape=[jax.ShapeDtypeStruct(o, F32) for o in o...]
    unnamed x64 -> x34, local copies, waits for them, and re-layouts: 3.46 us -> 0.11 us
    reshape x3 -> x0, other arithmetic: 2.94 us -> none  [fold_local(): return joined.reshape(dims_of)]
  transfers between devices with their start and end apart: 20 -> 7, of which waited for: 12 -> 5; matrix products, arithmetic and copies ran while one was open for 8% -> 0% of each run, Pallas kernels for 0% -> 5%
where the time goes in v1:
time: 35.7 us; the launch traced here: 35.6 us
  waiting for transfers between devices  14.7 us (41%)
  starting transfers between devices  11.6 us (32%)
  Pallas kernels  7.3 us (20%)
  other arithmetic  1.07 us (3%)
  between operations  0.85 us (2%)
    ppermute x2, waiting for transfers between devices, shards(): odd = lambda v: lax.ppermute(v, 'dom', swap_pairs(dom, 1))  7.3 us
    pallas_call x4, Pallas kernels, run(): pl.pallas_call(kernel, out_shape=[jax.ShapeDtypeStruct(o, F32) for o in o...  7.3 us
    ppermute x2, starting transfers between devices, shards(): odd = lambda v: lax.ppermute(v, 'dom', swap_pairs(dom, 1))  6.63 us
    ppermute x1, waiting for transfers between devices, shards(): others = [lax.ppermute(raw, 'sub', [(0, 1), (1, 0)])]  4.98 us
    ppermute x4, starting transfers between devices, shards(): even = lambda v: lax.ppermute(v, 'dom', swap_pairs(dom, 0))  3.63 us
    ppermute x4, waiting for transfers between devices, shards(): even = lambda v: lax.ppermute(v, 'dom', swap_pairs(dom, 0))  2.39 us
    ppermute x1, starting transfers between devices, shards(): others = [lax.ppermute(raw, 'sub', [(0, 1), (1, 0)])]  1.3 us
    another operation x1, other arithmetic, shards(): raw = jnp.stack([rhs_local, coefficient])  1.07 us
  transfers between devices with their start and end apart: 7, of which 5 were waited for; matrix products, arithmetic and copies ran while one was open for 0% of the time, Pallas kernels for 5%

profile of v1, /device:TPU:19, one launch (start us, length us, event | category | flops | bytes accessed | tf_op | source)
XLA Modules:
  0.0 35.6 jit_solution(6770029259321195292)
XLA Ops:
  0.6 0.0 copy-start
  0.6 0.0 copy-start.1
  0.6 0.0 copy-start.6
  0.7 0.0 copy-start.11
  0.7 0.0 copy-start.12
  0.7 1.1 %pad_maximum_fusion = f32[2,8,32,128]{3,2,1,0:T(8,128)S(1)} fusion(f32[1,8,32,128]{3,2,1,0:T(8,128)} %bitcast.3, f32[1,8,32,128]{3,2,1,0:T(8,128)} %bitcast.2), kind=kLoop, calls=%fused_computation | loop fusion | flops 65536 | bytes 524288 | tf_op jit(solution)/shard_map/stack | solution.py:619
  1.8 0.0 copy-start.2
  1.8 0.0 copy-start.3
  1.8 1.3 %collective-permute-start.1 = (f32[2,8,32,128]{3,2,1,0:T(8,128)S(1)}, f32[2,8,32,128]{3,2,1,0:T(8,128)S(1)}, u32[]{:S(2)}, u32[]{:S(2)}) collective-permute-start(f32[2,8,32,128]{3,2,1,0:T(8,128)S(1)} %pad_maximum_fusion), channel_id=1, source_target_pairs={{0,1},{1,0},{2,3},{3,2},{4,5},{5,4},{6,7},{7,6},{8,9},{9,8},{10,11... | collective-permute-start | bytes 786440 | tf_op jit(solution)/shard_map/ppermute | solution.py:623
  3.1 1.0 %collective-permute-start = (f32[2,8,32,128]{3,2,1,0:T(8,128)S(1)}, f32[2,8,32,128]{3,2,1,0:T(8,128)S(1)}, u32[]{:S(2)}, u32[]{:S(2)}) collective-permute-start(f32[2,8,32,128]{3,2,1,0:T(8,128)S(1)} %pad_maximum_fusion), channel_id=1, source_target_pairs={{0,2},{2,0},{4,6},{6,4},{8,10},{10,8},{12,14},{14,12},{16,18},{18,... | collective-permute-start | bytes 786440 | tf_op jit(solution)/shard_map/ppermute | solution.py:617
  4.0 5.0 %collective-permute-done.1.refs_3_ = f32[2,8,32,128]{3,2,1,0:T(8,128)S(1)} collective-permute-done((f32[2,8,32,128]{3,2,1,0:T(8,128)S(1)}, f32[2,8,32,128]{3,2,1,0:T(8,128)S(1)}, u32[]{:S(2)}, u32[]{:S(2)}) %collective-permute-start.1) | collective-permute-done | bytes 262176 | tf_op jit(solution)/shard_map/ppermute | solution.py:623
  9.0 1.5 %collective-permute-start.2 = (f32[2,8,32,128]{3,2,1,0:T(8,128)S(1)}, f32[2,8,32,128]{3,2,1,0:T(8,128)S(1)}, u32[]{:S(2)}, u32[]{:S(2)}) collective-permute-start(f32[2,8,32,128]{3,2,1,0:T(8,128)S(1)} %collective-permute-done.1.refs_3_), channel_id=1, source_target_pairs={{0,2},{2,0},{4,6},{6,4},{8,10},{10,8},{12,14},{14,12},{16,18},{18,... | collective-permute-start | bytes 786440 | tf_op jit(solution)/shard_map/ppermute | solution.py:617
  10.6 0.0 collective-permute-done.refs_2_
  10.6 1.2 %collective-permute-done.2.refs_4_ = f32[2,8,32,128]{3,2,1,0:T(8,128)S(1)} collective-permute-done((f32[2,8,32,128]{3,2,1,0:T(8,128)S(1)}, f32[2,8,32,128]{3,2,1,0:T(8,128)S(1)}, u32[]{:S(2)}, u32[]{:S(2)}) %collective-permute-start.2) | collective-permute-done | bytes 262176 | tf_op jit(solution)/shard_map/ppermute | solution.py:617
  11.7 0.0 copy-done
  11.7 0.0 copy-done.1
  11.7 0.0 copy-done.6
  11.7 0.0 copy-done.11
  11.7 0.0 copy-done.12
  11.8 0.0 copy-start.15
  11.8 1.2 %shard_map.176 = (f32[5,64,128]{2,1,0:T(8,128)S(1)}, f32[16,64,128]{2,1,0:T(8,128)S(1)}, f32[16,64,128]{2,1,0:T(8,128)S(1)}, f32[16,64,128]{2,1,0:T(8,128)S(1)},...) custom-call(f32[8,32,128]{2,1,0:T(8,128)S(1)} %copy-done, f32[8,32,128]{2,1,0:T(8,128)S(1)} %copy-done.1, ...), custom_call_target="tpu_custom_call" | custom-call | tf_op jit(solution)/shard_map/pallas_call | solution.py:595
  13.0 0.0 copy-start.14
  13.0 3.4 %collective-permute-start.3 = (f32[5,64,128]{2,1,0:T(8,128)S(1)}, f32[5,64,128]{2,1,0:T(8,128)S(1)}, u32[]{:S(2)}, u32[]{:S(2)}) collective-permute-start(f32[5,64,128]{2,1,0:T(8,128)S(1)} %get-tuple-element.13), channel_id=1, source_target_pairs={{2,4},{4,2},{6,8},{8,6},{10,12},{12,10},{14,16},{16,14},{18,20},{2... | collective-permute-start | bytes 491528 | tf_op jit(solution)/shard_map/ppermute | solution.py:618
  16.4 4.2 %collective-permute-done.3.refs_0_ = f32[5,64,128]{2,1,0:T(8,128)S(1)} collective-permute-done((f32[5,64,128]{2,1,0:T(8,128)S(1)}, f32[5,64,128]{2,1,0:T(8,128)S(1)}, u32[]{:S(2)}, u32[]{:S(2)}) %collective-permute-start.3) | collective-permute-done | bytes 163872 | tf_op jit(solution)/shard_map/ppermute | solution.py:618
  20.6 1.1 %collective-permute-start.4 = (f32[5,64,128]{2,1,0:T(8,128)S(1)}, f32[5,64,128]{2,1,0:T(8,128)S(1)}, u32[]{:S(2)}, u32[]{:S(2)}) collective-permute-start(f32[5,64,128]{2,1,0:T(8,128)S(1)} %collective-permute-done.3.refs_0_), channel_id=1, source_target_pairs={{0,2},{2,0},{4,6},{6,4},{8,10},{10,8},{12,14},{14,12},{16,18},{18,... | collective-permute-start | bytes 491528 | tf_op jit(solution)/shard_map/ppermute | solution.py:617
  21.7 0.0 copy-done.2
  21.7 0.0 copy-done.3
  21.7 0.0 copy-done.15
  21.7 0.0 copy-done.14
  21.7 0.0 copy-start.4
  21.8 0.0 copy-start.5
  21.8 0.0 copy-start.9
  21.8 0.0 copy-start.10
  21.8 1.6 %shard_map.177 = (f32[2,27,8,128]{3,2,1,0:T(8,128)S(1)}, f32[2,2,8,128]{3,2,1,0:T(8,128)S(1)}) custom-call(f32[16,64,128]{2,1,0:T(8,128)S(1)} %get-tuple-element.14.w_ref.refs_2_, f32[16,64,128]{2,1,0:T(8,128)S(1)} %get-tuple-element.18.rhs_ref, f32[24,64]{1,0:T(8,128)S(1)} %copy-done.15, f32[128,384]{1,0:T(8,128)S(1)} %copy-done.3, ...), custom_call_target="tpu_custom_call" | custom-call | tf_op jit(solution)/shard_map/pallas_call | solution.py:595
  23.4 0.0 collective-permute-done.4.refs_1_
  23.4 0.0 copy-done.4
  23.5 0.0 copy-done.5
  23.5 0.0 copy-done.9
  23.5 0.0 copy-done.10
  23.5 0.0 copy-start.7
  23.5 0.0 copy-start.8
  23.5 0.0 copy-start.13
  23.5 0.0 copy-start.16
  23.5 3.1 %shard_map.178 = (f32[8,32,128]{2,1,0:T(8,128)S(1)}, f32[12,8,128]{2,1,0:T(8,128)S(1)}, f32[10,8,128]{2,1,0:T(8,128)S(1)}) custom-call(f32[5,64,128]{2,1,0:T(8,128)S(1)} %collective-permute-done.3.refs_0_, f32[5,64,128]{2,1,0:T(8,128)S(1)} %collective-permute-done.4.refs_1_, f32[16,64,128]{2,1,0:T(8,128)S(1)} %get-tuple-element.14.w_ref.refs_2_, ...), custom_call_target="tpu_custom_call" | custom-call | tf_op jit(solution)/shard_map/pallas_call | solution.py:595
  26.6 3.2 %collective-permute-start.5 = (f32[12,8,128]{2,1,0:T(8,128)S(1)}, f32[12,8,128]{2,1,0:T(8,128)S(1)}, u32[]{:S(2)}, u32[]{:S(2)}) collective-permute-start(f32[12,8,128]{2,1,0:T(8,128)S(1)} %get-tuple-element.21), channel_id=1, source_target_pairs={{2,4},{4,2},{6,8},{8,6},{10,12},{12,10},{14,16},{16,14},{18,20},{2... | collective-permute-start | bytes 147464 | tf_op jit(solution)/shard_map/ppermute | solution.py:618
  29.8 3.1 %collective-permute-done.5.refs_0_ = f32[12,8,128]{2,1,0:T(8,128)S(1)} collective-permute-done((f32[12,8,128]{2,1,0:T(8,128)S(1)}, f32[12,8,128]{2,1,0:T(8,128)S(1)}, u32[]{:S(2)}, u32[]{:S(2)}) %collective-permute-start.5) | collective-permute-done | bytes 49184 | tf_op jit(solution)/shard_map/ppermute | solution.py:618
  32.9 0.0 collective-permute-start.6
  32.9 1.2 %collective-permute-done.6.refs_1_ = f32[12,8,128]{2,1,0:T(8,128)S(1)} collective-permute-done((f32[12,8,128]{2,1,0:T(8,128)S(1)}, f32[12,8,128]{2,1,0:T(8,128)S(1)}, u32[]{:S(2)}, u32[]{:S(2)}) %collective-permute-start.6) | collective-permute-done | bytes 49184 | tf_op jit(solution)/shard_map/ppermute | solution.py:617
  34.2 0.0 copy-done.7
  34.2 0.0 copy-done.8
  34.2 0.0 copy-done.13
  34.2 0.0 copy-done.16
  34.2 1.4 %shard_map.179 = (f32[8,32,128]{2,1,0:T(8,128)}, f32[2,8,32]{2,1,0:T(8,128)}) custom-call(f32[12,8,128]{2,1,0:T(8,128)S(1)} %collective-permute-done.5.refs_0_, f32[12,8,128]{2,1,0:T(8,128)S(1)} %collective-permute-done.6.refs_1_, f32[8,32,128]{2,1,0:T(8,128)S(1)} %get-tuple-element.22.refs_2_, f32[10,8,128]{2,1,0:T(8,128)S(1)} %get-tuple-element.23.refs_3_, ...), custom_call_target="tpu_custom_call" | custom-call | tf_op jit(solution)/shard_map/pallas_call | solution.py:595
Async XLA Ops:
  0.6 11.1 %copy-start = (f32[8,32,128]{2,1,0:T(8,128)S(1)}, f32[8,32,128]{2,1,0:T(8,128)}, u32[]{:S(2)}) copy-start(f32[8,32,128]{2,1,0:T(8,128)} %refs_0_.1) | copy-start | bytes 393220
  0.6 11.1 %copy-start.1 = (f32[8,32,128]{2,1,0:T(8,128)S(1)}, f32[8,32,128]{2,1,0:T(8,128)}, u32[]{:S(2)}) copy-start(f32[8,32,128]{2,1,0:T(8,128)} %refs_1_.1) | copy-start | bytes 393220
  0.6 11.1 %copy-start.6 = (bf16[384,128]{1,0:T(8,128)(2,1)S(1)}, bf16[384,128]{1,0:T(8,128)(2,1)}, u32[]{:S(2)}) copy-start(bf16[384,128]{1,0:T(8,128)(2,1)} %constant.32.clone.refs_5_) | copy-start | bytes 294916
  0.7 11.1 %copy-start.11 = (f32[8,8,128]{2,1,0:T(8,128)S(1)}, f32[8,8,128]{2,1,0:T(8,128)}, u32[]{:S(2)}) copy-start(f32[8,8,128]{2,1,0:T(8,128)} %constant.44.clone.refs_7_) | copy-start | bytes 98308
  0.7 11.1 %copy-start.12 = (bf16[64,192]{1,0:T(8,128)(2,1)S(1)}, bf16[64,192]{1,0:T(8,128)(2,1)}, u32[]{:S(2)}) copy-start(bf16[64,192]{1,0:T(8,128)(2,1)} %constant.35.clone.refs_6_) | copy-start | bytes 73732
  1.8 20.0 %copy-start.2 = (f32[256,128]{1,0:T(8,128)S(1)}, f32[256,128]{1,0:T(8,128)}, u32[]{:S(2)}) copy-start(f32[256,128]{1,0:T(8,128)} %constant.37.clone.rz.refs_13_) | copy-start | bytes 393220
  1.8 20.0 %copy-start.3 = (f32[128,384]{1,0:T(8,128)S(1)}, f32[128,384]{1,0:T(8,128)}, u32[]{:S(2)}) copy-start(f32[128,384]{1,0:T(8,128)} %constant.39.clone.mz) | copy-start | bytes 589828
  1.8 7.2 %collective-permute-start.1 = (f32[2,8,32,128]{3,2,1,0:T(8,128)S(1)}, f32[2,8,32,128]{3,2,1,0:T(8,128)S(1)}, u32[]{:S(2)}, u32[]{:S(2)}) collective-permute-start(f32[2,8,32,128]{3,2,1,0:T(8,128)S(1)} %pad_maximum_fusion), channel_id=1, source_target_pairs={{0,1},{1,0},{2,3},{3,2},{4,5},{5,4},{6,7},{7,6},{8,9},{9,8},{10,11... | collective-permute-start | bytes 786440 | tf_op jit(solution)/shard_map/ppermute | solution.py:623
  3.1 7.5 %collective-permute-start = (f32[2,8,32,128]{3,2,1,0:T(8,128)S(1)}, f32[2,8,32,128]{3,2,1,0:T(8,128)S(1)}, u32[]{:S(2)}, u32[]{:S(2)}) collective-permute-start(f32[2,8,32,128]{3,2,1,0:T(8,128)S(1)} %pad_maximum_fusion), channel_id=1, source_target_pairs={{0,2},{2,0},{4,6},{6,4},{8,10},{10,8},{12,14},{14,12},{16,18},{18,... | collective-permute-start | bytes 786440 | tf_op jit(solution)/shard_map/ppermute | solution.py:617
  9.0 2.7 %collective-permute-start.2 = (f32[2,8,32,128]{3,2,1,0:T(8,128)S(1)}, f32[2,8,32,128]{3,2,1,0:T(8,128)S(1)}, u32[]{:S(2)}, u32[]{:S(2)}) collective-permute-start(f32[2,8,32,128]{3,2,1,0:T(8,128)S(1)} %collective-permute-done.1.refs_3_), channel_id=1, source_target_pairs={{0,2},{2,0},{4,6},{6,4},{8,10},{10,8},{12,14},{14,12},{16,18},{18,... | collective-permute-start | bytes 786440 | tf_op jit(solution)/shard_map/ppermute | solution.py:617
  11.8 10.0 %copy-start.15 = (f32[24,64]{1,0:T(8,128)S(1)}, f32[24,64]{1,0:T(8,128)}, u32[]{:S(2)}) copy-start(f32[24,64]{1,0:T(8,128)} %constant.38.clone.my) | copy-start | bytes 18436
  13.0 8.8 %copy-start.14 = (f32[8,128]{1,0:T(8,128)S(1)}, f32[8,128]{1,0:T(8,128)}, u32[]{:S(2)}) copy-start(f32[8,128]{1,0:T(8,128)} %constant.36.clone.ry.refs_12_) | copy-start | bytes 12292
  13.0 7.6 %collective-permute-start.3 = (f32[5,64,128]{2,1,0:T(8,128)S(1)}, f32[5,64,128]{2,1,0:T(8,128)S(1)}, u32[]{:S(2)}, u32[]{:S(2)}) collective-permute-start(f32[5,64,128]{2,1,0:T(8,128)S(1)} %get-tuple-element.13), channel_id=1, source_target_pairs={{2,4},{4,2},{6,8},{8,6},{10,12},{12,10},{14,16},{16,14},{18,20},{2... | collective-permute-start | bytes 491528 | tf_op jit(solution)/shard_map/ppermute | solution.py:618
  20.6 2.8 %collective-permute-start.4 = (f32[5,64,128]{2,1,0:T(8,128)S(1)}, f32[5,64,128]{2,1,0:T(8,128)S(1)}, u32[]{:S(2)}, u32[]{:S(2)}) collective-permute-start(f32[5,64,128]{2,1,0:T(8,128)S(1)} %collective-permute-done.3.refs_0_), channel_id=1, source_target_pairs={{0,2},{2,0},{4,6},{6,4},{8,10},{10,8},{12,14},{14,12},{16,18},{18,... | collective-permute-start | bytes 491528 | tf_op jit(solution)/shard_map/ppermute | solution.py:617
  21.7 1.7 %copy-start.4 = (bf16[384,128]{1,0:T(8,128)(2,1)S(1)}, bf16[384,128]{1,0:T(8,128)(2,1)}, u32[]{:S(2)}) copy-start(bf16[384,128]{1,0:T(8,128)(2,1)} %constant.31.clone.refs_9_) | copy-start | bytes 294916
  21.8 1.7 %copy-start.5 = (bf16[384,128]{1,0:T(8,128)(2,1)S(1)}, bf16[384,128]{1,0:T(8,128)(2,1)}, u32[]{:S(2)}) copy-start(bf16[384,128]{1,0:T(8,128)(2,1)} %constant.30.clone.refs_8_) | copy-start | bytes 294916
  21.8 1.7 %copy-start.9 = (bf16[64,192]{1,0:T(8,128)(2,1)S(1)}, bf16[64,192]{1,0:T(8,128)(2,1)}, u32[]{:S(2)}) copy-start(bf16[64,192]{1,0:T(8,128)(2,1)} %constant.34.clone.refs_11_) | copy-start | bytes 73732
  21.8 1.7 %copy-start.10 = (bf16[64,192]{1,0:T(8,128)(2,1)S(1)}, bf16[64,192]{1,0:T(8,128)(2,1)}, u32[]{:S(2)}) copy-start(bf16[64,192]{1,0:T(8,128)(2,1)} %constant.33.clone.refs_10_) | copy-start | bytes 73732
  23.5 10.7 %copy-start.7 = (f32[128,32]{1,0:T(8,128)S(1)}, f32[128,32]{1,0:T(8,128)}, u32[]{:S(2)}) copy-start(f32[128,32]{1,0:T(8,128)} %constant.43.clone.refs_8_) | copy-start | bytes 49156
  23.5 10.7 %copy-start.8 = (f32[128,128]{1,0:T(8,128)S(1)}, f32[128,128]{1,0:T(8,128)}, u32[]{:S(2)}) copy-start(f32[128,128]{1,0:T(8,128)} %constant.41.clone.refs_6_) | copy-start | bytes 196612
  23.5 10.7 %copy-start.13 = (f32[64,8]{1,0:T(8,128)S(1)}, f32[64,8]{1,0:T(8,128)}, u32[]{:S(2)}) copy-start(f32[64,8]{1,0:T(8,128)} %constant.40.clone.refs_5_) | copy-start | bytes 6148
  23.5 10.6 %copy-start.16 = (f32[16,8]{1,0:T(8,128)S(1)}, f32[16,8]{1,0:T(8,128)}, u32[]{:S(2)}) copy-start(f32[16,8]{1,0:T(8,128)} %constant.42.clone.refs_7_) | copy-start | bytes 1540
  26.6 6.3 %collective-permute-start.5 = (f32[12,8,128]{2,1,0:T(8,128)S(1)}, f32[12,8,128]{2,1,0:T(8,128)S(1)}, u32[]{:S(2)}, u32[]{:S(2)}) collective-permute-start(f32[12,8,128]{2,1,0:T(8,128)S(1)} %get-tuple-element.21), channel_id=1, source_target_pairs={{2,4},{4,2},{6,8},{8,6},{10,12},{12,10},{14,16},{16,14},{18,20},{2... | collective-permute-start | bytes 147464 | tf_op jit(solution)/shard_map/ppermute | solution.py:618
  32.9 1.2 %collective-permute-start.6 = (f32[12,8,128]{2,1,0:T(8,128)S(1)}, f32[12,8,128]{2,1,0:T(8,128)S(1)}, u32[]{:S(2)}, u32[]{:S(2)}) collective-permute-start(f32[12,8,128]{2,1,0:T(8,128)S(1)} %collective-permute-done.5.refs_0_), channel_id=1, source_target_pairs={{0,2},{2,0},{4,6},{6,4},{8,10},{10,8},{12,14},{14,12},{16,18},{18,... | collective-permute-start | bytes 147464 | tf_op jit(solution)/shard_map/ppermute | solution.py:617

commit v2 on v1

--- a/solution.py
+++ b/solution.py
@@ -609,13 +609,22 @@
     return pairs
 
 
+def chip_pairs(dom, sub):
+    pairs = []
+    for a, b in swap_pairs(dom, 1):
+        pairs += [(a * sub + q, b * sub + q) for q in range(sub)]
+    for end in (0, dom - 1):
+        pairs += [(end * sub + a, end * sub + b) for a, b in swap_pairs(sub, 0)]
+    return pairs
+
+
 def shards(dom, sub, rhs_local, coefficient):
     size_x, own_y, nz = rhs_local.shape
     lay = Layout(own_y, nz, dom, sub)
     ny, cr = lay.ny, lay.cr
     t = {k: jnp.asarray(v) for k, v in make_tables(ny, nz, own_y, lay.wrap).items()}
     even = lambda v: lax.ppermute(v, "dom", swap_pairs(dom, 0))
-    odd = lambda v: lax.ppermute(v, "dom", swap_pairs(dom, 1))
+    odd = lambda v: lax.ppermute(v, ("dom", "sub"), chip_pairs(dom, sub))
     raw = jnp.stack([rhs_local, coefficient])
     if sub == 1:
         others = []
@@ -643,6 +652,7 @@
         [w, rhs, t["my"], t["mz"], t["ry"], t["rz"]],
         [(2, 27, cr, nz), (2, 2, cr, nz)],
     )
+    from_odd, g, r = lax.optimization_barrier((from_odd, g, r))
     from_mate = even(from_odd)
     sec, msg, state = run(
         functools.partial(second_kernel, lay),

time: 35.7 us -> 31.3 us (0.88)
  the two profiles are of different devices: /device:TPU:19 before, /device:TPU:7 now
where the time goes in v2:
time: 31.3 us; the launch traced here: 31.2 us
  waiting for transfers between devices  15 us (48%)
  Pallas kernels  7.3 us (23%)
  starting transfers between devices  6.85 us (22%)
  other arithmetic  1.07 us (3%)
  between operations  0.81 us (3%)
    pallas_call x4, Pallas kernels, run(): pl.pallas_call(kernel, out_shape=[jax.ShapeDtypeStruct(o, F32) for o in o...  7.3 us
    ppermute x1, waiting for transfers between devices, shards(): others = [lax.ppermute(raw, 'sub', [(0, 1), (1, 0)])]  5.99 us
    ppermute x2, waiting for transfers between devices, shards(): odd = lambda v: lax.ppermute(v, ('dom', 'sub'), chip_pairs(dom, sub))  5.63 us
    ppermute x4, starting transfers between devices, shards(): even = lambda v: lax.ppermute(v, 'dom', swap_pairs(dom, 0))  3.63 us
    ppermute x4, waiting for transfers between devices, shards(): even = lambda v: lax.ppermute(v, 'dom', swap_pairs(dom, 0))  3.42 us
    ppermute x2, starting transfers between devices, shards(): odd = lambda v: lax.ppermute(v, ('dom', 'sub'), chip_pairs(dom, sub))  2.93 us
    another operation x1, other arithmetic, shards(): raw = jnp.stack([rhs_local, coefficient])  1.07 us
  transfers between devices with their start and end apart: 7, of which 6 were waited for; matrix products, arithmetic and copies ran while one was open for 0% of the time, Pallas kernels for 5%

profile of v2, /device:TPU:7, one launch (start us, length us, event | category | flops | bytes accessed | tf_op | source)
XLA Modules:
  0.0 31.2 jit_solution(12443924474092262142)
XLA Ops:
  0.6 0.0 copy-start
  0.6 0.0 copy-start.1
  0.6 0.0 copy-start.6
  0.7 0.0 copy-start.11
  0.7 0.0 copy-start.12
  0.7 1.1 %pad_maximum_fusion = f32[2,8,32,128]{3,2,1,0:T(8,128)S(1)} fusion(f32[1,8,32,128]{3,2,1,0:T(8,128)} %bitcast.3, f32[1,8,32,128]{3,2,1,0:T(8,128)} %bitcast.2), kind=kLoop, calls=%fused_computation | loop fusion | flops 65536 | bytes 524288 | tf_op jit(solution)/shard_map/stack | solution.py:628
  1.8 0.0 copy-start.2
  1.8 0.0 copy-start.3
  1.8 0.3 collective-permute-start.1
  2.1 1.0 %collective-permute-start = (f32[2,8,32,128]{3,2,1,0:T(8,128)S(1)}, f32[2,8,32,128]{3,2,1,0:T(8,128)S(1)}, u32[]{:S(2)}, u32[]{:S(2)}) collective-permute-start(f32[2,8,32,128]{3,2,1,0:T(8,128)S(1)} %pad_maximum_fusion), channel_id=1, source_target_pairs={{0,2},{2,0},{4,6},{6,4},{8,10},{10,8},{12,14},{14,12},{16,18},{18,... | collective-permute-start | bytes 786440 | tf_op jit(solution)/shard_map/ppermute | solution.py:626
  3.0 6.0 %collective-permute-done.1.refs_3_ = f32[2,8,32,128]{3,2,1,0:T(8,128)S(1)} collective-permute-done((f32[2,8,32,128]{3,2,1,0:T(8,128)S(1)}, f32[2,8,32,128]{3,2,1,0:T(8,128)S(1)}, u32[]{:S(2)}, u32[]{:S(2)}) %collective-permute-start.1) | collective-permute-done | bytes 262176 | tf_op jit(solution)/shard_map/ppermute | solution.py:632
  9.0 1.5 %collective-permute-start.2 = (f32[2,8,32,128]{3,2,1,0:T(8,128)S(1)}, f32[2,8,32,128]{3,2,1,0:T(8,128)S(1)}, u32[]{:S(2)}, u32[]{:S(2)}) collective-permute-start(f32[2,8,32,128]{3,2,1,0:T(8,128)S(1)} %collective-permute-done.1.refs_3_), channel_id=1, source_target_pairs={{0,2},{2,0},{4,6},{6,4},{8,10},{10,8},{12,14},{14,12},{16,18},{18,... | collective-permute-start | bytes 786440 | tf_op jit(solution)/shard_map/ppermute | solution.py:626
  10.6 0.0 collective-permute-done.refs_2_
  10.6 1.2 %collective-permute-done.2.refs_4_ = f32[2,8,32,128]{3,2,1,0:T(8,128)S(1)} collective-permute-done((f32[2,8,32,128]{3,2,1,0:T(8,128)S(1)}, f32[2,8,32,128]{3,2,1,0:T(8,128)S(1)}, u32[]{:S(2)}, u32[]{:S(2)}) %collective-permute-start.2) | collective-permute-done | bytes 262176 | tf_op jit(solution)/shard_map/ppermute | solution.py:626
  11.7 0.0 copy-done
  11.7 0.0 copy-done.1
  11.7 0.0 copy-done.6
  11.7 0.0 copy-done.11
  11.7 0.0 copy-done.12
  11.8 0.0 copy-start.15
  11.8 1.2 %shard_map.176 = (f32[5,64,128]{2,1,0:T(8,128)S(1)}, f32[16,64,128]{2,1,0:T(8,128)S(1)}, f32[16,64,128]{2,1,0:T(8,128)S(1)}, f32[16,64,128]{2,1,0:T(8,128)S(1)},...) custom-call(f32[8,32,128]{2,1,0:T(8,128)S(1)} %copy-done, f32[8,32,128]{2,1,0:T(8,128)S(1)} %copy-done.1, ...), custom_call_target="tpu_custom_call" | custom-call | tf_op jit(solution)/shard_map/pallas_call | solution.py:595
  13.0 0.0 copy-start.14
  13.0 1.6 %collective-permute-start.3 = (f32[5,64,128]{2,1,0:T(8,128)S(1)}, f32[5,64,128]{2,1,0:T(8,128)S(1)}, u32[]{:S(2)}, u32[]{:S(2)}) collective-permute-start(f32[5,64,128]{2,1,0:T(8,128)S(1)} %get-tuple-element.16), channel_id=1, source_target_pairs={{2,4},{3,5},{4,2},{5,3},{6,8},{7,9},{8,6},{9,7},{10,12},{11,13},{1... | collective-permute-start | bytes 491528 | tf_op jit(solution)/shard_map/ppermute | solution.py:627
  14.6 0.0 copy-done.2
  14.6 0.0 copy-done.3
  14.6 0.0 copy-done.15
  14.6 0.0 copy-done.14
  14.6 0.0 copy-start.4
  14.6 0.0 copy-start.5
  14.6 0.0 copy-start.9
  14.6 0.0 copy-start.10
  14.6 1.6 %shard_map.177 = (f32[2,27,8,128]{3,2,1,0:T(8,128)S(1)}, f32[2,2,8,128]{3,2,1,0:T(8,128)S(1)}) custom-call(f32[16,64,128]{2,1,0:T(8,128)S(1)} %get-tuple-element.17.w_ref.refs_2_, f32[16,64,128]{2,1,0:T(8,128)S(1)} %get-tuple-element.18.rhs_ref, f32[24,64]{1,0:T(8,128)S(1)} %copy-done.15, f32[128,384]{1,0:T(8,128)S(1)} %copy-done.3, ...), custom_call_target="tpu_custom_call" | custom-call | tf_op jit(solution)/shard_map/pallas_call | solution.py:595
  16.3 2.5 %collective-permute-done.3.refs_0_ = f32[5,64,128]{2,1,0:T(8,128)S(1)} collective-permute-done((f32[5,64,128]{2,1,0:T(8,128)S(1)}, f32[5,64,128]{2,1,0:T(8,128)S(1)}, u32[]{:S(2)}, u32[]{:S(2)}) %collective-permute-start.3) | collective-permute-done | bytes 163872 | tf_op jit(solution)/shard_map/ppermute | solution.py:627
  18.8 1.1 %collective-permute-start.4 = (f32[5,64,128]{2,1,0:T(8,128)S(1)}, f32[5,64,128]{2,1,0:T(8,128)S(1)}, u32[]{:S(2)}, u32[]{:S(2)}) collective-permute-start(f32[5,64,128]{2,1,0:T(8,128)S(1)} %collective-permute-done.3.refs_0_), channel_id=1, source_target_pairs={{0,2},{2,0},{4,6},{6,4},{8,10},{10,8},{12,14},{14,12},{16,18},{18,... | collective-permute-start | bytes 491528 | tf_op jit(solution)/shard_map/ppermute | solution.py:626
  19.9 1.0 %collective-permute-done.4.refs_1_ = f32[5,64,128]{2,1,0:T(8,128)S(1)} collective-permute-done((f32[5,64,128]{2,1,0:T(8,128)S(1)}, f32[5,64,128]{2,1,0:T(8,128)S(1)}, u32[]{:S(2)}, u32[]{:S(2)}) %collective-permute-start.4) | collective-permute-done | bytes 163872 | tf_op jit(solution)/shard_map/ppermute | solution.py:626
  20.9 0.0 copy-done.4
  20.9 0.0 copy-done.5
  20.9 0.0 copy-done.9
  20.9 0.0 copy-done.10
  20.9 0.0 copy-start.7
  21.0 0.0 copy-start.8
  21.0 0.0 copy-start.13
  21.0 0.0 copy-start.16
  21.0 3.1 %shard_map.178 = (f32[8,32,128]{2,1,0:T(8,128)S(1)}, f32[12,8,128]{2,1,0:T(8,128)S(1)}, f32[10,8,128]{2,1,0:T(8,128)S(1)}) custom-call(f32[5,64,128]{2,1,0:T(8,128)S(1)} %collective-permute-done.3.refs_0_, f32[5,64,128]{2,1,0:T(8,128)S(1)} %collective-permute-done.4.refs_1_, f32[16,64,128]{2,1,0:T(8,128)S(1)} %get-tuple-element.17.w_ref.refs_2_, ...), custom_call_target="tpu_custom_call" | custom-call | tf_op jit(solution)/shard_map/pallas_call | solution.py:595
  24.1 1.3 %collective-permute-start.5 = (f32[12,8,128]{2,1,0:T(8,128)S(1)}, f32[12,8,128]{2,1,0:T(8,128)S(1)}, u32[]{:S(2)}, u32[]{:S(2)}) collective-permute-start(f32[12,8,128]{2,1,0:T(8,128)S(1)} %get-tuple-element.27), channel_id=1, source_target_pairs={{2,4},{3,5},{4,2},{5,3},{6,8},{7,9},{8,6},{9,7},{10,12},{11,13},{1... | collective-permute-start | bytes 147464 | tf_op jit(solution)/shard_map/ppermute | solution.py:627
  25.4 3.1 %collective-permute-done.5.refs_0_ = f32[12,8,128]{2,1,0:T(8,128)S(1)} collective-permute-done((f32[12,8,128]{2,1,0:T(8,128)S(1)}, f32[12,8,128]{2,1,0:T(8,128)S(1)}, u32[]{:S(2)}, u32[]{:S(2)}) %collective-permute-start.5) | collective-permute-done | bytes 49184 | tf_op jit(solution)/shard_map/ppermute | solution.py:627
  28.5 0.0 collective-permute-start.6
  28.5 1.2 %collective-permute-done.6.refs_1_ = f32[12,8,128]{2,1,0:T(8,128)S(1)} collective-permute-done((f32[12,8,128]{2,1,0:T(8,128)S(1)}, f32[12,8,128]{2,1,0:T(8,128)S(1)}, u32[]{:S(2)}, u32[]{:S(2)}) %collective-permute-start.6) | collective-permute-done | bytes 49184 | tf_op jit(solution)/shard_map/ppermute | solution.py:626
  29.8 0.0 copy-done.7
  29.8 0.0 copy-done.8
  29.8 0.0 copy-done.13
  29.8 0.0 copy-done.16
  29.8 1.4 %shard_map.179 = (f32[8,32,128]{2,1,0:T(8,128)}, f32[2,8,32]{2,1,0:T(8,128)}) custom-call(f32[12,8,128]{2,1,0:T(8,128)S(1)} %collective-permute-done.5.refs_0_, f32[12,8,128]{2,1,0:T(8,128)S(1)} %collective-permute-done.6.refs_1_, f32[8,32,128]{2,1,0:T(8,128)S(1)} %get-tuple-element.28.refs_2_, f32[10,8,128]{2,1,0:T(8,128)S(1)} %get-tuple-element.29.refs_3_, ...), custom_call_target="tpu_custom_call" | custom-call | tf_op jit(solution)/shard_map/pallas_call | solution.py:595
Async XLA Ops:
  0.6 11.1 %copy-start = (f32[8,32,128]{2,1,0:T(8,128)S(1)}, f32[8,32,128]{2,1,0:T(8,128)}, u32[]{:S(2)}) copy-start(f32[8,32,128]{2,1,0:T(8,128)} %refs_0_.1) | copy-start | bytes 393220
  0.6 11.1 %copy-start.1 = (f32[8,32,128]{2,1,0:T(8,128)S(1)}, f32[8,32,128]{2,1,0:T(8,128)}, u32[]{:S(2)}) copy-start(f32[8,32,128]{2,1,0:T(8,128)} %refs_1_.1) | copy-start | bytes 393220
  0.6 11.1 %copy-start.6 = (bf16[384,128]{1,0:T(8,128)(2,1)S(1)}, bf16[384,128]{1,0:T(8,128)(2,1)}, u32[]{:S(2)}) copy-start(bf16[384,128]{1,0:T(8,128)(2,1)} %constant.32.clone.refs_5_) | copy-start | bytes 294916
  0.7 11.1 %copy-start.11 = (f32[8,8,128]{2,1,0:T(8,128)S(1)}, f32[8,8,128]{2,1,0:T(8,128)}, u32[]{:S(2)}) copy-start(f32[8,8,128]{2,1,0:T(8,128)} %constant.44.clone.refs_7_) | copy-start | bytes 98308
  0.7 11.1 %copy-start.12 = (bf16[64,192]{1,0:T(8,128)(2,1)S(1)}, bf16[64,192]{1,0:T(8,128)(2,1)}, u32[]{:S(2)}) copy-start(bf16[64,192]{1,0:T(8,128)(2,1)} %constant.35.clone.refs_6_) | copy-start | bytes 73732
  1.8 12.8 %copy-start.2 = (f32[256,128]{1,0:T(8,128)S(1)}, f32[256,128]{1,0:T(8,128)}, u32[]{:S(2)}) copy-start(f32[256,128]{1,0:T(8,128)} %constant.37.clone.rz.refs_13_) | copy-start | bytes 393220
  1.8 12.8 %copy-start.3 = (f32[128,384]{1,0:T(8,128)S(1)}, f32[128,384]{1,0:T(8,128)}, u32[]{:S(2)}) copy-start(f32[128,384]{1,0:T(8,128)} %constant.39.clone.mz) | copy-start | bytes 589828
  1.8 7.2 %collective-permute-start.1 = (f32[2,8,32,128]{3,2,1,0:T(8,128)S(1)}, f32[2,8,32,128]{3,2,1,0:T(8,128)S(1)}, u32[]{:S(2)}, u32[]{:S(2)}) collective-permute-start(f32[2,8,32,128]{3,2,1,0:T(8,128)S(1)} %pad_maximum_fusion), channel_id=1, source_target_pairs={{0,1},{1,0},{2,3},{3,2},{4,5},{5,4},{6,7},{7,6},{8,9},{9,8},{10,11... | collective-permute-start | bytes 786440 | tf_op jit(solution)/shard_map/ppermute | solution.py:632
  2.1 8.5 %collective-permute-start = (f32[2,8,32,128]{3,2,1,0:T(8,128)S(1)}, f32[2,8,32,128]{3,2,1,0:T(8,128)S(1)}, u32[]{:S(2)}, u32[]{:S(2)}) collective-permute-start(f32[2,8,32,128]{3,2,1,0:T(8,128)S(1)} %pad_maximum_fusion), channel_id=1, source_target_pairs={{0,2},{2,0},{4,6},{6,4},{8,10},{10,8},{12,14},{14,12},{16,18},{18,... | collective-permute-start | bytes 786440 | tf_op jit(solution)/shard_map/ppermute | solution.py:626
  9.0 2.7 %collective-permute-start.2 = (f32[2,8,32,128]{3,2,1,0:T(8,128)S(1)}, f32[2,8,32,128]{3,2,1,0:T(8,128)S(1)}, u32[]{:S(2)}, u32[]{:S(2)}) collective-permute-start(f32[2,8,32,128]{3,2,1,0:T(8,128)S(1)} %collective-permute-done.1.refs_3_), channel_id=1, source_target_pairs={{0,2},{2,0},{4,6},{6,4},{8,10},{10,8},{12,14},{14,12},{16,18},{18,... | collective-permute-start | bytes 786440 | tf_op jit(solution)/shard_map/ppermute | solution.py:626
  11.8 2.8 %copy-start.15 = (f32[24,64]{1,0:T(8,128)S(1)}, f32[24,64]{1,0:T(8,128)}, u32[]{:S(2)}) copy-start(f32[24,64]{1,0:T(8,128)} %constant.38.clone.my) | copy-start | bytes 18436
  13.0 1.6 %copy-start.14 = (f32[8,128]{1,0:T(8,128)S(1)}, f32[8,128]{1,0:T(8,128)}, u32[]{:S(2)}) copy-start(f32[8,128]{1,0:T(8,128)} %constant.36.clone.ry.refs_12_) | copy-start | bytes 12292
  13.0 5.8 %collective-permute-start.3 = (f32[5,64,128]{2,1,0:T(8,128)S(1)}, f32[5,64,128]{2,1,0:T(8,128)S(1)}, u32[]{:S(2)}, u32[]{:S(2)}) collective-permute-start(f32[5,64,128]{2,1,0:T(8,128)S(1)} %get-tuple-element.16), channel_id=1, source_target_pairs={{2,4},{3,5},{4,2},{5,3},{6,8},{7,9},{8,6},{9,7},{10,12},{11,13},{1... | collective-permute-start | bytes 491528 | tf_op jit(solution)/shard_map/ppermute | solution.py:627
  14.6 6.4 %copy-start.4 = (bf16[384,128]{1,0:T(8,128)(2,1)S(1)}, bf16[384,128]{1,0:T(8,128)(2,1)}, u32[]{:S(2)}) copy-start(bf16[384,128]{1,0:T(8,128)(2,1)} %constant.31.clone.refs_9_) | copy-start | bytes 294916
  14.6 6.4 %copy-start.5 = (bf16[384,128]{1,0:T(8,128)(2,1)S(1)}, bf16[384,128]{1,0:T(8,128)(2,1)}, u32[]{:S(2)}) copy-start(bf16[384,128]{1,0:T(8,128)(2,1)} %constant.30.clone.refs_8_) | copy-start | bytes 294916
  14.6 6.3 %copy-start.9 = (bf16[64,192]{1,0:T(8,128)(2,1)S(1)}, bf16[64,192]{1,0:T(8,128)(2,1)}, u32[]{:S(2)}) copy-start(bf16[64,192]{1,0:T(8,128)(2,1)} %constant.34.clone.refs_11_) | copy-start | bytes 73732
  14.6 6.3 %copy-start.10 = (bf16[64,192]{1,0:T(8,128)(2,1)S(1)}, bf16[64,192]{1,0:T(8,128)(2,1)}, u32[]{:S(2)}) copy-start(bf16[64,192]{1,0:T(8,128)(2,1)} %constant.33.clone.refs_10_) | copy-start | bytes 73732
  18.8 2.2 %collective-permute-start.4 = (f32[5,64,128]{2,1,0:T(8,128)S(1)}, f32[5,64,128]{2,1,0:T(8,128)S(1)}, u32[]{:S(2)}, u32[]{:S(2)}) collective-permute-start(f32[5,64,128]{2,1,0:T(8,128)S(1)} %collective-permute-done.3.refs_0_), channel_id=1, source_target_pairs={{0,2},{2,0},{4,6},{6,4},{8,10},{10,8},{12,14},{14,12},{16,18},{18,... | collective-permute-start | bytes 491528 | tf_op jit(solution)/shard_map/ppermute | solution.py:626
  20.9 8.8 %copy-start.7 = (f32[128,32]{1,0:T(8,128)S(1)}, f32[128,32]{1,0:T(8,128)}, u32[]{:S(2)}) copy-start(f32[128,32]{1,0:T(8,128)} %constant.43.clone.refs_8_) | copy-start | bytes 49156
  21.0 8.8 %copy-start.8 = (f32[128,128]{1,0:T(8,128)S(1)}, f32[128,128]{1,0:T(8,128)}, u32[]{:S(2)}) copy-start(f32[128,128]{1,0:T(8,128)} %constant.41.clone.refs_6_) | copy-start | bytes 196612
  21.0 8.8 %copy-start.13 = (f32[64,8]{1,0:T(8,128)S(1)}, f32[64,8]{1,0:T(8,128)}, u32[]{:S(2)}) copy-start(f32[64,8]{1,0:T(8,128)} %constant.40.clone.refs_5_) | copy-start | bytes 6148
  21.0 8.8 %copy-start.16 = (f32[16,8]{1,0:T(8,128)S(1)}, f32[16,8]{1,0:T(8,128)}, u32[]{:S(2)}) copy-start(f32[16,8]{1,0:T(8,128)} %constant.42.clone.refs_7_) | copy-start | bytes 1540
  24.1 4.5 %collective-permute-start.5 = (f32[12,8,128]{2,1,0:T(8,128)S(1)}, f32[12,8,128]{2,1,0:T(8,128)S(1)}, u32[]{:S(2)}, u32[]{:S(2)}) collective-permute-start(f32[12,8,128]{2,1,0:T(8,128)S(1)} %get-tuple-element.27), channel_id=1, source_target_pairs={{2,4},{3,5},{4,2},{5,3},{6,8},{7,9},{8,6},{9,7},{10,12},{11,13},{1... | collective-permute-start | bytes 147464 | tf_op jit(solution)/shard_map/ppermute | solution.py:627
  28.5 1.2 %collective-permute-start.6 = (f32[12,8,128]{2,1,0:T(8,128)S(1)}, f32[12,8,128]{2,1,0:T(8,128)S(1)}, u32[]{:S(2)}, u32[]{:S(2)}) collective-permute-start(f32[12,8,128]{2,1,0:T(8,128)S(1)} %collective-permute-done.5.refs_0_), channel_id=1, source_target_pairs={{0,2},{2,0},{4,6},{6,4},{8,10},{10,8},{12,14},{14,12},{16,18},{18,... | collective-permute-start | bytes 147464 | tf_op jit(solution)/shard_map/ppermute | solution.py:626

commit v3 on v2

v3 whole, which is shorter than its diff:
```python
import functools

import jax
import jax.numpy as jnp
import numpy as np
from jax import lax
from jax.experimental import pallas as pl
from jax.experimental.pallas import tpu as pltpu
from jax.sharding import PartitionSpec as P

N = 8
SPARE = 3 * N
HALO = 3 * N
THETA = 1.1
DELTA = 0.9
SIGMA = THETA / DELTA
RHO0 = 1.0 / SIGMA
RHO1 = 1.0 / (2.0 * SIGMA - RHO0)
F32 = jnp.float32
BF16 = jnp.bfloat16
VMEM_LIMIT = 48 * 1024 * 1024


def legendre_value(points, degree):
    previous = np.ones(points.shape)
    current = points.copy()
    for level in range(1, degree):
        following = ((2 * level + 1) * points * current - level * previous) / (level + 1)
        previous = current
        current = following
    return current


def tables():
    degree = 7
    points = np.array(
        [
            -1.0,
            -0.8717401485096066,
            -0.5917001814331423,
            -0.2092992179024789,
            0.2092992179024789,
            0.5917001814331423,
            0.8717401485096066,
            1.0,
        ]
    )
    values = legendre_value(points, degree)
    weights = 2.0 / (degree * (degree + 1) * values**2)
    derivative = np.zeros((8, 8))
    for row_at in range(8):
        for col_at in range(8):
            if row_at != col_at:
                derivative[row_at, col_at] = values[row_at] / (
                    values[col_at] * (points[row_at] - points[col_at])
                )
    derivative[0, 0] = -degree * (degree + 1) / 4.0
    derivative[7, 7] = degree * (degree + 1) / 4.0
    interp = np.stack([(1.0 - points) / 2.0, (1.0 + points) / 2.0], axis=1)
    return derivative, weights, interp


DM, WEIGHTS, INTERP = tables()
MULT = np.array([2.0] + [1.0] * 6 + [2.0])
RHO = MULT[:, None] * INTERP
DRHO = DM @ RHO


def blockdiag(block, count):
    return np.kron(np.eye(count), block)


def hi_lo(matrix):
    hi = matrix.astype(jnp.bfloat16)
    lo = (matrix - hi.astype(np.float64)).astype(jnp.bfloat16)
    return hi, lo


def right_table(matrix):
    hi, lo = hi_lo(matrix)
    return np.concatenate([hi, hi, lo], axis=0).astype(np.float32)


def left_table(matrix):
    hi, lo = hi_lo(matrix)
    return np.concatenate([hi, hi, lo], axis=1).astype(np.float32)


def vertex_table(per_node, elements, columns, count=8):
    out = np.zeros((count * elements, columns))
    for e in range(elements):
        for i in range(2):
            out[count * e : count * (e + 1), e + i] += per_node[:, i]
    return out


def moment_table(per_node, elements, columns):
    out = np.zeros((8 * elements, columns))
    for e in range(elements):
        out[8 * e : 8 * e + 8, e] = per_node
    return out


PAIRS = [(0, 0), (0, 1), (1, 1)]
MASS = [INTERP[:, i] * INTERP[:, j] for i, j in PAIRS]


def round_up(value, to):
    return -(-value // to) * to


def make_tables(ny, nz, own_y):
    ey, ez = ny // N, nz // N
    cr = round_up(ey + 1, 8)
    t = {}
    t["z_d"] = right_table(blockdiag(DM, ez).T)
    t["z_dt"] = right_table(blockdiag(DM, ez))
    t["z_sq"] = right_table(blockdiag(DM * DM, ez))
    t["y_d"] = left_table(blockdiag(DM, ey))
    t["y_dt"] = left_table(blockdiag(DM, ey).T)
    t["y_sq"] = left_table(blockdiag(DM * DM, ey).T)
    t["y_sq_own"] = left_table(blockdiag(DM * DM, own_y // N).T)
    py = vertex_table(RHO, ey, cr)
    dpy = blockdiag(DM, ey) @ py
    pz = vertex_table(RHO, ez, nz)
    dpz = blockdiag(DM, ez) @ pz
    t["ry"] = left_table(np.concatenate([py, dpy], axis=0).T)
    t["ry_one"] = left_table(py.T)
    t["rz"] = right_table(np.concatenate([pz, dpz], axis=0))
    t["rz_one"] = right_table(pz)
    t["my"] = left_table(np.concatenate([moment_table(m, ey, cr) for m in MASS], axis=1).T)
    t["mz"] = right_table(np.concatenate([moment_table(m, ez, nz) for m in MASS], axis=1))
    own_ey = own_y // N
    py = vertex_table(INTERP, own_ey, cr)
    t["py"] = left_table(np.concatenate([py, vertex_table(np.eye(2), own_ey, cr, 2)], axis=0))
    pz = vertex_table(INTERP, ez, nz).T
    sz = vertex_table(np.eye(2), ez, nz, 2).T
    t["pz"] = right_table(np.concatenate([pz, sz], axis=1))
    cols = np.concatenate([DM.T, DM.T[[N - 1]], DM.T[[0]]], axis=0)
    t["line"] = np.broadcast_to(cols[:, :, None], (N + 2, N, nz)).astype(np.float32)
    w3 = WEIGHTS[:, None, None] * WEIGHTS[None, :, None] * np.ones((1, 1, nz))
    t["w3"] = (w3 * np.tile(WEIGHTS, ez)[None, None, :]).astype(np.float32)
    return t


def even_odd(matrix, values, sign):
    even = [values[b] + values[7 - b] for b in range(4)]
    odd = [values[b] - values[7 - b] for b in range(4)]
    out = [None] * 8
    for a in range(4):
        pe = po = None
        for b in range(4):
            ce = float((matrix[a, b] + matrix[a, 7 - b]) / 2.0)
            co = float((matrix[a, b] - matrix[a, 7 - b]) / 2.0)
            te = ce * even[b]
            to = co * odd[b]
            pe = te if pe is None else pe + te
            po = to if po is None else po + to
        out[a] = pe + po
        out[7 - a] = pe - po if sign > 0 else po - pe
    return out


def split(x):
    hi = x.astype(BF16)
    lo = (x - hi.astype(F32)).astype(BF16)
    return hi, lo


def dot(a, b):
    return jnp.dot(a, b, preferred_element_type=F32)


def z_apply(hi, lo, table):
    return dot(jnp.concatenate([hi, lo, hi], axis=1), table.astype(BF16))


def y_apply(hi, lo, table):
    return dot(table.astype(BF16), jnp.concatenate([hi, lo, hi], axis=0))


def assemble_yz(v):
    ny, nz = v.shape
    row = lax.broadcasted_iota(jnp.int32, (N, nz), 0)
    lane = lax.broadcasted_iota(jnp.int32, (1, nz), 1)
    top = (row == N - 1).astype(F32)
    bottom = (row == 0).astype(F32)
    blocks = [v[N * e : N * e + N] for e in range(ny // N)]
    ups = [pltpu.roll(b, N - 1, 0) for b in blocks]
    downs = [pltpu.roll(b, 1, 0) for b in blocks]
    out = []
    for e, b in enumerate(blocks):
        if e + 1 < len(blocks):
            b = b + top * ups[e + 1]
        if e > 0:
            b = b + bottom * downs[e - 1]
        out.append(b)
    v = jnp.concatenate(out, axis=0)
    last = ((lane % N == N - 1) & (lane < nz - 1)).astype(F32)
    first = ((lane % N == 0) & (lane > 0)).astype(F32)
    return v + last * pltpu.roll(v, nz - 1, 1) + first * pltpu.roll(v, 1, 1)


def yz_mask(ny, nz, start, total):
    row = lax.broadcasted_iota(jnp.int32, (ny, nz), 0) + start
    lane = lax.broadcasted_iota(jnp.int32, (ny, nz), 1)
    return (row > 0) & (row < total - 1) & (lane > 0) & (lane < nz - 1)


class Layout:
    def __init__(self, own_y, nz, dom, sub):
        self.own_y, self.nz, self.dom, self.sub = own_y, nz, dom, sub
        self.blocks = min(sub, 3)
        self.ny = own_y + HALO * (self.blocks - 1)
        self.total_y = own_y * sub
        self.ey, self.ez = self.ny // N, nz // N
        self.cr = round_up(self.ey + 1, 8)

    def where(self):
        d = lax.axis_index("dom")
        h = lax.axis_index("sub")
        parity = lax.rem(d, 2)
        pair = lax.div(d, 2)
        if self.sub == 1:
            start, offset = 0, 0
        elif self.sub == 2:
            start, offset = h * (self.own_y - HALO), h * HALO
        else:
            start, offset = h * self.own_y - HALO, HALO
        low = (pair > 0).astype(F32)
        high = (pair < self.dom // 2 - 1).astype(F32)
        return parity, h, start, offset, low, high

    def sent_rows(self, h):
        y = self.own_y
        down = (y - HALO, y - HALO)
        up = (0, HALO - 1)
        if self.sub == 1:
            return []
        if self.sub == 2:
            return [tuple(h * u + (1 - h) * v for u, v in zip(up, down))]
        return [down, up]

    def far_rows(self, h):
        if self.sub == 1:
            return []
        if self.sub == 2:
            return [(1 - h) * (self.ny - 1)]
        return [0, self.ny - 1]

    def used_rows(self, h):
        if self.sub == 1:
            return []
        if self.sub == 2:
            return [h * (self.own_y - HALO)]
        return [self.own_y - HALO, 0]

    def interfaces(self, h):
        if self.sub == 1:
            return []
        if self.sub == 2:
            return [self.own_y - h * (self.own_y - HALO)]
        return [HALO, HALO + self.own_y]


def aligned(start, size):
    return pl.ds(start if isinstance(start, int) else pl.multiple_of(start, N), size)


def gather_window(lay, own, others, h, store):
    y = lay.own_y
    if lay.sub == 1:
        store(pl.ds(0, y), own)
    elif lay.sub == 2:
        store(aligned(h * HALO, y), own)
        store(aligned((1 - h) * y, HALO), others[0])
    else:
        store(pl.ds(0, HALO), others[0])
        store(pl.ds(HALO, y), own)
        store(pl.ds(HALO + y, HALO), others[1])


def line_rows(lay, h):
    if lay.sub == 1:
        return []
    if lay.sub == 2:
        return [(lay.own_y - 1) * (1 - h)]
    return [0, lay.own_y - 1]


def line_count(lay):
    return 0 if lay.sub == 1 else 1 if lay.sub == 2 else 2


def own_kernel(lay, raw, z_sq, y_sq, w3, face, w_out, d_out, r_out, sx_out, *packs):
    rhs, coef = raw.at[0], raw.at[1]
    y, nz = lay.own_y, lay.nz
    parity, h = lay.where()[:2]
    table3 = w3[...]
    for e in range(y // N):
        rows = pl.ds(N * e, N)
        w = [coef[a, rows, :] * table3[a] for a in range(N)]
        dx = even_odd((DM * DM).T, w, 1)
        for a in range(N):
            w_out[a, rows, :] = w[a]
            d_out[a, rows, :] = dx[a]
    hi, lo = split(w_out[...].reshape(N * y, nz))
    dz = z_apply(hi, lo, z_sq[...])
    sx_out[...] = assemble_yz(d_out[(N - 1) * parity])
    for a in range(N):
        cut = slice(a * y, (a + 1) * y)
        dy = y_apply(hi[cut], lo[cut], y_sq[...])
        d_out[a] = assemble_yz(d_out[a] + dz[cut] + dy)
        r_out[a] = assemble_yz(rhs[a])
    inner = (N - 1) * (1 - parity)
    face[0] = r_out[inner]
    face[1] = d_out[inner]
    for pack, (first, far) in zip(packs, lay.sent_rows(h)):
        for side, field in ((0, r_out), (1, d_out)):
            for a in range(N):
                pack[side, pl.ds(a * HALO, HALO), :] = raw[side, a, aligned(first, HALO), :]
                pack[side, pl.ds(N * HALO + a, 1), :] = field[a, pl.ds(far, 1), :]


def message_kernel(lay, w, d, r, sx, face, msg, u_s, d_s, r_s):
    y, nz = lay.own_y, lay.nz
    parity, h, start, offset, low, high = lay.where()
    mask = yz_mask(y, nz, h * y, lay.total_y)
    scale = mask.astype(F32) * (1.0 / THETA)
    odd = parity.astype(F32)
    for a in range(N):
        dd, rr = d[a], r[a]
        keep = scale
        if a in (0, N - 1):
            inner = odd if a == 0 else 1.0 - odd
            dd = dd + inner * face[1]
            rr = rr + inner * face[0]
            keep = scale * inner
        d_s[a] = dd
        r_s[a] = rr
        u_s[a] = keep * rr / jnp.where(mask, dd, 1.0)
    col = [jnp.where(parity == 0, float(DM[a, 0]), float(DM[a, N - 1])) for a in range(N)]
    acc = []
    for e in range(y // N):
        rows = pl.ds(N * e, N)
        g = even_odd(DM, [u_s[a, rows, :] for a in range(N)], -1)
        total = None
        for a in range(N):
            term = (w[a, rows, :] * g[a]) * col[a]
            total = term if total is None else total + term
        acc.append(total)
    outer = (N - 1) * parity
    msg[pl.ds(0, y), :] = r[outer]
    msg[pl.ds(y, y), :] = d[outer]
    msg[pl.ds(2 * y, y), :] = sx[...]
    msg[pl.ds(3 * y, y), :] = w[outer]
    msg[pl.ds(4 * y, y), :] = assemble_yz(jnp.concatenate(acc, axis=0))
    base = 5 * y
    for row in line_rows(lay, h):
        for field in (r_s, d_s, w):
            for a in range(N):
                msg[pl.ds(base + a, 1), :] = field[a, pl.ds(row, 1), :]
            base += N
    msg[pl.ds(base, SPARE), :] = jnp.zeros((SPARE, nz), F32)


def gradient_flux(lay, u_ref, w_ref, planes, z_d, y_d, fx, fy, fz):
    ny, nz = lay.ny, lay.nz
    for el in range(2):
        for e in range(lay.ey):
            rows = pl.ds(N * e, N)
            u = [u_ref[N * el + a, rows, :] for a in range(N)]
            g = even_odd(DM, u, -1)
            for a in range(N):
                fx[N * el + a, rows, :] = w_ref[N * el + a, rows, :] * g[a]
    first, count = planes[0], len(planes)
    hi, lo = split(u_ref[pl.ds(first, count)].reshape(count * ny, nz))
    gz = z_apply(hi, lo, z_d[...])
    for p in planes:
        cut = slice((p - first) * ny, (p - first + 1) * ny)
        gy = y_apply(hi[cut], lo[cut], y_d[...])
        w = w_ref[p]
        fy[p] = w * gy
        fz[p] = w * gz[cut]


def deep_kernel(lay, n_other, *refs):
    own, mate = refs[:2]
    other = refs[2 : 2 + n_other]
    mate_other = [refs[2 + n_other + 2 * k :][:2] for k in range(n_other)]
    refs = refs[2 + 3 * n_other :]
    z_sq, y_sq, z_d, z_dt, y_d, y_dt, w3 = refs[:7]
    w_out, rhs_out, sec_out, lin_out, ends = refs[7:12]
    d_s, r_s, u_s, inv_s, fx, fy, fz, back = refs[12:]
    ny, nz = lay.ny, lay.nz
    last = 2 * N - 1
    parity, h, start, offset, low, high = lay.where()
    for side, target in ((0, rhs_out), (1, w_out)):
        for base, block, pieces in (
            (parity * N, own, [o.at[side] for o in other]),
            ((1 - parity) * N, mate, [o[side] for o in mate_other]),
        ):
            for a in range(N):

                def put(rows, value):
                    target[base + a, rows, :] = value

                cut = pl.ds(a * HALO, HALO)
                gather_window(lay, block[side, a], [o[cut, :] for o in pieces], h, put)
    table3 = w3[...]
    for el in range(2):
        outer = DM[:, 0] if el == 0 else DM[:, N - 1]
        for e in range(lay.ey):
            rows = pl.ds(N * e, N)
            w = [w_out[N * el + a, rows, :] * table3[a] for a in range(N)]
            dx = even_odd((DM * DM).T, w, 1)
            cx = even_odd(DM.T, [float(outer[a]) * w[a] for a in range(N)], -1)
            for a in range(N):
                w_out[N * el + a, rows, :] = w[a]
                d_s[N * el + a, rows, :] = dx[a]
                lin_out[N * el + a, rows, :] = cx[a]
    hi, lo = split(w_out[...].reshape(2 * N * ny, nz))
    dz = z_apply(hi, lo, z_sq[...])
    mask = yz_mask(ny, nz, start, lay.total_y)
    inside = mask.astype(F32)
    for p in range(2 * N):
        cut = slice(p * ny, (p + 1) * ny)
        dy = y_apply(hi[cut], lo[cut], y_sq[...])
        d_s[p] = assemble_yz(d_s[p] + dz[cut] + dy)
        r_s[p] = assemble_yz(rhs_out[p])
    for k, row in enumerate(lay.far_rows(h)):
        for side, target in ((0, r_s), (1, d_s)):
            for base, piece in (
                (parity * N, other[k].at[side]),
                ((1 - parity) * N, mate_other[k][side]),
            ):
                for a in range(N):
                    target[base + a, pl.ds(row, 1), :] = piece[pl.ds(N * HALO + a, 1), :]
    for s in (d_s, r_s):
        both = s[N - 1] + s[N]
        s[N - 1] = both
        s[N] = both
    ends[0, 0] = r_s[0]
    ends[0, 1] = d_s[0]
    ends[1, 0] = r_s[last]
    ends[1, 1] = d_s[last]
    zero = jnp.zeros((ny, nz), F32)
    u_s[0] = zero
    u_s[last] = zero
    for p in range(1, last):
        inv = inside / jnp.where(mask, d_s[p], 1.0)
        inv_s[p] = inv
        u_s[p] = inv * r_s[p] * (1.0 / THETA)
    middle = list(range(1, last))
    gradient_flux(lay, u_s, w_out, middle, z_d, y_d, fx, fy, fz)
    for el in range(2):
        for e in range(lay.ey):
            rows = pl.ds(N * e, N)
            b = even_odd(DM.T, [fx[N * el + a, rows, :] for a in range(N)], -1)
            for a in range(N):
                back[N * el + a, rows, :] = b[a]
    hi, lo = split(fz[pl.ds(1, last - 1)].reshape((last - 1) * ny, nz))
    bz = z_apply(hi, lo, z_dt[...])
    for p in middle:
        hi, lo = split(fy[p])
        by = y_apply(hi, lo, y_dt[...])
        back[p] = assemble_yz(back[p] + by + bz[(p - 1) * ny : p * ny])
    both = back[N - 1] + back[N]
    back[N - 1] = both
    back[N] = both
    for p in range(2 * N):
        linear = assemble_yz(lin_out[p])
        if p in (0, last):
            lin_out[p] = linear
            sec_out[p] = assemble_yz(back[p])
        else:
            inv = (2.0 * RHO1 / DELTA) * inv_s[p]
            lin_out[p] = -inv * linear
            sec_out[p] = (1.0 + RHO1 * RHO0) * u_s[p] + inv * (r_s[p] - back[p])


def coarse_tables_kernel(lay, w_ref, rhs_ref, my, mz, ry, rz, g_out, r_out):
    ny, nz, cr = lay.ny, lay.nz, lay.cr
    lhs = []
    for el in range(2):
        for m in MASS:
            total = None
            for a in range(N):
                term = float(m[a]) * w_ref[N * el + a]
                total = term if total is None else total + term
            lhs.append(total)
    along_z = z_apply(*split(jnp.concatenate(lhs, axis=0)), mz[...])
    for el in range(2):
        mom = {}
        for alpha in range(3):
            at = (3 * el + alpha) * ny
            block = y_apply(*split(along_z[at : at + ny]), my[...])
            for beta in range(3):
                for gamma in range(3):
                    mom[alpha, beta, gamma] = block[
                        beta * cr : (beta + 1) * cr, gamma * nz : (gamma + 1) * nz
                    ]
        x_sum, y_sum, z_sum = {}, {}, {}
        for i in range(3):
            for j in range(3):
                x_sum[i, j] = mom[0, i, j] + 2.0 * mom[1, i, j] + mom[2, i, j]
                y_sum[i, j] = mom[i, 0, j] + 2.0 * mom[i, 1, j] + mom[i, 2, j]
                z_sum[i, j] = mom[i, j, 0] + 2.0 * mom[i, j, 1] + mom[i, j, 2]
        sign = (1.0, -1.0, 1.0)
        for alpha in range(3):
            for beta in range(3):
                for gamma in range(3):
                    g_out[el, 9 * alpha + 3 * beta + gamma] = 0.25 * (
                        sign[alpha] * x_sum[beta, gamma]
                        + sign[beta] * y_sum[alpha, gamma]
                        + sign[gamma] * z_sum[alpha, beta]
                    )
    sums = []
    for el in range(2):
        for i in range(2):
            total = None
            for a in range(N):
                term = float(RHO[a, i]) * rhs_ref[N * el + a]
                total = term if total is None else total + term
            sums.append(total)
    part = y_apply(*split(jnp.concatenate(sums, axis=1)), ry[...])
    rows = jnp.concatenate([part[:, k * nz : (k + 1) * nz] for k in range(4)], axis=0)
    full = z_apply(*split(rows), rz[...])
    for k in range(4):
        r_out[k] = full[k * cr : (k + 1) * cr]


def pair_index(i, j):
    return i + j


def shifted(c, q, r):
    if q:
        c = pltpu.roll(c, c.shape[0] - 1, 0)
    if r:
        c = pltpu.roll(c, c.shape[1] - 1, 1)
    return c


def scatter(parts):
    cr, nz = parts[0, 0].shape
    first = parts[0, 0] + pltpu.roll(parts[0, 1], 1, 1)
    second = parts[1, 0] + pltpu.roll(parts[1, 1], 1, 1)
    return first + pltpu.roll(second, 1, 0)


def gathered(c):
    return {(q, r): shifted(c, q, r) for q in range(2) for r in range(2)}


def face_apply(entry, c, out=None):
    out = {} if out is None else out
    for j in range(2):
        for k in range(2):
            for q in range(2):
                for r in range(2):
                    term = entry(pair_index(j, q), pair_index(k, r)) * c[q, r]
                    out[j, k] = term if (j, k) not in out else out[j, k] + term
    return out


def coarse_diag(entry):
    return scatter({(j, k): entry(2 * j, 2 * k) for j in range(2) for k in range(2)})


def coarse_mask(lay, start):
    row = lax.broadcasted_iota(jnp.int32, (lay.cr, lay.nz), 0) + lax.div(start, N)
    lane = lax.broadcasted_iota(jnp.int32, (lay.cr, lay.nz), 1)
    return (row > 0) & (row < lay.total_y // N) & (lane > 0) & (lane < lay.ez)


def unpack_sides(lay, pieces, mate_pieces, line, parity, h, start, win):
    y, nz = lay.own_y, lay.nz
    for side, group in ((parity, pieces), (1 - parity, mate_pieces)):
        for k in range(5):

            def put(rows, value):
                win[side, k, rows, :] = value

            others = [
                g[aligned(k * y + first, HALO), :] for g, first in zip(group[1:], lay.used_rows(h))
            ]
            gather_window(lay, group[0][pl.ds(k * y, y), :], others, h, put)
    is_even = parity == 0
    lane = lax.broadcasted_iota(jnp.int32, (N, nz), 1)
    node = lax.broadcasted_iota(jnp.int32, (N, nz), 0)
    lane_in = (lane > 0) & (lane < nz - 1)
    flank = lax.broadcasted_iota(jnp.int32, (1, nz), 1)
    last = ((flank % N == N - 1) & (flank < nz - 1)).astype(F32)
    first = ((flank % N == 0) & (flank > 0)).astype(F32)
    for b, begin in enumerate(lay.interfaces(h), 1):
        above, below = pl.ds(begin - 1, 1), pl.ds(begin, 1)
        for side in range(2):
            for k in range(3):
                both = win[side, k, above, :] + win[side, k, below, :]
                win[side, k, above, :] = both
                win[side, k, below, :] = both
        for side in range(2):
            outer = N - 1 if side == 0 else 0

            def field(k):
                def of(group):
                    if lay.sub == 2:
                        one, two, at_one, at_two = group[0], group[1], 0, 0
                    else:
                        order = [group[1], group[0], group[2]]
                        one, two, at_one, at_two = order[b - 1], order[b], 1, 0
                    base = 5 * y + k * N
                    return (
                        one[pl.ds(base + 3 * N * at_one, N), :]
                        + two[pl.ds(base + 3 * N * at_two, N), :]
                    )
                mine, theirs = of(pieces), of(mate_pieces)
                if side == 0:
                    return jnp.where(is_even, mine, theirs)
                return jnp.where(is_even, theirs, mine)

            r, d, w = field(0), field(1), field(2)
            row = start + begin
            ok = lane_in & (node != outer) & (row > 0) & (row < lay.total_y)
            u = jnp.where(ok, r / jnp.where(ok, d, 1.0) * (1.0 / THETA), 0.0)
            g = None
            for a in range(N):
                term = line[a] * u[a : a + 1]
                g = term if g is None else g + term
            total = jnp.sum(line[N + side] * (w * g), axis=0, keepdims=True)
            total = total + last * pltpu.roll(total, nz - 1, 1) + first * pltpu.roll(total, 1, 1)
            win[side, 4, above, :] = total
            win[side, 4, below, :] = total


def second_kernel(lay, n_pieces, *refs):
    pieces, mate_pieces = refs[:n_pieces], refs[n_pieces : 2 * n_pieces]
    w_ref, sec_in, lin_in, ends, g_ref, r_ref = refs[2 * n_pieces : 2 * n_pieces + 6]
    refs = refs[2 * n_pieces + 6 :]
    z_d, z_dt, y_d, y_dt, ry, ry_one, rz, line = refs[:8]
    out, msg, state = refs[8:11]
    win, sec, fx, fy, fz = refs[11:]
    ny, nz, cr = lay.ny, lay.nz, lay.cr
    last = 2 * N - 1
    parity, h, start, offset, low, high = lay.where()
    mask = yz_mask(ny, nz, start, lay.total_y)
    inside = mask.astype(F32)
    is_even = parity == 0
    unpack_sides(lay, pieces, mate_pieces, line, parity, h, start, win)
    flags = (low, high)
    inv, res, u = [], [], []
    for side in range(2):
        valid = inside * flags[side]
        inv.append(valid / jnp.where(mask, ends[side, 1] + win[side, 1], 1.0))
        res.append(valid * (ends[side, 0] + win[side, 0]))
        u.append(inv[side] * res[side] * (1.0 / THETA))
    for p in range(1, last):
        value = sec_in[p]
        if p <= N:
            value = value + lin_in[min(p, N - 1)] * u[0]
        if p >= N - 1:
            value = value + lin_in[max(p, N)] * u[1]
        sec[p] = value
    weights = [w_ref[0] + win[0, 3], w_ref[last] + win[1, 3]]
    hi, lo = split(jnp.concatenate(u, axis=0))
    gz = z_apply(hi, lo, z_d[...])
    gy = y_apply(
        jnp.concatenate([hi[:ny], hi[ny:]], axis=1),
        jnp.concatenate([lo[:ny], lo[ny:]], axis=1),
        y_d[...],
    )
    weight_z = jnp.concatenate(weights, axis=0)
    weight_y = jnp.concatenate(weights, axis=1)
    bz = z_apply(*split(weight_z * gz), z_dt[...])
    by = y_apply(*split(weight_y * gy), y_dt[...])
    for side, p in ((0, 0), (1, last)):
        plane = assemble_yz(bz[side * ny : (side + 1) * ny] + by[:, side * nz : (side + 1) * nz])
        plane = plane + sec_in[p] + win[side, 4] + (lin_in[p] + win[side, 2]) * u[side]
        res_one = res[side] - inside * plane
        sec[p] = (1.0 + RHO1 * RHO0) * u[side] + (2.0 * RHO1 / DELTA) * inv[side] * res_one
    out[...] = sec[pl.ds(parity * N, N), pl.ds(pl.multiple_of(offset, N), lay.own_y), :]
    gradient_flux(lay, sec, w_ref, list(range(2 * N)), z_d, y_d, fx, fy, fz)
    sums = []
    for f, weight in ((fx, DRHO), (fy, RHO), (fz, RHO)):
        lanes = []
        for el in range(2):
            for i in range(2):
                total = None
                for a in range(N):
                    term = float(weight[a, i]) * f[N * el + a]
                    total = term if total is None else total + term
                lanes.append(total)
        sums.append(jnp.concatenate(lanes, axis=1))
    one = y_apply(*split(jnp.concatenate(sums[:2], axis=0)), ry[...])
    two = y_apply(*split(sums[2]), ry_one[...])
    rows = [
        jnp.concatenate([v[:, k * nz : (k + 1) * nz] for v in (one, two)], axis=1) for k in range(4)
    ]
    full = z_apply(*split(jnp.concatenate(rows, axis=0)), rz[...])
    r = {}
    for el in range(2):
        for i in range(2):
            k = 2 * el + i
            r[el, i] = r_ref[k] - full[k * cr : (k + 1) * cr]
    planes = [r[0, 0], r[0, 1] + r[1, 0], r[1, 1]]
    cmask = coarse_mask(lay, start)

    def entry(el, alpha):
        return lambda beta, gamma: g_ref[el, 9 * alpha + 3 * beta + gamma]

    d = [
        coarse_diag(entry(0, 0)),
        coarse_diag(entry(0, 2)) + coarse_diag(entry(1, 0)),
        coarse_diag(entry(1, 2)),
    ]
    cin = cmask.astype(F32)
    mid = (2.0 / 3.0) * cin * planes[1] / jnp.where(cmask, d[1], 1.0)
    c = gathered(mid)
    g_low = scatter(face_apply(entry(0, 1), c))
    g_high = scatter(face_apply(entry(1, 1), c))
    g_mid = scatter(face_apply(entry(1, 0), c, face_apply(entry(0, 2), c)))
    state[0] = planes[0]
    state[1] = planes[1]
    state[2] = planes[2]
    state[3] = d[0]
    state[4] = d[1]
    state[5] = d[2]
    state[6] = g_low
    state[7] = g_mid
    state[8] = g_high
    state[9] = mid
    send = [
        jnp.where(is_even, planes[0], planes[2]),
        jnp.where(is_even, d[0], d[2]),
        jnp.where(is_even, g_low, g_high),
    ]
    send += [jnp.where(is_even, g_ref[0, k], g_ref[1, 18 + k]) for k in range(9)]
    for k in range(3):
        packed = send[4 * k]
        for q in range(1, 4):
            packed = packed + pltpu.roll(send[4 * k + q], q * (nz // 4), 1)
        msg[k] = packed


def third_kernel(lay, *refs):
    own_msg, mate_msg, sec, state, g_ref, py, pz, out, coarse = refs
    ny, nz, cr = lay.ny, lay.nz, lay.cr
    parity, h, start, offset, low, high = lay.where()
    is_even = parity == 0
    cmask = coarse_mask(lay, start)
    cin = cmask.astype(F32)
    lo_msg, hi_msg = [], []
    for k in range(3):
        mine, theirs = own_msg[k], mate_msg[k]
        for target, packed in (
            (lo_msg, jnp.where(is_even, mine, theirs)),
            (hi_msg, jnp.where(is_even, theirs, mine)),
        ):
            target.append(packed)
            for q in range(1, 4):
                target.append(pltpu.roll(packed, nz - q * (nz // 4), 1))

    def entry(el, alpha):
        return lambda beta, gamma: g_ref[el, 9 * alpha + 3 * beta + gamma]

    def outer(at, m, flag, el, alpha):
        rhs = cin * flag * (state[at] + m[0])
        d = jnp.where(cmask, state[3 + at] + m[1], 1.0)
        one = (2.0 / 3.0) * rhs / d
        c = gathered(one)
        here = lambda beta, gamma: g_ref[el, 9 * alpha + 3 * beta + gamma] + m[3 + 3 * beta + gamma]
        image = scatter(face_apply(here, c)) + state[6 + at] + m[2]
        cross = face_apply(entry(el, 1), c)
        solution = one + (2.0 / 3.0) * (rhs - cin * flag * image) / d
        return solution, cross

    c_low, cross_low = outer(0, lo_msg, low, 0, 0)
    c_high, cross_high = outer(2, hi_msg, high, 1, 2)
    cross = scatter({k: cross_low[k] + cross_high[k] for k in cross_low})
    rhs = cin * state[1]
    d = jnp.where(cmask, state[4], 1.0)
    c_mid = state[9] + (2.0 / 3.0) * (rhs - cin * (state[7] + cross)) / d
    left = jnp.where(is_even, c_low, c_mid)
    right = jnp.where(is_even, c_mid, c_high)
    both = jnp.concatenate([left, right], axis=1)
    if lay.sub > 1:
        both = pltpu.roll(both, cr - lax.div(offset, N), 0)
    y, cy = lay.own_y, lay.own_y // 4
    along_y = y_apply(*split(both), py[...])
    along_y = jnp.concatenate([along_y[:, :nz], along_y[:, nz:]], axis=0)
    full = z_apply(*split(along_y), pz[...])
    inside = yz_mask(y, nz, start + offset, lay.total_y).astype(F32)
    q_left = inside * full[:y, :nz]
    q_right = inside * full[y + cy : 2 * y + cy, :nz]
    coarse[0] = full[y : y + cy, nz : nz + nz // 4]
    coarse[1] = full[2 * y + cy :, nz : nz + nz // 4]
    first_flag = jnp.where(is_even, low, 1.0)
    last_flag = jnp.where(is_even, 1.0, high)
    for a in range(N):
        add = float(INTERP[a, 0]) * q_left + float(INTERP[a, 1]) * q_right
        if a == 0:
            add = first_flag * add
        if a == N - 1:
            add = last_flag * add
        out[a] = sec[a] + add


def run(kernel, args, outs, scratch=()):
    return pl.pallas_call(
        kernel,
        out_shape=[jax.ShapeDtypeStruct(o, F32) for o in outs],
        in_specs=[pl.BlockSpec(memory_space=pltpu.VMEM)] * len(args),
        out_specs=[pl.BlockSpec(memory_space=pltpu.VMEM)] * len(outs),
        scratch_shapes=[pltpu.VMEM(s, F32) for s in scratch],
        compiler_params=pltpu.CompilerParams(vmem_limit_bytes=VMEM_LIMIT),
        cost_estimate=pl.CostEstimate(flops=1, bytes_accessed=1, transcendentals=0),
    )(*args)


def swap_pairs(count, first):
    pairs = []
    for i in range(first, count - 1, 2):
        pairs += [(i, i + 1), (i + 1, i)]
    return pairs


def chip_pairs(dom, sub, shift):
    pairs = []
    for a, b in swap_pairs(dom, 1):
        for q in range(sub):
            to = (q + shift) % sub if sub == 2 else q + shift
            if 0 <= to < sub:
                pairs.append((a * sub + q, b * sub + to))
    for end in (0, dom - 1):
        pairs += [(end * sub + a, end * sub + b) for a, b in swap_pairs(sub, 0)]
    return pairs


def shards(dom, sub, rhs_local, coefficient):
    size_x, own_y, nz = rhs_local.shape
    assert size_x == N and dom % 2 == 0 and (sub == 1 or own_y > HALO)
    lay = Layout(own_y, nz, dom, sub)
    ny, cr = lay.ny, lay.cr
    t = {k: jnp.asarray(v) for k, v in make_tables(ny, nz, own_y).items()}
    pick = lambda *names: [t[k] for k in names]
    even = lambda v: lax.ppermute(v, "dom", swap_pairs(dom, 0))
    odd = lambda v, k=0: lax.ppermute(v, ("dom", "sub"), chip_pairs(dom, sub, k))
    block = (N, own_y, nz)
    raw = jnp.stack([rhs_local, coefficient])
    n_other = 0 if sub == 1 else 1 if sub == 2 else 2
    face, w, d, r, sx, *packs = run(
        functools.partial(own_kernel, lay),
        [raw] + pick("z_sq", "y_sq_own", "w3"),
        [(2, own_y, nz), block, block, block, (own_y, nz)]
        + [(2, N * (HALO + 1), nz)] * n_other,
    )
    mate_face = even(face)
    if sub == 1:
        steps = []
    elif sub == 2:
        steps = [[(0, 1), (1, 0)]]
    else:
        up = [(i, i + 1) for i in range(sub - 1)]
        steps = [up, [(b, a) for a, b in up]]
    others = [lax.ppermute(pack, "sub", step) for pack, step in zip(packs, steps)]
    mate = even(raw)
    (msg,) = run(
        functools.partial(message_kernel, lay),
        [w, d, r, sx, mate_face],
        [(5 * own_y + 3 * N * line_count(lay) + SPARE, nz)],
        [block] * 3,
    )
    shifts = [0] if sub == 1 else [0, 1] if sub == 2 else [0, 1, -1]
    pieces = [odd(msg, k) for k in shifts]
    mate_others = [even(o[side]) for o in others for side in range(2)]
    pair = (2 * N, ny, nz)
    w, rhs, sec, lin, ends = run(
        functools.partial(deep_kernel, lay, n_other),
        [raw, mate, *others, *mate_others]
        + pick("z_sq", "y_sq", "z_d", "z_dt", "y_d", "y_dt", "w3"),
        [pair] * 4 + [(2, 2, ny, nz)],
        [pair] * 8,
    )
    pieces, sec = lax.optimization_barrier((pieces, sec))
    mate_pieces = [even(p) for p in pieces]
    g, r = run(
        functools.partial(coarse_tables_kernel, lay),
        [w, rhs] + pick("my", "mz", "ry_one", "rz_one"),
        [(2, 27, cr, nz), (4, cr, nz)],
    )
    sec, msg, state = run(
        functools.partial(second_kernel, lay, len(pieces)),
        [*pieces, *mate_pieces, w, sec, lin, ends, g, r]
        + pick("z_d", "z_dt", "y_d", "y_dt", "ry", "ry_one", "rz", "line"),
        [block, (3, cr, nz), (10, cr, nz)],
        [(2, 5, ny, nz)] + [pair] * 4,
    )
    from_odd = odd(msg)
    from_mate = even(from_odd)
    return tuple(
        run(
            functools.partial(third_kernel, lay),
            [from_odd, from_mate, sec, state, g] + pick("py", "pz"),
            [block, (size_x // 4, own_y // 4, nz // 4)],
        )
    )


def solution(mesh):
    dom, sub = mesh.shape["dom"], mesh.shape["sub"]
    return jax.shard_map(
        functools.partial(shards, dom, sub),
        mesh=mesh,
        in_specs=(P("dom", "sub", None), P("dom", "sub", None)),
        out_specs=(P("dom", "sub", None), P("dom", "sub", None)),
        check_vma=False,
    )
```

time: 31.3 us -> 25.6 us (0.82)
  the two profiles are of different devices: /device:TPU:7 before, /device:TPU:15 now
where the time goes in v3:
time: 25.6 us; the launch traced here: 25.5 us
  starting transfers between devices  10.5 us (41%)
  Pallas kernels  6.56 us (26%)
  waiting for transfers between devices  6.43 us (25%)
  other arithmetic  1.04 us (4%)
  between operations  0.81 us (3%)
    pallas_call x6, Pallas kernels, run(): pl.pallas_call(kernel, out_shape=[jax.ShapeDtypeStruct(o, F32) for o in o...  6.56 us
    ppermute x7, starting transfers between devices, shards(): even = lambda v: lax.ppermute(v, 'dom', swap_pairs(dom, 0))  5.55 us
    ppermute x3, starting transfers between devices, shards(): lax.ppermute(v, ('dom', 'sub'), chip_pairs(dom, sub, k))  4.66 us
    ppermute x7, waiting for transfers between devices, shards(): even = lambda v: lax.ppermute(v, 'dom', swap_pairs(dom, 0))  3.37 us
    ppermute x3, waiting for transfers between devices, shards(): lax.ppermute(v, ('dom', 'sub'), chip_pairs(dom, sub, k))  3.04 us
    another operation x1, other arithmetic, shards(): raw = jnp.stack([rhs_local, coefficient])  1.04 us
  transfers between devices with their start and end apart: 11, of which 6 were waited for; matrix products, arithmetic and copies ran while one was open for 0% of the time, Pallas kernels for 13%

profile of v3, /device:TPU:15, one launch (start us, length us, event | category | flops | bytes accessed | tf_op | source)
XLA Modules:
  0.0 25.5 jit_solution(2847274957106787065)
XLA Ops:
  0.6 0.0 copy-start.2
  0.6 0.0 copy-start.9
  0.7 0.0 copy-start.15
  0.7 1.0 %pad_maximum_fusion.raw.refs_0_ = f32[2,8,32,128]{3,2,1,0:T(8,128)S(1)} fusion(f32[1,8,32,128]{3,2,1,0:T(8,128)} %bitcast.6, f32[1,8,32,128]{3,2,1,0:T(8,128)} %bitcast.7), kind=kLoop, calls=%fused_computation | loop fusion | flops 65536 | bytes 524288 | tf_op jit(solution)/shard_map/stack | solution.py:850
  1.7 0.0 copy-done.2
  1.7 0.0 copy-done.9
  1.7 0.0 copy-done.15
  1.7 0.4 %shard_map.194 = (f32[2,32,128]{2,1,0:T(8,128)S(1)}, f32[8,32,128]{2,1,0:T(8,128)S(1)}, f32[8,32,128]{2,1,0:T(8,128)S(1)}, f32[8,32,128]{2,1,0:T(8,128)S(1)}, f3...) custom-call(f32[2,8,32,128]{3,2,1,0:T(8,128)S(1)} %pad_maximum_fusion.raw.refs_0_, f32[384,128]{1,0:T(8,128)S(1)} %copy-done.2, ...), custom_call_target="tpu_custom_call" | custom-call | flops 1 | bytes 1 | tf_op jit(solution)/shard_map/pallas_call | solution.py:810
  2.1 0.3 %collective-permute-start.4 = (f32[2,200,128]{2,1,0:T(8,128)S(1)}, f32[2,200,128]{2,1,0:T(8,128)S(1)}, u32[]{:S(2)}, u32[]{:S(2)}) collective-permute-start(f32[2,200,128]{2,1,0:T(8,128)S(1)} %get-tuple-element.26), channel_id=1, source_target_pairs={{0,1},{1,0},{2,3},{3,2},{4,5},{5,4},{6,7},{7,6},{8,9},{9,8},{10,11... | collective-permute-start | bytes 614408 | tf_op jit(solution)/shard_map/ppermute | solution.py:866
  2.4 1.0 %collective-permute-start = (f32[2,32,128]{2,1,0:T(8,128)S(1)}, f32[2,32,128]{2,1,0:T(8,128)S(1)}, u32[]{:S(2)}, u32[]{:S(2)}) collective-permute-start(f32[2,32,128]{2,1,0:T(8,128)S(1)} %get-tuple-element.25), channel_id=1, source_target_pairs={{0,2},{2,0},{4,6},{6,4},{8,10},{10,8},{12,14},{14,12},{16,18},{18,... | collective-permute-start | bytes 98312 | tf_op jit(solution)/shard_map/ppermute | solution.py:847
  3.4 0.0 collective-permute-start.3
  3.4 0.9 %collective-permute-done.face = f32[2,32,128]{2,1,0:T(8,128)S(1)} collective-permute-done((f32[2,32,128]{2,1,0:T(8,128)S(1)}, f32[2,32,128]{2,1,0:T(8,128)S(1)}, u32[]{:S(2)}, u32[]{:S(2)}) %collective-permute-start) | collective-permute-done | bytes 32800 | tf_op jit(solution)/shard_map/ppermute | solution.py:847
  4.2 0.0 copy-start.6
  4.2 0.0 copy-start.7
  4.2 0.0 copy-start.10
  4.2 0.2 shard_map.195
  4.4 0.0 copy-start
  4.4 0.0 copy-start.1
  4.4 2.5 %collective-permute-start.2 = (f32[208,128]{1,0:T(8,128)S(1)}, f32[208,128]{1,0:T(8,128)S(1)}, u32[]{:S(2)}, u32[]{:S(2)}) collective-permute-start(f32[208,128]{1,0:T(8,128)S(1)} %shard_map.195), channel_id=1, source_target_pairs={{2,5},{3,4},{4,3},{5,2},{6,9},{7,8},{8,7},{9,6},{10,13},{11,12},{1... | collective-permute-start | bytes 319496 | tf_op jit(solution)/shard_map/ppermute | solution.py:848
  7.0 1.1 %collective-permute-start.1 = (f32[208,128]{1,0:T(8,128)S(1)}, f32[208,128]{1,0:T(8,128)S(1)}, u32[]{:S(2)}, u32[]{:S(2)}) collective-permute-start(f32[208,128]{1,0:T(8,128)S(1)} %shard_map.195), channel_id=1, source_target_pairs={{2,4},{3,5},{4,2},{5,3},{6,8},{7,9},{8,6},{9,7},{10,12},{11,13},{1... | collective-permute-start | bytes 319496 | tf_op jit(solution)/shard_map/ppermute | solution.py:848
  8.1 0.0 collective-permute-done.4.refs_2_
  8.1 3.9 %collective-permute-start.6 = (f32[200,128]{1,0:T(8,128)S(1)}, f32[200,128]{1,0:T(8,128)S(1)}, u32[]{:S(2)}, u32[]{:S(2)}) collective-permute-start(f32[200,128]{1,0:T(8,128)S(1)} %get-tuple-element.40), channel_id=1, source_target_pairs={{0,2},{2,0},{4,6},{6,4},{8,10},{10,8},{12,14},{14,12},{16,18},{18,... | collective-permute-start | bytes 307208 | tf_op jit(solution)/shard_map/ppermute | solution.py:847
  12.0 0.0 copy-start.3
  12.0 0.0 copy-start.8
  12.1 0.0 copy-start.13
  12.1 0.1 collective-permute-start.5
  12.2 0.0 collective-permute-done.3.refs_1_
  12.2 0.8 %collective-permute-done.6.refs_4_ = f32[200,128]{1,0:T(8,128)S(1)} collective-permute-done((f32[200,128]{1,0:T(8,128)S(1)}, f32[200,128]{1,0:T(8,128)S(1)}, u32[]{:S(2)}, u32[]{:S(2)}) %collective-permute-start.6) | collective-permute-done | bytes 102432 | tf_op jit(solution)/shard_map/ppermute | solution.py:847
  13.0 0.4 %collective-permute-done.5.refs_3_ = f32[200,128]{1,0:T(8,128)S(1)} collective-permute-done((f32[200,128]{1,0:T(8,128)S(1)}, f32[200,128]{1,0:T(8,128)S(1)}, u32[]{:S(2)}, u32[]{:S(2)}) %collective-permute-start.5) | collective-permute-done | bytes 102432 | tf_op jit(solution)/shard_map/ppermute | solution.py:847
  13.4 0.0 copy-done.6
  13.4 0.0 copy-done.7
  13.4 0.0 copy-done.10
  13.4 0.0 copy-done
  13.4 0.0 copy-done.1
  13.4 0.0 copy-start.12
  13.4 2.5 %shard_map.196 = (f32[16,56,128]{2,1,0:T(8,128)S(1)}, f32[16,56,128]{2,1,0:T(8,128)S(1)}, f32[16,56,128]{2,1,0:T(8,128)S(1)}, f32[16,56,128]{2,1,0:T(8,128)S(1)}, f32[2,2,56,128]{3,2,1,0:T(8,128)S(1)}) custom-call(f32[2,8,32,128]{3,2,1,0:T(8,128)S(1)} %pad_maximum_fusion.raw.refs_0_, f32[2,8,32,128]{3,2,1,0:T(8,128)S(1)} %collective-permute-done.3.refs_1_, ...), custom_call_target="tpu_custom_call" | custom-call | flops 1 | bytes 1 | tf_op jit(solution)/shard_map/pallas_call | solution.py:810
  15.9 0.0 collective-permute-done.2.refs_1_
  15.9 0.0 collective-permute-done.1.refs_0_
  15.9 0.2 collective-permute-start.7
  16.1 0.4 %collective-permute-start.8 = (f32[208,128]{1,0:T(8,128)S(1)}, f32[208,128]{1,0:T(8,128)S(1)}, u32[]{:S(2)}, u32[]{:S(2)}) collective-permute-start(f32[208,128]{1,0:T(8,128)S(1)} %collective-permute-done.2.refs_1_), channel_id=1, source_target_pairs={{0,2},{2,0},{4,6},{6,4},{8,10},{10,8},{12,14},{14,12},{16,18},{18,... | collective-permute-start | bytes 319496 | tf_op jit(solution)/shard_map/ppermute | solution.py:847
  16.5 0.0 copy-done.3
  16.5 0.0 copy-done.8
  16.5 0.0 copy-done.13
  16.5 0.0 copy-done.12
  16.5 0.0 copy-start.4
  16.5 0.0 copy-start.11
  16.5 0.0 copy-start.16
  16.5 0.8 %shard_map.197 = (f32[2,27,8,128]{3,2,1,0:T(8,128)S(1)}, f32[4,8,128]{2,1,0:T(8,128)S(1)}) custom-call(f32[16,56,128]{2,1,0:T(8,128)S(1)} %get-tuple-element.30.w_ref.refs_4_, f32[16,56,128]{2,1,0:T(8,128)S(1)} %get-tuple-element.34.rhs_ref, f32[24,168]{1,0:T(8,128)S(1)} %copy-done.13, f32[384,384]{1,0:T(8,128)S(1)} %copy-done.3, f32[8,168]{1,0:T(8,128)S(1)} %copy-done.12, ...), custom_call_target="tpu_custom_call" | custom-call | flops 1 | bytes 1 | tf_op jit(solution)/shard_map/pallas_call | solution.py:810
  17.3 0.0 collective-permute-done.7.refs_2_
  17.3 0.1 collective-permute-done.8.refs_3_
  17.4 0.1 copy-done.4
  17.5 0.0 copy-done.11
  17.5 0.0 copy-done.16
  17.5 0.0 copy-start.5
  17.5 0.0 copy-start.14
  17.5 1.6 %shard_map.198 = (f32[8,32,128]{2,1,0:T(8,128)S(1)}, f32[3,8,128]{2,1,0:T(8,128)S(1)}, f32[10,8,128]{2,1,0:T(8,128)S(1)}) custom-call(f32[208,128]{1,0:T(8,128)S(1)} %collective-permute-done.1.refs_0_, f32[208,128]{1,0:T(8,128)S(1)} %collective-permute-done.2.refs_1_, f32[208,128]{1,0:T(8,128)S(1)} %collective-permute-done.7.refs_2_, ...), custom_call_target="tpu_custom_call" | custom-call | flops 1 | bytes 1 | tf_op jit(solution)/shard_map/pallas_call | solution.py:810
  19.1 1.0 %collective-permute-start.9 = (f32[3,8,128]{2,1,0:T(8,128)S(1)}, f32[3,8,128]{2,1,0:T(8,128)S(1)}, u32[]{:S(2)}, u32[]{:S(2)}) collective-permute-start(f32[3,8,128]{2,1,0:T(8,128)S(1)} %get-tuple-element.37), channel_id=1, source_target_pairs={{2,4},{3,5},{4,2},{5,3},{6,8},{7,9},{8,6},{9,7},{10,12},{11,13},{1... | collective-permute-start | bytes 36872 | tf_op jit(solution)/shard_map/ppermute | solution.py:848
  20.1 3.0 %collective-permute-done.9.refs_0_ = f32[3,8,128]{2,1,0:T(8,128)S(1)} collective-permute-done((f32[3,8,128]{2,1,0:T(8,128)S(1)}, f32[3,8,128]{2,1,0:T(8,128)S(1)}, u32[]{:S(2)}, u32[]{:S(2)}) %collective-permute-start.9) | collective-permute-done | bytes 12320 | tf_op jit(solution)/shard_map/ppermute | solution.py:848
  23.1 0.0 collective-permute-start.10
  23.1 1.2 %collective-permute-done.10.refs_1_ = f32[3,8,128]{2,1,0:T(8,128)S(1)} collective-permute-done((f32[3,8,128]{2,1,0:T(8,128)S(1)}, f32[3,8,128]{2,1,0:T(8,128)S(1)}, u32[]{:S(2)}, u32[]{:S(2)}) %collective-permute-start.10) | collective-permute-done | bytes 12320 | tf_op jit(solution)/shard_map/ppermute | solution.py:847
  24.3 0.0 copy-done.5
  24.3 0.0 copy-done.14
  24.3 1.2 %shard_map.199 = (f32[8,32,128]{2,1,0:T(8,128)}, f32[2,8,32]{2,1,0:T(8,128)}) custom-call(f32[3,8,128]{2,1,0:T(8,128)S(1)} %collective-permute-done.9.refs_0_, f32[3,8,128]{2,1,0:T(8,128)S(1)} %collective-permute-done.10.refs_1_, f32[8,32,128]{2,1,0:T(8,128)S(1)} %get-tuple-element.38.refs_2_, f32[10,8,128]{2,1,0:T(8,128)S(1)} %get-tuple-element.39.refs_3_, ...), custom_call_target="tpu_custom_call" | custom-call | flops 1 | bytes 1 | tf_op jit(solution)/shard_map/pallas_call | solution.py:810
  (1 shorter events, 0.0 us)
Async XLA Ops:
  0.6 1.1 %copy-start.2 = (f32[384,128]{1,0:T(8,128)S(1)}, f32[384,128]{1,0:T(8,128)}, u32[]{:S(2)}) copy-start(f32[384,128]{1,0:T(8,128)} %constant.36.clone.z_sq.refs_5_) | copy-start | bytes 589828
  0.6 1.1 %copy-start.9 = (f32[8,8,128]{2,1,0:T(8,128)S(1)}, f32[8,8,128]{2,1,0:T(8,128)}, u32[]{:S(2)}) copy-start(f32[8,8,128]{2,1,0:T(8,128)} %constant.50.clone.w3.refs_11_) | copy-start | bytes 98308
  0.7 1.1 %copy-start.15 = (f32[32,96]{1,0:T(8,128)S(1)}, f32[32,96]{1,0:T(8,128)}, u32[]{:S(2)}) copy-start(f32[32,96]{1,0:T(8,128)} %constant.40.clone.y_sq) | copy-start | bytes 36868
  2.1 6.0 %collective-permute-start.4 = (f32[2,200,128]{2,1,0:T(8,128)S(1)}, f32[2,200,128]{2,1,0:T(8,128)S(1)}, u32[]{:S(2)}, u32[]{:S(2)}) collective-permute-start(f32[2,200,128]{2,1,0:T(8,128)S(1)} %get-tuple-element.26), channel_id=1, source_target_pairs={{0,1},{1,0},{2,3},{3,2},{4,5},{5,4},{6,7},{7,6},{8,9},{9,8},{10,11... | collective-permute-start | bytes 614408 | tf_op jit(solution)/shard_map/ppermute | solution.py:866
  2.4 1.8 %collective-permute-start = (f32[2,32,128]{2,1,0:T(8,128)S(1)}, f32[2,32,128]{2,1,0:T(8,128)S(1)}, u32[]{:S(2)}, u32[]{:S(2)}) collective-permute-start(f32[2,32,128]{2,1,0:T(8,128)S(1)} %get-tuple-element.25), channel_id=1, source_target_pairs={{0,2},{2,0},{4,6},{6,4},{8,10},{10,8},{12,14},{14,12},{16,18},{18,... | collective-permute-start | bytes 98312 | tf_op jit(solution)/shard_map/ppermute | solution.py:847
  3.4 8.8 %collective-permute-start.3 = (f32[2,8,32,128]{3,2,1,0:T(8,128)S(1)}, f32[2,8,32,128]{3,2,1,0:T(8,128)S(1)}, u32[]{:S(2)}, u32[]{:S(2)}) collective-permute-start(f32[2,8,32,128]{3,2,1,0:T(8,128)S(1)} %pad_maximum_fusion.raw.refs_0_), channel_id=1, source_target_pairs={{0,2},{2,0},{4,6},{6,4},{8,10},{10,8},{12,14},{14,12},{16,18},{18,... | collective-permute-start | bytes 786440 | tf_op jit(solution)/shard_map/ppermute | solution.py:847
  4.2 9.1 %copy-start.6 = (f32[56,168]{1,0:T(8,128)S(1)}, f32[56,168]{1,0:T(8,128)}, u32[]{:S(2)}) copy-start(f32[56,168]{1,0:T(8,128)} %constant.38.clone.refs_10_.refs_13_) | copy-start | bytes 112900
  4.2 9.1 %copy-start.7 = (f32[56,168]{1,0:T(8,128)S(1)}, f32[56,168]{1,0:T(8,128)}, u32[]{:S(2)}) copy-start(f32[56,168]{1,0:T(8,128)} %constant.37.clone.refs_9_.refs_12_) | copy-start | bytes 112900
  4.2 9.1 %copy-start.10 = (f32[56,168]{1,0:T(8,128)S(1)}, f32[56,168]{1,0:T(8,128)}, u32[]{:S(2)}) copy-start(f32[56,168]{1,0:T(8,128)} %constant.39.clone.refs_6_) | copy-start | bytes 112900
  4.4 8.9 %copy-start = (f32[384,128]{1,0:T(8,128)S(1)}, f32[384,128]{1,0:T(8,128)}, u32[]{:S(2)}) copy-start(f32[384,128]{1,0:T(8,128)} %constant.35.clone.refs_8_.refs_11_) | copy-start | bytes 589828
  4.4 9.0 %copy-start.1 = (f32[384,128]{1,0:T(8,128)S(1)}, f32[384,128]{1,0:T(8,128)}, u32[]{:S(2)}) copy-start(f32[384,128]{1,0:T(8,128)} %constant.34.clone.refs_7_.refs_10_) | copy-start | bytes 589828
  4.4 11.4 %collective-permute-start.2 = (f32[208,128]{1,0:T(8,128)S(1)}, f32[208,128]{1,0:T(8,128)S(1)}, u32[]{:S(2)}, u32[]{:S(2)}) collective-permute-start(f32[208,128]{1,0:T(8,128)S(1)} %shard_map.195), channel_id=1, source_target_pairs={{2,5},{3,4},{4,3},{5,2},{6,9},{7,8},{8,7},{9,6},{10,13},{11,12},{1... | collective-permute-start | bytes 319496 | tf_op jit(solution)/shard_map/ppermute | solution.py:848
  7.0 8.9 %collective-permute-start.1 = (f32[208,128]{1,0:T(8,128)S(1)}, f32[208,128]{1,0:T(8,128)S(1)}, u32[]{:S(2)}, u32[]{:S(2)}) collective-permute-start(f32[208,128]{1,0:T(8,128)S(1)} %shard_map.195), channel_id=1, source_target_pairs={{2,4},{3,5},{4,2},{5,3},{6,8},{7,9},{8,6},{9,7},{10,12},{11,13},{1... | collective-permute-start | bytes 319496 | tf_op jit(solution)/shard_map/ppermute | solution.py:848
  8.1 4.8 %collective-permute-start.6 = (f32[200,128]{1,0:T(8,128)S(1)}, f32[200,128]{1,0:T(8,128)S(1)}, u32[]{:S(2)}, u32[]{:S(2)}) collective-permute-start(f32[200,128]{1,0:T(8,128)S(1)} %get-tuple-element.40), channel_id=1, source_target_pairs={{0,2},{2,0},{4,6},{6,4},{8,10},{10,8},{12,14},{14,12},{16,18},{18,... | collective-permute-start | bytes 307208 | tf_op jit(solution)/shard_map/ppermute | solution.py:847
  12.0 4.4 %copy-start.3 = (f32[384,384]{1,0:T(8,128)S(1)}, f32[384,384]{1,0:T(8,128)}, u32[]{:S(2)}) copy-start(f32[384,384]{1,0:T(8,128)} %constant.46.clone.mz) | copy-start | bytes 1769476
  12.0 4.4 %copy-start.8 = (f32[384,128]{1,0:T(8,128)S(1)}, f32[384,128]{1,0:T(8,128)}, u32[]{:S(2)}) copy-start(f32[384,128]{1,0:T(8,128)} %constant.44.clone.rz) | copy-start | bytes 589828
  12.1 4.4 %copy-start.13 = (f32[24,168]{1,0:T(8,128)S(1)}, f32[24,168]{1,0:T(8,128)}, u32[]{:S(2)}) copy-start(f32[24,168]{1,0:T(8,128)} %constant.45.clone.my) | copy-start | bytes 48388
  12.1 1.3 %collective-permute-start.5 = (f32[200,128]{1,0:T(8,128)S(1)}, f32[200,128]{1,0:T(8,128)S(1)}, u32[]{:S(2)}, u32[]{:S(2)}) collective-permute-start(f32[200,128]{1,0:T(8,128)S(1)} %get-tuple-element.41), channel_id=1, source_target_pairs={{0,2},{2,0},{4,6},{6,4},{8,10},{10,8},{12,14},{14,12},{16,18},{18,... | collective-permute-start | bytes 307208 | tf_op jit(solution)/shard_map/ppermute | solution.py:847
  13.4 3.1 %copy-start.12 = (f32[8,168]{1,0:T(8,128)S(1)}, f32[8,168]{1,0:T(8,128)}, u32[]{:S(2)}) copy-start(f32[8,168]{1,0:T(8,128)} %constant.42.clone.ry.refs_15_) | copy-start | bytes 16132
  15.9 1.4 %collective-permute-start.7 = (f32[208,128]{1,0:T(8,128)S(1)}, f32[208,128]{1,0:T(8,128)S(1)}, u32[]{:S(2)}, u32[]{:S(2)}) collective-permute-start(f32[208,128]{1,0:T(8,128)S(1)} %collective-permute-done.1.refs_0_), channel_id=1, source_target_pairs={{0,2},{2,0},{4,6},{6,4},{8,10},{10,8},{12,14},{14,12},{16,18},{18,... | collective-permute-start | bytes 319496 | tf_op jit(solution)/shard_map/ppermute | solution.py:847
  16.1 1.3 %collective-permute-start.8 = (f32[208,128]{1,0:T(8,128)S(1)}, f32[208,128]{1,0:T(8,128)S(1)}, u32[]{:S(2)}, u32[]{:S(2)}) collective-permute-start(f32[208,128]{1,0:T(8,128)S(1)} %collective-permute-done.2.refs_1_), channel_id=1, source_target_pairs={{0,2},{2,0},{4,6},{6,4},{8,10},{10,8},{12,14},{14,12},{16,18},{18,... | collective-permute-start | bytes 319496 | tf_op jit(solution)/shard_map/ppermute | solution.py:847
  16.5 1.0 %copy-start.4 = (f32[768,128]{1,0:T(8,128)S(1)}, f32[768,128]{1,0:T(8,128)}, u32[]{:S(2)}) copy-start(f32[768,128]{1,0:T(8,128)} %constant.43.clone.refs_16_) | copy-start | bytes 1179652
  16.5 1.0 %copy-start.11 = (f32[10,8,128]{2,1,0:T(8,128)S(1)}, f32[10,8,128]{2,1,0:T(8,128)}, u32[]{:S(2)}) copy-start(f32[10,8,128]{2,1,0:T(8,128)} %constant.49.clone.refs_17_) | copy-start | bytes 122884
  16.5 1.0 %copy-start.16 = (f32[8,336]{1,0:T(8,128)S(1)}, f32[8,336]{1,0:T(8,128)}, u32[]{:S(2)}) copy-start(f32[8,336]{1,0:T(8,128)} %constant.41.clone.refs_14_) | copy-start | bytes 32260
  17.5 6.8 %copy-start.5 = (f32[384,160]{1,0:T(8,128)S(1)}, f32[384,160]{1,0:T(8,128)}, u32[]{:S(2)}) copy-start(f32[384,160]{1,0:T(8,128)} %constant.48.clone.refs_6_) | copy-start | bytes 737284
  17.5 6.8 %copy-start.14 = (f32[40,24]{1,0:T(8,128)S(1)}, f32[40,24]{1,0:T(8,128)}, u32[]{:S(2)}) copy-start(f32[40,24]{1,0:T(8,128)} %constant.47.clone.refs_5_) | copy-start | bytes 11524
  19.1 4.0 %collective-permute-start.9 = (f32[3,8,128]{2,1,0:T(8,128)S(1)}, f32[3,8,128]{2,1,0:T(8,128)S(1)}, u32[]{:S(2)}, u32[]{:S(2)}) collective-permute-start(f32[3,8,128]{2,1,0:T(8,128)S(1)} %get-tuple-element.37), channel_id=1, source_target_pairs={{2,4},{3,5},{4,2},{5,3},{6,8},{7,9},{8,6},{9,7},{10,12},{11,13},{1... | collective-permute-start | bytes 36872 | tf_op jit(solution)/shard_map/ppermute | solution.py:848
  23.1 1.2 %collective-permute-start.10 = (f32[3,8,128]{2,1,0:T(8,128)S(1)}, f32[3,8,128]{2,1,0:T(8,128)S(1)}, u32[]{:S(2)}, u32[]{:S(2)}) collective-permute-start(f32[3,8,128]{2,1,0:T(8,128)S(1)} %collective-permute-done.9.refs_0_), channel_id=1, source_target_pairs={{0,2},{2,0},{4,6},{6,4},{8,10},{10,8},{12,14},{14,12},{16,18},{18,... | collective-permute-start | bytes 36872 | tf_op jit(solution)/shard_map/ppermute | solution.py:847

commit v4 on v3

--- a/solution.py
+++ b/solution.py
@@ -9,7 +9,7 @@
 from jax.sharding import PartitionSpec as P
 
 N = 8
-SPARE = 3 * N
+SPARE = N
 HALO = 3 * N
 THETA = 1.1
 DELTA = 0.9
@@ -175,30 +175,49 @@
     return dot(jnp.concatenate([hi, lo, hi], axis=1), table.astype(BF16))
 
 
-def y_apply(hi, lo, table):
-    return dot(table.astype(BF16), jnp.concatenate([hi, lo, hi], axis=0))
+def y_apply(x, table):
+    hi = x.astype(BF16).astype(F32)
+    parts = jnp.concatenate([hi, x - hi, hi], axis=0).astype(BF16)
+    return dot(table.astype(BF16), parts)
+
+
+def y_planes(get, planes, table):
+    table = table.astype(BF16)
+    out = {}
+    for p, q in zip(planes[::2], planes[1::2]):
+        both = y_apply(jnp.concatenate([get(p), get(q)], axis=1), table)
+        nz = both.shape[1] // 2
+        out[p], out[q] = both[:, :nz], both[:, nz:]
+    return out
 
 
 def assemble_yz(v):
     ny, nz = v.shape
     row = lax.broadcasted_iota(jnp.int32, (N, nz), 0)
-    lane = lax.broadcasted_iota(jnp.int32, (1, nz), 1)
+    lane = lax.broadcasted_iota(jnp.int32, (ny, nz), 1)
+    is_top = row == 0
+    flip = (N - 1) - row
+    blocks = [v[N * e : N * e + N] for e in range(ny // N)]
     top = (row == N - 1).astype(F32)
     bottom = (row == 0).astype(F32)
-    blocks = [v[N * e : N * e + N] for e in range(ny // N)]
-    ups = [pltpu.roll(b, N - 1, 0) for b in blocks]
-    downs = [pltpu.roll(b, 1, 0) for b in blocks]
     out = []
     for e, b in enumerate(blocks):
-        if e + 1 < len(blocks):
-            b = b + top * ups[e + 1]
-        if e > 0:
-            b = b + bottom * downs[e - 1]
-        out.append(b)
+        if len(blocks) == 1:
+            out.append(b)
+            continue
+        if e == 0:
+            near, mask = blocks[1], top
+        elif e + 1 == len(blocks):
+            near, mask = blocks[e - 1], bottom
+        else:
+            near, mask = jnp.where(is_top, blocks[e + 1], blocks[e - 1]), top + bottom
+        out.append(b + mask * jnp.take_along_axis(near, flip, axis=0))
     v = jnp.concatenate(out, axis=0)
-    last = ((lane % N == N - 1) & (lane < nz - 1)).astype(F32)
-    first = ((lane % N == 0) & (lane > 0)).astype(F32)
-    return v + last * pltpu.roll(v, nz - 1, 1) + first * pltpu.roll(v, 1, 1)
+    last = (lane % N == N - 1) & (lane < nz - 1)
+    first = (lane % N == 0) & (lane > 0)
+    other = lane + jnp.where(last, 1, 0) - jnp.where(first, 1, 0)
+    mask = (last | first).astype(F32)
+    return v + mask * jnp.take_along_axis(v, other, axis=1)
 
 
 def yz_mask(ny, nz, start, total):
@@ -248,13 +267,6 @@
             return [(1 - h) * (self.ny - 1)]
         return [0, self.ny - 1]
 
-    def used_rows(self, h):
-        if self.sub == 1:
-            return []
-        if self.sub == 2:
-            return [h * (self.own_y - HALO)]
-        return [self.own_y - HALO, 0]
-
     def interfaces(self, h):
         if self.sub == 1:
             return []
@@ -278,6 +290,25 @@
         store(pl.ds(0, HALO), others[0])
         store(pl.ds(HALO, y), own)
         store(pl.ds(HALO + y, HALO), others[1])
+
+
+PACK = 2 * N + 2 * N * HALO
+CUTS = [0, 2 * N + 5 * HALO, 2 * N + 10 * HALO, PACK]
+
+
+def pack_rows(side, a):
+    return pl.ds(2 * N + (side * N + a) * HALO, HALO)
+
+
+class Pieces:
+    def __init__(self, refs):
+        self.refs = refs
+
+    def __getitem__(self, rows):
+        if len(self.refs) == 1:
+            return self.refs[0][rows, :]
+        k = max(i for i in range(len(self.refs)) if CUTS[i] <= rows.start)
+        return self.refs[k][pl.ds(rows.start - CUTS[k], rows.size), :]
 
 
 def line_rows(lay, h):
@@ -307,10 +338,9 @@
     hi, lo = split(w_out[...].reshape(N * y, nz))
     dz = z_apply(hi, lo, z_sq[...])
     sx_out[...] = assemble_yz(d_out[(N - 1) * parity])
+    dy = y_planes(lambda a: w_out[a], list(range(N)), y_sq[...])
     for a in range(N):
-        cut = slice(a * y, (a + 1) * y)
-        dy = y_apply(hi[cut], lo[cut], y_sq[...])
-        d_out[a] = assemble_yz(d_out[a] + dz[cut] + dy)
+        d_out[a] = assemble_yz(d_out[a] + dz[a * y : (a + 1) * y] + dy[a])
         r_out[a] = assemble_yz(rhs[a])
     inner = (N - 1) * (1 - parity)
     face[0] = r_out[inner]
@@ -318,11 +348,12 @@
     for pack, (first, far) in zip(packs, lay.sent_rows(h)):
         for side, field in ((0, r_out), (1, d_out)):
             for a in range(N):
-                pack[side, pl.ds(a * HALO, HALO), :] = raw[side, a, aligned(first, HALO), :]
-                pack[side, pl.ds(N * HALO + a, 1), :] = field[a, pl.ds(far, 1), :]
-
-
-def message_kernel(lay, w, d, r, sx, face, msg, u_s, d_s, r_s):
+                pack[pack_rows(side, a), :] = raw[side, a, aligned(first, HALO), :]
+                pack[pl.ds(side * N + a, 1), :] = field[a, pl.ds(far, 1), :]
+
+
+def message_kernel(lay, w, d, r, sx, face, *refs):
+    msg, *side_msgs, u_s, d_s, r_s = refs
     y, nz = lay.own_y, lay.nz
     parity, h, start, offset, low, high = lay.where()
     mask = yz_mask(y, nz, h * y, lay.total_y)
@@ -361,7 +392,12 @@
             for a in range(N):
                 msg[pl.ds(base + a, 1), :] = field[a, pl.ds(row, 1), :]
             base += N
-    msg[pl.ds(base, SPARE), :] = jnp.zeros((SPARE, nz), F32)
+    for out, (first, _) in zip(side_msgs, lay.sent_rows(h)):
+        for k in range(5):
+            out[pl.ds(k * HALO, HALO), :] = msg[aligned(k * y + first, HALO), :]
+        lines = base - 5 * y
+        out[pl.ds(5 * HALO, lines), :] = msg[pl.ds(5 * y, lines), :]
+        out[pl.ds(5 * HALO + lines, SPARE), :] = jnp.zeros((SPARE, nz), F32)
 
 
 def gradient_flux(lay, u_ref, w_ref, planes, z_d, y_d, fx, fy, fz):
@@ -376,70 +412,75 @@
     first, count = planes[0], len(planes)
     hi, lo = split(u_ref[pl.ds(first, count)].reshape(count * ny, nz))
     gz = z_apply(hi, lo, z_d[...])
+    gy = y_planes(lambda p: u_ref[p], planes, y_d[...])
     for p in planes:
-        cut = slice((p - first) * ny, (p - first + 1) * ny)
-        gy = y_apply(hi[cut], lo[cut], y_d[...])
         w = w_ref[p]
-        fy[p] = w * gy
-        fz[p] = w * gz[cut]
-
-
-def deep_kernel(lay, n_other, *refs):
-    own, mate = refs[:2]
-    other = refs[2 : 2 + n_other]
-    mate_other = [refs[2 + n_other + 2 * k :][:2] for k in range(n_other)]
-    refs = refs[2 + 3 * n_other :]
+        fy[p] = w * gy[p]
+        fz[p] = w * gz[(p - first) * ny : (p - first + 1) * ny]
+
+
+def element_sums(lay, base, parity, h, block, pieces, tables, outs):
+    z_sq, y_sq, w3 = tables
+    w_out, rhs_out, d_s, r_s, lin = outs
+    ny, nz = lay.ny, lay.nz
+    for side, target in ((0, rhs_out), (1, w_out)):
+        for a in range(N):
+
+            def put(rows, value):
+                target[base + a, rows, :] = value
+
+            gather_window(lay, block[side, a], [o[pack_rows(side, a)] for o in pieces], h, put)
+    table3 = w3[...]
+    outer = [jnp.where(parity == 0, float(DM[a, 0]), float(DM[a, N - 1])) for a in range(N)]
+    for e in range(lay.ey):
+        rows = pl.ds(N * e, N)
+        w = [w_out[base + a, rows, :] * table3[a] for a in range(N)]
+        dx = even_odd((DM * DM).T, w, 1)
+        cx = even_odd(DM.T, [outer[a] * w[a] for a in range(N)], -1)
+        for a in range(N):
+            w_out[base + a, rows, :] = w[a]
+            d_s[base + a, rows, :] = dx[a]
+            lin[base + a, rows, :] = cx[a]
+    dz = z_apply(*split(w_out[pl.ds(base, N)].reshape(N * ny, nz)), z_sq[...])
+    dy = y_planes(lambda a: w_out[base + a], list(range(N)), y_sq[...])
+    for a in range(N):
+        d_s[base + a] = assemble_yz(d_s[base + a] + dz[a * ny : (a + 1) * ny] + dy[a])
+        r_s[base + a] = assemble_yz(rhs_out[base + a])
+        lin[base + a] = assemble_yz(lin[base + a])
+    for piece, row in zip(pieces, lay.far_rows(h)):
+        for side, target in ((0, r_s), (1, d_s)):
+            for a in range(N):
+                target[base + a, pl.ds(row, 1), :] = piece[pl.ds(side * N + a, 1)]
+
+
+def near_kernel(lay, own, *refs):
+    n_other = len(refs) - 8
+    other, tables, outs = refs[:n_other], refs[n_other : n_other + 3], refs[n_other + 3 :]
+    parity, h = lay.where()[:2]
+    pieces = [Pieces([o]) for o in other]
+    element_sums(lay, parity * N, parity, h, own, pieces, tables, outs)
+
+
+def deep_kernel(lay, n_other, mate, *refs):
+    cuts = len(CUTS) - 1
+    mate_other = [Pieces(refs[cuts * k : cuts * (k + 1)]) for k in range(n_other)]
+    refs = refs[cuts * n_other + 5 :]
     z_sq, y_sq, z_d, z_dt, y_d, y_dt, w3 = refs[:7]
-    w_out, rhs_out, sec_out, lin_out, ends = refs[7:12]
-    d_s, r_s, u_s, inv_s, fx, fy, fz, back = refs[12:]
+    w_out, rhs_out, d_s, r_s, lin_out, sec_out, ends = refs[7:14]
+    u_s, inv_s, fx, fy, fz, back = refs[14:]
     ny, nz = lay.ny, lay.nz
     last = 2 * N - 1
     parity, h, start, offset, low, high = lay.where()
-    for side, target in ((0, rhs_out), (1, w_out)):
-        for base, block, pieces in (
-            (parity * N, own, [o.at[side] for o in other]),
-            ((1 - parity) * N, mate, [o[side] for o in mate_other]),
-        ):
-            for a in range(N):
-
-                def put(rows, value):
-                    target[base + a, rows, :] = value
-
-                cut = pl.ds(a * HALO, HALO)
-                gather_window(lay, block[side, a], [o[cut, :] for o in pieces], h, put)
-    table3 = w3[...]
-    for el in range(2):
-        outer = DM[:, 0] if el == 0 else DM[:, N - 1]
-        for e in range(lay.ey):
-            rows = pl.ds(N * e, N)
-            w = [w_out[N * el + a, rows, :] * table3[a] for a in range(N)]
-            dx = even_odd((DM * DM).T, w, 1)
-            cx = even_odd(DM.T, [float(outer[a]) * w[a] for a in range(N)], -1)
-            for a in range(N):
-                w_out[N * el + a, rows, :] = w[a]
-                d_s[N * el + a, rows, :] = dx[a]
-                lin_out[N * el + a, rows, :] = cx[a]
-    hi, lo = split(w_out[...].reshape(2 * N * ny, nz))
-    dz = z_apply(hi, lo, z_sq[...])
-    mask = yz_mask(ny, nz, start, lay.total_y)
-    inside = mask.astype(F32)
-    for p in range(2 * N):
-        cut = slice(p * ny, (p + 1) * ny)
-        dy = y_apply(hi[cut], lo[cut], y_sq[...])
-        d_s[p] = assemble_yz(d_s[p] + dz[cut] + dy)
-        r_s[p] = assemble_yz(rhs_out[p])
-    for k, row in enumerate(lay.far_rows(h)):
-        for side, target in ((0, r_s), (1, d_s)):
-            for base, piece in (
-                (parity * N, other[k].at[side]),
-                ((1 - parity) * N, mate_other[k][side]),
-            ):
-                for a in range(N):
-                    target[base + a, pl.ds(row, 1), :] = piece[pl.ds(N * HALO + a, 1), :]
+    element_sums(
+        lay, (1 - parity) * N, 1 - parity, h, mate, mate_other, (z_sq, y_sq, w3),
+        (w_out, rhs_out, d_s, r_s, lin_out),
+    )
     for s in (d_s, r_s):
         both = s[N - 1] + s[N]
         s[N - 1] = both
         s[N] = both
+    mask = yz_mask(ny, nz, start, lay.total_y)
+    inside = mask.astype(F32)
     ends[0, 0] = r_s[0]
     ends[0, 1] = d_s[0]
     ends[1, 0] = r_s[last]
@@ -461,21 +502,18 @@
                 back[N * el + a, rows, :] = b[a]
     hi, lo = split(fz[pl.ds(1, last - 1)].reshape((last - 1) * ny, nz))
     bz = z_apply(hi, lo, z_dt[...])
+    by = y_planes(lambda p: fy[p], middle, y_dt[...])
     for p in middle:
-        hi, lo = split(fy[p])
-        by = y_apply(hi, lo, y_dt[...])
-        back[p] = assemble_yz(back[p] + by + bz[(p - 1) * ny : p * ny])
+        back[p] = assemble_yz(back[p] + by[p] + bz[(p - 1) * ny : p * ny])
     both = back[N - 1] + back[N]
     back[N - 1] = both
     back[N] = both
     for p in range(2 * N):
-        linear = assemble_yz(lin_out[p])
         if p in (0, last):
-            lin_out[p] = linear
             sec_out[p] = assemble_yz(back[p])
         else:
             inv = (2.0 * RHO1 / DELTA) * inv_s[p]
-            lin_out[p] = -inv * linear
+            lin_out[p] = -inv * lin_out[p]
             sec_out[p] = (1.0 + RHO1 * RHO0) * u_s[p] + inv * (r_s[p] - back[p])
 
 
@@ -494,7 +532,7 @@
         mom = {}
         for alpha in range(3):
             at = (3 * el + alpha) * ny
-            block = y_apply(*split(along_z[at : at + ny]), my[...])
+            block = y_apply(along_z[at : at + ny], my[...])
             for beta in range(3):
                 for gamma in range(3):
                     mom[alpha, beta, gamma] = block[
@@ -523,7 +561,7 @@
                 term = float(RHO[a, i]) * rhs_ref[N * el + a]
                 total = term if total is None else total + term
             sums.append(total)
-    part = y_apply(*split(jnp.concatenate(sums, axis=1)), ry[...])
+    part = y_apply(jnp.concatenate(sums, axis=1), ry[...])
     rows = jnp.concatenate([part[:, k * nz : (k + 1) * nz] for k in range(4)], axis=0)
     full = z_apply(*split(rows), rz[...])
     for k in range(4):
@@ -582,9 +620,7 @@
             def put(rows, value):
                 win[side, k, rows, :] = value
 
-            others = [
-                g[aligned(k * y + first, HALO), :] for g, first in zip(group[1:], lay.used_rows(h))
-            ]
+            others = [g[pl.ds(k * HALO, HALO), :] for g in group[1:]]
             gather_window(lay, group[0][pl.ds(k * y, y), :], others, h, put)
     is_even = parity == 0
     lane = lax.broadcasted_iota(jnp.int32, (N, nz), 1)
@@ -605,16 +641,15 @@
 
             def field(k):
                 def of(group):
+                    own_lines, other_lines = 5 * y + k * N, 5 * HALO + k * N
                     if lay.sub == 2:
-                        one, two, at_one, at_two = group[0], group[1], 0, 0
+                        mine, theirs = own_lines, other_lines
+                        near = group[1]
                     else:
-                        order = [group[1], group[0], group[2]]
-                        one, two, at_one, at_two = order[b - 1], order[b], 1, 0
-                    base = 5 * y + k * N
-                    return (
-                        one[pl.ds(base + 3 * N * at_one, N), :]
-                        + two[pl.ds(base + 3 * N * at_two, N), :]
-                    )
+                        mine = own_lines + 3 * N * (b - 1)
+                        theirs = other_lines + 3 * N * (2 - b)
+                        near = group[b]
+                    return group[0][pl.ds(mine, N), :] + near[pl.ds(theirs, N), :]
                 mine, theirs = of(pieces), of(mate_pieces)
                 if side == 0:
                     return jnp.where(is_even, mine, theirs)
@@ -665,15 +700,11 @@
     weights = [w_ref[0] + win[0, 3], w_ref[last] + win[1, 3]]
     hi, lo = split(jnp.concatenate(u, axis=0))
     gz = z_apply(hi, lo, z_d[...])
-    gy = y_apply(
-        jnp.concatenate([hi[:ny], hi[ny:]], axis=1),
-        jnp.concatenate([lo[:ny], lo[ny:]], axis=1),
-        y_d[...],
-    )
+    gy = y_apply(jnp.concatenate(u, axis=1), y_d[...])
     weight_z = jnp.concatenate(weights, axis=0)
     weight_y = jnp.concatenate(weights, axis=1)
     bz = z_apply(*split(weight_z * gz), z_dt[...])
-    by = y_apply(*split(weight_y * gy), y_dt[...])
+    by = y_apply(weight_y * gy, y_dt[...])
     for side, p in ((0, 0), (1, last)):
         plane = assemble_yz(bz[side * ny : (side + 1) * ny] + by[:, side * nz : (side + 1) * nz])
         plane = plane + sec_in[p] + win[side, 4] + (lin_in[p] + win[side, 2]) * u[side]
@@ -692,8 +723,8 @@
                     total = term if total is None else total + term
                 lanes.append(total)
         sums.append(jnp.concatenate(lanes, axis=1))
-    one = y_apply(*split(jnp.concatenate(sums[:2], axis=0)), ry[...])
-    two = y_apply(*split(sums[2]), ry_one[...])
+    one = y_apply(jnp.concatenate(sums[:2], axis=0), ry[...])
+    two = y_apply(sums[2], ry_one[...])
     rows = [
         jnp.concatenate([v[:, k * nz : (k + 1) * nz] for v in (one, two)], axis=1) for k in range(4)
     ]
@@ -787,7 +818,7 @@
     if lay.sub > 1:
         both = pltpu.roll(both, cr - lax.div(offset, N), 0)
     y, cy = lay.own_y, lay.own_y // 4
-    along_y = y_apply(*split(both), py[...])
+    along_y = y_apply(both, py[...])
     along_y = jnp.concatenate([along_y[:, :nz], along_y[:, nz:]], axis=0)
     full = z_apply(*split(along_y), pz[...])
     inside = yz_mask(y, nz, start + offset, lay.total_y).astype(F32)
@@ -806,7 +837,7 @@
         out[a] = sec[a] + add
 
 
-def run(kernel, args, outs, scratch=()):
+def run(kernel, args, outs, scratch=(), aliases={}):
     return pl.pallas_call(
         kernel,
         out_shape=[jax.ShapeDtypeStruct(o, F32) for o in outs],
@@ -814,6 +845,7 @@
         out_specs=[pl.BlockSpec(memory_space=pltpu.VMEM)] * len(outs),
         scratch_shapes=[pltpu.VMEM(s, F32) for s in scratch],
         compiler_params=pltpu.CompilerParams(vmem_limit_bytes=VMEM_LIMIT),
+        input_output_aliases=aliases,
         cost_estimate=pl.CostEstimate(flops=1, bytes_accessed=1, transcendentals=0),
     )(*args)
 
@@ -853,7 +885,7 @@
         functools.partial(own_kernel, lay),
         [raw] + pick("z_sq", "y_sq_own", "w3"),
         [(2, own_y, nz), block, block, block, (own_y, nz)]
-        + [(2, N * (HALO + 1), nz)] * n_other,
+        + [(PACK, nz)] * n_other,
     )
     mate_face = even(face)
     if sub == 1:
@@ -865,22 +897,28 @@
         steps = [up, [(b, a) for a, b in up]]
     others = [lax.ppermute(pack, "sub", step) for pack, step in zip(packs, steps)]
     mate = even(raw)
-    (msg,) = run(
+    lines = 3 * N * line_count(lay)
+    msgs = run(
         functools.partial(message_kernel, lay),
         [w, d, r, sx, mate_face],
-        [(5 * own_y + 3 * N * line_count(lay) + SPARE, nz)],
+        [(5 * own_y + lines, nz)] + [(5 * HALO + lines + SPARE, nz)] * n_other,
         [block] * 3,
     )
     shifts = [0] if sub == 1 else [0, 1] if sub == 2 else [0, 1, -1]
-    pieces = [odd(msg, k) for k in shifts]
-    mate_others = [even(o[side]) for o in others for side in range(2)]
+    pieces = [odd(msg, k) for msg, k in zip(msgs, shifts)]
+    mate_others = [even(o[a:b]) for o in others for a, b in zip(CUTS, CUTS[1:])]
     pair = (2 * N, ny, nz)
-    w, rhs, sec, lin, ends = run(
+    arrays = run(
+        functools.partial(near_kernel, lay),
+        [raw, *others] + pick("z_sq", "y_sq", "w3"),
+        [pair] * 5,
+    )
+    w, rhs, _, _, lin, sec, ends = run(
         functools.partial(deep_kernel, lay, n_other),
-        [raw, mate, *others, *mate_others]
-        + pick("z_sq", "y_sq", "z_d", "z_dt", "y_d", "y_dt", "w3"),
-        [pair] * 4 + [(2, 2, ny, nz)],
-        [pair] * 8,
+        [mate, *mate_others, *arrays] + pick("z_sq", "y_sq", "z_d", "z_dt", "y_d", "y_dt", "w3"),
+        [pair] * 6 + [(2, 2, ny, nz)],
+        [pair] * 6,
+        {1 + len(mate_others) + k: k for k in range(5)},
     )
     pieces, sec = lax.optimization_barrier((pieces, sec))
     mate_pieces = [even(p) for p in pieces]

time: 25.6 us -> 24.2 us (0.945)
  the two profiles are of different devices: /device:TPU:15 before, /device:TPU:31 now
where the time goes in v4:
time: 24.2 us; the launch traced here: 23.8 us
  waiting for transfers between devices  9.33 us (39%)
  Pallas kernels  6.23 us (26%)
  starting transfers between devices  6.05 us (25%)
  other arithmetic  1.04 us (4%)
  between operations  0.87 us (4%)
  local copies, waits for them, and re-layouts  0.25 us (1%)
    pallas_call x7, Pallas kernels, run(): pl.pallas_call(kernel, out_shape=[jax.ShapeDtypeStruct(o, F32) for o in o...  6.23 us
    ppermute x1, waiting for transfers between devices, shards(): lax.ppermute(pack, 'sub', step)  4.38 us
    ppermute x8, starting transfers between devices, shards(): even = lambda v: lax.ppermute(v, 'dom', swap_pairs(dom, 0))  4.03 us
    ppermute x3, waiting for transfers between devices, shards(): lax.ppermute(v, ('dom', 'sub'), chip_pairs(dom, sub, k))  2.62 us
    ppermute x8, waiting for transfers between devices, shards(): even = lambda v: lax.ppermute(v, 'dom', swap_pairs(dom, 0))  2.33 us
    ppermute x3, starting transfers between devices, shards(): lax.ppermute(v, ('dom', 'sub'), chip_pairs(dom, sub, k))  1.74 us
    another operation x1, other arithmetic, shards(): raw = jnp.stack([rhs_local, coefficient])  1.04 us
  transfers between devices with their start and end apart: 12, of which 6 were waited for; matrix products, arithmetic and copies ran while one was open for 0% of the time, Pallas kernels for 15%

profile of v4, /device:TPU:31, one launch (start us, length us, event | category | flops | bytes accessed | tf_op | source)
XLA Modules:
  0.0 23.8 jit_solution(940786550429102886)
XLA Ops:
  0.6 0.0 copy-start
  0.6 0.0 copy-start.6
  0.7 0.0 copy-start.15
  0.7 1.0 %pad_maximum_fusion.raw.own = f32[2,8,32,128]{3,2,1,0:T(8,128)S(1)} fusion(f32[1,8,32,128]{3,2,1,0:T(8,128)} %bitcast.2, f32[1,8,32,128]{3,2,1,0:T(8,128)} %bitcast.3), kind=kLoop, calls=%fused_computation | loop fusion | flops 65536 | bytes 524288 | tf_op jit(solution)/shard_map/stack | solution.py:882
  1.7 0.7 %collective-permute-start.3 = (f32[2,8,32,128]{3,2,1,0:T(8,128)S(1)}, f32[2,8,32,128]{3,2,1,0:T(8,128)S(1)}, u32[]{:S(2)}, u32[]{:S(2)}) collective-permute-start(f32[2,8,32,128]{3,2,1,0:T(8,128)S(1)} %pad_maximum_fusion.raw.own), channel_id=1, source_target_pairs={{0,2},{2,0},{4,6},{6,4},{8,10},{10,8},{12,14},{14,12},{16,18},{18,... | collective-permute-start | bytes 786440 | tf_op jit(solution)/shard_map/ppermute | solution.py:879
  2.4 0.0 copy-done
  2.5 0.0 copy-done.6
  2.5 0.0 copy-done.15
  2.5 0.3 %shard_map.194 = (f32[2,32,128]{2,1,0:T(8,128)S(1)}, f32[8,32,128]{2,1,0:T(8,128)S(1)}, f32[8,32,128]{2,1,0:T(8,128)S(1)}, f32[8,32,128]{2,1,0:T(8,128)S(1)}, f3...) custom-call(f32[2,8,32,128]{3,2,1,0:T(8,128)S(1)} %pad_maximum_fusion.raw.own, f32[384,128]{1,0:T(8,128)S(1)} %copy-done, ...), custom_call_target="tpu_custom_call" | custom-call | flops 1 | bytes 1 | tf_op jit(solution)/shard_map/pallas_call | solution.py:841
  2.8 0.3 %collective-permute-start.4 = (f32[400,128]{1,0:T(8,128)S(1)}, f32[400,128]{1,0:T(8,128)S(1)}, u32[]{:S(2)}, u32[]{:S(2)}) collective-permute-start(f32[400,128]{1,0:T(8,128)S(1)} %get-tuple-element.35), channel_id=1, source_target_pairs={{0,1},{1,0},{2,3},{3,2},{4,5},{5,4},{6,7},{7,6},{8,9},{9,8},{10,11... | collective-permute-start | bytes 614408 | tf_op jit(solution)/shard_map/ppermute | solution.py:898
  3.1 0.3 %collective-permute-start = (f32[2,32,128]{2,1,0:T(8,128)S(1)}, f32[2,32,128]{2,1,0:T(8,128)S(1)}, u32[]{:S(2)}, u32[]{:S(2)}) collective-permute-start(f32[2,32,128]{2,1,0:T(8,128)S(1)} %get-tuple-element.32), channel_id=1, source_target_pairs={{0,2},{2,0},{4,6},{6,4},{8,10},{10,8},{12,14},{14,12},{16,18},{18,... | collective-permute-start | bytes 98312 | tf_op jit(solution)/shard_map/ppermute | solution.py:879
  3.4 0.9 %collective-permute-done.face = f32[2,32,128]{2,1,0:T(8,128)S(1)} collective-permute-done((f32[2,32,128]{2,1,0:T(8,128)S(1)}, f32[2,32,128]{2,1,0:T(8,128)S(1)}, u32[]{:S(2)}, u32[]{:S(2)}) %collective-permute-start) | collective-permute-done | bytes 32800 | tf_op jit(solution)/shard_map/ppermute | solution.py:879
  4.3 0.2 shard_map.195
  4.5 1.3 %collective-permute-start.1 = (f32[184,128]{1,0:T(8,128)S(1)}, f32[184,128]{1,0:T(8,128)S(1)}, u32[]{:S(2)}, u32[]{:S(2)}) collective-permute-start(f32[184,128]{1,0:T(8,128)S(1)} %get-tuple-element.33), channel_id=1, source_target_pairs={{2,4},{3,5},{4,2},{5,3},{6,8},{7,9},{8,6},{9,7},{10,12},{11,13},{1... | collective-permute-start | bytes 282632 | tf_op jit(solution)/shard_map/ppermute | solution.py:880
  5.7 0.2 collective-permute-start.2
  6.0 4.4 %collective-permute-done.4.refs_0_ = f32[400,128]{1,0:T(8,128)S(1)} collective-permute-done((f32[400,128]{1,0:T(8,128)S(1)}, f32[400,128]{1,0:T(8,128)S(1)}, u32[]{:S(2)}, u32[]{:S(2)}) %collective-permute-start.4) | collective-permute-done | bytes 204832 | tf_op jit(solution)/shard_map/ppermute | solution.py:898
  10.4 1.3 %collective-permute-start.7 = (f32[144,128]{1,0:T(8,128)S(1)}, f32[144,128]{1,0:T(8,128)S(1)}, u32[]{:S(2)}, u32[]{:S(2)}) collective-permute-start(f32[144,128]{1,0:T(8,128)S(1)} %slice.14), channel_id=1, source_target_pairs={{0,2},{2,0},{4,6},{6,4},{8,10},{10,8},{12,14},{14,12},{16,18},{18,... | collective-permute-start | bytes 221192 | tf_op jit(solution)/shard_map/ppermute | solution.py:879
  11.6 0.1 collective-permute-start.5
  11.7 0.0 copy-start.2
  11.7 0.0 copy-start.8
  11.8 0.0 copy-start.9
  11.8 0.0 collective-permute-done.3.mate
  11.8 0.5 %collective-permute-start.6 = (f32[120,128]{1,0:T(8,128)S(1)}, f32[120,128]{1,0:T(8,128)S(1)}, u32[]{:S(2)}, u32[]{:S(2)}) collective-permute-start(f32[120,128]{1,0:T(8,128)S(1)} %slice.13), channel_id=1, source_target_pairs={{0,2},{2,0},{4,6},{6,4},{8,10},{10,8},{12,14},{14,12},{16,18},{18,... | collective-permute-start | bytes 184328 | tf_op jit(solution)/shard_map/ppermute | solution.py:879
  12.3 0.1 copy-done.7
  12.4 0.5 %shard_map.196 = (f32[16,56,128]{2,1,0:T(8,128)S(1)}, f32[16,56,128]{2,1,0:T(8,128)S(1)}, f32[16,56,128]{2,1,0:T(8,128)S(1)}, f32[16,56,128]{2,1,0:T(8,128)S(1)}, f32[16,56,128]{2,1,0:T(8,128)S(1)}) custom-call(f32[2,8,32,128]{3,2,1,0:T(8,128)S(1)} %pad_maximum_fusion.raw.own, f32[400,128]{1,0:T(8,128)S(1)} %collective-permute-done.4.refs_0_, ...), custom_call_target="tpu_custom_call" | custom-call | flops 1 | bytes 1 | tf_op jit(solution)/shard_map/pallas_call | solution.py:841
  12.9 0.3 %collective-permute-done.6.refs_1_ = f32[120,128]{1,0:T(8,128)S(1)} collective-permute-done((f32[120,128]{1,0:T(8,128)S(1)}, f32[120,128]{1,0:T(8,128)S(1)}, u32[]{:S(2)}, u32[]{:S(2)}) %collective-permute-start.6) | collective-permute-done | bytes 61472 | tf_op jit(solution)/shard_map/ppermute | solution.py:879
  13.2 0.0 collective-permute-done.5.refs_0_
  13.2 0.0 collective-permute-done.7.refs_2_
  13.2 0.0 copy-done.1
  13.2 0.0 copy-done.2
  13.2 0.0 copy-done.8
  13.2 0.0 copy-done.9
  13.3 0.0 copy-start.3
  13.3 0.0 copy-start.10
  13.3 0.0 copy-start.12
  13.3 0.0 copy-start.13
  13.3 1.8 %shard_map.197 = (f32[16,56,128]{2,1,0:T(8,128)S(1)}, f32[16,56,128]{2,1,0:T(8,128)S(1)}, f32[16,56,128]{2,1,0:T(8,128)S(1)}, f32[16,56,128]{2,1,0:T(8,128)S(1)}...) custom-call(f32[2,8,32,128]{3,2,1,0:T(8,128)S(1)} %collective-permut, ...), custom_call_target="tpu_custom_call", output_to_operand_aliasing={{0}: (4, {}), {1}: (5, {}), {2}: (6, {}), {3}: (7, {}), {4}... | custom-call | flops 1 | bytes 1 | tf_op jit(solution)/shard_map/pallas_call | solution.py:841
  15.1 0.0 collective-permute-done.2.refs_1_
  15.1 0.0 collective-permute-done.1.refs_0_
  15.1 0.4 %collective-permute-start.8 = (f32[184,128]{1,0:T(8,128)S(1)}, f32[184,128]{1,0:T(8,128)S(1)}, u32[]{:S(2)}, u32[]{:S(2)}) collective-permute-start(f32[184,128]{1,0:T(8,128)S(1)} %collective-permute-done.1.refs_0_), channel_id=1, source_target_pairs={{0,2},{2,0},{4,6},{6,4},{8,10},{10,8},{12,14},{14,12},{16,18},{18,... | collective-permute-start | bytes 282632 | tf_op jit(solution)/shard_map/ppermute | solution.py:879
  15.5 0.1 collective-permute-start.9
  15.7 0.0 copy-done.3
  15.7 0.0 copy-done.10
  15.7 0.0 copy-done.12
  15.7 0.0 copy-done.13
  15.7 0.0 copy-start.5
  15.7 0.0 copy-start.11
  15.7 0.0 copy-start.16
  15.7 0.7 %shard_map.198 = (f32[2,27,8,128]{3,2,1,0:T(8,128)S(1)}, f32[4,8,128]{2,1,0:T(8,128)S(1)}) custom-call(f32[16,56,128]{2,1,0:T(8,128)S(1)} %get-tuple-element.44.w_ref.refs_4_, f32[16,56,128]{2,1,0:T(8,128)S(1)} %get-tuple-element.48.rhs_ref, f32[24,168]{1,0:T(8,128)S(1)} %copy-done.13, f32[384,384]{1,0:T(8,128)S(1)} %copy-done.3, f32[8,168]{1,0:T(8,128)S(1)} %copy-done.12, ...), custom_call_target="tpu_custom_call" | custom-call | flops 1 | bytes 1 | tf_op jit(solution)/shard_map/pallas_call | solution.py:841
  16.5 0.3 %collective-permute-done.9.refs_3_ = f32[152,128]{1,0:T(8,128)S(1)} collective-permute-done((f32[152,128]{1,0:T(8,128)S(1)}, f32[152,128]{1,0:T(8,128)S(1)}, u32[]{:S(2)}, u32[]{:S(2)}) %collective-permute-start.9) | collective-permute-done | bytes 77856 | tf_op jit(solution)/shard_map/ppermute | solution.py:879
  16.8 0.0 collective-permute-done.8.refs_2_
  16.8 0.0 copy-done.5
  16.8 0.0 copy-done.11
  16.8 0.0 copy-done.16
  16.8 0.0 copy-start.4
  16.8 0.0 copy-start.14
  16.9 1.5 %shard_map.199 = (f32[8,32,128]{2,1,0:T(8,128)S(1)}, f32[3,8,128]{2,1,0:T(8,128)S(1)}, f32[10,8,128]{2,1,0:T(8,128)S(1)}) custom-call(f32[184,128]{1,0:T(8,128)S(1)} %collective-permute-done.1.refs_0_, f32[152,128]{1,0:T(8,128)S(1)} %collective-permute-done.2.refs_1_, f32[184,128]{1,0:T(8,128)S(1)} %collective-permute-done.8.refs_2_, ...), custom_call_target="tpu_custom_call" | custom-call | flops 1 | bytes 1 | tf_op jit(solution)/shard_map/pallas_call | solution.py:841
  18.4 0.2 %collective-permute-start.10 = (f32[3,8,128]{2,1,0:T(8,128)S(1)}, f32[3,8,128]{2,1,0:T(8,128)S(1)}, u32[]{:S(2)}, u32[]{:S(2)}) collective-permute-start(f32[3,8,128]{2,1,0:T(8,128)S(1)} %get-tuple-element.51), channel_id=1, source_target_pairs={{2,4},{3,5},{4,2},{5,3},{6,8},{7,9},{8,6},{9,7},{10,12},{11,13},{1... | collective-permute-start | bytes 36872 | tf_op jit(solution)/shard_map/ppermute | solution.py:880
  18.6 2.6 %collective-permute-done.10.refs_0_ = f32[3,8,128]{2,1,0:T(8,128)S(1)} collective-permute-done((f32[3,8,128]{2,1,0:T(8,128)S(1)}, f32[3,8,128]{2,1,0:T(8,128)S(1)}, u32[]{:S(2)}, u32[]{:S(2)}) %collective-permute-start.10) | collective-permute-done | bytes 12320 | tf_op jit(solution)/shard_map/ppermute | solution.py:880
  21.2 0.5 %collective-permute-start.11 = (f32[3,8,128]{2,1,0:T(8,128)S(1)}, f32[3,8,128]{2,1,0:T(8,128)S(1)}, u32[]{:S(2)}, u32[]{:S(2)}) collective-permute-start(f32[3,8,128]{2,1,0:T(8,128)S(1)} %collective-permute-done.10.refs_0_), channel_id=1, source_target_pairs={{0,2},{2,0},{4,6},{6,4},{8,10},{10,8},{12,14},{14,12},{16,18},{18,... | collective-permute-start | bytes 36872 | tf_op jit(solution)/shard_map/ppermute | solution.py:879
  21.7 0.8 %collective-permute-done.11.refs_1_ = f32[3,8,128]{2,1,0:T(8,128)S(1)} collective-permute-done((f32[3,8,128]{2,1,0:T(8,128)S(1)}, f32[3,8,128]{2,1,0:T(8,128)S(1)}, u32[]{:S(2)}, u32[]{:S(2)}) %collective-permute-start.11) | collective-permute-done | bytes 12320 | tf_op jit(solution)/shard_map/ppermute | solution.py:879
  22.6 0.0 copy-done.4
  22.6 0.0 copy-done.14
  22.6 1.2 %shard_map.200 = (f32[8,32,128]{2,1,0:T(8,128)}, f32[2,8,32]{2,1,0:T(8,128)}) custom-call(f32[3,8,128]{2,1,0:T(8,128)S(1)} %collective-permute-done.10.refs_0_, f32[3,8,128]{2,1,0:T(8,128)S(1)} %collective-permute-done.11.refs_1_, f32[8,32,128]{2,1,0:T(8,128)S(1)} %get-tuple-element.52.refs_2_, f32[10,8,128]{2,1,0:T(8,128)S(1)} %get-tuple-element.53.refs_3_, ...), custom_call_target="tpu_custom_call" | custom-call | flops 1 | bytes 1 | tf_op jit(solution)/shard_map/pallas_call | solution.py:841
  (5 shorter events, 0.0 us)
Async XLA Ops:
  0.6 1.8 %copy-start = (f32[384,128]{1,0:T(8,128)S(1)}, f32[384,128]{1,0:T(8,128)}, u32[]{:S(2)}) copy-start(f32[384,128]{1,0:T(8,128)} %constant.36.clone.z_sq.refs_1_.refs_8_) | copy-start | bytes 589828
  0.6 1.8 %copy-start.6 = (f32[8,8,128]{2,1,0:T(8,128)S(1)}, f32[8,8,128]{2,1,0:T(8,128)}, u32[]{:S(2)}) copy-start(f32[8,8,128]{2,1,0:T(8,128)} %constant.50.clone.w3.refs_3_.refs_14_) | copy-start | bytes 98308
  0.7 1.8 %copy-start.15 = (f32[32,96]{1,0:T(8,128)S(1)}, f32[32,96]{1,0:T(8,128)}, u32[]{:S(2)}) copy-start(f32[32,96]{1,0:T(8,128)} %constant.40.clone.y_sq) | copy-start | bytes 36868
  1.7 10.1 %collective-permute-start.3 = (f32[2,8,32,128]{3,2,1,0:T(8,128)S(1)}, f32[2,8,32,128]{3,2,1,0:T(8,128)S(1)}, u32[]{:S(2)}, u32[]{:S(2)}) collective-permute-start(f32[2,8,32,128]{3,2,1,0:T(8,128)S(1)} %pad_maximum_fusion.raw.own), channel_id=1, source_target_pairs={{0,2},{2,0},{4,6},{6,4},{8,10},{10,8},{12,14},{14,12},{16,18},{18,... | collective-permute-start | bytes 786440 | tf_op jit(solution)/shard_map/ppermute | solution.py:879
  2.8 7.6 %collective-permute-start.4 = (f32[400,128]{1,0:T(8,128)S(1)}, f32[400,128]{1,0:T(8,128)S(1)}, u32[]{:S(2)}, u32[]{:S(2)}) collective-permute-start(f32[400,128]{1,0:T(8,128)S(1)} %get-tuple-element.35), channel_id=1, source_target_pairs={{0,1},{1,0},{2,3},{3,2},{4,5},{5,4},{6,7},{7,6},{8,9},{9,8},{10,11... | collective-permute-start | bytes 614408 | tf_op jit(solution)/shard_map/ppermute | solution.py:898
  3.1 1.2 %collective-permute-start = (f32[2,32,128]{2,1,0:T(8,128)S(1)}, f32[2,32,128]{2,1,0:T(8,128)S(1)}, u32[]{:S(2)}, u32[]{:S(2)}) collective-permute-start(f32[2,32,128]{2,1,0:T(8,128)S(1)} %get-tuple-element.32), channel_id=1, source_target_pairs={{0,2},{2,0},{4,6},{6,4},{8,10},{10,8},{12,14},{14,12},{16,18},{18,... | collective-permute-start | bytes 98312 | tf_op jit(solution)/shard_map/ppermute | solution.py:879
  4.5 10.6 %collective-permute-start.1 = (f32[184,128]{1,0:T(8,128)S(1)}, f32[184,128]{1,0:T(8,128)S(1)}, u32[]{:S(2)}, u32[]{:S(2)}) collective-permute-start(f32[184,128]{1,0:T(8,128)S(1)} %get-tuple-element.33), channel_id=1, source_target_pairs={{2,4},{3,5},{4,2},{5,3},{6,8},{7,9},{8,6},{9,7},{10,12},{11,13},{1... | collective-permute-start | bytes 282632 | tf_op jit(solution)/shard_map/ppermute | solution.py:880
  5.7 9.4 %collective-permute-start.2 = (f32[152,128]{1,0:T(8,128)S(1)}, f32[152,128]{1,0:T(8,128)S(1)}, u32[]{:S(2)}, u32[]{:S(2)}) collective-permute-start(f32[152,128]{1,0:T(8,128)S(1)} %get-tuple-element.34), channel_id=1, source_target_pairs={{2,5},{3,4},{4,3},{5,2},{6,9},{7,8},{8,7},{9,6},{10,13},{11,12},{1... | collective-permute-start | bytes 233480 | tf_op jit(solution)/shard_map/ppermute | solution.py:880
  10.4 2.9 %collective-permute-start.7 = (f32[144,128]{1,0:T(8,128)S(1)}, f32[144,128]{1,0:T(8,128)S(1)}, u32[]{:S(2)}, u32[]{:S(2)}) collective-permute-start(f32[144,128]{1,0:T(8,128)S(1)} %slice.14), channel_id=1, source_target_pairs={{0,2},{2,0},{4,6},{6,4},{8,10},{10,8},{12,14},{14,12},{16,18},{18,... | collective-permute-start | bytes 221192 | tf_op jit(solution)/shard_map/ppermute | solution.py:879
  11.6 0.8 %copy-start.7 = (f32[56,168]{1,0:T(8,128)S(1)}, f32[56,168]{1,0:T(8,128)}, u32[]{:S(2)}) copy-start(f32[56,168]{1,0:T(8,128)} %constant.39.clone.refs_2_.refs_9_) | copy-start | bytes 112900
  11.6 1.6 %collective-permute-start.5 = (f32[136,128]{1,0:T(8,128)S(1)}, f32[136,128]{1,0:T(8,128)S(1)}, u32[]{:S(2)}, u32[]{:S(2)}) collective-permute-start(f32[136,128]{1,0:T(8,128)S(1)} %slice.12), channel_id=1, source_target_pairs={{0,2},{2,0},{4,6},{6,4},{8,10},{10,8},{12,14},{14,12},{16,18},{18,... | collective-permute-start | bytes 208904 | tf_op jit(solution)/shard_map/ppermute | solution.py:879
  11.7 1.5 %copy-start.1 = (f32[384,128]{1,0:T(8,128)S(1)}, f32[384,128]{1,0:T(8,128)}, u32[]{:S(2)}) copy-start(f32[384,128]{1,0:T(8,128)} %constant.35.clone.refs_11_) | copy-start | bytes 589828
  11.7 1.5 %copy-start.2 = (f32[384,128]{1,0:T(8,128)S(1)}, f32[384,128]{1,0:T(8,128)}, u32[]{:S(2)}) copy-start(f32[384,128]{1,0:T(8,128)} %constant.34.clone.refs_10_) | copy-start | bytes 589828
  11.7 1.5 %copy-start.8 = (f32[56,168]{1,0:T(8,128)S(1)}, f32[56,168]{1,0:T(8,128)}, u32[]{:S(2)}) copy-start(f32[56,168]{1,0:T(8,128)} %constant.38.clone.refs_13_) | copy-start | bytes 112900
  11.8 1.5 %copy-start.9 = (f32[56,168]{1,0:T(8,128)S(1)}, f32[56,168]{1,0:T(8,128)}, u32[]{:S(2)}) copy-start(f32[56,168]{1,0:T(8,128)} %constant.37.clone.refs_12_) | copy-start | bytes 112900
  11.8 1.4 %collective-permute-start.6 = (f32[120,128]{1,0:T(8,128)S(1)}, f32[120,128]{1,0:T(8,128)S(1)}, u32[]{:S(2)}, u32[]{:S(2)}) collective-permute-start(f32[120,128]{1,0:T(8,128)S(1)} %slice.13), channel_id=1, source_target_pairs={{0,2},{2,0},{4,6},{6,4},{8,10},{10,8},{12,14},{14,12},{16,18},{18,... | collective-permute-start | bytes 184328 | tf_op jit(solution)/shard_map/ppermute | solution.py:879
  13.3 2.4 %copy-start.3 = (f32[384,384]{1,0:T(8,128)S(1)}, f32[384,384]{1,0:T(8,128)}, u32[]{:S(2)}) copy-start(f32[384,384]{1,0:T(8,128)} %constant.46.clone.mz) | copy-start | bytes 1769476
  13.3 2.4 %copy-start.10 = (f32[384,128]{1,0:T(8,128)S(1)}, f32[384,128]{1,0:T(8,128)}, u32[]{:S(2)}) copy-start(f32[384,128]{1,0:T(8,128)} %constant.44.clone.rz) | copy-start | bytes 589828
  13.3 2.4 %copy-start.12 = (f32[8,168]{1,0:T(8,128)S(1)}, f32[8,168]{1,0:T(8,128)}, u32[]{:S(2)}) copy-start(f32[8,168]{1,0:T(8,128)} %constant.42.clone.ry.refs_15_) | copy-start | bytes 16132
  13.3 2.4 %copy-start.13 = (f32[24,168]{1,0:T(8,128)S(1)}, f32[24,168]{1,0:T(8,128)}, u32[]{:S(2)}) copy-start(f32[24,168]{1,0:T(8,128)} %constant.45.clone.my) | copy-start | bytes 48388
  15.1 1.7 %collective-permute-start.8 = (f32[184,128]{1,0:T(8,128)S(1)}, f32[184,128]{1,0:T(8,128)S(1)}, u32[]{:S(2)}, u32[]{:S(2)}) collective-permute-start(f32[184,128]{1,0:T(8,128)S(1)} %collective-permute-done.1.refs_0_), channel_id=1, source_target_pairs={{0,2},{2,0},{4,6},{6,4},{8,10},{10,8},{12,14},{14,12},{16,18},{18,... | collective-permute-start | bytes 282632 | tf_op jit(solution)/shard_map/ppermute | solution.py:879
  15.5 1.3 %collective-permute-start.9 = (f32[152,128]{1,0:T(8,128)S(1)}, f32[152,128]{1,0:T(8,128)S(1)}, u32[]{:S(2)}, u32[]{:S(2)}) collective-permute-start(f32[152,128]{1,0:T(8,128)S(1)} %collective-permute-done.2.refs_1_), channel_id=1, source_target_pairs={{0,2},{2,0},{4,6},{6,4},{8,10},{10,8},{12,14},{14,12},{16,18},{18,... | collective-permute-start | bytes 233480 | tf_op jit(solution)/shard_map/ppermute | solution.py:879
  15.7 1.1 %copy-start.5 = (f32[768,128]{1,0:T(8,128)S(1)}, f32[768,128]{1,0:T(8,128)}, u32[]{:S(2)}) copy-start(f32[768,128]{1,0:T(8,128)} %constant.43.clone.refs_16_) | copy-start | bytes 1179652
  15.7 1.1 %copy-start.11 = (f32[10,8,128]{2,1,0:T(8,128)S(1)}, f32[10,8,128]{2,1,0:T(8,128)}, u32[]{:S(2)}) copy-start(f32[10,8,128]{2,1,0:T(8,128)} %constant.49.clone.refs_17_) | copy-start | bytes 122884
  15.7 1.1 %copy-start.16 = (f32[8,336]{1,0:T(8,128)S(1)}, f32[8,336]{1,0:T(8,128)}, u32[]{:S(2)}) copy-start(f32[8,336]{1,0:T(8,128)} %constant.41.clone.refs_14_) | copy-start | bytes 32260
  16.8 5.7 %copy-start.4 = (f32[384,160]{1,0:T(8,128)S(1)}, f32[384,160]{1,0:T(8,128)}, u32[]{:S(2)}) copy-start(f32[384,160]{1,0:T(8,128)} %constant.48.clone.refs_6_) | copy-start | bytes 737284
  16.8 5.7 %copy-start.14 = (f32[40,24]{1,0:T(8,128)S(1)}, f32[40,24]{1,0:T(8,128)}, u32[]{:S(2)}) copy-start(f32[40,24]{1,0:T(8,128)} %constant.47.clone.refs_5_) | copy-start | bytes 11524
  18.4 2.9 %collective-permute-start.10 = (f32[3,8,128]{2,1,0:T(8,128)S(1)}, f32[3,8,128]{2,1,0:T(8,128)S(1)}, u32[]{:S(2)}, u32[]{:S(2)}) collective-permute-start(f32[3,8,128]{2,1,0:T(8,128)S(1)} %get-tuple-element.51), channel_id=1, source_target_pairs={{2,4},{3,5},{4,2},{5,3},{6,8},{7,9},{8,6},{9,7},{10,12},{11,13},{1... | collective-permute-start | bytes 36872 | tf_op jit(solution)/shard_map/ppermute | solution.py:880
  21.2 1.3 %collective-permute-start.11 = (f32[3,8,128]{2,1,0:T(8,128)S(1)}, f32[3,8,128]{2,1,0:T(8,128)S(1)}, u32[]{:S(2)}, u32[]{:S(2)}) collective-permute-start(f32[3,8,128]{2,1,0:T(8,128)S(1)} %collective-permute-done.10.refs_0_), channel_id=1, source_target_pairs={{0,2},{2,0},{4,6},{6,4},{8,10},{10,8},{12,14},{14,12},{16,18},{18,... | collective-permute-start | bytes 36872 | tf_op jit(solution)/shard_map/ppermute | solution.py:879

commit v5 on v4

--- a/solution.py
+++ b/solution.py
@@ -78,7 +78,8 @@
 
 def right_table(matrix):
     hi, lo = hi_lo(matrix)
-    return np.concatenate([hi, hi, lo], axis=0).astype(np.float32)
+    top = np.concatenate([hi, lo], axis=1)
+    return np.concatenate([top, np.concatenate([hi, 0 * lo], axis=1)], axis=0).astype(np.float32)
 
 
 def left_table(matrix):
@@ -118,13 +119,17 @@
     t["z_sq"] = right_table(blockdiag(DM * DM, ez))
     t["y_d"] = left_table(blockdiag(DM, ey))
     t["y_dt"] = left_table(blockdiag(DM, ey).T)
-    t["y_sq"] = left_table(blockdiag(DM * DM, ey).T)
-    t["y_sq_own"] = left_table(blockdiag(DM * DM, own_y // N).T)
+    for count in range(1, own_y // N + 1):
+        t["y_sq", count] = left_table(blockdiag(DM * DM, count).T)
+        t["y_d", count] = left_table(blockdiag(DM, count))
+        t["y_dt", count] = left_table(blockdiag(DM, count).T)
     py = vertex_table(RHO, ey, cr)
     dpy = blockdiag(DM, ey) @ py
     pz = vertex_table(RHO, ez, nz)
     dpz = blockdiag(DM, ez) @ pz
-    t["ry"] = left_table(np.concatenate([py, dpy], axis=0).T)
+    zero = np.zeros_like(py)
+    ry = np.concatenate([np.concatenate([py, dpy, zero]), np.concatenate([zero, zero, py])], axis=1)
+    t["ry"] = np.concatenate(hi_lo(ry.T), axis=0).astype(np.float32)
     t["ry_one"] = left_table(py.T)
     t["rz"] = right_table(np.concatenate([pz, dpz], axis=0))
     t["rz_one"] = right_table(pz)
@@ -172,7 +177,9 @@
 
 
 def z_apply(hi, lo, table):
-    return dot(jnp.concatenate([hi, lo, hi], axis=1), table.astype(BF16))
+    both = dot(jnp.concatenate([hi, lo], axis=1), table.astype(BF16))
+    half = both.shape[1] // 2
+    return both[:, :half] + both[:, half:]
 
 
 def y_apply(x, table):
@@ -266,6 +273,27 @@
         if self.sub == 2:
             return [(1 - h) * (self.ny - 1)]
         return [0, self.ny - 1]
+
+    def other_starts(self, h):
+        if self.sub == 1:
+            return []
+        if self.sub == 2:
+            return [(1 - h) * self.own_y]
+        return [0, HALO + self.own_y]
+
+    def early_rows(self, h):
+        if self.sub == 1:
+            return 0, self.own_y
+        if self.sub == 2:
+            return h * (HALO + N), self.own_y - N
+        return HALO + N, self.own_y - 2 * N
+
+    def late_starts(self, h):
+        if self.sub == 1:
+            return []
+        if self.sub == 2:
+            return [(1 - h) * (self.own_y - N)]
+        return [0, self.own_y + HALO - N]
 
     def interfaces(self, h):
         if self.sub == 1:
@@ -400,40 +428,81 @@
         out[pl.ds(5 * HALO + lines, SPARE), :] = jnp.zeros((SPARE, nz), F32)
 
 
-def gradient_flux(lay, u_ref, w_ref, planes, z_d, y_d, fx, fy, fz):
-    ny, nz = lay.ny, lay.nz
+def flux_x(lay, u_ref, w_ref, first, count, fx):
     for el in range(2):
-        for e in range(lay.ey):
-            rows = pl.ds(N * e, N)
+        for e in range(count // N):
+            rows, to = aligned(first + N * e, N), pl.ds(N * e, N)
             u = [u_ref[N * el + a, rows, :] for a in range(N)]
             g = even_odd(DM, u, -1)
             for a in range(N):
-                fx[N * el + a, rows, :] = w_ref[N * el + a, rows, :] * g[a]
-    first, count = planes[0], len(planes)
-    hi, lo = split(u_ref[pl.ds(first, count)].reshape(count * ny, nz))
-    gz = z_apply(hi, lo, z_d[...])
-    gy = y_planes(lambda p: u_ref[p], planes, y_d[...])
-    for p in planes:
-        w = w_ref[p]
-        fy[p] = w * gy[p]
-        fz[p] = w * gz[(p - first) * ny : (p - first + 1) * ny]
-
-
-def element_sums(lay, base, parity, h, block, pieces, tables, outs):
+                fx[N * el + a, to, :] = w_ref[N * el + a, rows, :] * g[a]
+
+
+def flux_yz(lay, u_ref, w_ref, planes, first, count, z_d, y_d, fy, fz):
+    part, to = aligned(first, count), pl.ds(0, count)
+    u = jnp.concatenate([u_ref[p, part, :] for p in planes], axis=0)
+    gz = z_apply(*split(u), z_d[...])
+    gy = y_planes(lambda p: u_ref[p, part, :], planes, y_d[...])
+    for k, p in enumerate(planes):
+        w = w_ref[p, part, :]
+        fy[p, to, :] = w * gy[p]
+        fz[p, to, :] = w * gz[k * count : (k + 1) * count]
+
+
+def operate(lay, u_ref, w_ref, back, first, count, tables, fx, fy, fz):
+    z_d, z_dt, y_d, y_dt = tables
+    nz = lay.nz
+    middle = list(range(1, 2 * N - 1))
+    flux_x(lay, u_ref, w_ref, first, count, fx)
+    flux_yz(lay, u_ref, w_ref, middle, first, count, z_d, y_d, fy, fz)
+    to, part = pl.ds(0, count), aligned(first, count)
+    for el in range(2):
+        for e in range(count // N):
+            rows, here = aligned(first + N * e, N), pl.ds(N * e, N)
+            b = even_odd(DM.T, [fx[N * el + a, here, :] for a in range(N)], -1)
+            for a in range(N):
+                back[N * el + a, rows, :] = b[a]
+    n = len(middle)
+    bz = z_apply(*split(fz[pl.ds(1, n), to, :].reshape(n * count, nz)), z_dt[...])
+    by = y_planes(lambda p: fy[p, to, :], middle, y_dt[...])
+    for p in middle:
+        back[p, part, :] = back[p, part, :] + by[p] + bz[(p - 1) * count : p * count]
+
+
+def smooth_start(lay, d, r, inv, u, first, count, start):
+    part = aligned(first, count)
+    mask = yz_mask(count, lay.nz, start + first, lay.total_y)
+    inside = mask.astype(F32)
+    zero = jnp.zeros((count, lay.nz), F32)
+    for p in range(2 * N):
+        if p in (0, 2 * N - 1):
+            u[p, part, :] = zero
+        else:
+            i = inside / jnp.where(mask, d[p, part, :], 1.0)
+            inv[p, part, :] = i
+            u[p, part, :] = i * r[p, part, :] * (1.0 / THETA)
+
+
+def sum_middle(fields, first, count):
+    part = aligned(first, count)
+    for s in fields:
+        both = s[N - 1, part, :] + s[N, part, :]
+        s[N - 1, part, :] = both
+        s[N, part, :] = both
+
+
+def element_sums(lay, base, parity, first, count, source, tables, outs):
     z_sq, y_sq, w3 = tables
-    w_out, rhs_out, d_s, r_s, lin = outs
-    ny, nz = lay.ny, lay.nz
+    w_out, rhs_out, d_s, r_s, lin = outs[:5]
+    nz = lay.nz
+    part = aligned(first, count)
     for side, target in ((0, rhs_out), (1, w_out)):
         for a in range(N):
-
-            def put(rows, value):
-                target[base + a, rows, :] = value
-
-            gather_window(lay, block[side, a], [o[pack_rows(side, a)] for o in pieces], h, put)
+            target[base + a, part, :] = source(side, a)
     table3 = w3[...]
     outer = [jnp.where(parity == 0, float(DM[a, 0]), float(DM[a, N - 1])) for a in range(N)]
-    for e in range(lay.ey):
-        rows = pl.ds(N * e, N)
+    for e in range(count // N):
+        rows = aligned(first + N * e, N)
         w = [w_out[base + a, rows, :] * table3[a] for a in range(N)]
         dx = even_odd((DM * DM).T, w, 1)
         cx = even_odd(DM.T, [outer[a] * w[a] for a in range(N)], -1)
@@ -441,80 +510,87 @@
             w_out[base + a, rows, :] = w[a]
             d_s[base + a, rows, :] = dx[a]
             lin[base + a, rows, :] = cx[a]
-    dz = z_apply(*split(w_out[pl.ds(base, N)].reshape(N * ny, nz)), z_sq[...])
-    dy = y_planes(lambda a: w_out[base + a], list(range(N)), y_sq[...])
+    dz = z_apply(*split(w_out[pl.ds(base, N), part, :].reshape(N * count, nz)), z_sq[...])
+    dy = y_planes(lambda a: w_out[base + a, part, :], list(range(N)), y_sq[...])
     for a in range(N):
-        d_s[base + a] = assemble_yz(d_s[base + a] + dz[a * ny : (a + 1) * ny] + dy[a])
-        r_s[base + a] = assemble_yz(rhs_out[base + a])
-        lin[base + a] = assemble_yz(lin[base + a])
-    for piece, row in zip(pieces, lay.far_rows(h)):
+        d_local = d_s[base + a, part, :] + dz[a * count : (a + 1) * count] + dy[a]
+        d_s[base + a, part, :] = assemble_yz(d_local)
+        r_s[base + a, part, :] = assemble_yz(rhs_out[base + a, part, :])
+        lin[base + a, part, :] = assemble_yz(lin[base + a, part, :])
+
+
+def other_sums(lay, base, parity, h, pieces, tables, outs):
+    d_s, r_s = outs[2:4]
+    for piece, first, row in zip(pieces, lay.other_starts(h), lay.far_rows(h)):
+        source = lambda side, a, piece=piece: piece[pack_rows(side, a)]
+        element_sums(lay, base, parity, first, HALO, source, tables, outs)
         for side, target in ((0, r_s), (1, d_s)):
             for a in range(N):
                 target[base + a, pl.ds(row, 1), :] = piece[pl.ds(side * N + a, 1)]
 
 
-def near_kernel(lay, own, *refs):
-    n_other = len(refs) - 8
-    other, tables, outs = refs[:n_other], refs[n_other : n_other + 3], refs[n_other + 3 :]
+ARRAYS = 8
+
+
+def early_kernel(lay, own, mate, *refs):
+    z_sq, y_sq, w3 = refs[:3]
+    tables, outs, scratch = refs[3:7], refs[7 : 7 + ARRAYS], refs[7 + ARRAYS :]
+    w, _, d, r, _, inv, u, back = outs
+    parity, h, start, offset, low, high = lay.where()
+    for base, el, block in ((parity * N, parity, own), ((1 - parity) * N, 1 - parity, mate)):
+        source = lambda side, a, block=block: block[side, a]
+        element_sums(lay, base, el, offset, lay.own_y, source, (z_sq, y_sq, w3), outs)
+    sum_middle((d, r), offset, lay.own_y)
+    smooth_start(lay, d, r, inv, u, offset, lay.own_y, start)
+    first, count = lay.early_rows(h)
+    operate(lay, u, w, back, first, count, tables, *scratch)
+
+
+def near_kernel(lay, n_other, *refs):
+    other, tables = refs[:n_other], refs[n_other : n_other + 3]
+    outs = refs[n_other + 3 + ARRAYS :]
     parity, h = lay.where()[:2]
-    pieces = [Pieces([o]) for o in other]
-    element_sums(lay, parity * N, parity, h, own, pieces, tables, outs)
-
-
-def deep_kernel(lay, n_other, mate, *refs):
+    other_sums(lay, parity * N, parity, h, [Pieces([o]) for o in other], tables, outs)
+
+
+def deep_kernel(lay, n_other, *refs):
     cuts = len(CUTS) - 1
     mate_other = [Pieces(refs[cuts * k : cuts * (k + 1)]) for k in range(n_other)]
-    refs = refs[cuts * n_other + 5 :]
-    z_sq, y_sq, z_d, z_dt, y_d, y_dt, w3 = refs[:7]
-    w_out, rhs_out, d_s, r_s, lin_out, sec_out, ends = refs[7:14]
-    u_s, inv_s, fx, fy, fz, back = refs[14:]
-    ny, nz = lay.ny, lay.nz
+    refs = refs[cuts * n_other :]
+    z_sq, y_sq, w3 = refs[:3]
+    tables = refs[3:7]
+    refs = refs[7 + ARRAYS :]
+    outs, sec_out, ends = refs[:ARRAYS], refs[ARRAYS], refs[ARRAYS + 1]
+    scratch = refs[ARRAYS + 2 :]
+    w, _, d, r, lin, inv, u, back = outs
     last = 2 * N - 1
     parity, h, start, offset, low, high = lay.where()
-    element_sums(
-        lay, (1 - parity) * N, 1 - parity, h, mate, mate_other, (z_sq, y_sq, w3),
-        (w_out, rhs_out, d_s, r_s, lin_out),
-    )
-    for s in (d_s, r_s):
-        both = s[N - 1] + s[N]
-        s[N - 1] = both
-        s[N] = both
-    mask = yz_mask(ny, nz, start, lay.total_y)
-    inside = mask.astype(F32)
-    ends[0, 0] = r_s[0]
-    ends[0, 1] = d_s[0]
-    ends[1, 0] = r_s[last]
-    ends[1, 1] = d_s[last]
-    zero = jnp.zeros((ny, nz), F32)
-    u_s[0] = zero
-    u_s[last] = zero
+    other_sums(lay, (1 - parity) * N, 1 - parity, h, mate_other, (z_sq, y_sq, w3), outs)
+    for first in lay.other_starts(h):
+        sum_middle((d, r), first, HALO)
+    for begin in lay.interfaces(h):
+        above, below = pl.ds(begin - 1, 1), pl.ds(begin, 1)
+        for s in (d, r, lin):
+            for p in range(2 * N):
+                both = s[p, above, :] + s[p, below, :]
+                s[p, above, :] = both
+                s[p, below, :] = both
+    for side, p in ((0, 0), (1, last)):
+        ends[side, 0] = r[p]
+        ends[side, 1] = d[p]
+    for first in lay.late_starts(h):
+        smooth_start(lay, d, r, inv, u, first, HALO + N, start)
+        operate(lay, u, w, back, first, HALO + N, tables, *scratch)
     for p in range(1, last):
-        inv = inside / jnp.where(mask, d_s[p], 1.0)
-        inv_s[p] = inv
-        u_s[p] = inv * r_s[p] * (1.0 / THETA)
-    middle = list(range(1, last))
-    gradient_flux(lay, u_s, w_out, middle, z_d, y_d, fx, fy, fz)
-    for el in range(2):
-        for e in range(lay.ey):
-            rows = pl.ds(N * e, N)
-            b = even_odd(DM.T, [fx[N * el + a, rows, :] for a in range(N)], -1)
-            for a in range(N):
-                back[N * el + a, rows, :] = b[a]
-    hi, lo = split(fz[pl.ds(1, last - 1)].reshape((last - 1) * ny, nz))
-    bz = z_apply(hi, lo, z_dt[...])
-    by = y_planes(lambda p: fy[p], middle, y_dt[...])
-    for p in middle:
-        back[p] = assemble_yz(back[p] + by[p] + bz[(p - 1) * ny : p * ny])
-    both = back[N - 1] + back[N]
-    back[N - 1] = both
-    back[N] = both
+        back[p] = assemble_yz(back[p])
+    sum_middle((back,), 0, lay.ny)
     for p in range(2 * N):
         if p in (0, last):
             sec_out[p] = assemble_yz(back[p])
         else:
-            inv = (2.0 * RHO1 / DELTA) * inv_s[p]
-            lin_out[p] = -inv * lin_out[p]
-            sec_out[p] = (1.0 + RHO1 * RHO0) * u_s[p] + inv * (r_s[p] - back[p])
+            i = (2.0 * RHO1 / DELTA) * inv[p]
+            lin[p] = -i * lin[p]
+            sec_out[p] = (1.0 + RHO1 * RHO0) * u[p] + i * (r[p] - back[p])
 
 
 def coarse_tables_kernel(lay, w_ref, rhs_ref, my, mz, ry, rz, g_out, r_out):
@@ -697,6 +773,7 @@
         if p >= N - 1:
             value = value + lin_in[max(p, N)] * u[1]
         sec[p] = value
+    flux_yz(lay, sec, w_ref, list(range(1, last)), 0, ny, z_d, y_d, fy, fz)
     weights = [w_ref[0] + win[0, 3], w_ref[last] + win[1, 3]]
     hi, lo = split(jnp.concatenate(u, axis=0))
     gz = z_apply(hi, lo, z_d[...])
@@ -711,7 +788,8 @@
         res_one = res[side] - inside * plane
         sec[p] = (1.0 + RHO1 * RHO0) * u[side] + (2.0 * RHO1 / DELTA) * inv[side] * res_one
     out[...] = sec[pl.ds(parity * N, N), pl.ds(pl.multiple_of(offset, N), lay.own_y), :]
-    gradient_flux(lay, sec, w_ref, list(range(2 * N)), z_d, y_d, fx, fy, fz)
+    flux_yz(lay, sec, w_ref, [0, last], 0, ny, z_d, y_d, fy, fz)
+    flux_x(lay, sec, w_ref, 0, ny, fx)
     sums = []
     for f, weight in ((fx, DRHO), (fy, RHO), (fz, RHO)):
         lanes = []
@@ -723,10 +801,14 @@
                     total = term if total is None else total + term
                 lanes.append(total)
         sums.append(jnp.concatenate(lanes, axis=1))
-    one = y_apply(jnp.concatenate(sums[:2], axis=0), ry[...])
-    two = y_apply(sums[2], ry_one[...])
+    data = jnp.concatenate(sums, axis=0)
+    hi = data.astype(BF16).astype(F32)
+    parts = jnp.concatenate([hi, data - hi], axis=1).astype(BF16)
+    both = dot(ry[...].astype(BF16), parts)
+    both = both[: 2 * cr, : 4 * nz] + both[2 * cr :, : 4 * nz] + both[: 2 * cr, 4 * nz :]
     rows = [
-        jnp.concatenate([v[:, k * nz : (k + 1) * nz] for v in (one, two)], axis=1) for k in range(4)
+        jnp.concatenate([v[:, k * nz : (k + 1) * nz] for v in (both[:cr], both[cr:])], axis=1)
+        for k in range(4)
     ]
     full = z_apply(*split(jnp.concatenate(rows, axis=0)), rz[...])
     r = {}
@@ -883,7 +965,7 @@
     n_other = 0 if sub == 1 else 1 if sub == 2 else 2
     face, w, d, r, sx, *packs = run(
         functools.partial(own_kernel, lay),
-        [raw] + pick("z_sq", "y_sq_own", "w3"),
+        [raw, t["z_sq"], t["y_sq", own_y // N], t["w3"]],
         [(2, own_y, nz), block, block, block, (own_y, nz)]
         + [(PACK, nz)] * n_other,
     )
@@ -906,21 +988,36 @@
     )
     shifts = [0] if sub == 1 else [0, 1] if sub == 2 else [0, 1, -1]
     pieces = [odd(msg, k) for msg, k in zip(msgs, shifts)]
+    pair = (2 * N, ny, nz)
+    count = lay.early_rows(0)[1] // N
+    arrays = run(
+        functools.partial(early_kernel, lay),
+        [raw, mate, t["z_sq"], t["y_sq", own_y // N], t["w3"]]
+        + [t["z_d"], t["z_dt"], t["y_d", count], t["y_dt", count]],
+        [pair] * ARRAYS,
+        [(2 * N, count * N, nz)] * 3,
+    )
+    others, arrays = lax.optimization_barrier((others, arrays))
     mate_others = [even(o[a:b]) for o in others for a, b in zip(CUTS, CUTS[1:])]
-    pair = (2 * N, ny, nz)
     arrays = run(
-        functools.partial(near_kernel, lay),
-        [raw, *others] + pick("z_sq", "y_sq", "w3"),
-        [pair] * 5,
+        functools.partial(near_kernel, lay, n_other),
+        [*others, t["z_sq"], t["y_sq", HALO // N], t["w3"], *arrays],
+        [pair] * ARRAYS,
+        (),
+        {n_other + 3 + k: k for k in range(ARRAYS)},
     )
-    w, rhs, _, _, lin, sec, ends = run(
+    pieces[0], arrays = lax.optimization_barrier((pieces[0], arrays))
+    late = lambda *names: [t[k, HALO // N + 1] for k in names]
+    sums = [t["z_sq"], t["y_sq", HALO // N], t["w3"]]
+    w, rhs, _, _, lin, _, _, _, sec, ends = run(
         functools.partial(deep_kernel, lay, n_other),
-        [mate, *mate_others, *arrays] + pick("z_sq", "y_sq", "z_d", "z_dt", "y_d", "y_dt", "w3"),
-        [pair] * 6 + [(2, 2, ny, nz)],
-        [pair] * 6,
-        {1 + len(mate_others) + k: k for k in range(5)},
+        [*mate_others, *sums, t["z_d"], t["z_dt"], *late("y_d", "y_dt"), *arrays],
+        [pair] * (ARRAYS + 1) + [(2, 2, ny, nz)],
+        [(2 * N, HALO + N, nz)] * 3,
+        {len(mate_others) + 7 + k: k for k in range(ARRAYS)},
     )
-    pieces, sec = lax.optimization_barrier((pieces, sec))
+    later, sec = lax.optimization_barrier((pieces[1:], sec))
+    pieces = pieces[:1] + later
     mate_pieces = [even(p) for p in pieces]
     g, r = run(
         functools.partial(coarse_tables_kernel, lay),

time: 24.2 us -> 23.3 us (0.963)
  waiting for transfers between devices: 9.33 us -> 8.2 us
    ppermute x1, waiting for transfers between devices: 4.38 us -> 3.46 us  [shards(): lax.ppermute(pack, 'sub', step)]
    pallas_call x7 -> x8, Pallas kernels: 6.23 us -> 6.46 us  [run(): pl.pallas_call(kernel, out_shape=[jax.ShapeDtypeStruct(o, F32) for o in o...]
  transfers between devices with their start and end apart: 12 -> 12, of which waited for: 6 -> 6; matrix products, arithmetic and copies ran while one was open for 0% -> 0% of each run, Pallas kernels for 15% -> 16%
where the time goes in v5:
time: 23.3 us; the launch traced here: 22.9 us
  waiting for transfers between devices  8.2 us (35%)
  Pallas kernels  6.46 us (28%)
  starting transfers between devices  5.95 us (26%)
  other arithmetic  1.02 us (4%)
  between operations  0.86 us (4%)
  local copies, waits for them, and re-layouts  0.4 us (2%)
    pallas_call x8, Pallas kernels, run(): pl.pallas_call(kernel, out_shape=[jax.ShapeDtypeStruct(o, F32) for o in o...  6.46 us
    ppermute x8, starting transfers between devices, shards(): even = lambda v: lax.ppermute(v, 'dom', swap_pairs(dom, 0))  3.91 us
    ppermute x1, waiting for transfers between devices, shards(): lax.ppermute(pack, 'sub', step)  3.46 us
    ppermute x3, waiting for transfers between devices, shards(): lax.ppermute(v, ('dom', 'sub'), chip_pairs(dom, sub, k))  2.61 us
    ppermute x8, waiting for transfers between devices, shards(): even = lambda v: lax.ppermute(v, 'dom', swap_pairs(dom, 0))  2.13 us
    ppermute x3, starting transfers between devices, shards(): lax.ppermute(v, ('dom', 'sub'), chip_pairs(dom, sub, k))  1.75 us
    another operation x1, other arithmetic, shards(): raw = jnp.stack([rhs_local, coefficient])  1.02 us
  transfers between devices with their start and end apart: 12, of which 6 were waited for; matrix products, arithmetic and copies ran while one was open for 0% of the time, Pallas kernels for 16%

profile of v5, /device:TPU:31, one launch (start us, length us, event | category | flops | bytes accessed | tf_op | source)
XLA Modules:
  0.0 22.9 jit_solution(1869059946254080683)
XLA Ops:
  0.6 0.0 copy-start
  0.6 0.0 copy-start.4
  0.7 0.0 copy-start.8
  0.7 1.0 %pad_maximum_fusion.raw.own = f32[2,8,32,128]{3,2,1,0:T(8,128)S(1)} fusion(f32[1,8,32,128]{3,2,1,0:T(8,128)} %bitcast.2, f32[1,8,32,128]{3,2,1,0:T(8,128)} %bitcast.3), kind=kLoop, calls=%fused_computation | loop fusion | flops 65536 | bytes 524288 | tf_op jit(solution)/shard_map/stack | solution.py:964
  1.7 0.7 %collective-permute-start.3 = (f32[2,8,32,128]{3,2,1,0:T(8,128)S(1)}, f32[2,8,32,128]{3,2,1,0:T(8,128)S(1)}, u32[]{:S(2)}, u32[]{:S(2)}) collective-permute-start(f32[2,8,32,128]{3,2,1,0:T(8,128)S(1)} %pad_maximum_fusion.raw.own), channel_id=1, source_target_pairs={{0,2},{2,0},{4,6},{6,4},{8,10},{10,8},{12,14},{14,12},{16,18},{18,... | collective-permute-start | bytes 786440 | tf_op jit(solution)/shard_map/ppermute | solution.py:961
  2.4 0.0 copy-done
  2.4 0.0 copy-done.4
  2.4 0.0 copy-done.8
  2.5 0.3 %shard_map.230 = (f32[2,32,128]{2,1,0:T(8,128)S(1)}, f32[8,32,128]{2,1,0:T(8,128)S(1)}, f32[8,32,128]{2,1,0:T(8,128)S(1)}, f32[8,32,128]{2,1,0:T(8,128)S(1)}, f3...) custom-call(f32[2,8,32,128]{3,2,1,0:T(8,128)S(1)} %pad_maximum_fusion.raw.own, f32[256,256]{1,0:T(8,128)S(1)} %copy-done, ...), custom_call_target="tpu_custom_call" | custom-call | flops 1 | bytes 1 | tf_op jit(solution)/shard_map/pallas_call | solution.py:923
  2.8 0.0 copy-start.1
  2.8 0.3 %collective-permute-start.2 = (f32[400,128]{1,0:T(8,128)S(1)}, f32[400,128]{1,0:T(8,128)S(1)}, u32[]{:S(2)}, u32[]{:S(2)}) collective-permute-start(f32[400,128]{1,0:T(8,128)S(1)} %get-tuple-element.62), channel_id=1, source_target_pairs={{0,1},{1,0},{2,3},{3,2},{4,5},{5,4},{6,7},{7,6},{8,9},{9,8},{10,11... | collective-permute-start | bytes 614408 | tf_op jit(solution)/shard_map/ppermute | solution.py:980
  3.1 0.3 %collective-permute-start = (f32[2,32,128]{2,1,0:T(8,128)S(1)}, f32[2,32,128]{2,1,0:T(8,128)S(1)}, u32[]{:S(2)}, u32[]{:S(2)}) collective-permute-start(f32[2,32,128]{2,1,0:T(8,128)S(1)} %get-tuple-element.60), channel_id=1, source_target_pairs={{0,2},{2,0},{4,6},{6,4},{8,10},{10,8},{12,14},{14,12},{16,18},{18,... | collective-permute-start | bytes 98312 | tf_op jit(solution)/shard_map/ppermute | solution.py:961
  3.4 0.9 %collective-permute-done.face = f32[2,32,128]{2,1,0:T(8,128)S(1)} collective-permute-done((f32[2,32,128]{2,1,0:T(8,128)S(1)}, f32[2,32,128]{2,1,0:T(8,128)S(1)}, u32[]{:S(2)}, u32[]{:S(2)}) %collective-permute-start) | collective-permute-done | bytes 32800 | tf_op jit(solution)/shard_map/ppermute | solution.py:961
  4.3 0.2 shard_map.231
  4.5 1.3 %collective-permute-start.1 = (f32[184,128]{1,0:T(8,128)S(1)}, f32[184,128]{1,0:T(8,128)S(1)}, u32[]{:S(2)}, u32[]{:S(2)}) collective-permute-start(f32[184,128]{1,0:T(8,128)S(1)} %get-tuple-element.61), channel_id=1, source_target_pairs={{2,4},{3,5},{4,2},{5,3},{6,8},{7,9},{8,6},{9,7},{10,12},{11,13},{1... | collective-permute-start | bytes 282632 | tf_op jit(solution)/shard_map/ppermute | solution.py:962
  5.8 0.2 collective-permute-start.4
  6.0 0.0 collective-permute-done.3.mate
  6.0 0.0 copy-done.2
  6.0 0.0 copy-done.1
  6.0 0.0 copy-done.19
  6.0 0.0 copy-done.20
  6.0 0.9 %shard_map.232 = (f32[16,56,128]{2,1,0:T(8,128)S(1)}, f32[16,56,128]{2,1,0:T(8,128)S(1)}, f32[16,56,128]{2,1,0:T(8,128)S(1)}, f32[16,56,128]{2,1,0:T(8,128)S(1)}...) custom-call(f32[2,8,32,128]{3,2,1,0:T(8,128)S(1)} %pad_maximum_fusio, ...), custom_call_target="tpu_custom_call" | custom-call | flops 1 | bytes 1 | tf_op jit(solution)/shard_map/pallas_call | solution.py:923
  6.9 3.5 %collective-permute-done.2.refs_0_ = f32[400,128]{1,0:T(8,128)S(1)} collective-permute-done((f32[400,128]{1,0:T(8,128)S(1)}, f32[400,128]{1,0:T(8,128)S(1)}, u32[]{:S(2)}, u32[]{:S(2)}) %collective-permute-start.2) | collective-permute-done | bytes 204832 | tf_op jit(solution)/shard_map/ppermute | solution.py:980
  10.4 1.3 %collective-permute-start.7 = (f32[144,128]{1,0:T(8,128)S(1)}, f32[144,128]{1,0:T(8,128)S(1)}, u32[]{:S(2)}, u32[]{:S(2)}) collective-permute-start(f32[144,128]{1,0:T(8,128)S(1)} %slice.11), channel_id=1, source_target_pairs={{0,2},{2,0},{4,6},{6,4},{8,10},{10,8},{12,14},{14,12},{16,18},{18,... | collective-permute-start | bytes 221192 | tf_op jit(solution)/shard_map/ppermute | solution.py:961
  11.6 0.1 collective-permute-start.5
  11.7 0.5 %collective-permute-start.6 = (f32[120,128]{1,0:T(8,128)S(1)}, f32[120,128]{1,0:T(8,128)S(1)}, u32[]{:S(2)}, u32[]{:S(2)}) collective-permute-start(f32[120,128]{1,0:T(8,128)S(1)} %slice.10), channel_id=1, source_target_pairs={{0,2},{2,0},{4,6},{6,4},{8,10},{10,8},{12,14},{14,12},{16,18},{18,... | collective-permute-start | bytes 184328 | tf_op jit(solution)/shard_map/ppermute | solution.py:961
  12.2 0.1 copy-done.11
  12.3 0.3 %shard_map.233 = (f32[16,56,128]{2,1,0:T(8,128)S(1)}, f32[16,56,128]{2,1,0:T(8,128)S(1)}, f32[16,56,128]{2,1,0:T(8,128)S(1)}, f32[16,56,128]{2,1,0:T(8,128)S(1)}...) custom-call(f32[400,128]{1,0:T(8,128)S(1)} %collective-permute-done., ...), custom_call_target="tpu_custom_call", output_to_operand_aliasing={{0}: (4, {}), {1}: (5, {}), {2}: (6, {}), {3}: (7, {}), {4}... | custom-call | flops 1 | bytes 1 | tf_op jit(solution)/shard_map/pallas_call | solution.py:923
  12.6 0.0 collective-permute-done.1.refs_0_
  12.7 0.0 copy-start.3
  12.7 0.0 copy-start.7
  12.7 0.0 copy-start.15
  12.7 0.1 collective-permute-start.8
  12.8 0.3 %collective-permute-done.6.refs_1_ = f32[120,128]{1,0:T(8,128)S(1)} collective-permute-done((f32[120,128]{1,0:T(8,128)S(1)}, f32[120,128]{1,0:T(8,128)S(1)}, u32[]{:S(2)}, u32[]{:S(2)}) %collective-permute-start.6) | collective-permute-done | bytes 61472 | tf_op jit(solution)/shard_map/ppermute | solution.py:961
  13.1 0.0 collective-permute-done.5.refs_0_
  13.1 0.0 collective-permute-done.7.refs_2_
  13.1 0.0 copy-done.17
  13.1 0.0 copy-done.18
  13.1 0.0 copy-start.14
  13.1 1.2 %shard_map.234 = (f32[16,56,128]{2,1,0:T(8,128)S(1)}, f32[16,56,128]{2,1,0:T(8,128)S(1)}, f32[16,56,128]{2,1,0:T(8,128)S(1)}, f32[16,56,128]{2,1,0:T(8,128)S(1)}...) custom-call(f32[136,128]{1,0:T(8,128)S(1)} %collective-permute-done., ...), custom_call_target="tpu_custom_call", output_to_operand_aliasing={{0}: (10, {}), {1}: (11, {}), {2}: (12, {}), {3}: (13, {}),... | custom-call | flops 1 | bytes 1 | tf_op jit(solution)/shard_map/pallas_call | solution.py:923
  14.4 0.0 collective-permute-done.4.refs_1_
  14.4 0.4 %collective-permute-start.9 = (f32[152,128]{1,0:T(8,128)S(1)}, f32[152,128]{1,0:T(8,128)S(1)}, u32[]{:S(2)}, u32[]{:S(2)}) collective-permute-start(f32[152,128]{1,0:T(8,128)S(1)} %collective-permute-done.4.refs_1_), channel_id=1, source_target_pairs={{0,2},{2,0},{4,6},{6,4},{8,10},{10,8},{12,14},{14,12},{16,18},{18,... | collective-permute-start | bytes 233480 | tf_op jit(solution)/shard_map/ppermute | solution.py:961
  14.8 0.0 copy-done.3
  14.8 0.0 copy-done.7
  14.8 0.0 copy-done.15
  14.8 0.0 copy-start.5
  14.8 0.0 copy-start.9
  14.8 0.0 copy-start.10
  14.9 0.0 copy-start.12
  14.9 0.0 copy-start.13
  14.9 0.8 %shard_map.235 = (f32[2,27,8,128]{3,2,1,0:T(8,128)S(1)}, f32[4,8,128]{2,1,0:T(8,128)S(1)}) custom-call(f32[16,56,128]{2,1,0:T(8,128)S(1)} %get-tuple-element.100.w_ref.refs_4_, f32[16,56,128]{2,1,0:T(8,128)S(1)} %get-tuple-element.104.rhs_ref, f32[24,168]{1,0:T(8,128)S(1)} %copy-done.15, f32[256,768]{1,0:T(8,128)S(1)} %copy-done.3, f32[8,168]{1,0:T(8,128)S(1)} %copy-done.14, ...), custom_call_target="tpu_custom_call" | custom-call | flops 1 | bytes 1 | tf_op jit(solution)/shard_map/pallas_call | solution.py:923
  15.6 0.0 collective-permute-done.8.refs_2_
  15.6 0.1 collective-permute-done.9.refs_3_
  15.7 0.1 copy-done.5
  15.9 0.0 copy-done.9
  15.9 0.0 copy-start.6
  15.9 0.0 copy-start.16
  15.9 1.5 %shard_map.236 = (f32[8,32,128]{2,1,0:T(8,128)S(1)}, f32[3,8,128]{2,1,0:T(8,128)S(1)}, f32[10,8,128]{2,1,0:T(8,128)S(1)}) custom-call(f32[184,128]{1,0:T(8,128)S(1)} %collective-permute-done.1.refs_0_, f32[152,128]{1,0:T(8,128)S(1)} %collective-permute-done.4.refs_1_, f32[184,128]{1,0:T(8,128)S(1)} %collective-permute-done.8.refs_2_, ...), custom_call_target="tpu_custom_call" | custom-call | flops 1 | bytes 1 | tf_op jit(solution)/shard_map/pallas_call | solution.py:923
  17.4 0.2 %collective-permute-start.10 = (f32[3,8,128]{2,1,0:T(8,128)S(1)}, f32[3,8,128]{2,1,0:T(8,128)S(1)}, u32[]{:S(2)}, u32[]{:S(2)}) collective-permute-start(f32[3,8,128]{2,1,0:T(8,128)S(1)} %get-tuple-element.107), channel_id=1, source_target_pairs={{2,4},{3,5},{4,2},{5,3},{6,8},{7,9},{8,6},{9,7},{10,12},{11,13},{1... | collective-permute-start | bytes 36872 | tf_op jit(solution)/shard_map/ppermute | solution.py:962
  17.7 2.6 %collective-permute-done.10.refs_0_ = f32[3,8,128]{2,1,0:T(8,128)S(1)} collective-permute-done((f32[3,8,128]{2,1,0:T(8,128)S(1)}, f32[3,8,128]{2,1,0:T(8,128)S(1)}, u32[]{:S(2)}, u32[]{:S(2)}) %collective-permute-start.10) | collective-permute-done | bytes 12320 | tf_op jit(solution)/shard_map/ppermute | solution.py:962
  20.3 0.5 %collective-permute-start.11 = (f32[3,8,128]{2,1,0:T(8,128)S(1)}, f32[3,8,128]{2,1,0:T(8,128)S(1)}, u32[]{:S(2)}, u32[]{:S(2)}) collective-permute-start(f32[3,8,128]{2,1,0:T(8,128)S(1)} %collective-permute-done.10.refs_0_), channel_id=1, source_target_pairs={{0,2},{2,0},{4,6},{6,4},{8,10},{10,8},{12,14},{14,12},{16,18},{18,... | collective-permute-start | bytes 36872 | tf_op jit(solution)/shard_map/ppermute | solution.py:961
  20.8 0.8 %collective-permute-done.11.refs_1_ = f32[3,8,128]{2,1,0:T(8,128)S(1)} collective-permute-done((f32[3,8,128]{2,1,0:T(8,128)S(1)}, f32[3,8,128]{2,1,0:T(8,128)S(1)}, u32[]{:S(2)}, u32[]{:S(2)}) %collective-permute-start.11) | collective-permute-done | bytes 12320 | tf_op jit(solution)/shard_map/ppermute | solution.py:961
  21.6 0.0 copy-done.6
  21.6 1.3 %shard_map.237 = (f32[8,32,128]{2,1,0:T(8,128)}, f32[2,8,32]{2,1,0:T(8,128)}) custom-call(f32[3,8,128]{2,1,0:T(8,128)S(1)} %collective-permute-done.10.refs_0_, f32[3,8,128]{2,1,0:T(8,128)S(1)} %collective-permute-done.11.refs_1_, f32[8,32,128]{2,1,0:T(8,128)S(1)} %get-tuple-element.108.refs_2_, f32[10,8,128]{2,1,0:T(8,128)S(1)} %get-tuple-element.109.refs_3_, ...), custom_call_target="tpu_custom_call" | custom-call | flops 1 | bytes 1 | tf_op jit(solution)/shard_map/pallas_call | solution.py:923
  (14 shorter events, 0.0 us)
Async XLA Ops:
  0.6 1.8 %copy-start = (f32[256,256]{1,0:T(8,128)S(1)}, f32[256,256]{1,0:T(8,128)}, u32[]{:S(2)}) copy-start(f32[256,256]{1,0:T(8,128)} %constant.44.clone.z_sq.refs_0_.refs_1_.refs_3_) | copy-start | bytes 786436
  0.6 1.8 %copy-start.4 = (f32[8,8,128]{2,1,0:T(8,128)S(1)}, f32[8,8,128]{2,1,0:T(8,128)}, u32[]{:S(2)}) copy-start(f32[8,8,128]{2,1,0:T(8,128)} %constant.62.clone.w3.refs_2_.refs_3_.refs_5_) | copy-start | bytes 98308
  0.7 1.8 %copy-start.8 = (f32[32,96]{1,0:T(8,128)S(1)}, f32[32,96]{1,0:T(8,128)}, u32[]{:S(2)}) copy-start(f32[32,96]{1,0:T(8,128)} %constant.50.clone.y_sq.refs_1_) | copy-start | bytes 36868
  1.7 4.3 %collective-permute-start.3 = (f32[2,8,32,128]{3,2,1,0:T(8,128)S(1)}, f32[2,8,32,128]{3,2,1,0:T(8,128)S(1)}, u32[]{:S(2)}, u32[]{:S(2)}) collective-permute-start(f32[2,8,32,128]{3,2,1,0:T(8,128)S(1)} %pad_maximum_fusion.raw.own), channel_id=1, source_target_pairs={{0,2},{2,0},{4,6},{6,4},{8,10},{10,8},{12,14},{14,12},{16,18},{18,... | collective-permute-start | bytes 786440 | tf_op jit(solution)/shard_map/ppermute | solution.py:961
  2.4 3.5 %copy-start.2 = (f32[256,256]{1,0:T(8,128)S(1)}, f32[256,256]{1,0:T(8,128)}, u32[]{:S(2)}) copy-start(f32[256,256]{1,0:T(8,128)} %constant.43.clone.refs_4_.refs_7_.refs_11_) | copy-start | bytes 786436
  2.8 3.2 %copy-start.1 = (f32[256,256]{1,0:T(8,128)S(1)}, f32[256,256]{1,0:T(8,128)}, u32[]{:S(2)}) copy-start(f32[256,256]{1,0:T(8,128)} %constant.42.clone.refs_3_.refs_6_.refs_10_) | copy-start | bytes 786436
  2.8 7.6 %collective-permute-start.2 = (f32[400,128]{1,0:T(8,128)S(1)}, f32[400,128]{1,0:T(8,128)S(1)}, u32[]{:S(2)}, u32[]{:S(2)}) collective-permute-start(f32[400,128]{1,0:T(8,128)S(1)} %get-tuple-element.62), channel_id=1, source_target_pairs={{0,1},{1,0},{2,3},{3,2},{4,5},{5,4},{6,7},{7,6},{8,9},{9,8},{10,11... | collective-permute-start | bytes 614408 | tf_op jit(solution)/shard_map/ppermute | solution.py:980
  3.1 1.2 %collective-permute-start = (f32[2,32,128]{2,1,0:T(8,128)S(1)}, f32[2,32,128]{2,1,0:T(8,128)S(1)}, u32[]{:S(2)}, u32[]{:S(2)}) collective-permute-start(f32[2,32,128]{2,1,0:T(8,128)S(1)} %get-tuple-element.60), channel_id=1, source_target_pairs={{0,2},{2,0},{4,6},{6,4},{8,10},{10,8},{12,14},{14,12},{16,18},{18,... | collective-permute-start | bytes 98312 | tf_op jit(solution)/shard_map/ppermute | solution.py:961
  4.3 1.7 %copy-start.19 = (f32[24,72]{1,0:T(8,128)S(1)}, f32[24,72]{1,0:T(8,128)}, u32[]{:S(2)}) copy-start(f32[24,72]{1,0:T(8,128)} %constant.48.clone.refs_5_) | copy-start | bytes 20740
  4.3 1.7 %copy-start.20 = (f32[24,72]{1,0:T(8,128)S(1)}, f32[24,72]{1,0:T(8,128)}, u32[]{:S(2)}) copy-start(f32[24,72]{1,0:T(8,128)} %constant.49.clone.refs_6_) | copy-start | bytes 20740
  4.5 8.2 %collective-permute-start.1 = (f32[184,128]{1,0:T(8,128)S(1)}, f32[184,128]{1,0:T(8,128)S(1)}, u32[]{:S(2)}, u32[]{:S(2)}) collective-permute-start(f32[184,128]{1,0:T(8,128)S(1)} %get-tuple-element.61), channel_id=1, source_target_pairs={{2,4},{3,5},{4,2},{5,3},{6,8},{7,9},{8,6},{9,7},{10,12},{11,13},{1... | collective-permute-start | bytes 282632 | tf_op jit(solution)/shard_map/ppermute | solution.py:962
  5.8 8.6 %collective-permute-start.4 = (f32[152,128]{1,0:T(8,128)S(1)}, f32[152,128]{1,0:T(8,128)S(1)}, u32[]{:S(2)}, u32[]{:S(2)}) collective-permute-start(f32[152,128]{1,0:T(8,128)S(1)} %get-tuple-element.89), channel_id=1, source_target_pairs={{2,5},{3,4},{4,3},{5,2},{6,9},{7,8},{8,7},{9,6},{10,13},{11,12},{1... | collective-permute-start | bytes 233480 | tf_op jit(solution)/shard_map/ppermute | solution.py:962
  10.4 2.8 %collective-permute-start.7 = (f32[144,128]{1,0:T(8,128)S(1)}, f32[144,128]{1,0:T(8,128)S(1)}, u32[]{:S(2)}, u32[]{:S(2)}) collective-permute-start(f32[144,128]{1,0:T(8,128)S(1)} %slice.11), channel_id=1, source_target_pairs={{0,2},{2,0},{4,6},{6,4},{8,10},{10,8},{12,14},{14,12},{16,18},{18,... | collective-permute-start | bytes 221192 | tf_op jit(solution)/shard_map/ppermute | solution.py:961
  11.6 0.7 %copy-start.11 = (f32[24,72]{1,0:T(8,128)S(1)}, f32[24,72]{1,0:T(8,128)}, u32[]{:S(2)}) copy-start(f32[24,72]{1,0:T(8,128)} %constant.47.clone.refs_2_.refs_4_) | copy-start | bytes 20740
  11.6 1.5 %collective-permute-start.5 = (f32[136,128]{1,0:T(8,128)S(1)}, f32[136,128]{1,0:T(8,128)S(1)}, u32[]{:S(2)}, u32[]{:S(2)}) collective-permute-start(f32[136,128]{1,0:T(8,128)S(1)} %slice.9), channel_id=1, source_target_pairs={{0,2},{2,0},{4,6},{6,4},{8,10},{10,8},{12,14},{14,12},{16,18},{18,... | collective-permute-start | bytes 208904 | tf_op jit(solution)/shard_map/ppermute | solution.py:961
  11.7 1.4 %collective-permute-start.6 = (f32[120,128]{1,0:T(8,128)S(1)}, f32[120,128]{1,0:T(8,128)S(1)}, u32[]{:S(2)}, u32[]{:S(2)}) collective-permute-start(f32[120,128]{1,0:T(8,128)S(1)} %slice.10), channel_id=1, source_target_pairs={{0,2},{2,0},{4,6},{6,4},{8,10},{10,8},{12,14},{14,12},{16,18},{18,... | collective-permute-start | bytes 184328 | tf_op jit(solution)/shard_map/ppermute | solution.py:961
  12.3 0.8 %copy-start.17 = (f32[32,96]{1,0:T(8,128)S(1)}, f32[32,96]{1,0:T(8,128)}, u32[]{:S(2)}) copy-start(f32[32,96]{1,0:T(8,128)} %constant.51.clone.refs_8_) | copy-start | bytes 36868
  12.3 0.8 %copy-start.18 = (f32[32,96]{1,0:T(8,128)S(1)}, f32[32,96]{1,0:T(8,128)}, u32[]{:S(2)}) copy-start(f32[32,96]{1,0:T(8,128)} %constant.52.clone.refs_9_) | copy-start | bytes 36868
  12.7 2.2 %copy-start.3 = (f32[256,768]{1,0:T(8,128)S(1)}, f32[256,768]{1,0:T(8,128)}, u32[]{:S(2)}) copy-start(f32[256,768]{1,0:T(8,128)} %constant.58.clone.mz) | copy-start | bytes 2359300
  12.7 2.1 %copy-start.7 = (f32[256,256]{1,0:T(8,128)S(1)}, f32[256,256]{1,0:T(8,128)}, u32[]{:S(2)}) copy-start(f32[256,256]{1,0:T(8,128)} %constant.56.clone.rz) | copy-start | bytes 786436
  12.7 2.1 %copy-start.15 = (f32[24,168]{1,0:T(8,128)S(1)}, f32[24,168]{1,0:T(8,128)}, u32[]{:S(2)}) copy-start(f32[24,168]{1,0:T(8,128)} %constant.57.clone.my) | copy-start | bytes 48388
  12.7 3.0 %collective-permute-start.8 = (f32[184,128]{1,0:T(8,128)S(1)}, f32[184,128]{1,0:T(8,128)S(1)}, u32[]{:S(2)}, u32[]{:S(2)}) collective-permute-start(f32[184,128]{1,0:T(8,128)S(1)} %collective-permute-done.1.refs_0_), channel_id=1, source_target_pairs={{0,2},{2,0},{4,6},{6,4},{8,10},{10,8},{12,14},{14,12},{16,18},{18,... | collective-permute-start | bytes 282632 | tf_op jit(solution)/shard_map/ppermute | solution.py:961
  13.1 1.7 %copy-start.14 = (f32[8,168]{1,0:T(8,128)S(1)}, f32[8,168]{1,0:T(8,128)}, u32[]{:S(2)}) copy-start(f32[8,168]{1,0:T(8,128)} %constant.54.clone.ry.refs_15_) | copy-start | bytes 16132
  14.4 1.3 %collective-permute-start.9 = (f32[152,128]{1,0:T(8,128)S(1)}, f32[152,128]{1,0:T(8,128)S(1)}, u32[]{:S(2)}, u32[]{:S(2)}) collective-permute-start(f32[152,128]{1,0:T(8,128)S(1)} %collective-permute-done.4.refs_1_), channel_id=1, source_target_pairs={{0,2},{2,0},{4,6},{6,4},{8,10},{10,8},{12,14},{14,12},{16,18},{18,... | collective-permute-start | bytes 233480 | tf_op jit(solution)/shard_map/ppermute | solution.py:961
  14.8 1.0 %copy-start.5 = (f32[512,256]{1,0:T(8,128)S(1)}, f32[512,256]{1,0:T(8,128)}, u32[]{:S(2)}) copy-start(f32[512,256]{1,0:T(8,128)} %constant.55.clone.refs_16_) | copy-start | bytes 1572868
  14.8 1.0 %copy-start.9 = (f32[56,168]{1,0:T(8,128)S(1)}, f32[56,168]{1,0:T(8,128)}, u32[]{:S(2)}) copy-start(f32[56,168]{1,0:T(8,128)} %constant.45.clone.refs_12_) | copy-start | bytes 112900
  14.8 1.0 %copy-start.10 = (f32[56,168]{1,0:T(8,128)S(1)}, f32[56,168]{1,0:T(8,128)}, u32[]{:S(2)}) copy-start(f32[56,168]{1,0:T(8,128)} %constant.46.clone.refs_13_) | copy-start | bytes 112900
  14.9 1.0 %copy-start.12 = (f32[10,8,128]{2,1,0:T(8,128)S(1)}, f32[10,8,128]{2,1,0:T(8,128)}, u32[]{:S(2)}) copy-start(f32[10,8,128]{2,1,0:T(8,128)} %constant.61.clone.refs_17_) | copy-start | bytes 122884
  14.9 1.0 %copy-start.13 = (f32[32,168]{1,0:T(8,128)S(1)}, f32[32,168]{1,0:T(8,128)}, u32[]{:S(2)}) copy-start(f32[32,168]{1,0:T(8,128)} %constant.53.clone.refs_14_) | copy-start | bytes 64516
  15.9 5.8 %copy-start.6 = (f32[256,320]{1,0:T(8,128)S(1)}, f32[256,320]{1,0:T(8,128)}, u32[]{:S(2)}) copy-start(f32[256,320]{1,0:T(8,128)} %constant.60.clone.refs_6_) | copy-start | bytes 983044
  15.9 5.8 %copy-start.16 = (f32[40,24]{1,0:T(8,128)S(1)}, f32[40,24]{1,0:T(8,128)}, u32[]{:S(2)}) copy-start(f32[40,24]{1,0:T(8,128)} %constant.59.clone.refs_5_) | copy-start | bytes 11524
  17.4 2.9 %collective-permute-start.10 = (f32[3,8,128]{2,1,0:T(8,128)S(1)}, f32[3,8,128]{2,1,0:T(8,128)S(1)}, u32[]{:S(2)}, u32[]{:S(2)}) collective-permute-start(f32[3,8,128]{2,1,0:T(8,128)S(1)} %get-tuple-element.107), channel_id=1, source_target_pairs={{2,4},{3,5},{4,2},{5,3},{6,8},{7,9},{8,6},{9,7},{10,12},{11,13},{1... | collective-permute-start | bytes 36872 | tf_op jit(solution)/shard_map/ppermute | solution.py:962
  20.3 1.3 %collective-permute-start.11 = (f32[3,8,128]{2,1,0:T(8,128)S(1)}, f32[3,8,128]{2,1,0:T(8,128)S(1)}, u32[]{:S(2)}, u32[]{:S(2)}) collective-permute-start(f32[3,8,128]{2,1,0:T(8,128)S(1)} %collective-permute-done.10.refs_0_), channel_id=1, source_target_pairs={{0,2},{2,0},{4,6},{6,4},{8,10},{10,8},{12,14},{14,12},{16,18},{18,... | collective-permute-start | bytes 36872 | tf_op jit(solution)/shard_map/ppermute | solution.py:961

commit v6 on v5

--- a/solution.py
+++ b/solution.py
@@ -16,6 +16,7 @@
 SIGMA = THETA / DELTA
 RHO0 = 1.0 / SIGMA
 RHO1 = 1.0 / (2.0 * SIGMA - RHO0)
+LANES = 128
 F32 = jnp.float32
 BF16 = jnp.bfloat16
 VMEM_LIMIT = 48 * 1024 * 1024
@@ -78,8 +79,8 @@
 
 def right_table(matrix):
     hi, lo = hi_lo(matrix)
-    top = np.concatenate([hi, lo], axis=1)
-    return np.concatenate([top, np.concatenate([hi, 0 * lo], axis=1)], axis=0).astype(np.float32)
+    full = np.concatenate([np.concatenate([hi, hi]), np.concatenate([lo, 0 * lo])], axis=1)
+    return np.stack(np.split(full, full.shape[1] // LANES, axis=1))
 
 
 def left_table(matrix):
@@ -135,9 +136,7 @@
     t["rz_one"] = right_table(pz)
     t["my"] = left_table(np.concatenate([moment_table(m, ey, cr) for m in MASS], axis=1).T)
     t["mz"] = right_table(np.concatenate([moment_table(m, ez, nz) for m in MASS], axis=1))
-    own_ey = own_y // N
-    py = vertex_table(INTERP, own_ey, cr)
-    t["py"] = left_table(np.concatenate([py, vertex_table(np.eye(2), own_ey, cr, 2)], axis=0))
+    t["py"] = np.broadcast_to(INTERP.T[:, :, None], (2, N, nz)).astype(np.float32)
     pz = vertex_table(INTERP, ez, nz).T
     sz = vertex_table(np.eye(2), ez, nz, 2).T
     t["pz"] = right_table(np.concatenate([pz, sz], axis=1))
@@ -177,7 +176,8 @@
 
 
 def z_apply(hi, lo, table):
-    both = dot(jnp.concatenate([hi, lo], axis=1), table.astype(BF16))
+    table = jnp.concatenate([table[k] for k in range(table.shape[0])], axis=1)
+    both = dot(jnp.concatenate([hi, lo], axis=1), table)
     half = both.shape[1] // 2
     return both[:, :half] + both[:, half:]
 
@@ -896,18 +896,24 @@
     c_mid = state[9] + (2.0 / 3.0) * (rhs - cin * (state[7] + cross)) / d
     left = jnp.where(is_even, c_low, c_mid)
     right = jnp.where(is_even, c_mid, c_high)
-    both = jnp.concatenate([left, right], axis=1)
-    if lay.sub > 1:
-        both = pltpu.roll(both, cr - lax.div(offset, N), 0)
-    y, cy = lay.own_y, lay.own_y // 4
-    along_y = y_apply(both, py[...])
-    along_y = jnp.concatenate([along_y[:, :nz], along_y[:, nz:]], axis=0)
-    full = z_apply(*split(along_y), pz[...])
-    inside = yz_mask(y, nz, start + offset, lay.total_y).astype(F32)
-    q_left = inside * full[:y, :nz]
-    q_right = inside * full[y + cy : 2 * y + cy, :nz]
-    coarse[0] = full[y : y + cy, nz : nz + nz // 4]
-    coarse[1] = full[2 * y + cy :, nz : nz + nz // 4]
+    both = jnp.concatenate([left, right], axis=0)
+    full = z_apply(*split(both), pz[...])
+    y = lay.own_y
+    mask = yz_mask(y, nz, start + offset, lay.total_y).astype(F32)
+    weight = [jnp.broadcast_to(py[i], (N, nz)) for i in range(2)]
+    q = []
+    for side in range(2):
+        rows = full[side * cr : (side + 1) * cr]
+        if lay.sub > 1:
+            rows = pltpu.roll(rows, cr - lax.div(offset, N), 0)
+        blocks = []
+        for e in range(y // N):
+            at = [rows[e + i : e + i + 1] for i in range(2)]
+            blocks.append(weight[0] * at[0][:, :nz] + weight[1] * at[1][:, :nz])
+            for i in range(2):
+                coarse[side, pl.ds(2 * e + i, 1), :] = at[i][:, nz : nz + nz // 4]
+        q.append(mask * jnp.concatenate(blocks, axis=0))
+    q_left, q_right = q
     first_flag = jnp.where(is_even, low, 1.0)
     last_flag = jnp.where(is_even, 1.0, high)
     for a in range(N):
@@ -978,7 +984,7 @@
         up = [(i, i + 1) for i in range(sub - 1)]
         steps = [up, [(b, a) for a, b in up]]
     others = [lax.ppermute(pack, "sub", step) for pack, step in zip(packs, steps)]
-    mate = even(raw)
+    mate = even(lax.optimization_barrier((raw, face))[0])
     lines = 3 * N * line_count(lay)
     msgs = run(
         functools.partial(message_kernel, lay),

time: 23.3 us -> 23.2 us (level)
  starting transfers between devices: 5.95 us -> 7.17 us
  waiting for transfers between devices: 8.2 us -> 7.09 us
    ppermute x8, starting transfers between devices: 3.91 us -> 5.19 us  [shards(): even = lambda v: lax.ppermute(v, 'dom', swap_pairs(dom, 0))]
    ppermute x1, waiting for transfers between devices: 3.46 us -> 2.64 us  [shards(): lax.ppermute(pack, 'sub', step)]
    ppermute x3, waiting for transfers between devices: 2.61 us -> 2.32 us  [shards(): lax.ppermute(v, ('dom', 'sub'), chip_pairs(dom, sub, k))]
  transfers between devices with their start and end apart: 12 -> 12, of which waited for: 6 -> 6; matrix products, arithmetic and copies ran while one was open for 0% -> 0% of each run, Pallas kernels for 16% -> 15%
where the time goes in v6:
time: 23.2 us; the launch traced here: 22.7 us
  starting transfers between devices  7.17 us (31%)
  waiting for transfers between devices  7.09 us (31%)
  Pallas kernels  6.25 us (27%)
  other arithmetic  1.04 us (4%)
  between operations  0.88 us (4%)
  local copies, waits for them, and re-layouts  0.3 us (1%)
    pallas_call x8, Pallas kernels, run(): pl.pallas_call(kernel, out_shape=[jax.ShapeDtypeStruct(o, F32) for o in o...  6.25 us
    ppermute x8, starting transfers between devices, shards(): even = lambda v: lax.ppermute(v, 'dom', swap_pairs(dom, 0))  5.19 us
    ppermute x1, waiting for transfers between devices, shards(): lax.ppermute(pack, 'sub', step)  2.64 us
    ppermute x3, waiting for transfers between devices, shards(): lax.ppermute(v, ('dom', 'sub'), chip_pairs(dom, sub, k))  2.32 us
    ppermute x8, waiting for transfers between devices, shards(): even = lambda v: lax.ppermute(v, 'dom', swap_pairs(dom, 0))  2.14 us
    ppermute x3, starting transfers between devices, shards(): lax.ppermute(v, ('dom', 'sub'), chip_pairs(dom, sub, k))  1.75 us
    another operation x1, other arithmetic, shards(): raw = jnp.stack([rhs_local, coefficient])  1.04 us
  transfers between devices with their start and end apart: 12, of which 6 were waited for; matrix products, arithmetic and copies ran while one was open for 0% of the time, Pallas kernels for 15%

profile of v6, /device:TPU:31, one launch (start us, length us, event | category | flops | bytes accessed | tf_op | source)
XLA Modules:
  0.0 22.7 jit_solution(6132601897222459825)
XLA Ops:
  0.6 0.0 copy-start
  0.6 0.0 copy-start.3
  0.7 0.0 copy-start.8
  0.7 1.0 %pad_maximum_fusion.raw.own = f32[2,8,32,128]{3,2,1,0:T(8,128)S(1)} fusion(f32[1,8,32,128]{3,2,1,0:T(8,128)} %bitcast.2, f32[1,8,32,128]{3,2,1,0:T(8,128)} %bitcast.3), kind=kLoop, calls=%fused_computation | loop fusion | flops 65536 | bytes 524288 | tf_op jit(solution)/shard_map/stack | solution.py:970
  1.7 0.0 copy-done
  1.7 0.0 copy-done.3
  1.7 0.0 copy-done.8
  1.7 0.3 %shard_map.230 = (f32[2,32,128]{2,1,0:T(8,128)S(1)}, f32[8,32,128]{2,1,0:T(8,128)S(1)}, f32[8,32,128]{2,1,0:T(8,128)S(1)}, f32[8,32,128]{2,1,0:T(8,128)S(1)}, f3...) custom-call(f32[2,8,32,128]{3,2,1,0:T(8,128)S(1)} %pad_maximum_fusion.raw.own, bf16[2,256,128]{2,1,0:T(8,128)(2,1)S(1)} %copy-done, ...), custom_call_target="tpu_custom_call" | custom-call | flops 1 | bytes 1 | tf_op jit(solution)/shard_map/pallas_call | solution.py:929
  2.1 0.7 %collective-permute-start.3 = (f32[2,8,32,128]{3,2,1,0:T(8,128)S(1)}, f32[2,8,32,128]{3,2,1,0:T(8,128)S(1)}, u32[]{:S(2)}, u32[]{:S(2)}) collective-permute-start(f32[2,8,32,128]{3,2,1,0:T(8,128)S(1)} %pad_maximum_fusion.raw.own), channel_id=1, source_target_pairs={{0,2},{2,0},{4,6},{6,4},{8,10},{10,8},{12,14},{14,12},{16,18},{18,... | collective-permute-start | bytes 786440 | tf_op jit(solution)/shard_map/ppermute | solution.py:967
  2.8 0.2 %collective-permute-start.2 = (f32[400,128]{1,0:T(8,128)S(1)}, f32[400,128]{1,0:T(8,128)S(1)}, u32[]{:S(2)}, u32[]{:S(2)}) collective-permute-start(f32[400,128]{1,0:T(8,128)S(1)} %get-tuple-element.63), channel_id=1, source_target_pairs={{0,1},{1,0},{2,3},{3,2},{4,5},{5,4},{6,7},{7,6},{8,9},{9,8},{10,11... | collective-permute-start | bytes 614408 | tf_op jit(solution)/shard_map/ppermute | solution.py:986
  3.1 0.3 %collective-permute-start = (f32[2,32,128]{2,1,0:T(8,128)S(1)}, f32[2,32,128]{2,1,0:T(8,128)S(1)}, u32[]{:S(2)}, u32[]{:S(2)}) collective-permute-start(f32[2,32,128]{2,1,0:T(8,128)S(1)} %get-tuple-element.61), channel_id=1, source_target_pairs={{0,2},{2,0},{4,6},{6,4},{8,10},{10,8},{12,14},{14,12},{16,18},{18,... | collective-permute-start | bytes 98312 | tf_op jit(solution)/shard_map/ppermute | solution.py:967
  3.4 0.9 %collective-permute-done.face = f32[2,32,128]{2,1,0:T(8,128)S(1)} collective-permute-done((f32[2,32,128]{2,1,0:T(8,128)S(1)}, f32[2,32,128]{2,1,0:T(8,128)S(1)}, u32[]{:S(2)}, u32[]{:S(2)}) %collective-permute-start) | collective-permute-done | bytes 32800 | tf_op jit(solution)/shard_map/ppermute | solution.py:967
  4.3 0.2 shard_map.231
  4.5 1.3 %collective-permute-start.1 = (f32[184,128]{1,0:T(8,128)S(1)}, f32[184,128]{1,0:T(8,128)S(1)}, u32[]{:S(2)}, u32[]{:S(2)}) collective-permute-start(f32[184,128]{1,0:T(8,128)S(1)} %get-tuple-element.62), channel_id=1, source_target_pairs={{2,4},{3,5},{4,2},{5,3},{6,8},{7,9},{8,6},{9,7},{10,12},{11,13},{1... | collective-permute-start | bytes 282632 | tf_op jit(solution)/shard_map/ppermute | solution.py:968
  5.7 0.2 collective-permute-start.4
  6.0 0.0 collective-permute-done.3.mate
  6.0 0.0 copy-done.1
  6.0 0.0 copy-done.2
  6.0 0.0 copy-done.18
  6.0 0.0 copy-done.19
  6.0 0.8 %shard_map.232 = (f32[16,56,128]{2,1,0:T(8,128)S(1)}, f32[16,56,128]{2,1,0:T(8,128)S(1)}, f32[16,56,128]{2,1,0:T(8,128)S(1)}, f32[16,56,128]{2,1,0:T(8,128)S(1)}...) custom-call(f32[2,8,32,128]{3,2,1,0:T(8,128)S(1)} %pad_maximum_fusio, ...), custom_call_target="tpu_custom_call" | custom-call | flops 1 | bytes 1 | tf_op jit(solution)/shard_map/pallas_call | solution.py:929
  6.8 2.6 %collective-permute-done.2.refs_0_ = f32[400,128]{1,0:T(8,128)S(1)} collective-permute-done((f32[400,128]{1,0:T(8,128)S(1)}, f32[400,128]{1,0:T(8,128)S(1)}, u32[]{:S(2)}, u32[]{:S(2)}) %collective-permute-start.2) | collective-permute-done | bytes 204832 | tf_op jit(solution)/shard_map/ppermute | solution.py:986
  9.5 2.1 %collective-permute-start.7 = (f32[144,128]{1,0:T(8,128)S(1)}, f32[144,128]{1,0:T(8,128)S(1)}, u32[]{:S(2)}, u32[]{:S(2)}) collective-permute-start(f32[144,128]{1,0:T(8,128)S(1)} %slice.11), channel_id=1, source_target_pairs={{0,2},{2,0},{4,6},{6,4},{8,10},{10,8},{12,14},{14,12},{16,18},{18,... | collective-permute-start | bytes 221192 | tf_op jit(solution)/shard_map/ppermute | solution.py:967
  11.6 0.1 collective-permute-start.5
  11.7 0.5 %collective-permute-start.6 = (f32[120,128]{1,0:T(8,128)S(1)}, f32[120,128]{1,0:T(8,128)S(1)}, u32[]{:S(2)}, u32[]{:S(2)}) collective-permute-start(f32[120,128]{1,0:T(8,128)S(1)} %slice.10), channel_id=1, source_target_pairs={{0,2},{2,0},{4,6},{6,4},{8,10},{10,8},{12,14},{14,12},{16,18},{18,... | collective-permute-start | bytes 184328 | tf_op jit(solution)/shard_map/ppermute | solution.py:967
  12.2 0.1 copy-done.11
  12.3 0.3 %shard_map.233 = (f32[16,56,128]{2,1,0:T(8,128)S(1)}, f32[16,56,128]{2,1,0:T(8,128)S(1)}, f32[16,56,128]{2,1,0:T(8,128)S(1)}, f32[16,56,128]{2,1,0:T(8,128)S(1)}...) custom-call(f32[400,128]{1,0:T(8,128)S(1)} %collective-permute-done., ...), custom_call_target="tpu_custom_call", output_to_operand_aliasing={{0}: (4, {}), {1}: (5, {}), {2}: (6, {}), {3}: (7, {}), {4}... | custom-call | flops 1 | bytes 1 | tf_op jit(solution)/shard_map/pallas_call | solution.py:929
  12.6 0.0 collective-permute-done.1.refs_0_
  12.6 0.0 copy-start.4
  12.7 0.0 copy-start.7
  12.7 0.0 copy-start.15
  12.7 0.1 collective-permute-start.8
  12.8 0.3 %collective-permute-done.6.refs_1_ = f32[120,128]{1,0:T(8,128)S(1)} collective-permute-done((f32[120,128]{1,0:T(8,128)S(1)}, f32[120,128]{1,0:T(8,128)S(1)}, u32[]{:S(2)}, u32[]{:S(2)}) %collective-permute-start.6) | collective-permute-done | bytes 61472 | tf_op jit(solution)/shard_map/ppermute | solution.py:967
  13.1 0.0 collective-permute-done.5.refs_0_
  13.1 0.0 collective-permute-done.7.refs_2_
  13.1 0.0 copy-done.16
  13.1 0.0 copy-done.17
  13.1 0.0 copy-start.14
  13.1 1.2 %shard_map.234 = (f32[16,56,128]{2,1,0:T(8,128)S(1)}, f32[16,56,128]{2,1,0:T(8,128)S(1)}, f32[16,56,128]{2,1,0:T(8,128)S(1)}, f32[16,56,128]{2,1,0:T(8,128)S(1)}...) custom-call(f32[136,128]{1,0:T(8,128)S(1)} %collective-permute-done., ...), custom_call_target="tpu_custom_call", output_to_operand_aliasing={{0}: (10, {}), {1}: (11, {}), {2}: (12, {}), {3}: (13, {}),... | custom-call | flops 1 | bytes 1 | tf_op jit(solution)/shard_map/pallas_call | solution.py:929
  14.4 0.0 collective-permute-done.4.refs_1_
  14.4 0.4 %collective-permute-start.9 = (f32[152,128]{1,0:T(8,128)S(1)}, f32[152,128]{1,0:T(8,128)S(1)}, u32[]{:S(2)}, u32[]{:S(2)}) collective-permute-start(f32[152,128]{1,0:T(8,128)S(1)} %collective-permute-done.4.refs_1_), channel_id=1, source_target_pairs={{0,2},{2,0},{4,6},{6,4},{8,10},{10,8},{12,14},{14,12},{16,18},{18,... | collective-permute-start | bytes 233480 | tf_op jit(solution)/shard_map/ppermute | solution.py:967
  14.8 0.0 copy-done.4
  14.8 0.0 copy-done.7
  14.8 0.0 copy-done.15
  14.8 0.0 copy-done.14
  14.8 0.0 copy-start.6
  14.8 0.0 copy-start.9
  14.8 0.0 copy-start.10
  14.8 0.0 copy-start.12
  14.9 0.0 copy-start.13
  14.9 0.8 %shard_map.235 = (f32[2,27,8,128]{3,2,1,0:T(8,128)S(1)}, f32[4,8,128]{2,1,0:T(8,128)S(1)}) custom-call(f32[16,56,128]{2,1,0:T(8,128)S(1)} %get-tuple-element.102.w_ref.refs_4_, f32[16,56,128]{2,1,0:T(8,128)S(1)} %get-tuple-element.106.rhs_ref, f32[24,168]{1,0:T(8,128)S(1)} %copy-done.15, bf16[6,256,128]{2,1,0:T(8,128)(2,1)S(1)} %copy-done.4, ...), custom_call_target="tpu_custom_call" | custom-call | flops 1 | bytes 1 | tf_op jit(solution)/shard_map/pallas_call | solution.py:929
  15.6 0.0 collective-permute-done.8.refs_2_
  15.6 0.1 collective-permute-done.9.refs_3_
  15.7 0.0 copy-done.6
  15.8 0.0 copy-done.9
  15.8 0.0 copy-done.10
  15.8 0.0 copy-start.5
  15.8 0.0 copy-start.20
  15.8 1.5 %shard_map.236 = (f32[8,32,128]{2,1,0:T(8,128)S(1)}, f32[3,8,128]{2,1,0:T(8,128)S(1)}, f32[10,8,128]{2,1,0:T(8,128)S(1)}) custom-call(f32[184,128]{1,0:T(8,128)S(1)} %collective-permute-done.1.refs_0_, f32[152,128]{1,0:T(8,128)S(1)} %collective-permute-done.4.refs_1_, f32[184,128]{1,0:T(8,128)S(1)} %collective-permute-done.8.refs_2_, ...), custom_call_target="tpu_custom_call" | custom-call | flops 1 | bytes 1 | tf_op jit(solution)/shard_map/pallas_call | solution.py:929
  17.3 0.2 %collective-permute-start.10 = (f32[3,8,128]{2,1,0:T(8,128)S(1)}, f32[3,8,128]{2,1,0:T(8,128)S(1)}, u32[]{:S(2)}, u32[]{:S(2)}) collective-permute-start(f32[3,8,128]{2,1,0:T(8,128)S(1)} %get-tuple-element.109), channel_id=1, source_target_pairs={{2,4},{3,5},{4,2},{5,3},{6,8},{7,9},{8,6},{9,7},{10,12},{11,13},{1... | collective-permute-start | bytes 36872 | tf_op jit(solution)/shard_map/ppermute | solution.py:968
  17.6 2.3 %collective-permute-done.10.refs_0_ = f32[3,8,128]{2,1,0:T(8,128)S(1)} collective-permute-done((f32[3,8,128]{2,1,0:T(8,128)S(1)}, f32[3,8,128]{2,1,0:T(8,128)S(1)}, u32[]{:S(2)}, u32[]{:S(2)}) %collective-permute-start.10) | collective-permute-done | bytes 12320 | tf_op jit(solution)/shard_map/ppermute | solution.py:968
  19.9 0.9 %collective-permute-start.11 = (f32[3,8,128]{2,1,0:T(8,128)S(1)}, f32[3,8,128]{2,1,0:T(8,128)S(1)}, u32[]{:S(2)}, u32[]{:S(2)}) collective-permute-start(f32[3,8,128]{2,1,0:T(8,128)S(1)} %collective-permute-done.10.refs_0_), channel_id=1, source_target_pairs={{0,2},{2,0},{4,6},{6,4},{8,10},{10,8},{12,14},{14,12},{16,18},{18,... | collective-permute-start | bytes 36872 | tf_op jit(solution)/shard_map/ppermute | solution.py:967
  20.8 0.8 %collective-permute-done.11.refs_1_ = f32[3,8,128]{2,1,0:T(8,128)S(1)} collective-permute-done((f32[3,8,128]{2,1,0:T(8,128)S(1)}, f32[3,8,128]{2,1,0:T(8,128)S(1)}, u32[]{:S(2)}, u32[]{:S(2)}) %collective-permute-start.11) | collective-permute-done | bytes 12320 | tf_op jit(solution)/shard_map/ppermute | solution.py:967
  21.6 1.1 %shard_map.237 = (f32[8,32,128]{2,1,0:T(8,128)}, f32[2,8,32]{2,1,0:T(8,128)}) custom-call(f32[3,8,128]{2,1,0:T(8,128)S(1)} %collective-permute-done.10.refs_0_, f32[3,8,128]{2,1,0:T(8,128)S(1)} %collective-permute-done.11.refs_1_, f32[8,32,128]{2,1,0:T(8,128)S(1)} %get-tuple-element.110.refs_2_, f32[10,8,128]{2,1,0:T(8,128)S(1)} %get-tuple-element.111.refs_3_, ...), custom_call_target="tpu_custom_call" | custom-call | flops 1 | bytes 1 | tf_op jit(solution)/shard_map/pallas_call | solution.py:929
  (14 shorter events, 0.0 us)
Async XLA Ops:
  0.6 1.1 %copy-start = (bf16[2,256,128]{2,1,0:T(8,128)(2,1)S(1)}, bf16[2,256,128]{2,1,0:T(8,128)(2,1)}, u32[]{:S(2)}) copy-start(bf16[2,256,128]{2,1,0:T(8,128)(2,1)} %constant.44.clone.z_sq.refs_0_.refs_1_.refs_3_) | copy-start | bytes 393220
  0.6 1.1 %copy-start.3 = (f32[8,8,128]{2,1,0:T(8,128)S(1)}, f32[8,8,128]{2,1,0:T(8,128)}, u32[]{:S(2)}) copy-start(f32[8,8,128]{2,1,0:T(8,128)} %constant.62.clone.w3.refs_2_.refs_3_.refs_5_) | copy-start | bytes 98308
  0.7 1.1 %copy-start.8 = (f32[32,96]{1,0:T(8,128)S(1)}, f32[32,96]{1,0:T(8,128)}, u32[]{:S(2)}) copy-start(f32[32,96]{1,0:T(8,128)} %constant.50.clone.y_sq.refs_1_) | copy-start | bytes 36868
  2.1 3.9 %collective-permute-start.3 = (f32[2,8,32,128]{3,2,1,0:T(8,128)S(1)}, f32[2,8,32,128]{3,2,1,0:T(8,128)S(1)}, u32[]{:S(2)}, u32[]{:S(2)}) collective-permute-start(f32[2,8,32,128]{3,2,1,0:T(8,128)S(1)} %pad_maximum_fusion.raw.own), channel_id=1, source_target_pairs={{0,2},{2,0},{4,6},{6,4},{8,10},{10,8},{12,14},{14,12},{16,18},{18,... | collective-permute-start | bytes 786440 | tf_op jit(solution)/shard_map/ppermute | solution.py:967
  2.8 6.7 %collective-permute-start.2 = (f32[400,128]{1,0:T(8,128)S(1)}, f32[400,128]{1,0:T(8,128)S(1)}, u32[]{:S(2)}, u32[]{:S(2)}) collective-permute-start(f32[400,128]{1,0:T(8,128)S(1)} %get-tuple-element.63), channel_id=1, source_target_pairs={{0,1},{1,0},{2,3},{3,2},{4,5},{5,4},{6,7},{7,6},{8,9},{9,8},{10,11... | collective-permute-start | bytes 614408 | tf_op jit(solution)/shard_map/ppermute | solution.py:986
  3.1 1.2 %collective-permute-start = (f32[2,32,128]{2,1,0:T(8,128)S(1)}, f32[2,32,128]{2,1,0:T(8,128)S(1)}, u32[]{:S(2)}, u32[]{:S(2)}) collective-permute-start(f32[2,32,128]{2,1,0:T(8,128)S(1)} %get-tuple-element.61), channel_id=1, source_target_pairs={{0,2},{2,0},{4,6},{6,4},{8,10},{10,8},{12,14},{14,12},{16,18},{18,... | collective-permute-start | bytes 98312 | tf_op jit(solution)/shard_map/ppermute | solution.py:967
  4.3 1.7 %copy-start.1 = (bf16[2,256,128]{2,1,0:T(8,128)(2,1)S(1)}, bf16[2,256,128]{2,1,0:T(8,128)(2,1)}, u32[]{:S(2)}) copy-start(bf16[2,256,128]{2,1,0:T(8,128)(2,1)} %constant.42.clone.refs_3_.refs_6_.refs_10_) | copy-start | bytes 393220
  4.3 1.7 %copy-start.2 = (bf16[2,256,128]{2,1,0:T(8,128)(2,1)S(1)}, bf16[2,256,128]{2,1,0:T(8,128)(2,1)}, u32[]{:S(2)}) copy-start(bf16[2,256,128]{2,1,0:T(8,128)(2,1)} %constant.43.clone.refs_4_.refs_7_.refs_11_) | copy-start | bytes 393220
  4.3 1.7 %copy-start.18 = (f32[24,72]{1,0:T(8,128)S(1)}, f32[24,72]{1,0:T(8,128)}, u32[]{:S(2)}) copy-start(f32[24,72]{1,0:T(8,128)} %constant.48.clone.refs_5_) | copy-start | bytes 20740
  4.3 1.7 %copy-start.19 = (f32[24,72]{1,0:T(8,128)S(1)}, f32[24,72]{1,0:T(8,128)}, u32[]{:S(2)}) copy-start(f32[24,72]{1,0:T(8,128)} %constant.49.clone.refs_6_) | copy-start | bytes 20740
  4.5 8.2 %collective-permute-start.1 = (f32[184,128]{1,0:T(8,128)S(1)}, f32[184,128]{1,0:T(8,128)S(1)}, u32[]{:S(2)}, u32[]{:S(2)}) collective-permute-start(f32[184,128]{1,0:T(8,128)S(1)} %get-tuple-element.62), channel_id=1, source_target_pairs={{2,4},{3,5},{4,2},{5,3},{6,8},{7,9},{8,6},{9,7},{10,12},{11,13},{1... | collective-permute-start | bytes 282632 | tf_op jit(solution)/shard_map/ppermute | solution.py:968
  5.7 8.6 %collective-permute-start.4 = (f32[152,128]{1,0:T(8,128)S(1)}, f32[152,128]{1,0:T(8,128)S(1)}, u32[]{:S(2)}, u32[]{:S(2)}) collective-permute-start(f32[152,128]{1,0:T(8,128)S(1)} %get-tuple-element.91), channel_id=1, source_target_pairs={{2,5},{3,4},{4,3},{5,2},{6,9},{7,8},{8,7},{9,6},{10,13},{11,12},{1... | collective-permute-start | bytes 233480 | tf_op jit(solution)/shard_map/ppermute | solution.py:968
  9.5 3.6 %collective-permute-start.7 = (f32[144,128]{1,0:T(8,128)S(1)}, f32[144,128]{1,0:T(8,128)S(1)}, u32[]{:S(2)}, u32[]{:S(2)}) collective-permute-start(f32[144,128]{1,0:T(8,128)S(1)} %slice.11), channel_id=1, source_target_pairs={{0,2},{2,0},{4,6},{6,4},{8,10},{10,8},{12,14},{14,12},{16,18},{18,... | collective-permute-start | bytes 221192 | tf_op jit(solution)/shard_map/ppermute | solution.py:967
  11.6 0.7 %copy-start.11 = (f32[24,72]{1,0:T(8,128)S(1)}, f32[24,72]{1,0:T(8,128)}, u32[]{:S(2)}) copy-start(f32[24,72]{1,0:T(8,128)} %constant.47.clone.refs_2_.refs_4_) | copy-start | bytes 20740
  11.6 1.5 %collective-permute-start.5 = (f32[136,128]{1,0:T(8,128)S(1)}, f32[136,128]{1,0:T(8,128)S(1)}, u32[]{:S(2)}, u32[]{:S(2)}) collective-permute-start(f32[136,128]{1,0:T(8,128)S(1)} %slice.9), channel_id=1, source_target_pairs={{0,2},{2,0},{4,6},{6,4},{8,10},{10,8},{12,14},{14,12},{16,18},{18,... | collective-permute-start | bytes 208904 | tf_op jit(solution)/shard_map/ppermute | solution.py:967
  11.7 1.4 %collective-permute-start.6 = (f32[120,128]{1,0:T(8,128)S(1)}, f32[120,128]{1,0:T(8,128)S(1)}, u32[]{:S(2)}, u32[]{:S(2)}) collective-permute-start(f32[120,128]{1,0:T(8,128)S(1)} %slice.10), channel_id=1, source_target_pairs={{0,2},{2,0},{4,6},{6,4},{8,10},{10,8},{12,14},{14,12},{16,18},{18,... | collective-permute-start | bytes 184328 | tf_op jit(solution)/shard_map/ppermute | solution.py:967
  12.3 0.8 %copy-start.16 = (f32[32,96]{1,0:T(8,128)S(1)}, f32[32,96]{1,0:T(8,128)}, u32[]{:S(2)}) copy-start(f32[32,96]{1,0:T(8,128)} %constant.51.clone.refs_8_) | copy-start | bytes 36868
  12.3 0.8 %copy-start.17 = (f32[32,96]{1,0:T(8,128)S(1)}, f32[32,96]{1,0:T(8,128)}, u32[]{:S(2)}) copy-start(f32[32,96]{1,0:T(8,128)} %constant.52.clone.refs_9_) | copy-start | bytes 36868
  12.6 2.2 %copy-start.4 = (bf16[6,256,128]{2,1,0:T(8,128)(2,1)S(1)}, bf16[6,256,128]{2,1,0:T(8,128)(2,1)}, u32[]{:S(2)}) copy-start(bf16[6,256,128]{2,1,0:T(8,128)(2,1)} %constant.58.clone.mz) | copy-start | bytes 1179652
  12.7 2.1 %copy-start.7 = (bf16[2,256,128]{2,1,0:T(8,128)(2,1)S(1)}, bf16[2,256,128]{2,1,0:T(8,128)(2,1)}, u32[]{:S(2)}) copy-start(bf16[2,256,128]{2,1,0:T(8,128)(2,1)} %constant.56.clone.rz) | copy-start | bytes 393220
  12.7 2.1 %copy-start.15 = (f32[24,168]{1,0:T(8,128)S(1)}, f32[24,168]{1,0:T(8,128)}, u32[]{:S(2)}) copy-start(f32[24,168]{1,0:T(8,128)} %constant.57.clone.my) | copy-start | bytes 48388
  12.7 3.0 %collective-permute-start.8 = (f32[184,128]{1,0:T(8,128)S(1)}, f32[184,128]{1,0:T(8,128)S(1)}, u32[]{:S(2)}, u32[]{:S(2)}) collective-permute-start(f32[184,128]{1,0:T(8,128)S(1)} %collective-permute-done.1.refs_0_), channel_id=1, source_target_pairs={{0,2},{2,0},{4,6},{6,4},{8,10},{10,8},{12,14},{14,12},{16,18},{18,... | collective-permute-start | bytes 282632 | tf_op jit(solution)/shard_map/ppermute | solution.py:967
  13.1 1.7 %copy-start.14 = (f32[8,168]{1,0:T(8,128)S(1)}, f32[8,168]{1,0:T(8,128)}, u32[]{:S(2)}) copy-start(f32[8,168]{1,0:T(8,128)} %constant.54.clone.ry.refs_15_) | copy-start | bytes 16132
  14.4 1.3 %collective-permute-start.9 = (f32[152,128]{1,0:T(8,128)S(1)}, f32[152,128]{1,0:T(8,128)S(1)}, u32[]{:S(2)}, u32[]{:S(2)}) collective-permute-start(f32[152,128]{1,0:T(8,128)S(1)} %collective-permute-done.4.refs_1_), channel_id=1, source_target_pairs={{0,2},{2,0},{4,6},{6,4},{8,10},{10,8},{12,14},{14,12},{16,18},{18,... | collective-permute-start | bytes 233480 | tf_op jit(solution)/shard_map/ppermute | solution.py:967
  14.8 1.0 %copy-start.6 = (bf16[2,512,128]{2,1,0:T(8,128)(2,1)S(1)}, bf16[2,512,128]{2,1,0:T(8,128)(2,1)}, u32[]{:S(2)}) copy-start(bf16[2,512,128]{2,1,0:T(8,128)(2,1)} %constant.55.clone.refs_16_) | copy-start | bytes 786436
  14.8 0.9 %copy-start.9 = (f32[56,168]{1,0:T(8,128)S(1)}, f32[56,168]{1,0:T(8,128)}, u32[]{:S(2)}) copy-start(f32[56,168]{1,0:T(8,128)} %constant.45.clone.refs_12_) | copy-start | bytes 112900
  14.8 0.9 %copy-start.10 = (f32[56,168]{1,0:T(8,128)S(1)}, f32[56,168]{1,0:T(8,128)}, u32[]{:S(2)}) copy-start(f32[56,168]{1,0:T(8,128)} %constant.46.clone.refs_13_) | copy-start | bytes 112900
  14.8 0.9 %copy-start.12 = (f32[10,8,128]{2,1,0:T(8,128)S(1)}, f32[10,8,128]{2,1,0:T(8,128)}, u32[]{:S(2)}) copy-start(f32[10,8,128]{2,1,0:T(8,128)} %constant.61.clone.refs_17_) | copy-start | bytes 122884
  14.9 0.9 %copy-start.13 = (f32[32,168]{1,0:T(8,128)S(1)}, f32[32,168]{1,0:T(8,128)}, u32[]{:S(2)}) copy-start(f32[32,168]{1,0:T(8,128)} %constant.53.clone.refs_14_) | copy-start | bytes 64516
  15.8 5.8 %copy-start.5 = (bf16[2,256,160]{2,1,0:T(8,128)(2,1)S(1)}, bf16[2,256,160]{2,1,0:T(8,128)(2,1)}, u32[]{:S(2)}) copy-start(bf16[2,256,160]{2,1,0:T(8,128)(2,1)} %constant.60.clone.refs_6_) | copy-start | bytes 491524
  15.8 5.8 %copy-start.20 = (f32[2,8,128]{2,1,0:T(8,128)S(1)}, f32[2,8,128]{2,1,0:T(8,128)}, u32[]{:S(2)}) copy-start(f32[2,8,128]{2,1,0:T(8,128)} %constant.59.clone.refs_5_) | copy-start | bytes 24580
  17.3 2.6 %collective-permute-start.10 = (f32[3,8,128]{2,1,0:T(8,128)S(1)}, f32[3,8,128]{2,1,0:T(8,128)S(1)}, u32[]{:S(2)}, u32[]{:S(2)}) collective-permute-start(f32[3,8,128]{2,1,0:T(8,128)S(1)} %get-tuple-element.109), channel_id=1, source_target_pairs={{2,4},{3,5},{4,2},{5,3},{6,8},{7,9},{8,6},{9,7},{10,12},{11,13},{1... | collective-permute-start | bytes 36872 | tf_op jit(solution)/shard_map/ppermute | solution.py:968
  19.9 1.7 %collective-permute-start.11 = (f32[3,8,128]{2,1,0:T(8,128)S(1)}, f32[3,8,128]{2,1,0:T(8,128)S(1)}, u32[]{:S(2)}, u32[]{:S(2)}) collective-permute-start(f32[3,8,128]{2,1,0:T(8,128)S(1)} %collective-permute-done.10.refs_0_), channel_id=1, source_target_pairs={{0,2},{2,0},{4,6},{6,4},{8,10},{10,8},{12,14},{14,12},{16,18},{18,... | collective-permute-start | bytes 36872 | tf_op jit(solution)/shard_map/ppermute | solution.py:967

commit v7 on v6

--- a/solution.py
+++ b/solution.py
@@ -9,7 +9,8 @@
 from jax.sharding import PartitionSpec as P
 
 N = 8
-SPARE = N
+SPARE = 4 * N
+PLANES = 4
 HALO = 3 * N
 THETA = 1.1
 DELTA = 0.9
@@ -120,7 +121,7 @@
     t["z_sq"] = right_table(blockdiag(DM * DM, ez))
     t["y_d"] = left_table(blockdiag(DM, ey))
     t["y_dt"] = left_table(blockdiag(DM, ey).T)
-    for count in range(1, own_y // N + 1):
+    for count in [*range(1, own_y // N + 1), ey]:
         t["y_sq", count] = left_table(blockdiag(DM * DM, count).T)
         t["y_d", count] = left_table(blockdiag(DM, count))
         t["y_dt", count] = left_table(blockdiag(DM, count).T)
@@ -351,7 +352,7 @@
     return 0 if lay.sub == 1 else 1 if lay.sub == 2 else 2
 
 
-def own_kernel(lay, raw, z_sq, y_sq, w3, face, w_out, d_out, r_out, sx_out, *packs):
+def own_kernel(lay, raw, z_sq, y_sq, w3, face, w_out, d_out, r_out, *packs):
     rhs, coef = raw.at[0], raw.at[1]
     y, nz = lay.own_y, lay.nz
     parity, h = lay.where()[:2]
@@ -365,7 +366,6 @@
             d_out[a, rows, :] = dx[a]
     hi, lo = split(w_out[...].reshape(N * y, nz))
     dz = z_apply(hi, lo, z_sq[...])
-    sx_out[...] = assemble_yz(d_out[(N - 1) * parity])
     dy = y_planes(lambda a: w_out[a], list(range(N)), y_sq[...])
     for a in range(N):
         d_out[a] = assemble_yz(d_out[a] + dz[a * y : (a + 1) * y] + dy[a])
@@ -380,7 +380,7 @@
                 pack[pl.ds(side * N + a, 1), :] = field[a, pl.ds(far, 1), :]
 
 
-def message_kernel(lay, w, d, r, sx, face, *refs):
+def message_kernel(lay, w, d, r, face, *refs):
     msg, *side_msgs, u_s, d_s, r_s = refs
     y, nz = lay.own_y, lay.nz
     parity, h, start, offset, low, high = lay.where()
@@ -411,21 +411,20 @@
     outer = (N - 1) * parity
     msg[pl.ds(0, y), :] = r[outer]
     msg[pl.ds(y, y), :] = d[outer]
-    msg[pl.ds(2 * y, y), :] = sx[...]
-    msg[pl.ds(3 * y, y), :] = w[outer]
-    msg[pl.ds(4 * y, y), :] = assemble_yz(jnp.concatenate(acc, axis=0))
-    base = 5 * y
+    msg[pl.ds(2 * y, y), :] = w[outer]
+    msg[pl.ds(3 * y, y), :] = assemble_yz(jnp.concatenate(acc, axis=0))
+    base = PLANES * y
     for row in line_rows(lay, h):
         for field in (r_s, d_s, w):
             for a in range(N):
                 msg[pl.ds(base + a, 1), :] = field[a, pl.ds(row, 1), :]
             base += N
     for out, (first, _) in zip(side_msgs, lay.sent_rows(h)):
-        for k in range(5):
+        for k in range(PLANES):
             out[pl.ds(k * HALO, HALO), :] = msg[aligned(k * y + first, HALO), :]
-        lines = base - 5 * y
-        out[pl.ds(5 * HALO, lines), :] = msg[pl.ds(5 * y, lines), :]
-        out[pl.ds(5 * HALO + lines, SPARE), :] = jnp.zeros((SPARE, nz), F32)
+        lines = base - PLANES * y
+        out[pl.ds(PLANES * HALO, lines), :] = msg[pl.ds(PLANES * y, lines), :]
+        out[pl.ds(PLANES * HALO + lines, SPARE), :] = jnp.zeros((SPARE, nz), F32)
 
 
 def flux_x(lay, u_ref, w_ref, first, count, fx):
@@ -532,13 +531,15 @@
 ARRAYS = 8
 
 
-def early_kernel(lay, own, mate, *refs):
+def early_kernel(lay, own, *refs):
+    mate, refs = refs[:2], refs[2:]
     z_sq, y_sq, w3 = refs[:3]
     tables, outs, scratch = refs[3:7], refs[7 : 7 + ARRAYS], refs[7 + ARRAYS :]
     w, _, d, r, _, inv, u, back = outs
     parity, h, start, offset, low, high = lay.where()
+    own = (own.at[0], own.at[1])
     for base, el, block in ((parity * N, parity, own), ((1 - parity) * N, 1 - parity, mate)):
-        source = lambda side, a, block=block: block[side, a]
+        source = lambda side, a, block=block: block[side][a]
         element_sums(lay, base, el, offset, lay.own_y, source, (z_sq, y_sq, w3), outs)
     sum_middle((d, r), offset, lay.own_y)
     smooth_start(lay, d, r, inv, u, offset, lay.own_y, start)
@@ -691,7 +692,7 @@
 def unpack_sides(lay, pieces, mate_pieces, line, parity, h, start, win):
     y, nz = lay.own_y, lay.nz
     for side, group in ((parity, pieces), (1 - parity, mate_pieces)):
-        for k in range(5):
+        for k in range(PLANES):
 
             def put(rows, value):
                 win[side, k, rows, :] = value
@@ -708,7 +709,7 @@
     for b, begin in enumerate(lay.interfaces(h), 1):
         above, below = pl.ds(begin - 1, 1), pl.ds(begin, 1)
         for side in range(2):
-            for k in range(3):
+            for k in range(2):
                 both = win[side, k, above, :] + win[side, k, below, :]
                 win[side, k, above, :] = both
                 win[side, k, below, :] = both
@@ -717,7 +718,7 @@
 
             def field(k):
                 def of(group):
-                    own_lines, other_lines = 5 * y + k * N, 5 * HALO + k * N
+                    own_lines, other_lines = PLANES * y + k * N, PLANES * HALO + k * N
                     if lay.sub == 2:
                         mine, theirs = own_lines, other_lines
                         near = group[1]
@@ -741,17 +742,17 @@
                 g = term if g is None else g + term
             total = jnp.sum(line[N + side] * (w * g), axis=0, keepdims=True)
             total = total + last * pltpu.roll(total, nz - 1, 1) + first * pltpu.roll(total, 1, 1)
-            win[side, 4, above, :] = total
-            win[side, 4, below, :] = total
+            win[side, 3, above, :] = total
+            win[side, 3, below, :] = total
 
 
 def second_kernel(lay, n_pieces, *refs):
     pieces, mate_pieces = refs[:n_pieces], refs[n_pieces : 2 * n_pieces]
     w_ref, sec_in, lin_in, ends, g_ref, r_ref = refs[2 * n_pieces : 2 * n_pieces + 6]
     refs = refs[2 * n_pieces + 6 :]
-    z_d, z_dt, y_d, y_dt, ry, ry_one, rz, line = refs[:8]
-    out, msg, state = refs[8:11]
-    win, sec, fx, fy, fz = refs[11:]
+    z_d, z_dt, z_sq, y_d, y_dt, y_sq, ry, rz, line = refs[:9]
+    out, msg, state = refs[9:12]
+    win, sec, fx, fy, fz = refs[12:]
     ny, nz, cr = lay.ny, lay.nz, lay.cr
     last = 2 * N - 1
     parity, h, start, offset, low, high = lay.where()
@@ -774,7 +775,7 @@
             value = value + lin_in[max(p, N)] * u[1]
         sec[p] = value
     flux_yz(lay, sec, w_ref, list(range(1, last)), 0, ny, z_d, y_d, fy, fz)
-    weights = [w_ref[0] + win[0, 3], w_ref[last] + win[1, 3]]
+    weights = [w_ref[0] + win[0, 2], w_ref[last] + win[1, 2]]
     hi, lo = split(jnp.concatenate(u, axis=0))
     gz = z_apply(hi, lo, z_d[...])
     gy = y_apply(jnp.concatenate(u, axis=1), y_d[...])
@@ -782,9 +783,14 @@
     weight_y = jnp.concatenate(weights, axis=1)
     bz = z_apply(*split(weight_z * gz), z_dt[...])
     by = y_apply(weight_y * gy, y_dt[...])
+    dz = z_apply(*split(jnp.concatenate([win[0, 2], win[1, 2]], axis=0)), z_sq[...])
+    dy = y_planes(lambda side: win[side, 2], [0, 1], y_sq[...])
+    dx = [
+        win[side, 1] - assemble_yz(dz[side * ny : (side + 1) * ny] + dy[side]) for side in range(2)
+    ]
     for side, p in ((0, 0), (1, last)):
         plane = assemble_yz(bz[side * ny : (side + 1) * ny] + by[:, side * nz : (side + 1) * nz])
-        plane = plane + sec_in[p] + win[side, 4] + (lin_in[p] + win[side, 2]) * u[side]
+        plane = plane + sec_in[p] + win[side, 3] + (lin_in[p] + dx[side]) * u[side]
         res_one = res[side] - inside * plane
         sec[p] = (1.0 + RHO1 * RHO0) * u[side] + (2.0 * RHO1 / DELTA) * inv[side] * res_one
     out[...] = sec[pl.ds(parity * N, N), pl.ds(pl.multiple_of(offset, N), lay.own_y), :]
@@ -969,10 +975,10 @@
     block = (N, own_y, nz)
     raw = jnp.stack([rhs_local, coefficient])
     n_other = 0 if sub == 1 else 1 if sub == 2 else 2
-    face, w, d, r, sx, *packs = run(
+    face, w, d, r, *packs = run(
         functools.partial(own_kernel, lay),
         [raw, t["z_sq"], t["y_sq", own_y // N], t["w3"]],
-        [(2, own_y, nz), block, block, block, (own_y, nz)]
+        [(2, own_y, nz), block, block, block]
         + [(PACK, nz)] * n_other,
     )
     mate_face = even(face)
@@ -984,12 +990,13 @@
         up = [(i, i + 1) for i in range(sub - 1)]
         steps = [up, [(b, a) for a, b in up]]
     others = [lax.ppermute(pack, "sub", step) for pack, step in zip(packs, steps)]
-    mate = even(lax.optimization_barrier((raw, face))[0])
+    raw_later = lax.optimization_barrier((raw, face))[0]
+    mate = [even(raw_later[side]) for side in range(2)]
     lines = 3 * N * line_count(lay)
     msgs = run(
         functools.partial(message_kernel, lay),
-        [w, d, r, sx, mate_face],
-        [(5 * own_y + lines, nz)] + [(5 * HALO + lines + SPARE, nz)] * n_other,
+        [w, d, r, mate_face],
+        [(PLANES * own_y + lines, nz)] + [(PLANES * HALO + lines + SPARE, nz)] * n_other,
         [block] * 3,
     )
     shifts = [0] if sub == 1 else [0, 1] if sub == 2 else [0, 1, -1]
@@ -998,7 +1005,7 @@
     count = lay.early_rows(0)[1] // N
     arrays = run(
         functools.partial(early_kernel, lay),
-        [raw, mate, t["z_sq"], t["y_sq", own_y // N], t["w3"]]
+        [raw, *mate, t["z_sq"], t["y_sq", own_y // N], t["w3"]]
         + [t["z_d"], t["z_dt"], t["y_d", count], t["y_dt", count]],
         [pair] * ARRAYS,
         [(2 * N, count * N, nz)] * 3,
@@ -1033,9 +1040,9 @@
     sec, msg, state = run(
         functools.partial(second_kernel, lay, len(pieces)),
         [*pieces, *mate_pieces, w, sec, lin, ends, g, r]
-        + pick("z_d", "z_dt", "y_d", "y_dt", "ry", "ry_one", "rz", "line"),
+        + pick("z_d", "z_dt", "z_sq", "y_d", "y_dt", ("y_sq", lay.ey), "ry", "rz", "line"),
         [block, (3, cr, nz), (10, cr, nz)],
-        [(2, 5, ny, nz)] + [pair] * 4,
+        [(2, PLANES, ny, nz)] + [pair] * 4,
     )
     from_odd = odd(msg)
     from_mate = even(from_odd)

time: 23.2 us -> 23 us (level); the launches traced: 22.7 us -> 22.8 us
  waiting for transfers between devices: 7.09 us -> 5.35 us
  starting transfers between devices: 7.17 us -> 8.86 us
    ppermute x1, waiting for transfers between devices: 2.64 us -> 0.67 us  [shards(): lax.ppermute(pack, 'sub', step)]
    ppermute x8 -> x9, starting transfers between devices: 5.19 us -> 7.05 us  [shards(): even = lambda v: lax.ppermute(v, 'dom', swap_pairs(dom, 0))]
    ppermute x8 -> x9, waiting for transfers between devices: 2.14 us -> 2.14 us  [shards(): even = lambda v: lax.ppermute(v, 'dom', swap_pairs(dom, 0))]
  transfers between devices with their start and end apart: 12 -> 13, of which waited for: 6 -> 6; matrix products, arithmetic and copies ran while one was open for 0% -> 0% of each run, Pallas kernels for 15% -> 14%
where the time goes in v7:
time: 23 us; the launch traced here: 22.8 us
  starting transfers between devices  8.86 us (39%)
  Pallas kernels  6.29 us (27%)
  waiting for transfers between devices  5.35 us (23%)
  other arithmetic  1.04 us (5%)
  between operations  0.91 us (4%)
  local copies, waits for them, and re-layouts  0.33 us (1%)
    ppermute x9, starting transfers between devices, shards(): even = lambda v: lax.ppermute(v, 'dom', swap_pairs(dom, 0))  7.05 us
    pallas_call x8, Pallas kernels, run(): pl.pallas_call(kernel, out_shape=[jax.ShapeDtypeStruct(o, F32) for o in o...  6.29 us
    ppermute x3, waiting for transfers between devices, shards(): lax.ppermute(v, ('dom', 'sub'), chip_pairs(dom, sub, k))  2.54 us
    ppermute x9, waiting for transfers between devices, shards(): even = lambda v: lax.ppermute(v, 'dom', swap_pairs(dom, 0))  2.14 us
    ppermute x3, starting transfers between devices, shards(): lax.ppermute(v, ('dom', 'sub'), chip_pairs(dom, sub, k))  1.52 us
    another operation x1, other arithmetic, shards(): raw = jnp.stack([rhs_local, coefficient])  1.04 us
    ppermute x1, waiting for transfers between devices, shards(): lax.ppermute(pack, 'sub', step)  0.67 us
  transfers between devices with their start and end apart: 13, of which 6 were waited for; matrix products, arithmetic and copies ran while one was open for 0% of the time, Pallas kernels for 14%

profile of v7, /device:TPU:31, one launch (start us, length us, event | category | flops | bytes accessed | tf_op | source)
XLA Modules:
  0.0 22.8 jit_solution(4762792760341213669)
XLA Ops:
  0.6 0.0 copy-start
  0.6 0.0 copy-start.3
  0.7 0.0 copy-start.8
  0.7 1.0 %pad_maximum_fusion.raw.own = f32[2,8,32,128]{3,2,1,0:T(8,128)S(1)} fusion(f32[1,8,32,128]{3,2,1,0:T(8,128)} %bitcast.6, f32[1,8,32,128]{3,2,1,0:T(8,128)} %bitcast.7), kind=kLoop, calls=%fused_computation | loop fusion | flops 65536 | bytes 524288 | tf_op jit(solution)/shard_map/stack | solution.py:976
  1.7 0.0 copy-done
  1.7 0.0 copy-done.3
  1.7 0.0 copy-done.8
  1.7 0.3 %shard_map.239 = (f32[2,32,128]{2,1,0:T(8,128)S(1)}, f32[8,32,128]{2,1,0:T(8,128)S(1)}, f32[8,32,128]{2,1,0:T(8,128)S(1)}, f32[8,32,128]{2,1,0:T(8,128)S(1)}, f32[400,128]{1,0:T(8,128)S(1)}) custom-call(f32[2,8,32,128]{3,2,1,0:T(8,128)S(1)} %pad_maximum_fusion.raw.own, bf16[2,256,128]{2,1,0:T(8,128)(2,1)S(1)} %copy-done, f32[32,96]{1,0:T(8,128)S(1)} %copy-done.8, ...), custom_call_target="tpu_custom_call" | custom-call | flops 1 | bytes 1 | tf_op jit(solution)/shard_map/pallas_call | solution.py:935
  2.1 0.3 %collective-permute-start.2 = (f32[400,128]{1,0:T(8,128)S(1)}, f32[400,128]{1,0:T(8,128)S(1)}, u32[]{:S(2)}, u32[]{:S(2)}) collective-permute-start(f32[400,128]{1,0:T(8,128)S(1)} %get-tuple-element.61), channel_id=1, source_target_pairs={{0,1},{1,0},{2,3},{3,2},{4,5},{5,4},{6,7},{7,6},{8,9},{9,8},{10,11... | collective-permute-start | bytes 614408 | tf_op jit(solution)/shard_map/ppermute | solution.py:992
  2.4 1.0 %collective-permute-start.3 = (f32[8,32,128]{2,1,0:T(8,128)S(1)}, f32[8,32,128]{2,1,0:T(8,128)S(1)}, u32[]{:S(2)}, u32[]{:S(2)}) collective-permute-start(f32[8,32,128]{2,1,0:T(8,128)S(1)} %get-tuple-element.111), channel_id=1, source_target_pairs={{0,2},{2,0},{4,6},{6,4},{8,10},{10,8},{12,14},{14,12},{16,18},{18,... | collective-permute-start | bytes 393224 | tf_op jit(solution)/shard_map/ppermute | solution.py:973
  3.4 0.1 collective-permute-start.4
  3.5 0.4 %collective-permute-start = (f32[2,32,128]{2,1,0:T(8,128)S(1)}, f32[2,32,128]{2,1,0:T(8,128)S(1)}, u32[]{:S(2)}, u32[]{:S(2)}) collective-permute-start(f32[2,32,128]{2,1,0:T(8,128)S(1)} %get-tuple-element.59), channel_id=1, source_target_pairs={{0,2},{2,0},{4,6},{6,4},{8,10},{10,8},{12,14},{14,12},{16,18},{18,... | collective-permute-start | bytes 98312 | tf_op jit(solution)/shard_map/ppermute | solution.py:973
  3.9 0.9 %collective-permute-done.face = f32[2,32,128]{2,1,0:T(8,128)S(1)} collective-permute-done((f32[2,32,128]{2,1,0:T(8,128)S(1)}, f32[2,32,128]{2,1,0:T(8,128)S(1)}, u32[]{:S(2)}, u32[]{:S(2)}) %collective-permute-start) | collective-permute-done | bytes 32800 | tf_op jit(solution)/shard_map/ppermute | solution.py:973
  4.8 0.2 shard_map.240
  5.0 1.3 %collective-permute-start.1 = (f32[152,128]{1,0:T(8,128)S(1)}, f32[152,128]{1,0:T(8,128)S(1)}, u32[]{:S(2)}, u32[]{:S(2)}) collective-permute-start(f32[152,128]{1,0:T(8,128)S(1)} %get-tuple-element.60), channel_id=1, source_target_pairs={{2,4},{3,5},{4,2},{5,3},{6,8},{7,9},{8,6},{9,7},{10,12},{11,13},{1... | collective-permute-start | bytes 233480 | tf_op jit(solution)/shard_map/ppermute | solution.py:974
  6.3 0.2 collective-permute-start.5
  6.5 0.0 collective-permute-done.3.refs_0_
  6.5 0.0 collective-permute-done.4.refs_1_
  6.5 0.0 copy-done.1
  6.5 0.0 copy-done.2
  6.5 0.0 copy-done.18
  6.5 0.0 copy-done.19
  6.5 0.9 %shard_map.241 = (f32[16,56,128]{2,1,0:T(8,128)S(1)}, f32[16,56,128]{2,1,0:T(8,128)S(1)}, f32[16,56,128]{2,1,0:T(8,128)S(1)}, f32[16,56,128]{2,1,0:T(8,128)S(1)}...) custom-call(f32[2,8,32,128]{3,2,1,0:T(8,128)S(1)} %pad_maximum_fusio, ...), custom_call_target="tpu_custom_call" | custom-call | flops 1 | bytes 1 | tf_op jit(solution)/shard_map/pallas_call | solution.py:935
  7.4 0.7 %collective-permute-done.2.refs_0_ = f32[400,128]{1,0:T(8,128)S(1)} collective-permute-done((f32[400,128]{1,0:T(8,128)S(1)}, f32[400,128]{1,0:T(8,128)S(1)}, u32[]{:S(2)}, u32[]{:S(2)}) %collective-permute-start.2) | collective-permute-done | bytes 204832 | tf_op jit(solution)/shard_map/ppermute | solution.py:992
  8.1 3.5 %collective-permute-start.8 = (f32[144,128]{1,0:T(8,128)S(1)}, f32[144,128]{1,0:T(8,128)S(1)}, u32[]{:S(2)}, u32[]{:S(2)}) collective-permute-start(f32[144,128]{1,0:T(8,128)S(1)} %slice.19), channel_id=1, source_target_pairs={{0,2},{2,0},{4,6},{6,4},{8,10},{10,8},{12,14},{14,12},{16,18},{18,... | collective-permute-start | bytes 221192 | tf_op jit(solution)/shard_map/ppermute | solution.py:973
  11.6 0.1 collective-permute-start.6
  11.7 0.5 %collective-permute-start.7 = (f32[120,128]{1,0:T(8,128)S(1)}, f32[120,128]{1,0:T(8,128)S(1)}, u32[]{:S(2)}, u32[]{:S(2)}) collective-permute-start(f32[120,128]{1,0:T(8,128)S(1)} %slice.18), channel_id=1, source_target_pairs={{0,2},{2,0},{4,6},{6,4},{8,10},{10,8},{12,14},{14,12},{16,18},{18,... | collective-permute-start | bytes 184328 | tf_op jit(solution)/shard_map/ppermute | solution.py:973
  12.2 0.1 copy-done.12
  12.3 0.3 %shard_map.242 = (f32[16,56,128]{2,1,0:T(8,128)S(1)}, f32[16,56,128]{2,1,0:T(8,128)S(1)}, f32[16,56,128]{2,1,0:T(8,128)S(1)}, f32[16,56,128]{2,1,0:T(8,128)S(1)}...) custom-call(f32[400,128]{1,0:T(8,128)S(1)} %collective-permute-done., ...), custom_call_target="tpu_custom_call", output_to_operand_aliasing={{0}: (4, {}), {1}: (5, {}), {2}: (6, {}), {3}: (7, {}), {4}... | custom-call | flops 1 | bytes 1 | tf_op jit(solution)/shard_map/pallas_call | solution.py:935
  12.6 0.0 collective-permute-done.1.refs_0_
  12.6 0.0 copy-start.4
  12.7 0.0 copy-start.7
  12.7 0.0 copy-start.15
  12.7 0.1 collective-permute-start.9
  12.8 0.3 %collective-permute-done.7.refs_1_ = f32[120,128]{1,0:T(8,128)S(1)} collective-permute-done((f32[120,128]{1,0:T(8,128)S(1)}, f32[120,128]{1,0:T(8,128)S(1)}, u32[]{:S(2)}, u32[]{:S(2)}) %collective-permute-start.7) | collective-permute-done | bytes 61472 | tf_op jit(solution)/shard_map/ppermute | solution.py:973
  13.1 0.0 collective-permute-done.6.refs_0_
  13.1 0.0 collective-permute-done.8.refs_2_
  13.1 0.0 copy-done.16
  13.1 0.0 copy-done.17
  13.1 0.0 copy-start.21
  13.1 1.2 %shard_map.243 = (f32[16,56,128]{2,1,0:T(8,128)S(1)}, f32[16,56,128]{2,1,0:T(8,128)S(1)}, f32[16,56,128]{2,1,0:T(8,128)S(1)}, f32[16,56,128]{2,1,0:T(8,128)S(1)}...) custom-call(f32[136,128]{1,0:T(8,128)S(1)} %collective-permute-done., ...), custom_call_target="tpu_custom_call", output_to_operand_aliasing={{0}: (10, {}), {1}: (11, {}), {2}: (12, {}), {3}: (13, {}),... | custom-call | flops 1 | bytes 1 | tf_op jit(solution)/shard_map/pallas_call | solution.py:935
  14.4 0.0 collective-permute-done.5.refs_1_
  14.4 0.4 %collective-permute-start.10 = (f32[152,128]{1,0:T(8,128)S(1)}, f32[152,128]{1,0:T(8,128)S(1)}, u32[]{:S(2)}, u32[]{:S(2)}) collective-permute-start(f32[152,128]{1,0:T(8,128)S(1)} %collective-permute-done.5.refs_1_), channel_id=1, source_target_pairs={{0,2},{2,0},{4,6},{6,4},{8,10},{10,8},{12,14},{14,12},{16,18},{18,... | collective-permute-start | bytes 233480 | tf_op jit(solution)/shard_map/ppermute | solution.py:973
  14.8 0.0 copy-done.4
  14.8 0.0 copy-start.5
  14.8 0.0 copy-start.9
  14.8 0.0 copy-start.10
  14.9 0.0 copy-start.11
  14.9 0.0 copy-start.13
  14.9 0.0 copy-start.14
  14.9 0.8 %shard_map.244 = (f32[2,27,8,128]{3,2,1,0:T(8,128)S(1)}, f32[4,8,128]{2,1,0:T(8,128)S(1)}) custom-call(f32[16,56,128]{2,1,0:T(8,128)S(1)} %get-tuple-element.100.w_ref.refs_4_, f32[16,56,128]{2,1,0:T(8,128)S(1)} %get-tuple-element.104.rhs_ref, f32[24,168]{1,0:T(8,128)S(1)} %copy-done.15, bf16[6,256,128]{2,1,0:T(8,128)(2,1)S(1)} %copy-done.4, ...), custom_call_target="tpu_custom_call" | custom-call | flops 1 | bytes 1 | tf_op jit(solution)/shard_map/pallas_call | solution.py:935
  15.7 0.0 collective-permute-done.9.refs_2_
  15.7 0.1 collective-permute-done.10.refs_3_
  15.7 0.0 copy-done.5
  15.8 0.0 copy-done.9
  15.8 0.0 copy-done.14
  15.8 0.0 copy-start.6
  15.8 0.0 copy-start.20
  15.8 1.6 %shard_map.245 = (f32[8,32,128]{2,1,0:T(8,128)S(1)}, f32[3,8,128]{2,1,0:T(8,128)S(1)}, f32[10,8,128]{2,1,0:T(8,128)S(1)}) custom-call(f32[152,128]{1,0:T(8,128)S(1)} %collective-permute-done.1.refs_0_, f32[152,128]{1,0:T(8,128)S(1)} %collective-permute-done.5.refs_1_, f32[152,128]{1,0:T(8,128)S(1)} %collective-permute-done.9.refs_2_, ...), custom_call_target="tpu_custom_call" | custom-call | flops 1 | bytes 1 | tf_op jit(solution)/shard_map/pallas_call | solution.py:935
  17.4 0.0 collective-permute-start.11
  17.4 2.5 %collective-permute-done.11.refs_0_ = f32[3,8,128]{2,1,0:T(8,128)S(1)} collective-permute-done((f32[3,8,128]{2,1,0:T(8,128)S(1)}, f32[3,8,128]{2,1,0:T(8,128)S(1)}, u32[]{:S(2)}, u32[]{:S(2)}) %collective-permute-start.11) | collective-permute-done | bytes 12320 | tf_op jit(solution)/shard_map/ppermute | solution.py:974
  19.9 0.9 %collective-permute-start.12 = (f32[3,8,128]{2,1,0:T(8,128)S(1)}, f32[3,8,128]{2,1,0:T(8,128)S(1)}, u32[]{:S(2)}, u32[]{:S(2)}) collective-permute-start(f32[3,8,128]{2,1,0:T(8,128)S(1)} %collective-permute-done.11.refs_0_), channel_id=1, source_target_pairs={{0,2},{2,0},{4,6},{6,4},{8,10},{10,8},{12,14},{14,12},{16,18},{18,... | collective-permute-start | bytes 36872 | tf_op jit(solution)/shard_map/ppermute | solution.py:973
  20.8 0.8 %collective-permute-done.12.refs_1_ = f32[3,8,128]{2,1,0:T(8,128)S(1)} collective-permute-done((f32[3,8,128]{2,1,0:T(8,128)S(1)}, f32[3,8,128]{2,1,0:T(8,128)S(1)}, u32[]{:S(2)}, u32[]{:S(2)}) %collective-permute-start.12) | collective-permute-done | bytes 12320 | tf_op jit(solution)/shard_map/ppermute | solution.py:973
  21.7 1.1 %shard_map.246 = (f32[8,32,128]{2,1,0:T(8,128)}, f32[2,8,32]{2,1,0:T(8,128)}) custom-call(f32[3,8,128]{2,1,0:T(8,128)S(1)} %collective-permute-done.11.refs_0_, f32[3,8,128]{2,1,0:T(8,128)S(1)} %collective-permute-done.12.refs_1_, f32[8,32,128]{2,1,0:T(8,128)S(1)} %get-tuple-element.108.refs_2_, f32[10,8,128]{2,1,0:T(8,128)S(1)} %get-tuple-element.109.refs_3_, ...), custom_call_target="tpu_custom_call" | custom-call | flops 1 | bytes 1 | tf_op jit(solution)/shard_map/pallas_call | solution.py:935
  (19 shorter events, 0.1 us)
Async XLA Ops:
  0.6 1.1 %copy-start = (bf16[2,256,128]{2,1,0:T(8,128)(2,1)S(1)}, bf16[2,256,128]{2,1,0:T(8,128)(2,1)}, u32[]{:S(2)}) copy-start(bf16[2,256,128]{2,1,0:T(8,128)(2,1)} %constant.46.clone.z_sq.refs_2_.refs_1_.refs_3_.refs_12_) | copy-start | bytes 393220
  0.6 1.1 %copy-start.3 = (f32[8,8,128]{2,1,0:T(8,128)S(1)}, f32[8,8,128]{2,1,0:T(8,128)}, u32[]{:S(2)}) copy-start(f32[8,8,128]{2,1,0:T(8,128)} %constant.65.clone.w3.refs_4_.refs_3_.refs_5_) | copy-start | bytes 98308
  0.7 1.1 %copy-start.8 = (f32[32,96]{1,0:T(8,128)S(1)}, f32[32,96]{1,0:T(8,128)}, u32[]{:S(2)}) copy-start(f32[32,96]{1,0:T(8,128)} %constant.52.clone.y_sq.refs_3_) | copy-start | bytes 36868
  2.1 6.0 %collective-permute-start.2 = (f32[400,128]{1,0:T(8,128)S(1)}, f32[400,128]{1,0:T(8,128)S(1)}, u32[]{:S(2)}, u32[]{:S(2)}) collective-permute-start(f32[400,128]{1,0:T(8,128)S(1)} %get-tuple-element.61), channel_id=1, source_target_pairs={{0,1},{1,0},{2,3},{3,2},{4,5},{5,4},{6,7},{7,6},{8,9},{9,8},{10,11... | collective-permute-start | bytes 614408 | tf_op jit(solution)/shard_map/ppermute | solution.py:992
  2.4 4.1 %collective-permute-start.3 = (f32[8,32,128]{2,1,0:T(8,128)S(1)}, f32[8,32,128]{2,1,0:T(8,128)S(1)}, u32[]{:S(2)}, u32[]{:S(2)}) collective-permute-start(f32[8,32,128]{2,1,0:T(8,128)S(1)} %get-tuple-element.111), channel_id=1, source_target_pairs={{0,2},{2,0},{4,6},{6,4},{8,10},{10,8},{12,14},{14,12},{16,18},{18,... | collective-permute-start | bytes 393224 | tf_op jit(solution)/shard_map/ppermute | solution.py:973
  3.4 3.1 %collective-permute-start.4 = (f32[8,32,128]{2,1,0:T(8,128)S(1)}, f32[8,32,128]{2,1,0:T(8,128)S(1)}, u32[]{:S(2)}, u32[]{:S(2)}) collective-permute-start(f32[8,32,128]{2,1,0:T(8,128)S(1)} %get-tuple-element.110), channel_id=1, source_target_pairs={{0,2},{2,0},{4,6},{6,4},{8,10},{10,8},{12,14},{14,12},{16,18},{18,... | collective-permute-start | bytes 393224 | tf_op jit(solution)/shard_map/ppermute | solution.py:973
  3.5 1.3 %collective-permute-start = (f32[2,32,128]{2,1,0:T(8,128)S(1)}, f32[2,32,128]{2,1,0:T(8,128)S(1)}, u32[]{:S(2)}, u32[]{:S(2)}) collective-permute-start(f32[2,32,128]{2,1,0:T(8,128)S(1)} %get-tuple-element.59), channel_id=1, source_target_pairs={{0,2},{2,0},{4,6},{6,4},{8,10},{10,8},{12,14},{14,12},{16,18},{18,... | collective-permute-start | bytes 98312 | tf_op jit(solution)/shard_map/ppermute | solution.py:973
  4.8 1.7 %copy-start.1 = (bf16[2,256,128]{2,1,0:T(8,128)(2,1)S(1)}, bf16[2,256,128]{2,1,0:T(8,128)(2,1)}, u32[]{:S(2)}) copy-start(bf16[2,256,128]{2,1,0:T(8,128)(2,1)} %constant.44.clone.refs_5_.refs_6_.refs_10_) | copy-start | bytes 393220
  4.8 1.7 %copy-start.2 = (bf16[2,256,128]{2,1,0:T(8,128)(2,1)S(1)}, bf16[2,256,128]{2,1,0:T(8,128)(2,1)}, u32[]{:S(2)}) copy-start(bf16[2,256,128]{2,1,0:T(8,128)(2,1)} %constant.45.clone.refs_6_.refs_7_.refs_11_) | copy-start | bytes 393220
  4.8 1.7 %copy-start.18 = (f32[24,72]{1,0:T(8,128)S(1)}, f32[24,72]{1,0:T(8,128)}, u32[]{:S(2)}) copy-start(f32[24,72]{1,0:T(8,128)} %constant.50.clone.refs_7_) | copy-start | bytes 20740
  4.8 1.7 %copy-start.19 = (f32[24,72]{1,0:T(8,128)S(1)}, f32[24,72]{1,0:T(8,128)}, u32[]{:S(2)}) copy-start(f32[24,72]{1,0:T(8,128)} %constant.51.clone.refs_8_) | copy-start | bytes 20740
  5.0 7.6 %collective-permute-start.1 = (f32[152,128]{1,0:T(8,128)S(1)}, f32[152,128]{1,0:T(8,128)S(1)}, u32[]{:S(2)}, u32[]{:S(2)}) collective-permute-start(f32[152,128]{1,0:T(8,128)S(1)} %get-tuple-element.60), channel_id=1, source_target_pairs={{2,4},{3,5},{4,2},{5,3},{6,8},{7,9},{8,6},{9,7},{10,12},{11,13},{1... | collective-permute-start | bytes 233480 | tf_op jit(solution)/shard_map/ppermute | solution.py:974
  6.3 8.1 %collective-permute-start.5 = (f32[152,128]{1,0:T(8,128)S(1)}, f32[152,128]{1,0:T(8,128)S(1)}, u32[]{:S(2)}, u32[]{:S(2)}) collective-permute-start(f32[152,128]{1,0:T(8,128)S(1)} %get-tuple-element.89), channel_id=1, source_target_pairs={{2,5},{3,4},{4,3},{5,2},{6,9},{7,8},{8,7},{9,6},{10,13},{11,12},{1... | collective-permute-start | bytes 233480 | tf_op jit(solution)/shard_map/ppermute | solution.py:974
  8.1 5.0 %collective-permute-start.8 = (f32[144,128]{1,0:T(8,128)S(1)}, f32[144,128]{1,0:T(8,128)S(1)}, u32[]{:S(2)}, u32[]{:S(2)}) collective-permute-start(f32[144,128]{1,0:T(8,128)S(1)} %slice.19), channel_id=1, source_target_pairs={{0,2},{2,0},{4,6},{6,4},{8,10},{10,8},{12,14},{14,12},{16,18},{18,... | collective-permute-start | bytes 221192 | tf_op jit(solution)/shard_map/ppermute | solution.py:973
  11.6 0.7 %copy-start.12 = (f32[24,72]{1,0:T(8,128)S(1)}, f32[24,72]{1,0:T(8,128)}, u32[]{:S(2)}) copy-start(f32[24,72]{1,0:T(8,128)} %constant.49.clone.refs_2_.refs_4_) | copy-start | bytes 20740
  11.6 1.5 %collective-permute-start.6 = (f32[136,128]{1,0:T(8,128)S(1)}, f32[136,128]{1,0:T(8,128)S(1)}, u32[]{:S(2)}, u32[]{:S(2)}) collective-permute-start(f32[136,128]{1,0:T(8,128)S(1)} %slice.17), channel_id=1, source_target_pairs={{0,2},{2,0},{4,6},{6,4},{8,10},{10,8},{12,14},{14,12},{16,18},{18,... | collective-permute-start | bytes 208904 | tf_op jit(solution)/shard_map/ppermute | solution.py:973
  11.7 1.4 %collective-permute-start.7 = (f32[120,128]{1,0:T(8,128)S(1)}, f32[120,128]{1,0:T(8,128)S(1)}, u32[]{:S(2)}, u32[]{:S(2)}) collective-permute-start(f32[120,128]{1,0:T(8,128)S(1)} %slice.18), channel_id=1, source_target_pairs={{0,2},{2,0},{4,6},{6,4},{8,10},{10,8},{12,14},{14,12},{16,18},{18,... | collective-permute-start | bytes 184328 | tf_op jit(solution)/shard_map/ppermute | solution.py:973
  12.3 0.8 %copy-start.16 = (f32[32,96]{1,0:T(8,128)S(1)}, f32[32,96]{1,0:T(8,128)}, u32[]{:S(2)}) copy-start(f32[32,96]{1,0:T(8,128)} %constant.53.clone.refs_8_) | copy-start | bytes 36868
  12.3 0.8 %copy-start.17 = (f32[32,96]{1,0:T(8,128)S(1)}, f32[32,96]{1,0:T(8,128)}, u32[]{:S(2)}) copy-start(f32[32,96]{1,0:T(8,128)} %constant.54.clone.refs_9_) | copy-start | bytes 36868
  12.6 2.2 %copy-start.4 = (bf16[6,256,128]{2,1,0:T(8,128)(2,1)S(1)}, bf16[6,256,128]{2,1,0:T(8,128)(2,1)}, u32[]{:S(2)}) copy-start(bf16[6,256,128]{2,1,0:T(8,128)(2,1)} %constant.61.clone.mz) | copy-start | bytes 1179652
  12.7 2.2 %copy-start.7 = (bf16[2,256,128]{2,1,0:T(8,128)(2,1)S(1)}, bf16[2,256,128]{2,1,0:T(8,128)(2,1)}, u32[]{:S(2)}) copy-start(bf16[2,256,128]{2,1,0:T(8,128)(2,1)} %constant.59.clone.rz) | copy-start | bytes 393220
  12.7 2.1 %copy-start.15 = (f32[24,168]{1,0:T(8,128)S(1)}, f32[24,168]{1,0:T(8,128)}, u32[]{:S(2)}) copy-start(f32[24,168]{1,0:T(8,128)} %constant.60.clone.my) | copy-start | bytes 48388
  12.7 3.0 %collective-permute-start.9 = (f32[152,128]{1,0:T(8,128)S(1)}, f32[152,128]{1,0:T(8,128)S(1)}, u32[]{:S(2)}, u32[]{:S(2)}) collective-permute-start(f32[152,128]{1,0:T(8,128)S(1)} %collective-permute-done.1.refs_0_), channel_id=1, source_target_pairs={{0,2},{2,0},{4,6},{6,4},{8,10},{10,8},{12,14},{14,12},{16,18},{18,... | collective-permute-start | bytes 233480 | tf_op jit(solution)/shard_map/ppermute | solution.py:973
  13.1 1.7 %copy-start.21 = (f32[8,168]{1,0:T(8,128)S(1)}, f32[8,168]{1,0:T(8,128)}, u32[]{:S(2)}) copy-start(f32[8,168]{1,0:T(8,128)} %constant.57.clone.ry) | copy-start | bytes 16132
  14.4 1.3 %collective-permute-start.10 = (f32[152,128]{1,0:T(8,128)S(1)}, f32[152,128]{1,0:T(8,128)S(1)}, u32[]{:S(2)}, u32[]{:S(2)}) collective-permute-start(f32[152,128]{1,0:T(8,128)S(1)} %collective-permute-done.5.refs_1_), channel_id=1, source_target_pairs={{0,2},{2,0},{4,6},{6,4},{8,10},{10,8},{12,14},{14,12},{16,18},{18,... | collective-permute-start | bytes 233480 | tf_op jit(solution)/shard_map/ppermute | solution.py:973
  14.8 1.0 %copy-start.5 = (bf16[2,512,128]{2,1,0:T(8,128)(2,1)S(1)}, bf16[2,512,128]{2,1,0:T(8,128)(2,1)}, u32[]{:S(2)}) copy-start(bf16[2,512,128]{2,1,0:T(8,128)(2,1)} %constant.58.clone.refs_17_) | copy-start | bytes 786436
  14.8 0.9 %copy-start.9 = (f32[56,168]{1,0:T(8,128)S(1)}, f32[56,168]{1,0:T(8,128)}, u32[]{:S(2)}) copy-start(f32[56,168]{1,0:T(8,128)} %constant.47.clone.refs_13_) | copy-start | bytes 112900
  14.8 0.9 %copy-start.10 = (f32[56,168]{1,0:T(8,128)S(1)}, f32[56,168]{1,0:T(8,128)}, u32[]{:S(2)}) copy-start(f32[56,168]{1,0:T(8,128)} %constant.48.clone.refs_14_) | copy-start | bytes 112900
  14.9 0.9 %copy-start.11 = (f32[56,168]{1,0:T(8,128)S(1)}, f32[56,168]{1,0:T(8,128)}, u32[]{:S(2)}) copy-start(f32[56,168]{1,0:T(8,128)} %constant.55.clone.refs_15_) | copy-start | bytes 112900
  14.9 0.9 %copy-start.13 = (f32[10,8,128]{2,1,0:T(8,128)S(1)}, f32[10,8,128]{2,1,0:T(8,128)}, u32[]{:S(2)}) copy-start(f32[10,8,128]{2,1,0:T(8,128)} %constant.64.clone.refs_18_) | copy-start | bytes 122884
  14.9 0.9 %copy-start.14 = (f32[32,168]{1,0:T(8,128)S(1)}, f32[32,168]{1,0:T(8,128)}, u32[]{:S(2)}) copy-start(f32[32,168]{1,0:T(8,128)} %constant.56.clone.refs_16_) | copy-start | bytes 64516
  15.8 5.9 %copy-start.6 = (bf16[2,256,160]{2,1,0:T(8,128)(2,1)S(1)}, bf16[2,256,160]{2,1,0:T(8,128)(2,1)}, u32[]{:S(2)}) copy-start(bf16[2,256,160]{2,1,0:T(8,128)(2,1)} %constant.63.clone.refs_6_) | copy-start | bytes 491524
  15.8 5.9 %copy-start.20 = (f32[2,8,128]{2,1,0:T(8,128)S(1)}, f32[2,8,128]{2,1,0:T(8,128)}, u32[]{:S(2)}) copy-start(f32[2,8,128]{2,1,0:T(8,128)} %constant.62.clone.refs_5_) | copy-start | bytes 24580
  17.4 2.6 %collective-permute-start.11 = (f32[3,8,128]{2,1,0:T(8,128)S(1)}, f32[3,8,128]{2,1,0:T(8,128)S(1)}, u32[]{:S(2)}, u32[]{:S(2)}) collective-permute-start(f32[3,8,128]{2,1,0:T(8,128)S(1)} %get-tuple-element.107), channel_id=1, source_target_pairs={{2,4},{3,5},{4,2},{5,3},{6,8},{7,9},{8,6},{9,7},{10,12},{11,13},{1... | collective-permute-start | bytes 36872 | tf_op jit(solution)/shard_map/ppermute | solution.py:974
  19.9 1.7 %collective-permute-start.12 = (f32[3,8,128]{2,1,0:T(8,128)S(1)}, f32[3,8,128]{2,1,0:T(8,128)S(1)}, u32[]{:S(2)}, u32[]{:S(2)}) collective-permute-start(f32[3,8,128]{2,1,0:T(8,128)S(1)} %collective-permute-done.11.refs_0_), channel_id=1, source_target_pairs={{0,2},{2,0},{4,6},{6,4},{8,10},{10,8},{12,14},{14,12},{16,18},{18,... | collective-permute-start | bytes 36872 | tf_op jit(solution)/shard_map/ppermute | solution.py:973

commit v8 on v7

--- a/solution.py
+++ b/solution.py
@@ -259,20 +259,18 @@
         return parity, h, start, offset, low, high
 
     def sent_rows(self, h):
-        y = self.own_y
-        down = (y - HALO, y - HALO)
-        up = (0, HALO - 1)
+        down = self.own_y - HALO
         if self.sub == 1:
             return []
         if self.sub == 2:
-            return [tuple(h * u + (1 - h) * v for u, v in zip(up, down))]
-        return [down, up]
+            return [((1 - h) * down, (down, HALO - 1))]
+        return [(down, down), (0, HALO - 1)]
 
     def far_rows(self, h):
         if self.sub == 1:
             return []
         if self.sub == 2:
-            return [(1 - h) * (self.ny - 1)]
+            return [(self.ny - 1, 0)]
         return [0, self.ny - 1]
 
     def other_starts(self, h):
@@ -344,8 +342,23 @@
     if lay.sub == 1:
         return []
     if lay.sub == 2:
-        return [(lay.own_y - 1) * (1 - h)]
+        return [(lay.own_y - 1, 0)]
     return [0, lay.own_y - 1]
+
+
+def load_row(field, a, row, h):
+    if isinstance(row, int):
+        return field[a, pl.ds(row, 1), :]
+    first, second = (field[a, pl.ds(r, 1), :] for r in row)
+    return jnp.where(h == 0, first, second)
+
+
+def store_row(field, a, row, h, value):
+    if isinstance(row, int):
+        field[a, pl.ds(row, 1), :] = value
+        return
+    for k, r in enumerate(row):
+        field[a, pl.ds(r, 1), :] = jnp.where(h == k, value, field[a, pl.ds(r, 1), :])
 
 
 def line_count(lay):
@@ -377,7 +390,7 @@
         for side, field in ((0, r_out), (1, d_out)):
             for a in range(N):
                 pack[pack_rows(side, a), :] = raw[side, a, aligned(first, HALO), :]
-                pack[pl.ds(side * N + a, 1), :] = field[a, pl.ds(far, 1), :]
+                pack[pl.ds(side * N + a, 1), :] = load_row(field, a, far, h)
 
 
 def message_kernel(lay, w, d, r, face, *refs):
@@ -417,7 +430,7 @@
     for row in line_rows(lay, h):
         for field in (r_s, d_s, w):
             for a in range(N):
-                msg[pl.ds(base + a, 1), :] = field[a, pl.ds(row, 1), :]
+                msg[pl.ds(base + a, 1), :] = load_row(field, a, row, h)
             base += N
     for out, (first, _) in zip(side_msgs, lay.sent_rows(h)):
         for k in range(PLANES):
@@ -525,7 +538,7 @@
         element_sums(lay, base, parity, first, HALO, source, tables, outs)
         for side, target in ((0, r_s), (1, d_s)):
             for a in range(N):
-                target[base + a, pl.ds(row, 1), :] = piece[pl.ds(side * N + a, 1)]
+                store_row(target, base + a, row, h, piece[pl.ds(side * N + a, 1)])
 
 
 ARRAYS = 8

time: 23 us -> 23.1 us (level)
  transfers between devices with their start and end apart: 13 -> 13, of which waited for: 6 -> 6; matrix products, arithmetic and copies ran while one was open for 0% -> 0% of each run, Pallas kernels for 14% -> 15%
where the time goes in v8:
time: 23.1 us; the launch traced here: 22.8 us
  starting transfers between devices  8.85 us (38%)
  Pallas kernels  6.36 us (28%)
  waiting for transfers between devices  5.35 us (23%)
  other arithmetic  1.04 us (5%)
  between operations  0.91 us (4%)
  local copies, waits for them, and re-layouts  0.33 us (1%)
    ppermute x9, starting transfers between devices, shards(): even = lambda v: lax.ppermute(v, 'dom', swap_pairs(dom, 0))  7.04 us
    pallas_call x8, Pallas kernels, run(): pl.pallas_call(kernel, out_shape=[jax.ShapeDtypeStruct(o, F32) for o in o...  6.36 us
    ppermute x3, waiting for transfers between devices, shards(): lax.ppermute(v, ('dom', 'sub'), chip_pairs(dom, sub, k))  2.54 us
    ppermute x9, waiting for transfers between devices, shards(): even = lambda v: lax.ppermute(v, 'dom', swap_pairs(dom, 0))  2.13 us
    ppermute x3, starting transfers between devices, shards(): lax.ppermute(v, ('dom', 'sub'), chip_pairs(dom, sub, k))  1.51 us
    another operation x1, other arithmetic, shards(): raw = jnp.stack([rhs_local, coefficient])  1.04 us
    ppermute x1, waiting for transfers between devices, shards(): lax.ppermute(pack, 'sub', step)  0.68 us
  transfers between devices with their start and end apart: 13, of which 6 were waited for; matrix products, arithmetic and copies ran while one was open for 0% of the time, Pallas kernels for 15%

profile of v8, /device:TPU:31, one launch (start us, length us, event | category | flops | bytes accessed | tf_op | source)
XLA Modules:
  0.0 22.8 jit_solution(3250911106674573471)
XLA Ops:
  0.6 0.0 copy-start
  0.6 0.0 copy-start.3
  0.7 0.0 copy-start.8
  0.7 1.0 %pad_maximum_fusion.raw.own = f32[2,8,32,128]{3,2,1,0:T(8,128)S(1)} fusion(f32[1,8,32,128]{3,2,1,0:T(8,128)} %bitcast.6, f32[1,8,32,128]{3,2,1,0:T(8,128)} %bitcast.7), kind=kLoop, calls=%fused_computation | loop fusion | flops 65536 | bytes 524288 | tf_op jit(solution)/shard_map/stack | solution.py:989
  1.7 0.0 copy-done
  1.7 0.0 copy-done.3
  1.7 0.0 copy-done.8
  1.7 0.3 %shard_map.239 = (f32[2,32,128]{2,1,0:T(8,128)S(1)}, f32[8,32,128]{2,1,0:T(8,128)S(1)}, f32[8,32,128]{2,1,0:T(8,128)S(1)}, f32[8,32,128]{2,1,0:T(8,128)S(1)}, f32[400,128]{1,0:T(8,128)S(1)}) custom-call(f32[2,8,32,128]{3,2,1,0:T(8,128)S(1)} %pad_maximum_fusion.raw.own, bf16[2,256,128]{2,1,0:T(8,128)(2,1)S(1)} %copy-done, f32[32,96]{1,0:T(8,128)S(1)} %copy-done.8, ...), custom_call_target="tpu_custom_call" | custom-call | flops 1 | bytes 1 | tf_op jit(solution)/shard_map/pallas_call | solution.py:948
  2.1 0.3 %collective-permute-start.2 = (f32[400,128]{1,0:T(8,128)S(1)}, f32[400,128]{1,0:T(8,128)S(1)}, u32[]{:S(2)}, u32[]{:S(2)}) collective-permute-start(f32[400,128]{1,0:T(8,128)S(1)} %get-tuple-element.61), channel_id=1, source_target_pairs={{0,1},{1,0},{2,3},{3,2},{4,5},{5,4},{6,7},{7,6},{8,9},{9,8},{10,11... | collective-permute-start | bytes 614408 | tf_op jit(solution)/shard_map/ppermute | solution.py:1005
  2.4 1.0 %collective-permute-start.3 = (f32[8,32,128]{2,1,0:T(8,128)S(1)}, f32[8,32,128]{2,1,0:T(8,128)S(1)}, u32[]{:S(2)}, u32[]{:S(2)}) collective-permute-start(f32[8,32,128]{2,1,0:T(8,128)S(1)} %get-tuple-element.111), channel_id=1, source_target_pairs={{0,2},{2,0},{4,6},{6,4},{8,10},{10,8},{12,14},{14,12},{16,18},{18,... | collective-permute-start | bytes 393224 | tf_op jit(solution)/shard_map/ppermute | solution.py:986
  3.4 0.1 collective-permute-start.4
  3.5 0.4 %collective-permute-start = (f32[2,32,128]{2,1,0:T(8,128)S(1)}, f32[2,32,128]{2,1,0:T(8,128)S(1)}, u32[]{:S(2)}, u32[]{:S(2)}) collective-permute-start(f32[2,32,128]{2,1,0:T(8,128)S(1)} %get-tuple-element.59), channel_id=1, source_target_pairs={{0,2},{2,0},{4,6},{6,4},{8,10},{10,8},{12,14},{14,12},{16,18},{18,... | collective-permute-start | bytes 98312 | tf_op jit(solution)/shard_map/ppermute | solution.py:986
  3.9 0.9 %collective-permute-done.face = f32[2,32,128]{2,1,0:T(8,128)S(1)} collective-permute-done((f32[2,32,128]{2,1,0:T(8,128)S(1)}, f32[2,32,128]{2,1,0:T(8,128)S(1)}, u32[]{:S(2)}, u32[]{:S(2)}) %collective-permute-start) | collective-permute-done | bytes 32800 | tf_op jit(solution)/shard_map/ppermute | solution.py:986
  4.8 0.2 shard_map.240
  5.0 1.3 %collective-permute-start.1 = (f32[152,128]{1,0:T(8,128)S(1)}, f32[152,128]{1,0:T(8,128)S(1)}, u32[]{:S(2)}, u32[]{:S(2)}) collective-permute-start(f32[152,128]{1,0:T(8,128)S(1)} %get-tuple-element.60), channel_id=1, source_target_pairs={{2,4},{3,5},{4,2},{5,3},{6,8},{7,9},{8,6},{9,7},{10,12},{11,13},{1... | collective-permute-start | bytes 233480 | tf_op jit(solution)/shard_map/ppermute | solution.py:987
  6.3 0.2 collective-permute-start.5
  6.5 0.0 collective-permute-done.3.refs_0_
  6.5 0.0 collective-permute-done.4.refs_1_
  6.5 0.0 copy-done.1
  6.5 0.0 copy-done.2
  6.5 0.0 copy-done.18
  6.5 0.0 copy-done.19
  6.5 0.9 %shard_map.241 = (f32[16,56,128]{2,1,0:T(8,128)S(1)}, f32[16,56,128]{2,1,0:T(8,128)S(1)}, f32[16,56,128]{2,1,0:T(8,128)S(1)}, f32[16,56,128]{2,1,0:T(8,128)S(1)}...) custom-call(f32[2,8,32,128]{3,2,1,0:T(8,128)S(1)} %pad_maximum_fusio, ...), custom_call_target="tpu_custom_call" | custom-call | flops 1 | bytes 1 | tf_op jit(solution)/shard_map/pallas_call | solution.py:948
  7.4 0.7 %collective-permute-done.2.refs_0_ = f32[400,128]{1,0:T(8,128)S(1)} collective-permute-done((f32[400,128]{1,0:T(8,128)S(1)}, f32[400,128]{1,0:T(8,128)S(1)}, u32[]{:S(2)}, u32[]{:S(2)}) %collective-permute-start.2) | collective-permute-done | bytes 204832 | tf_op jit(solution)/shard_map/ppermute | solution.py:1005
  8.1 3.5 %collective-permute-start.8 = (f32[144,128]{1,0:T(8,128)S(1)}, f32[144,128]{1,0:T(8,128)S(1)}, u32[]{:S(2)}, u32[]{:S(2)}) collective-permute-start(f32[144,128]{1,0:T(8,128)S(1)} %slice.19), channel_id=1, source_target_pairs={{0,2},{2,0},{4,6},{6,4},{8,10},{10,8},{12,14},{14,12},{16,18},{18,... | collective-permute-start | bytes 221192 | tf_op jit(solution)/shard_map/ppermute | solution.py:986
  11.6 0.1 collective-permute-start.6
  11.7 0.5 %collective-permute-start.7 = (f32[120,128]{1,0:T(8,128)S(1)}, f32[120,128]{1,0:T(8,128)S(1)}, u32[]{:S(2)}, u32[]{:S(2)}) collective-permute-start(f32[120,128]{1,0:T(8,128)S(1)} %slice.18), channel_id=1, source_target_pairs={{0,2},{2,0},{4,6},{6,4},{8,10},{10,8},{12,14},{14,12},{16,18},{18,... | collective-permute-start | bytes 184328 | tf_op jit(solution)/shard_map/ppermute | solution.py:986
  12.2 0.1 copy-done.12
  12.3 0.3 %shard_map.242 = (f32[16,56,128]{2,1,0:T(8,128)S(1)}, f32[16,56,128]{2,1,0:T(8,128)S(1)}, f32[16,56,128]{2,1,0:T(8,128)S(1)}, f32[16,56,128]{2,1,0:T(8,128)S(1)}...) custom-call(f32[400,128]{1,0:T(8,128)S(1)} %collective-permute-done., ...), custom_call_target="tpu_custom_call", output_to_operand_aliasing={{0}: (4, {}), {1}: (5, {}), {2}: (6, {}), {3}: (7, {}), {4}... | custom-call | flops 1 | bytes 1 | tf_op jit(solution)/shard_map/pallas_call | solution.py:948
  12.7 0.0 collective-permute-done.1.refs_0_
  12.7 0.0 copy-start.4
  12.7 0.0 copy-start.7
  12.7 0.0 copy-start.15
  12.7 0.1 collective-permute-start.9
  12.8 0.3 %collective-permute-done.7.refs_1_ = f32[120,128]{1,0:T(8,128)S(1)} collective-permute-done((f32[120,128]{1,0:T(8,128)S(1)}, f32[120,128]{1,0:T(8,128)S(1)}, u32[]{:S(2)}, u32[]{:S(2)}) %collective-permute-start.7) | collective-permute-done | bytes 61472 | tf_op jit(solution)/shard_map/ppermute | solution.py:986
  13.1 0.0 collective-permute-done.6.refs_0_
  13.1 0.0 collective-permute-done.8.refs_2_
  13.1 0.0 copy-done.16
  13.1 0.0 copy-done.17
  13.1 0.0 copy-start.21
  13.2 1.3 %shard_map.243 = (f32[16,56,128]{2,1,0:T(8,128)S(1)}, f32[16,56,128]{2,1,0:T(8,128)S(1)}, f32[16,56,128]{2,1,0:T(8,128)S(1)}, f32[16,56,128]{2,1,0:T(8,128)S(1)}...) custom-call(f32[136,128]{1,0:T(8,128)S(1)} %collective-permute-done., ...), custom_call_target="tpu_custom_call", output_to_operand_aliasing={{0}: (10, {}), {1}: (11, {}), {2}: (12, {}), {3}: (13, {}),... | custom-call | flops 1 | bytes 1 | tf_op jit(solution)/shard_map/pallas_call | solution.py:948
  14.4 0.0 collective-permute-done.5.refs_1_
  14.4 0.4 %collective-permute-start.10 = (f32[152,128]{1,0:T(8,128)S(1)}, f32[152,128]{1,0:T(8,128)S(1)}, u32[]{:S(2)}, u32[]{:S(2)}) collective-permute-start(f32[152,128]{1,0:T(8,128)S(1)} %collective-permute-done.5.refs_1_), channel_id=1, source_target_pairs={{0,2},{2,0},{4,6},{6,4},{8,10},{10,8},{12,14},{14,12},{16,18},{18,... | collective-permute-start | bytes 233480 | tf_op jit(solution)/shard_map/ppermute | solution.py:986
  14.9 0.0 copy-done.15
  14.9 0.0 copy-start.5
  14.9 0.0 copy-start.9
  14.9 0.0 copy-start.10
  14.9 0.0 copy-start.11
  14.9 0.0 copy-start.13
  14.9 0.0 copy-start.14
  14.9 0.8 %shard_map.244 = (f32[2,27,8,128]{3,2,1,0:T(8,128)S(1)}, f32[4,8,128]{2,1,0:T(8,128)S(1)}) custom-call(f32[16,56,128]{2,1,0:T(8,128)S(1)} %get-tuple-element.100.w_ref.refs_4_, f32[16,56,128]{2,1,0:T(8,128)S(1)} %get-tuple-element.104.rhs_ref, f32[24,168]{1,0:T(8,128)S(1)} %copy-done.15, bf16[6,256,128]{2,1,0:T(8,128)(2,1)S(1)} %copy-done.4, ...), custom_call_target="tpu_custom_call" | custom-call | flops 1 | bytes 1 | tf_op jit(solution)/shard_map/pallas_call | solution.py:948
  15.7 0.0 collective-permute-done.9.refs_2_
  15.7 0.1 collective-permute-done.10.refs_3_
  15.8 0.0 copy-done.5
  15.8 0.0 copy-done.13
  15.8 0.0 copy-done.14
  15.8 0.0 copy-start.6
  15.9 0.0 copy-start.20
  15.9 1.6 %shard_map.245 = (f32[8,32,128]{2,1,0:T(8,128)S(1)}, f32[3,8,128]{2,1,0:T(8,128)S(1)}, f32[10,8,128]{2,1,0:T(8,128)S(1)}) custom-call(f32[152,128]{1,0:T(8,128)S(1)} %collective-permute-done.1.refs_0_, f32[152,128]{1,0:T(8,128)S(1)} %collective-permute-done.5.refs_1_, f32[152,128]{1,0:T(8,128)S(1)} %collective-permute-done.9.refs_2_, ...), custom_call_target="tpu_custom_call" | custom-call | flops 1 | bytes 1 | tf_op jit(solution)/shard_map/pallas_call | solution.py:948
  17.4 0.0 collective-permute-start.11
  17.5 2.5 %collective-permute-done.11.refs_0_ = f32[3,8,128]{2,1,0:T(8,128)S(1)} collective-permute-done((f32[3,8,128]{2,1,0:T(8,128)S(1)}, f32[3,8,128]{2,1,0:T(8,128)S(1)}, u32[]{:S(2)}, u32[]{:S(2)}) %collective-permute-start.11) | collective-permute-done | bytes 12320 | tf_op jit(solution)/shard_map/ppermute | solution.py:987
  20.0 0.9 %collective-permute-start.12 = (f32[3,8,128]{2,1,0:T(8,128)S(1)}, f32[3,8,128]{2,1,0:T(8,128)S(1)}, u32[]{:S(2)}, u32[]{:S(2)}) collective-permute-start(f32[3,8,128]{2,1,0:T(8,128)S(1)} %collective-permute-done.11.refs_0_), channel_id=1, source_target_pairs={{0,2},{2,0},{4,6},{6,4},{8,10},{10,8},{12,14},{14,12},{16,18},{18,... | collective-permute-start | bytes 36872 | tf_op jit(solution)/shard_map/ppermute | solution.py:986
  20.9 0.8 %collective-permute-done.12.refs_1_ = f32[3,8,128]{2,1,0:T(8,128)S(1)} collective-permute-done((f32[3,8,128]{2,1,0:T(8,128)S(1)}, f32[3,8,128]{2,1,0:T(8,128)S(1)}, u32[]{:S(2)}, u32[]{:S(2)}) %collective-permute-start.12) | collective-permute-done | bytes 12320 | tf_op jit(solution)/shard_map/ppermute | solution.py:986
  21.7 1.1 %shard_map.246 = (f32[8,32,128]{2,1,0:T(8,128)}, f32[2,8,32]{2,1,0:T(8,128)}) custom-call(f32[3,8,128]{2,1,0:T(8,128)S(1)} %collective-permute-done.11.refs_0_, f32[3,8,128]{2,1,0:T(8,128)S(1)} %collective-permute-done.12.refs_1_, f32[8,32,128]{2,1,0:T(8,128)S(1)} %get-tuple-element.108.refs_2_, f32[10,8,128]{2,1,0:T(8,128)S(1)} %get-tuple-element.109.refs_3_, ...), custom_call_target="tpu_custom_call" | custom-call | flops 1 | bytes 1 | tf_op jit(solution)/shard_map/pallas_call | solution.py:948
  (19 shorter events, 0.1 us)
Async XLA Ops:
  0.6 1.1 %copy-start = (bf16[2,256,128]{2,1,0:T(8,128)(2,1)S(1)}, bf16[2,256,128]{2,1,0:T(8,128)(2,1)}, u32[]{:S(2)}) copy-start(bf16[2,256,128]{2,1,0:T(8,128)(2,1)} %constant.46.clone.z_sq.refs_2_.refs_1_.refs_3_.refs_12_) | copy-start | bytes 393220
  0.6 1.1 %copy-start.3 = (f32[8,8,128]{2,1,0:T(8,128)S(1)}, f32[8,8,128]{2,1,0:T(8,128)}, u32[]{:S(2)}) copy-start(f32[8,8,128]{2,1,0:T(8,128)} %constant.65.clone.w3.refs_4_.refs_3_.refs_5_) | copy-start | bytes 98308
  0.7 1.1 %copy-start.8 = (f32[32,96]{1,0:T(8,128)S(1)}, f32[32,96]{1,0:T(8,128)}, u32[]{:S(2)}) copy-start(f32[32,96]{1,0:T(8,128)} %constant.52.clone.y_sq.refs_3_) | copy-start | bytes 36868
  2.1 6.0 %collective-permute-start.2 = (f32[400,128]{1,0:T(8,128)S(1)}, f32[400,128]{1,0:T(8,128)S(1)}, u32[]{:S(2)}, u32[]{:S(2)}) collective-permute-start(f32[400,128]{1,0:T(8,128)S(1)} %get-tuple-element.61), channel_id=1, source_target_pairs={{0,1},{1,0},{2,3},{3,2},{4,5},{5,4},{6,7},{7,6},{8,9},{9,8},{10,11... | collective-permute-start | bytes 614408 | tf_op jit(solution)/shard_map/ppermute | solution.py:1005
  2.4 4.1 %collective-permute-start.3 = (f32[8,32,128]{2,1,0:T(8,128)S(1)}, f32[8,32,128]{2,1,0:T(8,128)S(1)}, u32[]{:S(2)}, u32[]{:S(2)}) collective-permute-start(f32[8,32,128]{2,1,0:T(8,128)S(1)} %get-tuple-element.111), channel_id=1, source_target_pairs={{0,2},{2,0},{4,6},{6,4},{8,10},{10,8},{12,14},{14,12},{16,18},{18,... | collective-permute-start | bytes 393224 | tf_op jit(solution)/shard_map/ppermute | solution.py:986
  3.4 3.1 %collective-permute-start.4 = (f32[8,32,128]{2,1,0:T(8,128)S(1)}, f32[8,32,128]{2,1,0:T(8,128)S(1)}, u32[]{:S(2)}, u32[]{:S(2)}) collective-permute-start(f32[8,32,128]{2,1,0:T(8,128)S(1)} %get-tuple-element.110), channel_id=1, source_target_pairs={{0,2},{2,0},{4,6},{6,4},{8,10},{10,8},{12,14},{14,12},{16,18},{18,... | collective-permute-start | bytes 393224 | tf_op jit(solution)/shard_map/ppermute | solution.py:986
  3.5 1.3 %collective-permute-start = (f32[2,32,128]{2,1,0:T(8,128)S(1)}, f32[2,32,128]{2,1,0:T(8,128)S(1)}, u32[]{:S(2)}, u32[]{:S(2)}) collective-permute-start(f32[2,32,128]{2,1,0:T(8,128)S(1)} %get-tuple-element.59), channel_id=1, source_target_pairs={{0,2},{2,0},{4,6},{6,4},{8,10},{10,8},{12,14},{14,12},{16,18},{18,... | collective-permute-start | bytes 98312 | tf_op jit(solution)/shard_map/ppermute | solution.py:986
  4.8 1.7 %copy-start.1 = (bf16[2,256,128]{2,1,0:T(8,128)(2,1)S(1)}, bf16[2,256,128]{2,1,0:T(8,128)(2,1)}, u32[]{:S(2)}) copy-start(bf16[2,256,128]{2,1,0:T(8,128)(2,1)} %constant.44.clone.refs_5_.refs_6_.refs_10_) | copy-start | bytes 393220
  4.8 1.7 %copy-start.2 = (bf16[2,256,128]{2,1,0:T(8,128)(2,1)S(1)}, bf16[2,256,128]{2,1,0:T(8,128)(2,1)}, u32[]{:S(2)}) copy-start(bf16[2,256,128]{2,1,0:T(8,128)(2,1)} %constant.45.clone.refs_6_.refs_7_.refs_11_) | copy-start | bytes 393220
  4.8 1.7 %copy-start.18 = (f32[24,72]{1,0:T(8,128)S(1)}, f32[24,72]{1,0:T(8,128)}, u32[]{:S(2)}) copy-start(f32[24,72]{1,0:T(8,128)} %constant.50.clone.refs_7_) | copy-start | bytes 20740
  4.8 1.7 %copy-start.19 = (f32[24,72]{1,0:T(8,128)S(1)}, f32[24,72]{1,0:T(8,128)}, u32[]{:S(2)}) copy-start(f32[24,72]{1,0:T(8,128)} %constant.51.clone.refs_8_) | copy-start | bytes 20740
  5.0 7.6 %collective-permute-start.1 = (f32[152,128]{1,0:T(8,128)S(1)}, f32[152,128]{1,0:T(8,128)S(1)}, u32[]{:S(2)}, u32[]{:S(2)}) collective-permute-start(f32[152,128]{1,0:T(8,128)S(1)} %get-tuple-element.60), channel_id=1, source_target_pairs={{2,4},{3,5},{4,2},{5,3},{6,8},{7,9},{8,6},{9,7},{10,12},{11,13},{1... | collective-permute-start | bytes 233480 | tf_op jit(solution)/shard_map/ppermute | solution.py:987
  6.3 8.2 %collective-permute-start.5 = (f32[152,128]{1,0:T(8,128)S(1)}, f32[152,128]{1,0:T(8,128)S(1)}, u32[]{:S(2)}, u32[]{:S(2)}) collective-permute-start(f32[152,128]{1,0:T(8,128)S(1)} %get-tuple-element.89), channel_id=1, source_target_pairs={{2,5},{3,4},{4,3},{5,2},{6,9},{7,8},{8,7},{9,6},{10,13},{11,12},{1... | collective-permute-start | bytes 233480 | tf_op jit(solution)/shard_map/ppermute | solution.py:987
  8.1 5.0 %collective-permute-start.8 = (f32[144,128]{1,0:T(8,128)S(1)}, f32[144,128]{1,0:T(8,128)S(1)}, u32[]{:S(2)}, u32[]{:S(2)}) collective-permute-start(f32[144,128]{1,0:T(8,128)S(1)} %slice.19), channel_id=1, source_target_pairs={{0,2},{2,0},{4,6},{6,4},{8,10},{10,8},{12,14},{14,12},{16,18},{18,... | collective-permute-start | bytes 221192 | tf_op jit(solution)/shard_map/ppermute | solution.py:986
  11.6 0.7 %copy-start.12 = (f32[24,72]{1,0:T(8,128)S(1)}, f32[24,72]{1,0:T(8,128)}, u32[]{:S(2)}) copy-start(f32[24,72]{1,0:T(8,128)} %constant.49.clone.refs_2_.refs_4_) | copy-start | bytes 20740
  11.6 1.5 %collective-permute-start.6 = (f32[136,128]{1,0:T(8,128)S(1)}, f32[136,128]{1,0:T(8,128)S(1)}, u32[]{:S(2)}, u32[]{:S(2)}) collective-permute-start(f32[136,128]{1,0:T(8,128)S(1)} %slice.17), channel_id=1, source_target_pairs={{0,2},{2,0},{4,6},{6,4},{8,10},{10,8},{12,14},{14,12},{16,18},{18,... | collective-permute-start | bytes 208904 | tf_op jit(solution)/shard_map/ppermute | solution.py:986
  11.7 1.4 %collective-permute-start.7 = (f32[120,128]{1,0:T(8,128)S(1)}, f32[120,128]{1,0:T(8,128)S(1)}, u32[]{:S(2)}, u32[]{:S(2)}) collective-permute-start(f32[120,128]{1,0:T(8,128)S(1)} %slice.18), channel_id=1, source_target_pairs={{0,2},{2,0},{4,6},{6,4},{8,10},{10,8},{12,14},{14,12},{16,18},{18,... | collective-permute-start | bytes 184328 | tf_op jit(solution)/shard_map/ppermute | solution.py:986
  12.3 0.8 %copy-start.16 = (f32[32,96]{1,0:T(8,128)S(1)}, f32[32,96]{1,0:T(8,128)}, u32[]{:S(2)}) copy-start(f32[32,96]{1,0:T(8,128)} %constant.53.clone.refs_8_) | copy-start | bytes 36868
  12.3 0.8 %copy-start.17 = (f32[32,96]{1,0:T(8,128)S(1)}, f32[32,96]{1,0:T(8,128)}, u32[]{:S(2)}) copy-start(f32[32,96]{1,0:T(8,128)} %constant.54.clone.refs_9_) | copy-start | bytes 36868
  12.7 2.2 %copy-start.4 = (bf16[6,256,128]{2,1,0:T(8,128)(2,1)S(1)}, bf16[6,256,128]{2,1,0:T(8,128)(2,1)}, u32[]{:S(2)}) copy-start(bf16[6,256,128]{2,1,0:T(8,128)(2,1)} %constant.61.clone.mz) | copy-start | bytes 1179652
  12.7 2.2 %copy-start.7 = (bf16[2,256,128]{2,1,0:T(8,128)(2,1)S(1)}, bf16[2,256,128]{2,1,0:T(8,128)(2,1)}, u32[]{:S(2)}) copy-start(bf16[2,256,128]{2,1,0:T(8,128)(2,1)} %constant.59.clone.rz) | copy-start | bytes 393220
  12.7 2.2 %copy-start.15 = (f32[24,168]{1,0:T(8,128)S(1)}, f32[24,168]{1,0:T(8,128)}, u32[]{:S(2)}) copy-start(f32[24,168]{1,0:T(8,128)} %constant.60.clone.my) | copy-start | bytes 48388
  12.7 3.0 %collective-permute-start.9 = (f32[152,128]{1,0:T(8,128)S(1)}, f32[152,128]{1,0:T(8,128)S(1)}, u32[]{:S(2)}, u32[]{:S(2)}) collective-permute-start(f32[152,128]{1,0:T(8,128)S(1)} %collective-permute-done.1.refs_0_), channel_id=1, source_target_pairs={{0,2},{2,0},{4,6},{6,4},{8,10},{10,8},{12,14},{14,12},{16,18},{18,... | collective-permute-start | bytes 233480 | tf_op jit(solution)/shard_map/ppermute | solution.py:986
  13.1 1.7 %copy-start.21 = (f32[8,168]{1,0:T(8,128)S(1)}, f32[8,168]{1,0:T(8,128)}, u32[]{:S(2)}) copy-start(f32[8,168]{1,0:T(8,128)} %constant.57.clone.ry) | copy-start | bytes 16132
  14.4 1.3 %collective-permute-start.10 = (f32[152,128]{1,0:T(8,128)S(1)}, f32[152,128]{1,0:T(8,128)S(1)}, u32[]{:S(2)}, u32[]{:S(2)}) collective-permute-start(f32[152,128]{1,0:T(8,128)S(1)} %collective-permute-done.5.refs_1_), channel_id=1, source_target_pairs={{0,2},{2,0},{4,6},{6,4},{8,10},{10,8},{12,14},{14,12},{16,18},{18,... | collective-permute-start | bytes 233480 | tf_op jit(solution)/shard_map/ppermute | solution.py:986
  14.9 1.0 %copy-start.5 = (bf16[2,512,128]{2,1,0:T(8,128)(2,1)S(1)}, bf16[2,512,128]{2,1,0:T(8,128)(2,1)}, u32[]{:S(2)}) copy-start(bf16[2,512,128]{2,1,0:T(8,128)(2,1)} %constant.58.clone.refs_17_) | copy-start | bytes 786436
  14.9 0.9 %copy-start.9 = (f32[56,168]{1,0:T(8,128)S(1)}, f32[56,168]{1,0:T(8,128)}, u32[]{:S(2)}) copy-start(f32[56,168]{1,0:T(8,128)} %constant.47.clone.refs_13_) | copy-start | bytes 112900
  14.9 0.9 %copy-start.10 = (f32[56,168]{1,0:T(8,128)S(1)}, f32[56,168]{1,0:T(8,128)}, u32[]{:S(2)}) copy-start(f32[56,168]{1,0:T(8,128)} %constant.48.clone.refs_14_) | copy-start | bytes 112900
  14.9 0.9 %copy-start.11 = (f32[56,168]{1,0:T(8,128)S(1)}, f32[56,168]{1,0:T(8,128)}, u32[]{:S(2)}) copy-start(f32[56,168]{1,0:T(8,128)} %constant.55.clone.refs_15_) | copy-start | bytes 112900
  14.9 0.9 %copy-start.13 = (f32[10,8,128]{2,1,0:T(8,128)S(1)}, f32[10,8,128]{2,1,0:T(8,128)}, u32[]{:S(2)}) copy-start(f32[10,8,128]{2,1,0:T(8,128)} %constant.64.clone.refs_18_) | copy-start | bytes 122884
  14.9 0.9 %copy-start.14 = (f32[32,168]{1,0:T(8,128)S(1)}, f32[32,168]{1,0:T(8,128)}, u32[]{:S(2)}) copy-start(f32[32,168]{1,0:T(8,128)} %constant.56.clone.refs_16_) | copy-start | bytes 64516
  15.8 5.9 %copy-start.6 = (bf16[2,256,160]{2,1,0:T(8,128)(2,1)S(1)}, bf16[2,256,160]{2,1,0:T(8,128)(2,1)}, u32[]{:S(2)}) copy-start(bf16[2,256,160]{2,1,0:T(8,128)(2,1)} %constant.63.clone.refs_6_) | copy-start | bytes 491524
  15.9 5.9 %copy-start.20 = (f32[2,8,128]{2,1,0:T(8,128)S(1)}, f32[2,8,128]{2,1,0:T(8,128)}, u32[]{:S(2)}) copy-start(f32[2,8,128]{2,1,0:T(8,128)} %constant.62.clone.refs_5_) | copy-start | bytes 24580
  17.4 2.6 %collective-permute-start.11 = (f32[3,8,128]{2,1,0:T(8,128)S(1)}, f32[3,8,128]{2,1,0:T(8,128)S(1)}, u32[]{:S(2)}, u32[]{:S(2)}) collective-permute-start(f32[3,8,128]{2,1,0:T(8,128)S(1)} %get-tuple-element.107), channel_id=1, source_target_pairs={{2,4},{3,5},{4,2},{5,3},{6,8},{7,9},{8,6},{9,7},{10,12},{11,13},{1... | collective-permute-start | bytes 36872 | tf_op jit(solution)/shard_map/ppermute | solution.py:987
  20.0 1.7 %collective-permute-start.12 = (f32[3,8,128]{2,1,0:T(8,128)S(1)}, f32[3,8,128]{2,1,0:T(8,128)S(1)}, u32[]{:S(2)}, u32[]{:S(2)}) collective-permute-start(f32[3,8,128]{2,1,0:T(8,128)S(1)} %collective-permute-done.11.refs_0_), channel_id=1, source_target_pairs={{0,2},{2,0},{4,6},{6,4},{8,10},{10,8},{12,14},{14,12},{16,18},{18,... | collective-permute-start | bytes 36872 | tf_op jit(solution)/shard_map/ppermute | solution.py:986

commit v9 on v8

--- a/solution.py
+++ b/solution.py
@@ -292,7 +292,8 @@
             return []
         if self.sub == 2:
             return [(1 - h) * (self.own_y - N)]
-        return [0, self.own_y + HALO - N]
+        size = HALO + N
+        return [*range(0, self.ny - size, size), self.ny - size]
 
     def interfaces(self, h):
         if self.sub == 1:

time: 23.1 us -> 23.1 us (level)
  no operation moved by 1% of the time
where the time goes in v9:
time: 23.1 us; the launch traced here: 22.8 us
  starting transfers between devices  8.85 us (38%)
  Pallas kernels  6.36 us (28%)
  waiting for transfers between devices  5.35 us (23%)
  other arithmetic  1.04 us (5%)
  between operations  0.91 us (4%)
  local copies, waits for them, and re-layouts  0.33 us (1%)
    ppermute x9, starting transfers between devices, shards(): even = lambda v: lax.ppermute(v, 'dom', swap_pairs(dom, 0))  7.04 us
    pallas_call x8, Pallas kernels, run(): pl.pallas_call(kernel, out_shape=[jax.ShapeDtypeStruct(o, F32) for o in o...  6.36 us
    ppermute x3, waiting for transfers between devices, shards(): lax.ppermute(v, ('dom', 'sub'), chip_pairs(dom, sub, k))  2.54 us
    ppermute x9, waiting for transfers between devices, shards(): even = lambda v: lax.ppermute(v, 'dom', swap_pairs(dom, 0))  2.13 us
    ppermute x3, starting transfers between devices, shards(): lax.ppermute(v, ('dom', 'sub'), chip_pairs(dom, sub, k))  1.51 us
    another operation x1, other arithmetic, shards(): raw = jnp.stack([rhs_local, coefficient])  1.04 us
    ppermute x1, waiting for transfers between devices, shards(): lax.ppermute(pack, 'sub', step)  0.68 us
  transfers between devices with their start and end apart: 13, of which 6 were waited for; matrix products, arithmetic and copies ran while one was open for 0% of the time, Pallas kernels for 15%

profile of v9, /device:TPU:31, one launch (start us, length us, event | category | flops | bytes accessed | tf_op | source)
XLA Modules:
  0.0 22.8 jit_solution(3250911106674573471)
XLA Ops:
  0.6 0.0 copy-start
  0.6 0.0 copy-start.3
  0.7 0.0 copy-start.8
  0.7 1.0 %pad_maximum_fusion.raw.own = f32[2,8,32,128]{3,2,1,0:T(8,128)S(1)} fusion(f32[1,8,32,128]{3,2,1,0:T(8,128)} %bitcast.6, f32[1,8,32,128]{3,2,1,0:T(8,128)} %bitcast.7), kind=kLoop, calls=%fused_computation | loop fusion | flops 65536 | bytes 524288 | tf_op jit(solution)/shard_map/stack | solution.py:990
  1.7 0.0 copy-done
  1.7 0.0 copy-done.3
  1.7 0.0 copy-done.8
  1.7 0.3 %shard_map.239 = (f32[2,32,128]{2,1,0:T(8,128)S(1)}, f32[8,32,128]{2,1,0:T(8,128)S(1)}, f32[8,32,128]{2,1,0:T(8,128)S(1)}, f32[8,32,128]{2,1,0:T(8,128)S(1)}, f32[400,128]{1,0:T(8,128)S(1)}) custom-call(f32[2,8,32,128]{3,2,1,0:T(8,128)S(1)} %pad_maximum_fusion.raw.own, bf16[2,256,128]{2,1,0:T(8,128)(2,1)S(1)} %copy-done, f32[32,96]{1,0:T(8,128)S(1)} %copy-done.8, ...), custom_call_target="tpu_custom_call" | custom-call | flops 1 | bytes 1 | tf_op jit(solution)/shard_map/pallas_call | solution.py:949
  2.1 0.3 %collective-permute-start.2 = (f32[400,128]{1,0:T(8,128)S(1)}, f32[400,128]{1,0:T(8,128)S(1)}, u32[]{:S(2)}, u32[]{:S(2)}) collective-permute-start(f32[400,128]{1,0:T(8,128)S(1)} %get-tuple-element.61), channel_id=1, source_target_pairs={{0,1},{1,0},{2,3},{3,2},{4,5},{5,4},{6,7},{7,6},{8,9},{9,8},{10,11... | collective-permute-start | bytes 614408 | tf_op jit(solution)/shard_map/ppermute | solution.py:1006
  2.4 1.0 %collective-permute-start.3 = (f32[8,32,128]{2,1,0:T(8,128)S(1)}, f32[8,32,128]{2,1,0:T(8,128)S(1)}, u32[]{:S(2)}, u32[]{:S(2)}) collective-permute-start(f32[8,32,128]{2,1,0:T(8,128)S(1)} %get-tuple-element.111), channel_id=1, source_target_pairs={{0,2},{2,0},{4,6},{6,4},{8,10},{10,8},{12,14},{14,12},{16,18},{18,... | collective-permute-start | bytes 393224 | tf_op jit(solution)/shard_map/ppermute | solution.py:987
  3.4 0.1 collective-permute-start.4
  3.5 0.4 %collective-permute-start = (f32[2,32,128]{2,1,0:T(8,128)S(1)}, f32[2,32,128]{2,1,0:T(8,128)S(1)}, u32[]{:S(2)}, u32[]{:S(2)}) collective-permute-start(f32[2,32,128]{2,1,0:T(8,128)S(1)} %get-tuple-element.59), channel_id=1, source_target_pairs={{0,2},{2,0},{4,6},{6,4},{8,10},{10,8},{12,14},{14,12},{16,18},{18,... | collective-permute-start | bytes 98312 | tf_op jit(solution)/shard_map/ppermute | solution.py:987
  3.9 0.9 %collective-permute-done.face = f32[2,32,128]{2,1,0:T(8,128)S(1)} collective-permute-done((f32[2,32,128]{2,1,0:T(8,128)S(1)}, f32[2,32,128]{2,1,0:T(8,128)S(1)}, u32[]{:S(2)}, u32[]{:S(2)}) %collective-permute-start) | collective-permute-done | bytes 32800 | tf_op jit(solution)/shard_map/ppermute | solution.py:987
  4.8 0.2 shard_map.240
  5.0 1.3 %collective-permute-start.1 = (f32[152,128]{1,0:T(8,128)S(1)}, f32[152,128]{1,0:T(8,128)S(1)}, u32[]{:S(2)}, u32[]{:S(2)}) collective-permute-start(f32[152,128]{1,0:T(8,128)S(1)} %get-tuple-element.60), channel_id=1, source_target_pairs={{2,4},{3,5},{4,2},{5,3},{6,8},{7,9},{8,6},{9,7},{10,12},{11,13},{1... | collective-permute-start | bytes 233480 | tf_op jit(solution)/shard_map/ppermute | solution.py:988
  6.3 0.2 collective-permute-start.5
  6.5 0.0 collective-permute-done.3.refs_0_
  6.5 0.0 collective-permute-done.4.refs_1_
  6.5 0.0 copy-done.1
  6.5 0.0 copy-done.2
  6.5 0.0 copy-done.18
  6.5 0.0 copy-done.19
  6.5 0.9 %shard_map.241 = (f32[16,56,128]{2,1,0:T(8,128)S(1)}, f32[16,56,128]{2,1,0:T(8,128)S(1)}, f32[16,56,128]{2,1,0:T(8,128)S(1)}, f32[16,56,128]{2,1,0:T(8,128)S(1)}...) custom-call(f32[2,8,32,128]{3,2,1,0:T(8,128)S(1)} %pad_maximum_fusio, ...), custom_call_target="tpu_custom_call" | custom-call | flops 1 | bytes 1 | tf_op jit(solution)/shard_map/pallas_call | solution.py:949
  7.4 0.7 %collective-permute-done.2.refs_0_ = f32[400,128]{1,0:T(8,128)S(1)} collective-permute-done((f32[400,128]{1,0:T(8,128)S(1)}, f32[400,128]{1,0:T(8,128)S(1)}, u32[]{:S(2)}, u32[]{:S(2)}) %collective-permute-start.2) | collective-permute-done | bytes 204832 | tf_op jit(solution)/shard_map/ppermute | solution.py:1006
  8.1 3.5 %collective-permute-start.8 = (f32[144,128]{1,0:T(8,128)S(1)}, f32[144,128]{1,0:T(8,128)S(1)}, u32[]{:S(2)}, u32[]{:S(2)}) collective-permute-start(f32[144,128]{1,0:T(8,128)S(1)} %slice.19), channel_id=1, source_target_pairs={{0,2},{2,0},{4,6},{6,4},{8,10},{10,8},{12,14},{14,12},{16,18},{18,... | collective-permute-start | bytes 221192 | tf_op jit(solution)/shard_map/ppermute | solution.py:987
  11.6 0.1 collective-permute-start.6
  11.7 0.5 %collective-permute-start.7 = (f32[120,128]{1,0:T(8,128)S(1)}, f32[120,128]{1,0:T(8,128)S(1)}, u32[]{:S(2)}, u32[]{:S(2)}) collective-permute-start(f32[120,128]{1,0:T(8,128)S(1)} %slice.18), channel_id=1, source_target_pairs={{0,2},{2,0},{4,6},{6,4},{8,10},{10,8},{12,14},{14,12},{16,18},{18,... | collective-permute-start | bytes 184328 | tf_op jit(solution)/shard_map/ppermute | solution.py:987
  12.2 0.1 copy-done.12
  12.3 0.3 %shard_map.242 = (f32[16,56,128]{2,1,0:T(8,128)S(1)}, f32[16,56,128]{2,1,0:T(8,128)S(1)}, f32[16,56,128]{2,1,0:T(8,128)S(1)}, f32[16,56,128]{2,1,0:T(8,128)S(1)}...) custom-call(f32[400,128]{1,0:T(8,128)S(1)} %collective-permute-done., ...), custom_call_target="tpu_custom_call", output_to_operand_aliasing={{0}: (4, {}), {1}: (5, {}), {2}: (6, {}), {3}: (7, {}), {4}... | custom-call | flops 1 | bytes 1 | tf_op jit(solution)/shard_map/pallas_call | solution.py:949
  12.7 0.0 collective-permute-done.1.refs_0_
  12.7 0.0 copy-start.4
  12.7 0.0 copy-start.7
  12.7 0.0 copy-start.15
  12.7 0.1 collective-permute-start.9
  12.8 0.3 %collective-permute-done.7.refs_1_ = f32[120,128]{1,0:T(8,128)S(1)} collective-permute-done((f32[120,128]{1,0:T(8,128)S(1)}, f32[120,128]{1,0:T(8,128)S(1)}, u32[]{:S(2)}, u32[]{:S(2)}) %collective-permute-start.7) | collective-permute-done | bytes 61472 | tf_op jit(solution)/shard_map/ppermute | solution.py:987
  13.1 0.0 collective-permute-done.6.refs_0_
  13.1 0.0 collective-permute-done.8.refs_2_
  13.1 0.0 copy-done.16
  13.1 0.0 copy-done.17
  13.1 0.0 copy-start.21
  13.2 1.3 %shard_map.243 = (f32[16,56,128]{2,1,0:T(8,128)S(1)}, f32[16,56,128]{2,1,0:T(8,128)S(1)}, f32[16,56,128]{2,1,0:T(8,128)S(1)}, f32[16,56,128]{2,1,0:T(8,128)S(1)}...) custom-call(f32[136,128]{1,0:T(8,128)S(1)} %collective-permute-done., ...), custom_call_target="tpu_custom_call", output_to_operand_aliasing={{0}: (10, {}), {1}: (11, {}), {2}: (12, {}), {3}: (13, {}),... | custom-call | flops 1 | bytes 1 | tf_op jit(solution)/shard_map/pallas_call | solution.py:949
  14.4 0.0 collective-permute-done.5.refs_1_
  14.4 0.4 %collective-permute-start.10 = (f32[152,128]{1,0:T(8,128)S(1)}, f32[152,128]{1,0:T(8,128)S(1)}, u32[]{:S(2)}, u32[]{:S(2)}) collective-permute-start(f32[152,128]{1,0:T(8,128)S(1)} %collective-permute-done.5.refs_1_), channel_id=1, source_target_pairs={{0,2},{2,0},{4,6},{6,4},{8,10},{10,8},{12,14},{14,12},{16,18},{18,... | collective-permute-start | bytes 233480 | tf_op jit(solution)/shard_map/ppermute | solution.py:987
  14.9 0.0 copy-done.15
  14.9 0.0 copy-start.5
  14.9 0.0 copy-start.9
  14.9 0.0 copy-start.10
  14.9 0.0 copy-start.11
  14.9 0.0 copy-start.13
  14.9 0.0 copy-start.14
  14.9 0.8 %shard_map.244 = (f32[2,27,8,128]{3,2,1,0:T(8,128)S(1)}, f32[4,8,128]{2,1,0:T(8,128)S(1)}) custom-call(f32[16,56,128]{2,1,0:T(8,128)S(1)} %get-tuple-element.100.w_ref.refs_4_, f32[16,56,128]{2,1,0:T(8,128)S(1)} %get-tuple-element.104.rhs_ref, f32[24,168]{1,0:T(8,128)S(1)} %copy-done.15, bf16[6,256,128]{2,1,0:T(8,128)(2,1)S(1)} %copy-done.4, ...), custom_call_target="tpu_custom_call" | custom-call | flops 1 | bytes 1 | tf_op jit(solution)/shard_map/pallas_call | solution.py:949
  15.7 0.0 collective-permute-done.9.refs_2_
  15.7 0.1 collective-permute-done.10.refs_3_
  15.8 0.0 copy-done.5
  15.8 0.0 copy-done.13
  15.8 0.0 copy-done.14
  15.8 0.0 copy-start.6
  15.9 0.0 copy-start.20
  15.9 1.6 %shard_map.245 = (f32[8,32,128]{2,1,0:T(8,128)S(1)}, f32[3,8,128]{2,1,0:T(8,128)S(1)}, f32[10,8,128]{2,1,0:T(8,128)S(1)}) custom-call(f32[152,128]{1,0:T(8,128)S(1)} %collective-permute-done.1.refs_0_, f32[152,128]{1,0:T(8,128)S(1)} %collective-permute-done.5.refs_1_, f32[152,128]{1,0:T(8,128)S(1)} %collective-permute-done.9.refs_2_, ...), custom_call_target="tpu_custom_call" | custom-call | flops 1 | bytes 1 | tf_op jit(solution)/shard_map/pallas_call | solution.py:949
  17.4 0.0 collective-permute-start.11
  17.5 2.5 %collective-permute-done.11.refs_0_ = f32[3,8,128]{2,1,0:T(8,128)S(1)} collective-permute-done((f32[3,8,128]{2,1,0:T(8,128)S(1)}, f32[3,8,128]{2,1,0:T(8,128)S(1)}, u32[]{:S(2)}, u32[]{:S(2)}) %collective-permute-start.11) | collective-permute-done | bytes 12320 | tf_op jit(solution)/shard_map/ppermute | solution.py:988
  20.0 0.9 %collective-permute-start.12 = (f32[3,8,128]{2,1,0:T(8,128)S(1)}, f32[3,8,128]{2,1,0:T(8,128)S(1)}, u32[]{:S(2)}, u32[]{:S(2)}) collective-permute-start(f32[3,8,128]{2,1,0:T(8,128)S(1)} %collective-permute-done.11.refs_0_), channel_id=1, source_target_pairs={{0,2},{2,0},{4,6},{6,4},{8,10},{10,8},{12,14},{14,12},{16,18},{18,... | collective-permute-start | bytes 36872 | tf_op jit(solution)/shard_map/ppermute | solution.py:987
  20.9 0.8 %collective-permute-done.12.refs_1_ = f32[3,8,128]{2,1,0:T(8,128)S(1)} collective-permute-done((f32[3,8,128]{2,1,0:T(8,128)S(1)}, f32[3,8,128]{2,1,0:T(8,128)S(1)}, u32[]{:S(2)}, u32[]{:S(2)}) %collective-permute-start.12) | collective-permute-done | bytes 12320 | tf_op jit(solution)/shard_map/ppermute | solution.py:987
  21.7 1.1 %shard_map.246 = (f32[8,32,128]{2,1,0:T(8,128)}, f32[2,8,32]{2,1,0:T(8,128)}) custom-call(f32[3,8,128]{2,1,0:T(8,128)S(1)} %collective-permute-done.11.refs_0_, f32[3,8,128]{2,1,0:T(8,128)S(1)} %collective-permute-done.12.refs_1_, f32[8,32,128]{2,1,0:T(8,128)S(1)} %get-tuple-element.108.refs_2_, f32[10,8,128]{2,1,0:T(8,128)S(1)} %get-tuple-element.109.refs_3_, ...), custom_call_target="tpu_custom_call" | custom-call | flops 1 | bytes 1 | tf_op jit(solution)/shard_map/pallas_call | solution.py:949
  (19 shorter events, 0.1 us)
Async XLA Ops:
  0.6 1.1 %copy-start = (bf16[2,256,128]{2,1,0:T(8,128)(2,1)S(1)}, bf16[2,256,128]{2,1,0:T(8,128)(2,1)}, u32[]{:S(2)}) copy-start(bf16[2,256,128]{2,1,0:T(8,128)(2,1)} %constant.46.clone.z_sq.refs_2_.refs_1_.refs_3_.refs_12_) | copy-start | bytes 393220
  0.6 1.1 %copy-start.3 = (f32[8,8,128]{2,1,0:T(8,128)S(1)}, f32[8,8,128]{2,1,0:T(8,128)}, u32[]{:S(2)}) copy-start(f32[8,8,128]{2,1,0:T(8,128)} %constant.65.clone.w3.refs_4_.refs_3_.refs_5_) | copy-start | bytes 98308
  0.7 1.1 %copy-start.8 = (f32[32,96]{1,0:T(8,128)S(1)}, f32[32,96]{1,0:T(8,128)}, u32[]{:S(2)}) copy-start(f32[32,96]{1,0:T(8,128)} %constant.52.clone.y_sq.refs_3_) | copy-start | bytes 36868
  2.1 6.0 %collective-permute-start.2 = (f32[400,128]{1,0:T(8,128)S(1)}, f32[400,128]{1,0:T(8,128)S(1)}, u32[]{:S(2)}, u32[]{:S(2)}) collective-permute-start(f32[400,128]{1,0:T(8,128)S(1)} %get-tuple-element.61), channel_id=1, source_target_pairs={{0,1},{1,0},{2,3},{3,2},{4,5},{5,4},{6,7},{7,6},{8,9},{9,8},{10,11... | collective-permute-start | bytes 614408 | tf_op jit(solution)/shard_map/ppermute | solution.py:1006
  2.4 4.1 %collective-permute-start.3 = (f32[8,32,128]{2,1,0:T(8,128)S(1)}, f32[8,32,128]{2,1,0:T(8,128)S(1)}, u32[]{:S(2)}, u32[]{:S(2)}) collective-permute-start(f32[8,32,128]{2,1,0:T(8,128)S(1)} %get-tuple-element.111), channel_id=1, source_target_pairs={{0,2},{2,0},{4,6},{6,4},{8,10},{10,8},{12,14},{14,12},{16,18},{18,... | collective-permute-start | bytes 393224 | tf_op jit(solution)/shard_map/ppermute | solution.py:987
  3.4 3.1 %collective-permute-start.4 = (f32[8,32,128]{2,1,0:T(8,128)S(1)}, f32[8,32,128]{2,1,0:T(8,128)S(1)}, u32[]{:S(2)}, u32[]{:S(2)}) collective-permute-start(f32[8,32,128]{2,1,0:T(8,128)S(1)} %get-tuple-element.110), channel_id=1, source_target_pairs={{0,2},{2,0},{4,6},{6,4},{8,10},{10,8},{12,14},{14,12},{16,18},{18,... | collective-permute-start | bytes 393224 | tf_op jit(solution)/shard_map/ppermute | solution.py:987
  3.5 1.3 %collective-permute-start = (f32[2,32,128]{2,1,0:T(8,128)S(1)}, f32[2,32,128]{2,1,0:T(8,128)S(1)}, u32[]{:S(2)}, u32[]{:S(2)}) collective-permute-start(f32[2,32,128]{2,1,0:T(8,128)S(1)} %get-tuple-element.59), channel_id=1, source_target_pairs={{0,2},{2,0},{4,6},{6,4},{8,10},{10,8},{12,14},{14,12},{16,18},{18,... | collective-permute-start | bytes 98312 | tf_op jit(solution)/shard_map/ppermute | solution.py:987
  4.8 1.7 %copy-start.1 = (bf16[2,256,128]{2,1,0:T(8,128)(2,1)S(1)}, bf16[2,256,128]{2,1,0:T(8,128)(2,1)}, u32[]{:S(2)}) copy-start(bf16[2,256,128]{2,1,0:T(8,128)(2,1)} %constant.44.clone.refs_5_.refs_6_.refs_10_) | copy-start | bytes 393220
  4.8 1.7 %copy-start.2 = (bf16[2,256,128]{2,1,0:T(8,128)(2,1)S(1)}, bf16[2,256,128]{2,1,0:T(8,128)(2,1)}, u32[]{:S(2)}) copy-start(bf16[2,256,128]{2,1,0:T(8,128)(2,1)} %constant.45.clone.refs_6_.refs_7_.refs_11_) | copy-start | bytes 393220
  4.8 1.7 %copy-start.18 = (f32[24,72]{1,0:T(8,128)S(1)}, f32[24,72]{1,0:T(8,128)}, u32[]{:S(2)}) copy-start(f32[24,72]{1,0:T(8,128)} %constant.50.clone.refs_7_) | copy-start | bytes 20740
  4.8 1.7 %copy-start.19 = (f32[24,72]{1,0:T(8,128)S(1)}, f32[24,72]{1,0:T(8,128)}, u32[]{:S(2)}) copy-start(f32[24,72]{1,0:T(8,128)} %constant.51.clone.refs_8_) | copy-start | bytes 20740
  5.0 7.6 %collective-permute-start.1 = (f32[152,128]{1,0:T(8,128)S(1)}, f32[152,128]{1,0:T(8,128)S(1)}, u32[]{:S(2)}, u32[]{:S(2)}) collective-permute-start(f32[152,128]{1,0:T(8,128)S(1)} %get-tuple-element.60), channel_id=1, source_target_pairs={{2,4},{3,5},{4,2},{5,3},{6,8},{7,9},{8,6},{9,7},{10,12},{11,13},{1... | collective-permute-start | bytes 233480 | tf_op jit(solution)/shard_map/ppermute | solution.py:988
  6.3 8.2 %collective-permute-start.5 = (f32[152,128]{1,0:T(8,128)S(1)}, f32[152,128]{1,0:T(8,128)S(1)}, u32[]{:S(2)}, u32[]{:S(2)}) collective-permute-start(f32[152,128]{1,0:T(8,128)S(1)} %get-tuple-element.89), channel_id=1, source_target_pairs={{2,5},{3,4},{4,3},{5,2},{6,9},{7,8},{8,7},{9,6},{10,13},{11,12},{1... | collective-permute-start | bytes 233480 | tf_op jit(solution)/shard_map/ppermute | solution.py:988
  8.1 5.0 %collective-permute-start.8 = (f32[144,128]{1,0:T(8,128)S(1)}, f32[144,128]{1,0:T(8,128)S(1)}, u32[]{:S(2)}, u32[]{:S(2)}) collective-permute-start(f32[144,128]{1,0:T(8,128)S(1)} %slice.19), channel_id=1, source_target_pairs={{0,2},{2,0},{4,6},{6,4},{8,10},{10,8},{12,14},{14,12},{16,18},{18,... | collective-permute-start | bytes 221192 | tf_op jit(solution)/shard_map/ppermute | solution.py:987
  11.6 0.7 %copy-start.12 = (f32[24,72]{1,0:T(8,128)S(1)}, f32[24,72]{1,0:T(8,128)}, u32[]{:S(2)}) copy-start(f32[24,72]{1,0:T(8,128)} %constant.49.clone.refs_2_.refs_4_) | copy-start | bytes 20740
  11.6 1.5 %collective-permute-start.6 = (f32[136,128]{1,0:T(8,128)S(1)}, f32[136,128]{1,0:T(8,128)S(1)}, u32[]{:S(2)}, u32[]{:S(2)}) collective-permute-start(f32[136,128]{1,0:T(8,128)S(1)} %slice.17), channel_id=1, source_target_pairs={{0,2},{2,0},{4,6},{6,4},{8,10},{10,8},{12,14},{14,12},{16,18},{18,... | collective-permute-start | bytes 208904 | tf_op jit(solution)/shard_map/ppermute | solution.py:987
  11.7 1.4 %collective-permute-start.7 = (f32[120,128]{1,0:T(8,128)S(1)}, f32[120,128]{1,0:T(8,128)S(1)}, u32[]{:S(2)}, u32[]{:S(2)}) collective-permute-start(f32[120,128]{1,0:T(8,128)S(1)} %slice.18), channel_id=1, source_target_pairs={{0,2},{2,0},{4,6},{6,4},{8,10},{10,8},{12,14},{14,12},{16,18},{18,... | collective-permute-start | bytes 184328 | tf_op jit(solution)/shard_map/ppermute | solution.py:987
  12.3 0.8 %copy-start.16 = (f32[32,96]{1,0:T(8,128)S(1)}, f32[32,96]{1,0:T(8,128)}, u32[]{:S(2)}) copy-start(f32[32,96]{1,0:T(8,128)} %constant.53.clone.refs_8_) | copy-start | bytes 36868
  12.3 0.8 %copy-start.17 = (f32[32,96]{1,0:T(8,128)S(1)}, f32[32,96]{1,0:T(8,128)}, u32[]{:S(2)}) copy-start(f32[32,96]{1,0:T(8,128)} %constant.54.clone.refs_9_) | copy-start | bytes 36868
  12.7 2.2 %copy-start.4 = (bf16[6,256,128]{2,1,0:T(8,128)(2,1)S(1)}, bf16[6,256,128]{2,1,0:T(8,128)(2,1)}, u32[]{:S(2)}) copy-start(bf16[6,256,128]{2,1,0:T(8,128)(2,1)} %constant.61.clone.mz) | copy-start | bytes 1179652
  12.7 2.2 %copy-start.7 = (bf16[2,256,128]{2,1,0:T(8,128)(2,1)S(1)}, bf16[2,256,128]{2,1,0:T(8,128)(2,1)}, u32[]{:S(2)}) copy-start(bf16[2,256,128]{2,1,0:T(8,128)(2,1)} %constant.59.clone.rz) | copy-start | bytes 393220
  12.7 2.2 %copy-start.15 = (f32[24,168]{1,0:T(8,128)S(1)}, f32[24,168]{1,0:T(8,128)}, u32[]{:S(2)}) copy-start(f32[24,168]{1,0:T(8,128)} %constant.60.clone.my) | copy-start | bytes 48388
  12.7 3.0 %collective-permute-start.9 = (f32[152,128]{1,0:T(8,128)S(1)}, f32[152,128]{1,0:T(8,128)S(1)}, u32[]{:S(2)}, u32[]{:S(2)}) collective-permute-start(f32[152,128]{1,0:T(8,128)S(1)} %collective-permute-done.1.refs_0_), channel_id=1, source_target_pairs={{0,2},{2,0},{4,6},{6,4},{8,10},{10,8},{12,14},{14,12},{16,18},{18,... | collective-permute-start | bytes 233480 | tf_op jit(solution)/shard_map/ppermute | solution.py:987
  13.1 1.7 %copy-start.21 = (f32[8,168]{1,0:T(8,128)S(1)}, f32[8,168]{1,0:T(8,128)}, u32[]{:S(2)}) copy-start(f32[8,168]{1,0:T(8,128)} %constant.57.clone.ry) | copy-start | bytes 16132
  14.4 1.3 %collective-permute-start.10 = (f32[152,128]{1,0:T(8,128)S(1)}, f32[152,128]{1,0:T(8,128)S(1)}, u32[]{:S(2)}, u32[]{:S(2)}) collective-permute-start(f32[152,128]{1,0:T(8,128)S(1)} %collective-permute-done.5.refs_1_), channel_id=1, source_target_pairs={{0,2},{2,0},{4,6},{6,4},{8,10},{10,8},{12,14},{14,12},{16,18},{18,... | collective-permute-start | bytes 233480 | tf_op jit(solution)/shard_map/ppermute | solution.py:987
  14.9 1.0 %copy-start.5 = (bf16[2,512,128]{2,1,0:T(8,128)(2,1)S(1)}, bf16[2,512,128]{2,1,0:T(8,128)(2,1)}, u32[]{:S(2)}) copy-start(bf16[2,512,128]{2,1,0:T(8,128)(2,1)} %constant.58.clone.refs_17_) | copy-start | bytes 786436
  14.9 0.9 %copy-start.9 = (f32[56,168]{1,0:T(8,128)S(1)}, f32[56,168]{1,0:T(8,128)}, u32[]{:S(2)}) copy-start(f32[56,168]{1,0:T(8,128)} %constant.47.clone.refs_13_) | copy-start | bytes 112900
  14.9 0.9 %copy-start.10 = (f32[56,168]{1,0:T(8,128)S(1)}, f32[56,168]{1,0:T(8,128)}, u32[]{:S(2)}) copy-start(f32[56,168]{1,0:T(8,128)} %constant.48.clone.refs_14_) | copy-start | bytes 112900
  14.9 0.9 %copy-start.11 = (f32[56,168]{1,0:T(8,128)S(1)}, f32[56,168]{1,0:T(8,128)}, u32[]{:S(2)}) copy-start(f32[56,168]{1,0:T(8,128)} %constant.55.clone.refs_15_) | copy-start | bytes 112900
  14.9 0.9 %copy-start.13 = (f32[10,8,128]{2,1,0:T(8,128)S(1)}, f32[10,8,128]{2,1,0:T(8,128)}, u32[]{:S(2)}) copy-start(f32[10,8,128]{2,1,0:T(8,128)} %constant.64.clone.refs_18_) | copy-start | bytes 122884
  14.9 0.9 %copy-start.14 = (f32[32,168]{1,0:T(8,128)S(1)}, f32[32,168]{1,0:T(8,128)}, u32[]{:S(2)}) copy-start(f32[32,168]{1,0:T(8,128)} %constant.56.clone.refs_16_) | copy-start | bytes 64516
  15.8 5.9 %copy-start.6 = (bf16[2,256,160]{2,1,0:T(8,128)(2,1)S(1)}, bf16[2,256,160]{2,1,0:T(8,128)(2,1)}, u32[]{:S(2)}) copy-start(bf16[2,256,160]{2,1,0:T(8,128)(2,1)} %constant.63.clone.refs_6_) | copy-start | bytes 491524
  15.9 5.9 %copy-start.20 = (f32[2,8,128]{2,1,0:T(8,128)S(1)}, f32[2,8,128]{2,1,0:T(8,128)}, u32[]{:S(2)}) copy-start(f32[2,8,128]{2,1,0:T(8,128)} %constant.62.clone.refs_5_) | copy-start | bytes 24580
  17.4 2.6 %collective-permute-start.11 = (f32[3,8,128]{2,1,0:T(8,128)S(1)}, f32[3,8,128]{2,1,0:T(8,128)S(1)}, u32[]{:S(2)}, u32[]{:S(2)}) collective-permute-start(f32[3,8,128]{2,1,0:T(8,128)S(1)} %get-tuple-element.107), channel_id=1, source_target_pairs={{2,4},{3,5},{4,2},{5,3},{6,8},{7,9},{8,6},{9,7},{10,12},{11,13},{1... | collective-permute-start | bytes 36872 | tf_op jit(solution)/shard_map/ppermute | solution.py:988
  20.0 1.7 %collective-permute-start.12 = (f32[3,8,128]{2,1,0:T(8,128)S(1)}, f32[3,8,128]{2,1,0:T(8,128)S(1)}, u32[]{:S(2)}, u32[]{:S(2)}) collective-permute-start(f32[3,8,128]{2,1,0:T(8,128)S(1)} %collective-permute-done.11.refs_0_), channel_id=1, source_target_pairs={{0,2},{2,0},{4,6},{6,4},{8,10},{10,8},{12,14},{14,12},{16,18},{18,... | collective-permute-start | bytes 36872 | tf_op jit(solution)/shard_map/ppermute | solution.py:987

commit v10 on v9

--- a/solution.py
+++ b/solution.py
@@ -20,7 +20,7 @@
 LANES = 128
 F32 = jnp.float32
 BF16 = jnp.bfloat16
-VMEM_LIMIT = 48 * 1024 * 1024
+VMEM_LIMIT = 24 * 1024 * 1024
 
 
 def legendre_value(points, degree):

time: 23.1 us -> 23.1 us (level)
  no operation moved by 1% of the time
where the time goes in v10:
time: 23.1 us; the launch traced here: 22.8 us
  starting transfers between devices  8.85 us (38%)
  Pallas kernels  6.36 us (28%)
  waiting for transfers between devices  5.35 us (23%)
  other arithmetic  1.04 us (5%)
  between operations  0.91 us (4%)
  local copies, waits for them, and re-layouts  0.33 us (1%)
    ppermute x9, starting transfers between devices, shards(): even = lambda v: lax.ppermute(v, 'dom', swap_pairs(dom, 0))  7.04 us
    pallas_call x8, Pallas kernels, run(): pl.pallas_call(kernel, out_shape=[jax.ShapeDtypeStruct(o, F32) for o in o...  6.36 us
    ppermute x3, waiting for transfers between devices, shards(): lax.ppermute(v, ('dom', 'sub'), chip_pairs(dom, sub, k))  2.54 us
    ppermute x9, waiting for transfers between devices, shards(): even = lambda v: lax.ppermute(v, 'dom', swap_pairs(dom, 0))  2.13 us
    ppermute x3, starting transfers between devices, shards(): lax.ppermute(v, ('dom', 'sub'), chip_pairs(dom, sub, k))  1.51 us
    another operation x1, other arithmetic, shards(): raw = jnp.stack([rhs_local, coefficient])  1.04 us
    ppermute x1, waiting for transfers between devices, shards(): lax.ppermute(pack, 'sub', step)  0.68 us
  transfers between devices with their start and end apart: 13, of which 6 were waited for; matrix products, arithmetic and copies ran while one was open for 0% of the time, Pallas kernels for 15%

profile of v10, /device:TPU:31, one launch (start us, length us, event | category | flops | bytes accessed | tf_op | source)
XLA Modules:
  0.0 22.8 jit_solution(11414151956456483280)
XLA Ops:
  0.6 0.0 copy-start
  0.6 0.0 copy-start.3
  0.7 0.0 copy-start.8
  0.7 1.0 %pad_maximum_fusion.raw.own = f32[2,8,32,128]{3,2,1,0:T(8,128)S(1)} fusion(f32[1,8,32,128]{3,2,1,0:T(8,128)} %bitcast.6, f32[1,8,32,128]{3,2,1,0:T(8,128)} %bitcast.7), kind=kLoop, calls=%fused_computation | loop fusion | flops 65536 | bytes 524288 | tf_op jit(solution)/shard_map/stack | solution.py:990
  1.7 0.0 copy-done
  1.7 0.0 copy-done.3
  1.7 0.0 copy-done.8
  1.7 0.3 %shard_map.239 = (f32[2,32,128]{2,1,0:T(8,128)S(1)}, f32[8,32,128]{2,1,0:T(8,128)S(1)}, f32[8,32,128]{2,1,0:T(8,128)S(1)}, f32[8,32,128]{2,1,0:T(8,128)S(1)}, f32[400,128]{1,0:T(8,128)S(1)}) custom-call(f32[2,8,32,128]{3,2,1,0:T(8,128)S(1)} %pad_maximum_fusion.raw.own, bf16[2,256,128]{2,1,0:T(8,128)(2,1)S(1)} %copy-done, f32[32,96]{1,0:T(8,128)S(1)} %copy-done.8, ...), custom_call_target="tpu_custom_call" | custom-call | flops 1 | bytes 1 | tf_op jit(solution)/shard_map/pallas_call | solution.py:949
  2.1 0.3 %collective-permute-start.2 = (f32[400,128]{1,0:T(8,128)S(1)}, f32[400,128]{1,0:T(8,128)S(1)}, u32[]{:S(2)}, u32[]{:S(2)}) collective-permute-start(f32[400,128]{1,0:T(8,128)S(1)} %get-tuple-element.61), channel_id=1, source_target_pairs={{0,1},{1,0},{2,3},{3,2},{4,5},{5,4},{6,7},{7,6},{8,9},{9,8},{10,11... | collective-permute-start | bytes 614408 | tf_op jit(solution)/shard_map/ppermute | solution.py:1006
  2.4 1.0 %collective-permute-start.3 = (f32[8,32,128]{2,1,0:T(8,128)S(1)}, f32[8,32,128]{2,1,0:T(8,128)S(1)}, u32[]{:S(2)}, u32[]{:S(2)}) collective-permute-start(f32[8,32,128]{2,1,0:T(8,128)S(1)} %get-tuple-element.111), channel_id=1, source_target_pairs={{0,2},{2,0},{4,6},{6,4},{8,10},{10,8},{12,14},{14,12},{16,18},{18,... | collective-permute-start | bytes 393224 | tf_op jit(solution)/shard_map/ppermute | solution.py:987
  3.4 0.1 collective-permute-start.4
  3.5 0.4 %collective-permute-start = (f32[2,32,128]{2,1,0:T(8,128)S(1)}, f32[2,32,128]{2,1,0:T(8,128)S(1)}, u32[]{:S(2)}, u32[]{:S(2)}) collective-permute-start(f32[2,32,128]{2,1,0:T(8,128)S(1)} %get-tuple-element.59), channel_id=1, source_target_pairs={{0,2},{2,0},{4,6},{6,4},{8,10},{10,8},{12,14},{14,12},{16,18},{18,... | collective-permute-start | bytes 98312 | tf_op jit(solution)/shard_map/ppermute | solution.py:987
  3.9 0.9 %collective-permute-done.face = f32[2,32,128]{2,1,0:T(8,128)S(1)} collective-permute-done((f32[2,32,128]{2,1,0:T(8,128)S(1)}, f32[2,32,128]{2,1,0:T(8,128)S(1)}, u32[]{:S(2)}, u32[]{:S(2)}) %collective-permute-start) | collective-permute-done | bytes 32800 | tf_op jit(solution)/shard_map/ppermute | solution.py:987
  4.8 0.2 shard_map.240
  5.0 1.3 %collective-permute-start.1 = (f32[152,128]{1,0:T(8,128)S(1)}, f32[152,128]{1,0:T(8,128)S(1)}, u32[]{:S(2)}, u32[]{:S(2)}) collective-permute-start(f32[152,128]{1,0:T(8,128)S(1)} %get-tuple-element.60), channel_id=1, source_target_pairs={{2,4},{3,5},{4,2},{5,3},{6,8},{7,9},{8,6},{9,7},{10,12},{11,13},{1... | collective-permute-start | bytes 233480 | tf_op jit(solution)/shard_map/ppermute | solution.py:988
  6.3 0.2 collective-permute-start.5
  6.5 0.0 collective-permute-done.3.refs_0_
  6.5 0.0 collective-permute-done.4.refs_1_
  6.5 0.0 copy-done.1
  6.5 0.0 copy-done.2
  6.5 0.0 copy-done.18
  6.5 0.0 copy-done.19
  6.5 0.9 %shard_map.241 = (f32[16,56,128]{2,1,0:T(8,128)S(1)}, f32[16,56,128]{2,1,0:T(8,128)S(1)}, f32[16,56,128]{2,1,0:T(8,128)S(1)}, f32[16,56,128]{2,1,0:T(8,128)S(1)}...) custom-call(f32[2,8,32,128]{3,2,1,0:T(8,128)S(1)} %pad_maximum_fusio, ...), custom_call_target="tpu_custom_call" | custom-call | flops 1 | bytes 1 | tf_op jit(solution)/shard_map/pallas_call | solution.py:949
  7.4 0.7 %collective-permute-done.2.refs_0_ = f32[400,128]{1,0:T(8,128)S(1)} collective-permute-done((f32[400,128]{1,0:T(8,128)S(1)}, f32[400,128]{1,0:T(8,128)S(1)}, u32[]{:S(2)}, u32[]{:S(2)}) %collective-permute-start.2) | collective-permute-done | bytes 204832 | tf_op jit(solution)/shard_map/ppermute | solution.py:1006
  8.1 3.5 %collective-permute-start.8 = (f32[144,128]{1,0:T(8,128)S(1)}, f32[144,128]{1,0:T(8,128)S(1)}, u32[]{:S(2)}, u32[]{:S(2)}) collective-permute-start(f32[144,128]{1,0:T(8,128)S(1)} %slice.19), channel_id=1, source_target_pairs={{0,2},{2,0},{4,6},{6,4},{8,10},{10,8},{12,14},{14,12},{16,18},{18,... | collective-permute-start | bytes 221192 | tf_op jit(solution)/shard_map/ppermute | solution.py:987
  11.6 0.1 collective-permute-start.6
  11.7 0.5 %collective-permute-start.7 = (f32[120,128]{1,0:T(8,128)S(1)}, f32[120,128]{1,0:T(8,128)S(1)}, u32[]{:S(2)}, u32[]{:S(2)}) collective-permute-start(f32[120,128]{1,0:T(8,128)S(1)} %slice.18), channel_id=1, source_target_pairs={{0,2},{2,0},{4,6},{6,4},{8,10},{10,8},{12,14},{14,12},{16,18},{18,... | collective-permute-start | bytes 184328 | tf_op jit(solution)/shard_map/ppermute | solution.py:987
  12.2 0.1 copy-done.12
  12.3 0.3 %shard_map.242 = (f32[16,56,128]{2,1,0:T(8,128)S(1)}, f32[16,56,128]{2,1,0:T(8,128)S(1)}, f32[16,56,128]{2,1,0:T(8,128)S(1)}, f32[16,56,128]{2,1,0:T(8,128)S(1)}...) custom-call(f32[400,128]{1,0:T(8,128)S(1)} %collective-permute-done., ...), custom_call_target="tpu_custom_call", output_to_operand_aliasing={{0}: (4, {}), {1}: (5, {}), {2}: (6, {}), {3}: (7, {}), {4}... | custom-call | flops 1 | bytes 1 | tf_op jit(solution)/shard_map/pallas_call | solution.py:949
  12.7 0.0 collective-permute-done.1.refs_0_
  12.7 0.0 copy-start.4
  12.7 0.0 copy-start.7
  12.7 0.0 copy-start.15
  12.7 0.1 collective-permute-start.9
  12.8 0.3 %collective-permute-done.7.refs_1_ = f32[120,128]{1,0:T(8,128)S(1)} collective-permute-done((f32[120,128]{1,0:T(8,128)S(1)}, f32[120,128]{1,0:T(8,128)S(1)}, u32[]{:S(2)}, u32[]{:S(2)}) %collective-permute-start.7) | collective-permute-done | bytes 61472 | tf_op jit(solution)/shard_map/ppermute | solution.py:987
  13.1 0.0 collective-permute-done.6.refs_0_
  13.1 0.0 collective-permute-done.8.refs_2_
  13.1 0.0 copy-done.16
  13.1 0.0 copy-done.17
  13.1 0.0 copy-start.21
  13.2 1.3 %shard_map.243 = (f32[16,56,128]{2,1,0:T(8,128)S(1)}, f32[16,56,128]{2,1,0:T(8,128)S(1)}, f32[16,56,128]{2,1,0:T(8,128)S(1)}, f32[16,56,128]{2,1,0:T(8,128)S(1)}...) custom-call(f32[136,128]{1,0:T(8,128)S(1)} %collective-permute-done., ...), custom_call_target="tpu_custom_call", output_to_operand_aliasing={{0}: (10, {}), {1}: (11, {}), {2}: (12, {}), {3}: (13, {}),... | custom-call | flops 1 | bytes 1 | tf_op jit(solution)/shard_map/pallas_call | solution.py:949
  14.4 0.0 collective-permute-done.5.refs_1_
  14.4 0.4 %collective-permute-start.10 = (f32[152,128]{1,0:T(8,128)S(1)}, f32[152,128]{1,0:T(8,128)S(1)}, u32[]{:S(2)}, u32[]{:S(2)}) collective-permute-start(f32[152,128]{1,0:T(8,128)S(1)} %collective-permute-done.5.refs_1_), channel_id=1, source_target_pairs={{0,2},{2,0},{4,6},{6,4},{8,10},{10,8},{12,14},{14,12},{16,18},{18,... | collective-permute-start | bytes 233480 | tf_op jit(solution)/shard_map/ppermute | solution.py:987
  14.9 0.0 copy-done.15
  14.9 0.0 copy-start.5
  14.9 0.0 copy-start.9
  14.9 0.0 copy-start.10
  14.9 0.0 copy-start.11
  14.9 0.0 copy-start.13
  14.9 0.0 copy-start.14
  14.9 0.8 %shard_map.244 = (f32[2,27,8,128]{3,2,1,0:T(8,128)S(1)}, f32[4,8,128]{2,1,0:T(8,128)S(1)}) custom-call(f32[16,56,128]{2,1,0:T(8,128)S(1)} %get-tuple-element.100.w_ref.refs_4_, f32[16,56,128]{2,1,0:T(8,128)S(1)} %get-tuple-element.104.rhs_ref, f32[24,168]{1,0:T(8,128)S(1)} %copy-done.15, bf16[6,256,128]{2,1,0:T(8,128)(2,1)S(1)} %copy-done.4, ...), custom_call_target="tpu_custom_call" | custom-call | flops 1 | bytes 1 | tf_op jit(solution)/shard_map/pallas_call | solution.py:949
  15.7 0.0 collective-permute-done.9.refs_2_
  15.7 0.1 collective-permute-done.10.refs_3_
  15.8 0.0 copy-done.5
  15.8 0.0 copy-done.13
  15.8 0.0 copy-done.14
  15.8 0.0 copy-start.6
  15.9 0.0 copy-start.20
  15.9 1.6 %shard_map.245 = (f32[8,32,128]{2,1,0:T(8,128)S(1)}, f32[3,8,128]{2,1,0:T(8,128)S(1)}, f32[10,8,128]{2,1,0:T(8,128)S(1)}) custom-call(f32[152,128]{1,0:T(8,128)S(1)} %collective-permute-done.1.refs_0_, f32[152,128]{1,0:T(8,128)S(1)} %collective-permute-done.5.refs_1_, f32[152,128]{1,0:T(8,128)S(1)} %collective-permute-done.9.refs_2_, ...), custom_call_target="tpu_custom_call" | custom-call | flops 1 | bytes 1 | tf_op jit(solution)/shard_map/pallas_call | solution.py:949
  17.4 0.0 collective-permute-start.11
  17.5 2.5 %collective-permute-done.11.refs_0_ = f32[3,8,128]{2,1,0:T(8,128)S(1)} collective-permute-done((f32[3,8,128]{2,1,0:T(8,128)S(1)}, f32[3,8,128]{2,1,0:T(8,128)S(1)}, u32[]{:S(2)}, u32[]{:S(2)}) %collective-permute-start.11) | collective-permute-done | bytes 12320 | tf_op jit(solution)/shard_map/ppermute | solution.py:988
  20.0 0.9 %collective-permute-start.12 = (f32[3,8,128]{2,1,0:T(8,128)S(1)}, f32[3,8,128]{2,1,0:T(8,128)S(1)}, u32[]{:S(2)}, u32[]{:S(2)}) collective-permute-start(f32[3,8,128]{2,1,0:T(8,128)S(1)} %collective-permute-done.11.refs_0_), channel_id=1, source_target_pairs={{0,2},{2,0},{4,6},{6,4},{8,10},{10,8},{12,14},{14,12},{16,18},{18,... | collective-permute-start | bytes 36872 | tf_op jit(solution)/shard_map/ppermute | solution.py:987
  20.9 0.8 %collective-permute-done.12.refs_1_ = f32[3,8,128]{2,1,0:T(8,128)S(1)} collective-permute-done((f32[3,8,128]{2,1,0:T(8,128)S(1)}, f32[3,8,128]{2,1,0:T(8,128)S(1)}, u32[]{:S(2)}, u32[]{:S(2)}) %collective-permute-start.12) | collective-permute-done | bytes 12320 | tf_op jit(solution)/shard_map/ppermute | solution.py:987
  21.7 1.1 %shard_map.246 = (f32[8,32,128]{2,1,0:T(8,128)}, f32[2,8,32]{2,1,0:T(8,128)}) custom-call(f32[3,8,128]{2,1,0:T(8,128)S(1)} %collective-permute-done.11.refs_0_, f32[3,8,128]{2,1,0:T(8,128)S(1)} %collective-permute-done.12.refs_1_, f32[8,32,128]{2,1,0:T(8,128)S(1)} %get-tuple-element.108.refs_2_, f32[10,8,128]{2,1,0:T(8,128)S(1)} %get-tuple-element.109.refs_3_, ...), custom_call_target="tpu_custom_call" | custom-call | flops 1 | bytes 1 | tf_op jit(solution)/shard_map/pallas_call | solution.py:949
  (19 shorter events, 0.1 us)
Async XLA Ops:
  0.6 1.1 %copy-start = (bf16[2,256,128]{2,1,0:T(8,128)(2,1)S(1)}, bf16[2,256,128]{2,1,0:T(8,128)(2,1)}, u32[]{:S(2)}) copy-start(bf16[2,256,128]{2,1,0:T(8,128)(2,1)} %constant.46.clone.z_sq.refs_2_.refs_1_.refs_3_.refs_12_) | copy-start | bytes 393220
  0.6 1.1 %copy-start.3 = (f32[8,8,128]{2,1,0:T(8,128)S(1)}, f32[8,8,128]{2,1,0:T(8,128)}, u32[]{:S(2)}) copy-start(f32[8,8,128]{2,1,0:T(8,128)} %constant.65.clone.w3.refs_4_.refs_3_.refs_5_) | copy-start | bytes 98308
  0.7 1.1 %copy-start.8 = (f32[32,96]{1,0:T(8,128)S(1)}, f32[32,96]{1,0:T(8,128)}, u32[]{:S(2)}) copy-start(f32[32,96]{1,0:T(8,128)} %constant.52.clone.y_sq.refs_3_) | copy-start | bytes 36868
  2.1 6.0 %collective-permute-start.2 = (f32[400,128]{1,0:T(8,128)S(1)}, f32[400,128]{1,0:T(8,128)S(1)}, u32[]{:S(2)}, u32[]{:S(2)}) collective-permute-start(f32[400,128]{1,0:T(8,128)S(1)} %get-tuple-element.61), channel_id=1, source_target_pairs={{0,1},{1,0},{2,3},{3,2},{4,5},{5,4},{6,7},{7,6},{8,9},{9,8},{10,11... | collective-permute-start | bytes 614408 | tf_op jit(solution)/shard_map/ppermute | solution.py:1006
  2.4 4.1 %collective-permute-start.3 = (f32[8,32,128]{2,1,0:T(8,128)S(1)}, f32[8,32,128]{2,1,0:T(8,128)S(1)}, u32[]{:S(2)}, u32[]{:S(2)}) collective-permute-start(f32[8,32,128]{2,1,0:T(8,128)S(1)} %get-tuple-element.111), channel_id=1, source_target_pairs={{0,2},{2,0},{4,6},{6,4},{8,10},{10,8},{12,14},{14,12},{16,18},{18,... | collective-permute-start | bytes 393224 | tf_op jit(solution)/shard_map/ppermute | solution.py:987
  3.4 3.1 %collective-permute-start.4 = (f32[8,32,128]{2,1,0:T(8,128)S(1)}, f32[8,32,128]{2,1,0:T(8,128)S(1)}, u32[]{:S(2)}, u32[]{:S(2)}) collective-permute-start(f32[8,32,128]{2,1,0:T(8,128)S(1)} %get-tuple-element.110), channel_id=1, source_target_pairs={{0,2},{2,0},{4,6},{6,4},{8,10},{10,8},{12,14},{14,12},{16,18},{18,... | collective-permute-start | bytes 393224 | tf_op jit(solution)/shard_map/ppermute | solution.py:987
  3.5 1.3 %collective-permute-start = (f32[2,32,128]{2,1,0:T(8,128)S(1)}, f32[2,32,128]{2,1,0:T(8,128)S(1)}, u32[]{:S(2)}, u32[]{:S(2)}) collective-permute-start(f32[2,32,128]{2,1,0:T(8,128)S(1)} %get-tuple-element.59), channel_id=1, source_target_pairs={{0,2},{2,0},{4,6},{6,4},{8,10},{10,8},{12,14},{14,12},{16,18},{18,... | collective-permute-start | bytes 98312 | tf_op jit(solution)/shard_map/ppermute | solution.py:987
  4.8 1.7 %copy-start.1 = (bf16[2,256,128]{2,1,0:T(8,128)(2,1)S(1)}, bf16[2,256,128]{2,1,0:T(8,128)(2,1)}, u32[]{:S(2)}) copy-start(bf16[2,256,128]{2,1,0:T(8,128)(2,1)} %constant.44.clone.refs_5_.refs_6_.refs_10_) | copy-start | bytes 393220
  4.8 1.7 %copy-start.2 = (bf16[2,256,128]{2,1,0:T(8,128)(2,1)S(1)}, bf16[2,256,128]{2,1,0:T(8,128)(2,1)}, u32[]{:S(2)}) copy-start(bf16[2,256,128]{2,1,0:T(8,128)(2,1)} %constant.45.clone.refs_6_.refs_7_.refs_11_) | copy-start | bytes 393220
  4.8 1.7 %copy-start.18 = (f32[24,72]{1,0:T(8,128)S(1)}, f32[24,72]{1,0:T(8,128)}, u32[]{:S(2)}) copy-start(f32[24,72]{1,0:T(8,128)} %constant.50.clone.refs_7_) | copy-start | bytes 20740
  4.8 1.7 %copy-start.19 = (f32[24,72]{1,0:T(8,128)S(1)}, f32[24,72]{1,0:T(8,128)}, u32[]{:S(2)}) copy-start(f32[24,72]{1,0:T(8,128)} %constant.51.clone.refs_8_) | copy-start | bytes 20740
  5.0 7.6 %collective-permute-start.1 = (f32[152,128]{1,0:T(8,128)S(1)}, f32[152,128]{1,0:T(8,128)S(1)}, u32[]{:S(2)}, u32[]{:S(2)}) collective-permute-start(f32[152,128]{1,0:T(8,128)S(1)} %get-tuple-element.60), channel_id=1, source_target_pairs={{2,4},{3,5},{4,2},{5,3},{6,8},{7,9},{8,6},{9,7},{10,12},{11,13},{1... | collective-permute-start | bytes 233480 | tf_op jit(solution)/shard_map/ppermute | solution.py:988
  6.3 8.2 %collective-permute-start.5 = (f32[152,128]{1,0:T(8,128)S(1)}, f32[152,128]{1,0:T(8,128)S(1)}, u32[]{:S(2)}, u32[]{:S(2)}) collective-permute-start(f32[152,128]{1,0:T(8,128)S(1)} %get-tuple-element.89), channel_id=1, source_target_pairs={{2,5},{3,4},{4,3},{5,2},{6,9},{7,8},{8,7},{9,6},{10,13},{11,12},{1... | collective-permute-start | bytes 233480 | tf_op jit(solution)/shard_map/ppermute | solution.py:988
  8.1 5.0 %collective-permute-start.8 = (f32[144,128]{1,0:T(8,128)S(1)}, f32[144,128]{1,0:T(8,128)S(1)}, u32[]{:S(2)}, u32[]{:S(2)}) collective-permute-start(f32[144,128]{1,0:T(8,128)S(1)} %slice.19), channel_id=1, source_target_pairs={{0,2},{2,0},{4,6},{6,4},{8,10},{10,8},{12,14},{14,12},{16,18},{18,... | collective-permute-start | bytes 221192 | tf_op jit(solution)/shard_map/ppermute | solution.py:987
  11.6 0.7 %copy-start.12 = (f32[24,72]{1,0:T(8,128)S(1)}, f32[24,72]{1,0:T(8,128)}, u32[]{:S(2)}) copy-start(f32[24,72]{1,0:T(8,128)} %constant.49.clone.refs_2_.refs_4_) | copy-start | bytes 20740
  11.6 1.5 %collective-permute-start.6 = (f32[136,128]{1,0:T(8,128)S(1)}, f32[136,128]{1,0:T(8,128)S(1)}, u32[]{:S(2)}, u32[]{:S(2)}) collective-permute-start(f32[136,128]{1,0:T(8,128)S(1)} %slice.17), channel_id=1, source_target_pairs={{0,2},{2,0},{4,6},{6,4},{8,10},{10,8},{12,14},{14,12},{16,18},{18,... | collective-permute-start | bytes 208904 | tf_op jit(solution)/shard_map/ppermute | solution.py:987
  11.7 1.4 %collective-permute-start.7 = (f32[120,128]{1,0:T(8,128)S(1)}, f32[120,128]{1,0:T(8,128)S(1)}, u32[]{:S(2)}, u32[]{:S(2)}) collective-permute-start(f32[120,128]{1,0:T(8,128)S(1)} %slice.18), channel_id=1, source_target_pairs={{0,2},{2,0},{4,6},{6,4},{8,10},{10,8},{12,14},{14,12},{16,18},{18,... | collective-permute-start | bytes 184328 | tf_op jit(solution)/shard_map/ppermute | solution.py:987
  12.3 0.8 %copy-start.16 = (f32[32,96]{1,0:T(8,128)S(1)}, f32[32,96]{1,0:T(8,128)}, u32[]{:S(2)}) copy-start(f32[32,96]{1,0:T(8,128)} %constant.53.clone.refs_8_) | copy-start | bytes 36868
  12.3 0.8 %copy-start.17 = (f32[32,96]{1,0:T(8,128)S(1)}, f32[32,96]{1,0:T(8,128)}, u32[]{:S(2)}) copy-start(f32[32,96]{1,0:T(8,128)} %constant.54.clone.refs_9_) | copy-start | bytes 36868
  12.7 2.2 %copy-start.4 = (bf16[6,256,128]{2,1,0:T(8,128)(2,1)S(1)}, bf16[6,256,128]{2,1,0:T(8,128)(2,1)}, u32[]{:S(2)}) copy-start(bf16[6,256,128]{2,1,0:T(8,128)(2,1)} %constant.61.clone.mz) | copy-start | bytes 1179652
  12.7 2.2 %copy-start.7 = (bf16[2,256,128]{2,1,0:T(8,128)(2,1)S(1)}, bf16[2,256,128]{2,1,0:T(8,128)(2,1)}, u32[]{:S(2)}) copy-start(bf16[2,256,128]{2,1,0:T(8,128)(2,1)} %constant.59.clone.rz) | copy-start | bytes 393220
  12.7 2.2 %copy-start.15 = (f32[24,168]{1,0:T(8,128)S(1)}, f32[24,168]{1,0:T(8,128)}, u32[]{:S(2)}) copy-start(f32[24,168]{1,0:T(8,128)} %constant.60.clone.my) | copy-start | bytes 48388
  12.7 3.0 %collective-permute-start.9 = (f32[152,128]{1,0:T(8,128)S(1)}, f32[152,128]{1,0:T(8,128)S(1)}, u32[]{:S(2)}, u32[]{:S(2)}) collective-permute-start(f32[152,128]{1,0:T(8,128)S(1)} %collective-permute-done.1.refs_0_), channel_id=1, source_target_pairs={{0,2},{2,0},{4,6},{6,4},{8,10},{10,8},{12,14},{14,12},{16,18},{18,... | collective-permute-start | bytes 233480 | tf_op jit(solution)/shard_map/ppermute | solution.py:987
  13.1 1.7 %copy-start.21 = (f32[8,168]{1,0:T(8,128)S(1)}, f32[8,168]{1,0:T(8,128)}, u32[]{:S(2)}) copy-start(f32[8,168]{1,0:T(8,128)} %constant.57.clone.ry) | copy-start | bytes 16132
  14.4 1.3 %collective-permute-start.10 = (f32[152,128]{1,0:T(8,128)S(1)}, f32[152,128]{1,0:T(8,128)S(1)}, u32[]{:S(2)}, u32[]{:S(2)}) collective-permute-start(f32[152,128]{1,0:T(8,128)S(1)} %collective-permute-done.5.refs_1_), channel_id=1, source_target_pairs={{0,2},{2,0},{4,6},{6,4},{8,10},{10,8},{12,14},{14,12},{16,18},{18,... | collective-permute-start | bytes 233480 | tf_op jit(solution)/shard_map/ppermute | solution.py:987
  14.9 1.0 %copy-start.5 = (bf16[2,512,128]{2,1,0:T(8,128)(2,1)S(1)}, bf16[2,512,128]{2,1,0:T(8,128)(2,1)}, u32[]{:S(2)}) copy-start(bf16[2,512,128]{2,1,0:T(8,128)(2,1)} %constant.58.clone.refs_17_) | copy-start | bytes 786436
  14.9 0.9 %copy-start.9 = (f32[56,168]{1,0:T(8,128)S(1)}, f32[56,168]{1,0:T(8,128)}, u32[]{:S(2)}) copy-start(f32[56,168]{1,0:T(8,128)} %constant.47.clone.refs_13_) | copy-start | bytes 112900
  14.9 0.9 %copy-start.10 = (f32[56,168]{1,0:T(8,128)S(1)}, f32[56,168]{1,0:T(8,128)}, u32[]{:S(2)}) copy-start(f32[56,168]{1,0:T(8,128)} %constant.48.clone.refs_14_) | copy-start | bytes 112900
  14.9 0.9 %copy-start.11 = (f32[56,168]{1,0:T(8,128)S(1)}, f32[56,168]{1,0:T(8,128)}, u32[]{:S(2)}) copy-start(f32[56,168]{1,0:T(8,128)} %constant.55.clone.refs_15_) | copy-start | bytes 112900
  14.9 0.9 %copy-start.13 = (f32[10,8,128]{2,1,0:T(8,128)S(1)}, f32[10,8,128]{2,1,0:T(8,128)}, u32[]{:S(2)}) copy-start(f32[10,8,128]{2,1,0:T(8,128)} %constant.64.clone.refs_18_) | copy-start | bytes 122884
  14.9 0.9 %copy-start.14 = (f32[32,168]{1,0:T(8,128)S(1)}, f32[32,168]{1,0:T(8,128)}, u32[]{:S(2)}) copy-start(f32[32,168]{1,0:T(8,128)} %constant.56.clone.refs_16_) | copy-start | bytes 64516
  15.8 5.9 %copy-start.6 = (bf16[2,256,160]{2,1,0:T(8,128)(2,1)S(1)}, bf16[2,256,160]{2,1,0:T(8,128)(2,1)}, u32[]{:S(2)}) copy-start(bf16[2,256,160]{2,1,0:T(8,128)(2,1)} %constant.63.clone.refs_6_) | copy-start | bytes 491524
  15.9 5.9 %copy-start.20 = (f32[2,8,128]{2,1,0:T(8,128)S(1)}, f32[2,8,128]{2,1,0:T(8,128)}, u32[]{:S(2)}) copy-start(f32[2,8,128]{2,1,0:T(8,128)} %constant.62.clone.refs_5_) | copy-start | bytes 24580
  17.4 2.6 %collective-permute-start.11 = (f32[3,8,128]{2,1,0:T(8,128)S(1)}, f32[3,8,128]{2,1,0:T(8,128)S(1)}, u32[]{:S(2)}, u32[]{:S(2)}) collective-permute-start(f32[3,8,128]{2,1,0:T(8,128)S(1)} %get-tuple-element.107), channel_id=1, source_target_pairs={{2,4},{3,5},{4,2},{5,3},{6,8},{7,9},{8,6},{9,7},{10,12},{11,13},{1... | collective-permute-start | bytes 36872 | tf_op jit(solution)/shard_map/ppermute | solution.py:988
  20.0 1.7 %collective-permute-start.12 = (f32[3,8,128]{2,1,0:T(8,128)S(1)}, f32[3,8,128]{2,1,0:T(8,128)S(1)}, u32[]{:S(2)}, u32[]{:S(2)}) collective-permute-start(f32[3,8,128]{2,1,0:T(8,128)S(1)} %collective-permute-done.11.refs_0_), channel_id=1, source_target_pairs={{0,2},{2,0},{4,6},{6,4},{8,10},{10,8},{12,14},{14,12},{16,18},{18,... | collective-permute-start | bytes 36872 | tf_op jit(solution)/shard_map/ppermute | solution.py:987
